TPU v7x, 32 devices: a whole 2x2x4 slice. The times are simulated.
32 devices in a mesh: section: 4 (over y, x), seq: 4 (over z), mp: 2 (over core).
Axes of the slice: x: 2, y: 2, z: 4, core: 2. Of those that a mesh axis runs over, the one named last changes fastest.
Arguments:
- query_rows: bfloat16 [4, 512, 2048], P('section', 'seq', 'mp'), may hold values from -150 to 150
- key_row_matrix: bfloat16 [4, 512, 1024], P('section', 'seq', 'mp'), may hold values from -13 to 13
- value_row_matrix: bfloat16 [4, 512, 1024], P('section', 'seq', 'mp'), may hold values from -6 to 6
- out_grad: bfloat16 [4, 512, 2048], P('section', 'seq', 'mp'), may hold values from -24 to 24
- w_query: bfloat16 [4, 5376, 2048], P('section', 'seq', 'mp'), may hold values from -0.078125 to 0.078125
- key_weight: bfloat16 [4, 5376, 1024], P('section', 'seq', 'mp'), may hold values from -0.078125 to 0.078125
- value_weight: bfloat16 [4, 5376, 1024], P('section', 'seq', 'mp'), may hold values from -0.078125 to 0.078125
- doc_ids: int32 [4, 512], P('section'), may hold values from 0 to 5, never falling along the last dimension, each value on 1 to 170 neighbouring positions
Outputs:
- upstream: bfloat16 [4, 512, 5376], P('section', None, ('seq', 'mp'))
All inputs are finite; a program needn't handle non-finite values.
Results may differ from a plain program's by a relative error of at most 0.0071.
Values may be sent and summed in bfloat16 or wider, within the bound.
No kernel may reach another device: no remote copies, remote signals or barrier semaphores. Data moves between devices by JAX's collectives and lax.ppermute only.
A program may use at most 64 MiB of HBM per device.

v0:
```python
from functools import reduce
import math

import jax
import jax.numpy as jnp
from jax import lax
from jax.sharding import PartitionSpec as P

HEAD_WIDTH = 128
WINDOW = 512


def from_behind(shard, axis, by):
    size = lax.axis_size(axis)
    pairs = [(i, i + by) for i in range(size) if 0 <= i + by < size]
    return lax.ppermute(shard, axis, pairs)


def passed_along(block, axis, distance):
    devices = range(lax.axis_size(axis))
    route = [((i - distance) % len(devices), i) for i in devices]
    return lax.ppermute(block, axis, route)


def per_device(
    query_rows,
    key_row_matrix,
    value_row_matrix,
    out_grad,
    w_query,
    key_weight,
    value_weight,
    doc_ids,
):
    query_here = query_rows[0]
    key_here = key_row_matrix[0]
    value_here = value_row_matrix[0]
    grad_here = out_grad[0]
    documents = doc_ids[0]
    row_count = query_here.shape[0]
    kv_cols = key_here.shape[1]
    kv_heads = kv_cols // HEAD_WIDTH
    group_width = query_here.shape[1] // kv_cols
    scaling = 1.0 / math.sqrt(HEAD_WIDTH)
    seq_count = lax.axis_size("seq")
    seq_place = lax.axis_index("seq")
    reach_now = min((WINDOW - 1) // row_count + 1, seq_count - 1)
    kv_local = jnp.concatenate([key_here, value_here], axis=1)
    rim_blocks = [from_behind(kv_local, "seq", distance) for distance in range(reach_now, 0, -1)]
    kv_blocks = rim_blocks + [kv_local]
    block_total = len(kv_blocks)
    span_rows = block_total * row_count
    first_row = seq_place * row_count
    padded_docs = jnp.concatenate([jnp.full((reach_now * row_count,), -1, jnp.int32), documents])
    key_docs = lax.dynamic_slice_in_dim(padded_docs, first_row, span_rows, 0)
    query_docs = lax.dynamic_slice_in_dim(documents, first_row, row_count, 0)
    query_pos = first_row + jnp.arange(row_count, dtype=jnp.int32)
    key_pos = first_row - reach_now * row_count + jnp.arange(span_rows, dtype=jnp.int32)
    offset = query_pos[:, None] - key_pos[None, :]
    allowed = (query_docs[:, None] == key_docs[None, :]) & (offset >= 0) & (offset < WINDOW)
    query_split = query_here.reshape(row_count, kv_heads, group_width, HEAD_WIDTH)
    grad_split = grad_here.reshape(row_count, kv_heads, group_width, HEAD_WIDTH)
    block_masks = [
        allowed[:, block_index * row_count : (block_index + 1) * row_count]
        for block_index in range(block_total)
    ]
    block_keys = [
        kv_block[:, :kv_cols].reshape(row_count, kv_heads, HEAD_WIDTH) for kv_block in kv_blocks
    ]
    block_values = [
        kv_block[:, kv_cols:].reshape(row_count, kv_heads, HEAD_WIDTH) for kv_block in kv_blocks
    ]

    def score_pair(key_block, mask_now):

        def make_fn():
            product = (
                jnp.einsum(
                    "igrd,jgd->grij", query_split, key_block, preferred_element_type=jnp.float32
                )
                * scaling
            )
            return jnp.where(mask_now[None, None], product, -jnp.inf)

        def empty_fn():
            return jnp.full((kv_heads, group_width, row_count, row_count), -jnp.inf, jnp.float32)

        return (make_fn, empty_fn)

    scores = []
    for block_index in range(block_total):
        make_fn, empty_fn = score_pair(block_keys[block_index], block_masks[block_index])
        scores.append(make_fn())
    row_max = reduce(
        jnp.maximum, [jnp.max(score_now, axis=-1, keepdims=True) for score_now in scores]
    )
    raised = [jnp.exp(score_now - row_max) for score_now in scores]
    row_total = reduce(
        jnp.add, [jnp.sum(raised_now, axis=-1, keepdims=True) for raised_now in raised]
    )
    weights_full = [raised_now / row_total for raised_now in raised]
    weights_half = [weight_now.astype(jnp.bfloat16) for weight_now in weights_full]

    def value_pair(weight_half, value_block):

        def make_fn():
            return jnp.einsum(
                "grij,jgd->igrd", weight_half, value_block, preferred_element_type=jnp.float32
            )

        def empty_fn():
            return jnp.zeros((row_count, kv_heads, group_width, HEAD_WIDTH), jnp.float32)

        return (make_fn, empty_fn)

    attended_terms = []
    for block_index in range(block_total):
        make_fn, empty_fn = value_pair(weights_half[block_index], block_values[block_index])
        attended_terms.append(make_fn())
    attended = reduce(jnp.add, attended_terms)
    delta_row = jnp.transpose(
        jnp.sum(grad_split.astype(jnp.float32) * attended, axis=-1), (1, 2, 0)
    )

    def grad_pair(weight_full, weight_half, key_block, value_block):

        def make_fn():
            grad_weights = jnp.einsum(
                "igrd,jgd->grij", grad_split, value_block, preferred_element_type=jnp.float32
            )
            grad_scores = (weight_full * (grad_weights - delta_row[..., None])).astype(jnp.bfloat16)
            query_term = jnp.einsum(
                "grij,jgd->igrd", grad_scores, key_block, preferred_element_type=jnp.float32
            )
            key_term = (
                jnp.einsum(
                    "grij,igrd->jgd", grad_scores, query_split, preferred_element_type=jnp.float32
                )
                * scaling
            )
            value_term = jnp.einsum(
                "grij,igrd->jgd", weight_half, grad_split, preferred_element_type=jnp.float32
            )
            kv_term = jnp.concatenate(
                [key_term.reshape(row_count, kv_cols), value_term.reshape(row_count, kv_cols)],
                axis=1,
            )
            return (query_term, kv_term)

        def empty_fn():
            return (
                jnp.zeros((row_count, kv_heads, group_width, HEAD_WIDTH), jnp.float32),
                jnp.zeros((row_count, 2 * kv_cols), jnp.float32),
            )

        return (make_fn, empty_fn)

    query_terms = []
    kv_terms = []
    for block_index in range(block_total):
        make_fn, empty_fn = grad_pair(
            weights_full[block_index],
            weights_half[block_index],
            block_keys[block_index],
            block_values[block_index],
        )
        query_term, kv_term = make_fn()
        query_terms.append(query_term)
        kv_terms.append(kv_term)
    query_grad = (
        (reduce(jnp.add, query_terms) * scaling)
        .astype(jnp.bfloat16)
        .reshape(row_count, kv_heads * group_width * HEAD_WIDTH)
    )
    kv_total = kv_terms[-1]
    for distance in range(1, reach_now + 1):
        kv_total = kv_total + from_behind(kv_terms[reach_now - distance], "seq", -distance)
    grad_matrix = jnp.concatenate([query_grad, kv_total.astype(jnp.bfloat16)], axis=1)
    weights_all = jnp.concatenate([w_query[0], key_weight[0], value_weight[0]], axis=1)
    partial_grad = lax.dot_general(
        lax.all_gather(grad_matrix, "seq", axis=0, tiled=True),
        weights_all,
        (((1,), (1,)), ((), ())),
        preferred_element_type=jnp.float32,
    )
    summed = lax.psum_scatter(partial_grad, "mp", scatter_dimension=1, tiled=True)
    grad_input = summed.astype(jnp.bfloat16)
    upstream = passed_along(grad_input, "section", -1)
    return upstream[None]


def solution(mesh):
    placed = (
        P("section", "seq", "mp"),
        P("section", "seq", "mp"),
        P("section", "seq", "mp"),
        P("section", "seq", "mp"),
        P("section", "seq", "mp"),
        P("section", "seq", "mp"),
        P("section", "seq", "mp"),
        P("section", None),
    )
    return jax.shard_map(
        per_device,
        mesh=mesh,
        in_specs=placed,
        out_specs=P("section", None, ("seq", "mp")),
        check_vma=False,
    )
```

profile of v0, /device:TPU:0, one launch (start us, length us, event | category | flops | bytes accessed | tf_op | source)
XLA Modules:
  0.0 179.1 jit_solution(8366415618593966935)
XLA Ops:
  6.5 0.0 all-gather.2.cloned.1.call-start
  6.5 1.1 copy.50
  7.6 1.0 copy.51
  8.7 4.9 %collective-permute-start.2 = (bf16[128,1024]{0,1:T(8,128)(2,1)S(1)}, bf16[128,1024]{0,1:T(8,128)(2,1)S(1)}, u32[]{:S(2)}, u32[]{:S(2)}) collective-permute-start(bf16[128,1024]{0,1:T(8,128)(2,1)S(1)} %pad_maximum_fusion.4), channel_id=1, source_target_pairs={{0,2},{2,4},{4,6},{1,3},{3,5},{5,7},{8,10},{10,12},{12,14},{9,11},... | collective-permute-start | bytes 786440 | tf_op jit(solution)/shard_map/ppermute | solution.py:16
  13.6 3.3 %collective-permute-start = (bf16[128,1024]{0,1:T(8,128)(2,1)S(1)}, bf16[128,1024]{0,1:T(8,128)(2,1)S(1)}, u32[]{:S(2)}, u32[]{:S(2)}) collective-permute-start(bf16[128,1024]{0,1:T(8,128)(2,1)S(1)} %pad_maximum_fusion.4), channel_id=1, source_target_pairs={{0,6},{1,7},{8,14},{9,15},{16,22},{17,23},{24,30},{25,31}} | collective-permute-start | bytes 786440 | tf_op jit(solution)/shard_map/ppermute | solution.py:16
  16.9 1.9 %collective-permute-start.1 = (bf16[128,1024]{0,1:T(8,128)(2,1)S(1)}, bf16[128,1024]{0,1:T(8,128)(2,1)S(1)}, u32[]{:S(2)}, u32[]{:S(2)}) collective-permute-start(bf16[128,1024]{0,1:T(8,128)(2,1)S(1)} %pad_maximum_fusion.4), channel_id=1, source_target_pairs={{0,4},{2,6},{1,5},{3,7},{8,12},{10,14},{9,13},{11,15},{16,20},{18,... | collective-permute-start | bytes 786440 | tf_op jit(solution)/shard_map/ppermute | solution.py:16
  18.8 0.7 dynamic-slice_bitcast_fusion
  19.5 0.8 pad_dynamic-slice_fusion
  20.2 0.2 fusion.52
  20.5 0.9 reshape_squeeze.13
  21.4 0.9 reshape_squeeze.15
  22.4 1.1 copy.155
  23.5 0.1 copy.118
  23.6 0.0 copy-done
  23.6 0.2 copy.60
  23.8 0.3 fusion.64
  24.1 0.0 collective-permute-done.2
  24.1 0.3 fusion.65
  24.4 1.5 collective-permute-done
  26.0 0.3 fusion.66
  26.3 4.2 %collective-permute-done.1 = bf16[128,1024]{0,1:T(8,128)(2,1)S(1)} collective-permute-done((bf16[128,1024]{0,1:T(8,128)(2,1)S(1)}, bf16[128,1024]{0,1:T(8,128)(2,1)S(1)}, u32[]{:S(2)}, u32[]{:S(2)}) %collective-permute-start.1) | collective-permute-done | bytes 262176 | tf_op jit(solution)/shard_map/ppermute | solution.py:16
  30.5 0.3 fusion.67
  30.8 0.4 fusion.46
  31.2 0.4 fusion.55
  31.5 0.2 fusion.68
  31.7 0.2 fusion.69
  32.0 0.3 convolution_bitcast_fusion.1
  32.2 0.3 fusion.35
  32.5 0.2 fusion.31
  32.8 0.3 fusion.32
  33.0 0.3 fusion.33
  33.3 0.3 fusion.34
  33.6 0.2 convolution_bitcast_fusion
  33.9 0.2 fusion.36
  34.1 0.2 fusion.71
  34.3 0.2 fusion.37
  34.5 0.2 fusion.73
  34.8 0.2 fusion.70
  35.0 0.2 fusion.38
  35.2 0.2 fusion.74
  35.5 0.2 fusion.75
  35.7 1.3 collective-permute-start.3
  37.1 1.3 collective-permute-start.4
  38.4 0.2 fusion.39
  38.7 1.3 collective-permute-start.5
  40.0 0.2 fusion.72
  40.2 0.0 copy-start.1
  40.2 0.3 fusion.30
  40.5 16.1 %collective-permute-done.3 = f32[128,1024]{0,1:T(8,128)S(1)} collective-permute-done((f32[128,1024]{0,1:T(8,128)S(1)}, f32[128,1024]{0,1:T(8,128)S(1)}, u32[]{:S(2)}, u32[]{:S(2)}) %collective-permute-start.3) | collective-permute-done | bytes 524320 | tf_op jit(solution)/shard_map/ppermute | solution.py:16
  56.6 34.1 %collective-permute-done.4 = f32[128,1024]{0,1:T(8,128)S(1)} collective-permute-done((f32[128,1024]{0,1:T(8,128)S(1)}, f32[128,1024]{0,1:T(8,128)S(1)}, u32[]{:S(2)}, u32[]{:S(2)}) %collective-permute-start.4) | collective-permute-done | bytes 524320 | tf_op jit(solution)/shard_map/ppermute | solution.py:16
  90.7 0.0 collective-permute-done.5
  90.7 0.2 fusion.42
  90.9 0.8 pad_maximum_fusion.3
  91.7 0.0 all-gather.2.cloned.1.call-update
  91.7 0.0 reduce-scatter.2.cloned.1.call-start
  91.8 44.6 %all-gather.2.cloned.1.call-done = bf16[512,2048]{0,1:T(8,128)(2,1)} async-done(((bf16[128,2048]{0,1:T(8,128)(2,1)}), bf16[512,2048]{0,1:T(8,128)(2,1)}) %all-gather.2.cloned.1.call-update) | async-done | bytes 2097168 | tf_op jit(solution)/shard_map/all_gather | solution.py:181
  136.4 0.0 copy-done.1
  136.4 7.0 %fusion = f32[512,1344]{0,1:T(8,128)} fusion(bf16[512,2048]{0,1:T(8,128)(2,1)} %all-gather.2.cloned.1.call-done, bf16[1344,512]{1,0:T(8,128)(2,1)} %bitcast.315, bf16[1344,512]{1,0:T(8,128)(2,1)} %bitcast.316, bf16[1344,1024]{1,0:T(8,128)(2,1)S(1)} %bitcast.314), kind=kOutput, calls=%fused_computation | convolution fusion | flops 2835087360 | bytes 10354688 | tf_op jit(solution)/shard_map/dot_general | solution.py:180
  143.4 0.0 reduce-scatter.2.cloned.1.call-update
  143.4 8.7 %reduce-scatter.2.cloned.1.call-done = f32[512,672]{0,1:T(8,128)} async-done(((f32[512,1344]{0,1:T(8,128)}), f32[512,672]{0,1:T(8,128)}) %reduce-scatter.2.cloned.1.call-update) | async-done | bytes 1376272 | tf_op jit(solution)/shard_map/reduce_scatter | solution.py:186
  152.1 1.4 convert_element_type.47
  153.5 2.8 %collective-permute-start.6 = (bf16[512,672]{0,1:T(8,128)(2,1)S(1)}, bf16[512,672]{0,1:T(8,128)(2,1)S(1)}, u32[]{:S(2)}, u32[]{:S(2)}) collective-permute-start(bf16[512,672]{0,1:T(8,128)(2,1)S(1)} %convert_element_type.47), channel_id=1, source_target_pairs={{8,0},{16,8},{24,16},{0,24},{9,1},{17,9},{25,17},{1,25},{10,2},{18... | collective-permute-start | bytes 2064392 | tf_op jit(solution)/shard_map/ppermute | solution.py:22
  156.3 15.1 %collective-permute-done.6 = bf16[512,672]{0,1:T(8,128)(2,1)S(1)} collective-permute-done((bf16[512,672]{0,1:T(8,128)(2,1)S(1)}, bf16[512,672]{0,1:T(8,128)(2,1)S(1)}, u32[]{:S(2)}, u32[]{:S(2)}) %collective-permute-start.6) | collective-permute-done | bytes 688160 | tf_op jit(solution)/shard_map/ppermute | solution.py:22
  171.4 0.8 copy.161
  (12 shorter events, 0.2 us)
Async XLA Ops:
  6.5 17.1 %copy-start = (bf16[1,128,1024]{2,1,0:T(8,128)(2,1)S(1)}, bf16[1,128,1024]{2,1,0:T(8,128)(2,1)}, u32[]{:S(2)}) copy-start(bf16[1,128,1024]{2,1,0:T(8,128)(2,1)} %param.11) | copy-start | bytes 786436
  6.5 129.8 %all-gather.2.cloned.1.call-start = ((), (), s32[]{:S(2)}) async-start(), calls=%async_computation.1 | async-start | bytes 2621440 | tf_op jit(solution)/shard_map/all_gather | solution.py:181
  8.7 15.4 %collective-permute-start.2 = (bf16[128,1024]{0,1:T(8,128)(2,1)S(1)}, bf16[128,1024]{0,1:T(8,128)(2,1)S(1)}, u32[]{:S(2)}, u32[]{:S(2)}) collective-permute-start(bf16[128,1024]{0,1:T(8,128)(2,1)S(1)} %pad_maximum_fusion.4), channel_id=1, source_target_pairs={{0,2},{2,4},{4,6},{1,3},{3,5},{5,7},{8,10},{10,12},{12,14},{9,11},... | collective-permute-start | bytes 786440 | tf_op jit(solution)/shard_map/ppermute | solution.py:16
  13.6 12.3 %collective-permute-start = (bf16[128,1024]{0,1:T(8,128)(2,1)S(1)}, bf16[128,1024]{0,1:T(8,128)(2,1)S(1)}, u32[]{:S(2)}, u32[]{:S(2)}) collective-permute-start(bf16[128,1024]{0,1:T(8,128)(2,1)S(1)} %pad_maximum_fusion.4), channel_id=1, source_target_pairs={{0,6},{1,7},{8,14},{9,15},{16,22},{17,23},{24,30},{25,31}} | collective-permute-start | bytes 786440 | tf_op jit(solution)/shard_map/ppermute | solution.py:16
  16.9 13.5 %collective-permute-start.1 = (bf16[128,1024]{0,1:T(8,128)(2,1)S(1)}, bf16[128,1024]{0,1:T(8,128)(2,1)S(1)}, u32[]{:S(2)}, u32[]{:S(2)}) collective-permute-start(bf16[128,1024]{0,1:T(8,128)(2,1)S(1)} %pad_maximum_fusion.4), channel_id=1, source_target_pairs={{0,4},{2,6},{1,5},{3,7},{8,12},{10,14},{9,13},{11,15},{16,20},{18,... | collective-permute-start | bytes 786440 | tf_op jit(solution)/shard_map/ppermute | solution.py:16
  35.7 20.8 %collective-permute-start.3 = (f32[128,1024]{0,1:T(8,128)S(1)}, f32[128,1024]{0,1:T(8,128)S(1)}, u32[]{:S(2)}, u32[]{:S(2)}) collective-permute-start(f32[128,1024]{0,1:T(8,128)S(1)} %pad_maximum_fusion), channel_id=1, source_target_pairs={{2,0},{4,2},{6,4},{3,1},{5,3},{7,5},{10,8},{12,10},{14,12},{11,9},... | collective-permute-start | bytes 1572872 | tf_op jit(solution)/shard_map/ppermute | solution.py:16
  37.1 53.6 %collective-permute-start.4 = (f32[128,1024]{0,1:T(8,128)S(1)}, f32[128,1024]{0,1:T(8,128)S(1)}, u32[]{:S(2)}, u32[]{:S(2)}) collective-permute-start(f32[128,1024]{0,1:T(8,128)S(1)} %pad_maximum_fusion.1), channel_id=1, source_target_pairs={{4,0},{6,2},{5,1},{7,3},{12,8},{14,10},{13,9},{15,11},{20,16},{22,... | collective-permute-start | bytes 1572872 | tf_op jit(solution)/shard_map/ppermute | solution.py:16
  38.7 52.1 %collective-permute-start.5 = (f32[128,1024]{0,1:T(8,128)S(1)}, f32[128,1024]{0,1:T(8,128)S(1)}, u32[]{:S(2)}, u32[]{:S(2)}) collective-permute-start(f32[128,1024]{0,1:T(8,128)S(1)} %pad_maximum_fusion.2), channel_id=1, source_target_pairs={{6,0},{7,1},{14,8},{15,9},{22,16},{23,17},{30,24},{31,25}} | collective-permute-start | bytes 1572872 | tf_op jit(solution)/shard_map/ppermute | solution.py:16
  40.2 96.2 %copy-start.1 = (bf16[1,1344,1024]{2,1,0:T(8,128)(2,1)S(1)}, bf16[1,1344,1024]{2,1,0:T(8,128)(2,1)}, u32[]{:S(2)}) copy-start(bf16[1,1344,1024]{2,1,0:T(8,128)(2,1)} %param.12) | copy-start | bytes 8257540
  91.7 60.4 %reduce-scatter.2.cloned.1.call-start = ((), (), s32[]{:S(2)}) async-start(), calls=%async_computation.2 | async-start | bytes 4128768 | tf_op jit(solution)/shard_map/reduce_scatter | solution.py:186
  153.5 17.9 %collective-permute-start.6 = (bf16[512,672]{0,1:T(8,128)(2,1)S(1)}, bf16[512,672]{0,1:T(8,128)(2,1)S(1)}, u32[]{:S(2)}, u32[]{:S(2)}) collective-permute-start(bf16[512,672]{0,1:T(8,128)(2,1)S(1)} %convert_element_type.47), channel_id=1, source_target_pairs={{8,0},{16,8},{24,16},{0,24},{9,1},{17,9},{25,17},{1,25},{10,2},{18... | collective-permute-start | bytes 2064392 | tf_op jit(solution)/shard_map/ppermute | solution.py:22
Sparse Core Ops, SparseCore 0:
  91.9 44.4 all-gather.1
  143.5 8.5 reduce-scatter.1
where the time goes:
time: 179 us
  waiting for transfers between devices  124 us (69%)
  starting transfers between devices  16.8 us (9%)
  between operations  13.8 us (8%)
  matrix products  12.9 us (7%)
  local copies, waits for them, and re-layouts  6.98 us (4%)
  other arithmetic  4.28 us (2%)
    ppermute x6, waiting for transfers between devices, from_behind(): return lax.ppermute(shard, axis, pairs)  55.9 us
    all_gather x1, waiting for transfers between devices, per_device(): lax.all_gather(grad_matrix, 'seq', axis=0, tiled=True)  44.6 us
    ppermute x1, waiting for transfers between devices, passed_along(): return lax.ppermute(block, axis, route)  15.1 us
    ppermute x6, starting transfers between devices, from_behind(): return lax.ppermute(shard, axis, pairs)  14 us
    reduce_scatter x1, waiting for transfers between devices, per_device(): lax.psum_scatter(partial_grad, 'mp', scatter_dimension=1, tiled=True)  8.71 us
    dot_general x1, matrix products, per_device(): lax.dot_general(lax.all_gather(grad_matrix, 'seq', axis=0, tiled=True), w...  7 us
  transfers between devices with their start and end apart: 9, of which 7 were waited for; matrix products, arithmetic and copies ran while one was open for 4% of the time, Pallas kernels for 0%

commit v1 on v0

v1 whole, which is shorter than its diff:
```python
import functools
import math

import jax
import jax.numpy as jnp
from jax import lax
from jax.experimental import pallas as pl
from jax.experimental.pallas import tpu as pltpu
from jax.sharding import PartitionSpec as P

HEAD_WIDTH = 128
WINDOW = 512
MASKED = -1e30


def dot(left, right, left_dim, right_dim):
    return lax.dot_general(
        left,
        right,
        (((left_dim,), (right_dim,)), ((), ())),
        preferred_element_type=jnp.float32,
    )


def attention_kernel(kv_heads, group_width, halo_rows, *refs):
    halo_count = len(halo_rows)
    query_ref, grad_ref, kv_ref, bias_ref = refs[:4]
    halo_refs = refs[4 : 4 + halo_count]
    grad_query_ref, grad_kv_ref = refs[4 + halo_count : 6 + halo_count]
    grad_halo_refs = refs[6 + halo_count :]
    rows = query_ref.shape[0]
    kv_cols = kv_heads * HEAD_WIDTH
    scaling = 1.0 / math.sqrt(HEAD_WIDTH)
    bias = jnp.concatenate([bias_ref[...]] * group_width, axis=1)
    for group in range(kv_heads):
        heads = [group * group_width + member for member in range(group_width)]
        query = jnp.concatenate(
            [query_ref[:, h * HEAD_WIDTH : (h + 1) * HEAD_WIDTH] for h in heads], axis=0
        )
        grad = jnp.concatenate(
            [grad_ref[:, h * HEAD_WIDTH : (h + 1) * HEAD_WIDTH] for h in heads], axis=0
        )
        key_cols = slice(group * HEAD_WIDTH, (group + 1) * HEAD_WIDTH)
        value_cols = slice(kv_cols + group * HEAD_WIDTH, kv_cols + (group + 1) * HEAD_WIDTH)
        blocks = [*halo_refs, kv_ref]
        key = jnp.concatenate([block[:, key_cols] for block in blocks], axis=0)
        value = jnp.concatenate([block[:, value_cols] for block in blocks], axis=0)
        scores = dot(key, query, 1, 1) * scaling + bias
        raised = jnp.exp(scores - jnp.max(scores, axis=0, keepdims=True))
        weights = raised * (1.0 / jnp.sum(raised, axis=0, keepdims=True))
        weights_half = weights.astype(jnp.bfloat16)
        grad_weights = dot(value, grad, 1, 1)
        delta = jnp.sum(weights_half.astype(jnp.float32) * grad_weights, axis=0, keepdims=True)
        grad_scores = (weights * (grad_weights - delta)).astype(jnp.bfloat16)
        grad_query = (dot(grad_scores, key, 0, 0) * scaling).astype(jnp.bfloat16)
        for member, h in enumerate(heads):
            grad_query_ref[:, h * HEAD_WIDTH : (h + 1) * HEAD_WIDTH] = grad_query[
                member * rows : (member + 1) * rows
            ]
        grad_key = dot(grad_scores, query, 1, 0) * scaling
        grad_value = dot(weights_half, grad, 1, 0)
        start = 0
        for size, out_ref in zip([*halo_rows, rows], [*grad_halo_refs, grad_kv_ref]):
            out_ref[:, key_cols] = grad_key[start : start + size].astype(out_ref.dtype)
            out_ref[:, value_cols] = grad_value[start : start + size].astype(out_ref.dtype)
            start += size


def attention_backward(query, grad, kv, bias, halos):
    rows, query_cols = query.shape
    kv_cols = kv.shape[1] // 2
    kv_heads = kv_cols // HEAD_WIDTH
    group_width = query_cols // kv_cols
    halo_rows = [halo.shape[0] for halo in halos]
    span = bias.shape[0]
    whole = pl.BlockSpec(memory_space=pltpu.VMEM)
    outs = [
        jax.ShapeDtypeStruct((rows, query_cols), jnp.bfloat16),
        jax.ShapeDtypeStruct((rows, 2 * kv_cols), jnp.float32),
        *[jax.ShapeDtypeStruct((size, 2 * kv_cols), jnp.bfloat16) for size in halo_rows],
    ]
    return pl.pallas_call(
        functools.partial(attention_kernel, kv_heads, group_width, halo_rows),
        out_shape=outs,
        in_specs=[whole] * (4 + len(halos)),
        out_specs=[whole] * len(outs),
        compiler_params=pltpu.CompilerParams(vmem_limit_bytes=32 * 1024 * 1024),
        cost_estimate=pl.CostEstimate(
            flops=12 * rows * span * query_cols,
            bytes_accessed=4 * rows * query_cols * 2,
            transcendentals=rows * span * kv_heads * group_width,
        ),
    )(query, grad, kv, bias, *halos)


def moved(block, axis, by, first=0):
    size = lax.axis_size(axis)
    if by > 0:
        sources = range(first, size - by)
    else:
        sources = range(-by, size - first)
    return lax.ppermute(block, axis, [(i, i + by) for i in sources])


def passed_along(block, axis, distance):
    devices = range(lax.axis_size(axis))
    return lax.ppermute(block, axis, [((i - distance) % len(devices), i) for i in devices])


def per_device(
    query_rows,
    key_row_matrix,
    value_row_matrix,
    out_grad,
    w_query,
    key_weight,
    value_weight,
    doc_ids,
):
    documents = doc_ids[0]
    tokens = documents.shape[0]
    rows = query_rows.shape[1]
    kv_cols = key_row_matrix.shape[2]
    shards = lax.axis_size("seq")
    place = lax.axis_index("seq")
    core = lax.axis_index("mp")
    back = min(WINDOW, tokens // 3) - 1
    halo_rows = []
    while sum(halo_rows) < back and len(halo_rows) < shards - 1:
        halo_rows.append(min(rows, -(-(back - sum(halo_rows)) // 16) * 16))
    kv = jnp.concatenate([key_row_matrix[0], value_row_matrix[0]], axis=1)
    halos = [moved(kv[rows - size :], "seq", d) for d, size in enumerate(halo_rows, 1)]
    reach = sum(halo_rows)
    first_row = place * rows
    key_docs = lax.dynamic_slice_in_dim(
        jnp.concatenate([jnp.full((reach,), -1, jnp.int32), documents]), first_row, reach + rows, 0
    )
    query_docs = lax.dynamic_slice_in_dim(documents, first_row, rows, 0)
    offset = (
        jnp.arange(rows, dtype=jnp.int32)[None, :]
        + reach
        - jnp.arange(reach + rows, dtype=jnp.int32)[:, None]
    )
    allowed = (query_docs[None, :] == key_docs[:, None]) & (offset >= 0) & (offset < WINDOW)
    bias = jnp.where(allowed, 0.0, MASKED).astype(jnp.float32)
    grad_query, grad_kv, *grad_halos = attention_backward(
        query_rows[0], out_grad[0], kv, bias, halos[::-1]
    )
    for d, part in enumerate(grad_halos[::-1], 1):
        part = moved(part, "seq", -d).astype(jnp.float32)
        grad_kv = grad_kv + jnp.pad(part, ((rows - part.shape[0], 0), (0, 0)))
    grad_kv = grad_kv.astype(jnp.bfloat16)

    def chain(piece):
        up, down = piece, piece
        arrived = []
        for step in range(1, shards):
            if 2 * step > shards + 1:
                both = [(i, i + 1) for i in range(step - 1, shards - 1)]
                both += [(i, i - 1) for i in range(1, shards - step + 1)]
                up = down = lax.ppermute(up, "seq", both)
                arrived.append([up])
                continue
            up = moved(up, "seq", 1, step - 1)
            down = moved(down, "seq", -1, step - 1)
            if 2 * step >= shards:
                up = down = jnp.where(place >= step, up, down)
                arrived.append([up])
            else:
                arrived.append([up, down])
        return arrived

    def finished(query_part, kv_part):
        partial = (
            dot(query_part, w_query[0], 1, 1)
            + dot(kv_part[:, :kv_cols], key_weight[0], 1, 1)
            + dot(kv_part[:, kv_cols:], value_weight[0], 1, 1)
        )
        half = partial.shape[1] // 2
        low, high = partial[:, :half], partial[:, half:]
        keep = jnp.where(core == 0, low, high)
        give = jnp.where(core == 0, high, low).astype(jnp.bfloat16)
        got = passed_along(give, "mp", 1)
        total = (keep + got.astype(jnp.float32)).astype(jnp.bfloat16)
        return passed_along(total, "section", -1)

    query_steps, kv_steps = chain(grad_query), chain(grad_kv)
    results = [[finished(grad_query, grad_kv)]]
    for query_parts, kv_parts in zip(query_steps, kv_steps):
        if len(query_parts) == 1:
            results.append([finished(query_parts[0], kv_parts[0])])
        else:
            joined = finished(
                jnp.concatenate(query_parts, axis=0), jnp.concatenate(kv_parts, axis=0)
            )
            results.append([joined[:rows], joined[rows:]])
    upstream = jnp.zeros((tokens, results[0][0].shape[1]), jnp.bfloat16)
    for s in range(shards):
        behind = results[s][0]
        ahead = results[(shards - s) % shards][-1]
        block = jnp.where(place >= s, behind, ahead)
        upstream = lax.dynamic_update_slice_in_dim(
            upstream, block, ((place - s) % shards) * rows, 0
        )
    return upstream[None]


def solution(mesh):
    placed = P("section", "seq", "mp")
    return jax.shard_map(
        per_device,
        mesh=mesh,
        in_specs=(placed,) * 7 + (P("section", None),),
        out_specs=P("section", None, ("seq", "mp")),
        check_vma=False,
    )
```

time: 179 us -> 115 us (0.64)
  waiting for transfers between devices: 124 us -> 45.8 us
  starting transfers between devices: 16.8 us -> 36.2 us
  between operations: 13.8 us -> 0.53 us
  local copies, waits for them, and re-layouts: 6.98 us -> 10.8 us
  Pallas kernels: 0 us -> 2.92 us
  other arithmetic: 4.28 us -> 6.9 us
    all_gather x1 -> x0, waiting for transfers between devices: 44.6 us -> none  [per_device(): lax.all_gather(grad_matrix, 'seq', axis=0, tiled=True)]
    ppermute x7 -> x22, waiting for transfers between devices: 71 us -> 45.8 us  [the longest x12 27.1 us: moved(): return lax.ppermute(block, axis, [(i, i + by) for i in sources])]
    ppermute x7 -> x22, starting transfers between devices: 16.7 us -> 36.2 us  [the longest x12 26.3 us: moved(): return lax.ppermute(block, axis, [(i, i + by) for i in sources])]
    reduce_scatter x1 -> x0, waiting for transfers between devices: 8.71 us -> none  [per_device(): lax.psum_scatter(partial_grad, 'mp', scatter_dimension=1, tiled=True)]
    unnamed x8 -> x29, local copies, waits for them, and re-layouts: 3.11 us -> 9.19 us
    another operation x4 -> x0, local copies, waits for them, and re-layouts: 3.14 us -> none  [the longest x1 1.12 us: per_device(): query_here.reshape(row_count, kv_heads, group_width, HEAD_WIDTH)]
    pallas_call x0 -> x1, Pallas kernels: none -> 2.92 us  [attention_backward(): pl.pallas_call(functools.partial(attention_kernel, kv_heads, group_width,...]
    convert_element_type x3 -> x9, other arithmetic: 1.96 us -> 3.97 us  [the longest x1 1.76 us: per_device(): grad_kv = grad_kv.astype(jnp.bfloat16)]
  transfers between devices with their start and end apart: 9 -> 22, of which waited for: 7 -> 9; matrix products, arithmetic and copies ran while one was open for 4% -> 16% of each run, Pallas kernels for 0% -> 0%
where the time goes in v1:
time: 115 us; the launch traced here: 114 us
  waiting for transfers between devices  45.8 us (40%)
  starting transfers between devices  36.2 us (31%)
  matrix products  11.3 us (10%)
  local copies, waits for them, and re-layouts  10.8 us (9%)
  other arithmetic  6.9 us (6%)
  Pallas kernels  2.92 us (3%)
    ppermute x12, waiting for transfers between devices, moved(): return lax.ppermute(block, axis, [(i, i + by) for i in sources])  27.1 us
    ppermute x12, starting transfers between devices, moved(): return lax.ppermute(block, axis, [(i, i + by) for i in sources])  26.3 us
    ppermute x8, waiting for transfers between devices, passed_along(): lax.ppermute(block, axis, [((i - distance) % len(devices), i) for i in de...  13.1 us
    dot_general x12, matrix products, dot(): lax.dot_general(left, right, (((left_dim,), (right_dim,)), ((), ())), pre...  11.3 us
    unnamed x29, local copies, waits for them, and re-layouts  9.19 us
    ppermute x8, starting transfers between devices, passed_along(): lax.ppermute(block, axis, [((i - distance) % len(devices), i) for i in de...  7.29 us
    ppermute x2, waiting for transfers between devices, chain(): up = down = lax.ppermute(up, 'seq', both)  5.55 us
    pallas_call x1, Pallas kernels, attention_backward(): pl.pallas_call(functools.partial(attention_kernel, kv_heads, group_width,...  2.92 us
  transfers between devices with their start and end apart: 22, of which 9 were waited for; matrix products, arithmetic and copies ran while one was open for 16% of the time, Pallas kernels for 0%

profile of v1, /device:TPU:0, one launch (start us, length us, event | category | flops | bytes accessed | tf_op | source)
XLA Modules:
  0.0 114.4 jit_solution(3450153712692933512)
XLA Ops:
  0.0 1.0 fusion.62
  1.0 5.9 %collective-permute-start = (bf16[48,1024]{1,0:T(8,128)(2,1)S(1)}, bf16[48,1024]{1,0:T(8,128)(2,1)S(1)}, u32[]{:S(2)}, u32[]{:S(2)}) collective-permute-start(bf16[48,1024]{1,0:T(8,128)(2,1)S(1)} %fusion.62), channel_id=1, source_target_pairs={{0,4},{2,6},{1,5},{3,7},{8,12},{10,14},{9,13},{11,15},{16,20},{18,... | collective-permute-start | bytes 294920 | tf_op jit(solution)/shard_map/ppermute | solution.py:102
  6.9 1.0 pad_maximum_fusion.refs_2_
  7.9 3.5 %collective-permute-start.1 = (bf16[128,1024]{1,0:T(8,128)(2,1)S(1)}, bf16[128,1024]{1,0:T(8,128)(2,1)S(1)}, u32[]{:S(2)}, u32[]{:S(2)}) collective-permute-start(bf16[128,1024]{1,0:T(8,128)(2,1)S(1)} %pad_maximum_fusion.refs_2_), channel_id=1, source_target_pairs={{0,2},{2,4},{4,6},{1,3},{3,5},{5,7},{8,10},{10,12},{12,14},{9,11},... | collective-permute-start | bytes 786440 | tf_op jit(solution)/shard_map/ppermute | solution.py:102
  11.4 0.7 copy-done.1
  12.1 0.8 pad_dynamic-slice_fusion
  12.9 0.7 fusion.63
  13.5 0.1 fusion.55.refs_3_
  13.7 0.6 copy-done.7
  14.3 2.4 %collective-permute-done.1.refs_5_ = bf16[128,1024]{1,0:T(8,128)(2,1)S(1)} collective-permute-done((bf16[128,1024]{1,0:T(8,128)(2,1)S(1)}, bf16[128,1024]{1,0:T(8,128)(2,1)S(1)}, u32[]{:S(2)}, u32[]{:S(2)}) %collective-permute-start.1) | collective-permute-done | bytes 262176 | tf_op jit(solution)/shard_map/ppermute | solution.py:102
  16.7 0.7 copy-done.5
  17.4 0.9 copy-done.2
  18.3 0.9 copy-done.3
  19.3 0.9 copy-done.4
  20.2 0.9 copy-done.6
  21.2 0.9 copy-done.8
  22.1 2.9 %shard_map.82 = (bf16[128,1024]{1,0:T(8,128)(2,1)S(1)}, f32[128,1024]{1,0:T(8,128)S(1)}, bf16[48,1024]{1,0:T(8,128)(2,1)}, bf16[128,1024]{1,0:T(8,128)(2,1)}) custom-call(bf16[128,1024]{1,0:T(8,128)(2,1)S(1)} %bitcast.61, bf16[128,1024]{1,0:T(8,128)(2,1)S(1)} %bitcast.62, bf16[128,1024]{1,0:T(8,128)(2,1)S(1)} %copy-done.2, f32[304,128]{1,0:T(8,128)S(1)} %fusion.55.refs_3_, ...), custom_call_target="tpu_custom_call" | custom-call | flops 478150656 | bytes 1048576 | tf_op jit(solution)/shard_map/pallas_call | solution.py:82
  25.0 1.3 %collective-permute-start.2 = (bf16[128,1024]{1,0:T(8,128)(2,1)}, bf16[128,1024]{1,0:T(8,128)(2,1)}, u32[]{:S(2)}, u32[]{:S(2)}) collective-permute-start(bf16[128,1024]{1,0:T(8,128)(2,1)} %get-tuple-element.11), channel_id=1, source_target_pairs={{2,0},{4,2},{6,4},{3,1},{5,3},{7,5},{10,8},{12,10},{14,12},{11,9},... | collective-permute-start | bytes 786440 | tf_op jit(solution)/shard_map/ppermute | solution.py:102
  26.3 1.3 %collective-permute-start.3 = (bf16[48,1024]{1,0:T(8,128)(2,1)}, bf16[48,1024]{1,0:T(8,128)(2,1)}, u32[]{:S(2)}, u32[]{:S(2)}) collective-permute-start(bf16[48,1024]{1,0:T(8,128)(2,1)} %get-tuple-element.12), channel_id=1, source_target_pairs={{4,0},{6,2},{5,1},{7,3},{12,8},{14,10},{13,9},{15,11},{20,16},{22,... | collective-permute-start | bytes 294920 | tf_op jit(solution)/shard_map/ppermute | solution.py:102
  27.6 1.3 %collective-permute-start.7 = (bf16[128,1024]{1,0:T(8,128)(2,1)S(1)}, bf16[128,1024]{1,0:T(8,128)(2,1)}, u32[]{:S(2)}, u32[]{:S(2)}) collective-permute-start(bf16[128,1024]{1,0:T(8,128)(2,1)S(1)} %get-tuple-element.9), channel_id=1, source_target_pairs={{2,0},{4,2},{6,4},{3,1},{5,3},{7,5},{10,8},{12,10},{14,12},{11,9},... | collective-permute-start | bytes 786440 | tf_op jit(solution)/shard_map/ppermute | solution.py:102
  28.9 6.3 %collective-permute-start.6 = (bf16[128,1024]{1,0:T(8,128)(2,1)S(1)}, bf16[128,1024]{1,0:T(8,128)(2,1)}, u32[]{:S(2)}, u32[]{:S(2)}) collective-permute-start(bf16[128,1024]{1,0:T(8,128)(2,1)S(1)} %get-tuple-element.9), channel_id=1, source_target_pairs={{0,2},{2,4},{4,6},{1,3},{3,5},{5,7},{8,10},{10,12},{12,14},{9,11},... | collective-permute-start | bytes 786440 | tf_op jit(solution)/shard_map/ppermute | solution.py:102
  35.2 7.3 %collective-permute-done.3 = bf16[48,1024]{1,0:T(8,128)(2,1)} collective-permute-done((bf16[48,1024]{1,0:T(8,128)(2,1)}, bf16[48,1024]{1,0:T(8,128)(2,1)}, u32[]{:S(2)}, u32[]{:S(2)}) %collective-permute-start.3) | collective-permute-done | bytes 98336 | tf_op jit(solution)/shard_map/ppermute | solution.py:102
  42.5 1.8 %add_convert_fusion.1 = bf16[128,1024]{1,0:T(8,128)(2,1)} fusion(f32[128,1024]{1,0:T(8,128)S(1)} %get-tuple-element.10, bf16[128,1024]{1,0:T(8,128)(2,1)} %collective-permute-done.2, bf16[48,1024]{1,0:T(8,128)(2,1)} %collective-permute-done.3), kind=kLoop, calls=%fused_computation.36 | loop fusion | flops 655360 | bytes 1146880 | tf_op jit(solution)/shard_map/convert_element_type | solution.py:152
  44.3 2.0 %fusion.32 = f32[128,1344]{0,1:T(8,128)S(1)} fusion(bf16[1,1344,512]{2,1,0:T(8,128)(2,1)} %param.14, bf16[128,1024]{1,0:T(8,128)(2,1)} %add_convert_fusion.1), kind=kOutput, calls=%fused_computation.21 | convolution fusion | flops 176160768 | bytes 2195456 | tf_op jit(solution)/shard_map/dot_general | solution.py:17
  46.3 1.4 %fusion.40 = f32[128,1344]{0,1:T(8,128)S(1)} fusion(bf16[1,1344,512]{2,1,0:T(8,128)(2,1)S(1)} %copy-done.10, bf16[128,1024]{1,0:T(8,128)(2,1)} %add_convert_fusion.1), kind=kOutput, calls=%fused_computation.29 | convolution fusion | flops 176160768 | bytes 2195456 | tf_op jit(solution)/shard_map/dot_general | solution.py:17
  47.7 0.9 fusion.11
  48.7 0.8 copy-done.12
  49.5 0.7 select_convert_fusion.3
  50.2 1.3 %collective-permute-start.8 = (bf16[128,1024]{1,0:T(8,128)(2,1)}, bf16[128,1024]{1,0:T(8,128)(2,1)S(1)}, u32[]{:S(2)}, u32[]{:S(2)}) collective-permute-start(bf16[128,1024]{1,0:T(8,128)(2,1)} %add_convert_fusion.1), channel_id=1, source_target_pairs={{0,2},{2,4},{4,6},{1,3},{3,5},{5,7},{8,10},{10,12},{12,14},{9,11},... | collective-permute-start | bytes 786440 | tf_op jit(solution)/shard_map/ppermute | solution.py:102
  51.6 1.4 %collective-permute-start.9 = (bf16[128,1024]{1,0:T(8,128)(2,1)}, bf16[128,1024]{1,0:T(8,128)(2,1)S(1)}, u32[]{:S(2)}, u32[]{:S(2)}) collective-permute-start(bf16[128,1024]{1,0:T(8,128)(2,1)} %add_convert_fusion.1), channel_id=1, source_target_pairs={{2,0},{4,2},{6,4},{3,1},{5,3},{7,5},{10,8},{12,10},{14,12},{11,9},... | collective-permute-start | bytes 786440 | tf_op jit(solution)/shard_map/ppermute | solution.py:102
  53.1 1.3 %collective-permute-start.13 = (bf16[128,1024]{1,0:T(8,128)(2,1)}, bf16[128,1024]{1,0:T(8,128)(2,1)S(1)}, u32[]{:S(2)}, u32[]{:S(2)}) collective-permute-start(bf16[128,1024]{1,0:T(8,128)(2,1)} %collective-permute-done.7), channel_id=1, source_target_pairs={{2,0},{4,2},{3,1},{5,3},{10,8},{12,10},{11,9},{13,11},{18,16},{20,... | collective-permute-start | bytes 786440 | tf_op jit(solution)/shard_map/ppermute | solution.py:102
  54.4 0.7 collective-permute-start.12
  55.1 1.1 add_convert_fusion.4
  56.2 2.5 %collective-permute-start.5 = (bf16[128,672]{0,1:T(8,128)(2,1)S(1)}, bf16[128,672]{0,1:T(8,128)(2,1)S(1)}, u32[]{:S(2)}, u32[]{:S(2)}) collective-permute-start(bf16[128,672]{0,1:T(8,128)(2,1)S(1)} %add_convert_fusion.4), channel_id=1, source_target_pairs={{8,0},{16,8},{24,16},{0,24},{9,1},{17,9},{25,17},{1,25},{10,2},{18... | collective-permute-start | bytes 516104 | tf_op jit(solution)/shard_map/ppermute | solution.py:107
  58.7 4.2 %collective-permute-done.9 = bf16[128,1024]{1,0:T(8,128)(2,1)S(1)} collective-permute-done((bf16[128,1024]{1,0:T(8,128)(2,1)}, bf16[128,1024]{1,0:T(8,128)(2,1)S(1)}, u32[]{:S(2)}, u32[]{:S(2)}) %collective-permute-start.9) | collective-permute-done | bytes 262176 | tf_op jit(solution)/shard_map/ppermute | solution.py:102
  63.0 0.6 fusion.30
  63.6 0.8 copy-done.11
  64.3 0.6 fusion.38
  64.9 3.3 %collective-permute-done.13 = bf16[128,1024]{1,0:T(8,128)(2,1)S(1)} collective-permute-done((bf16[128,1024]{1,0:T(8,128)(2,1)}, bf16[128,1024]{1,0:T(8,128)(2,1)S(1)}, u32[]{:S(2)}, u32[]{:S(2)}) %collective-permute-start.13) | collective-permute-done | bytes 262176 | tf_op jit(solution)/shard_map/ppermute | solution.py:102
  68.2 1.3 %collective-permute-start.14 = (bf16[128,1024]{1,0:T(8,128)(2,1)S(1)}, bf16[128,1024]{1,0:T(8,128)(2,1)S(1)}, u32[]{:S(2)}, u32[]{:S(2)}) collective-permute-start(bf16[128,1024]{1,0:T(8,128)(2,1)S(1)} %broadcast_select_fusion.1), channel_id=1, source_target_pairs={{4,6},{2,0},{5,7},{3,1},{12,14},{10,8},{13,15},{11,9},{20,22},{18,... | collective-permute-start | bytes 786440 | tf_op jit(solution)/shard_map/ppermute | solution.py:161
  69.5 1.3 %collective-permute-start.16 = (bf16[128,1024]{1,0:T(8,128)(2,1)S(1)}, bf16[128,1024]{1,0:T(8,128)(2,1)S(1)}, u32[]{:S(2)}, u32[]{:S(2)}) collective-permute-start(bf16[128,1024]{1,0:T(8,128)(2,1)S(1)} %collective-permute-done.9), channel_id=1, source_target_pairs={{2,0},{4,2},{3,1},{5,3},{10,8},{12,10},{11,9},{13,11},{18,16},{20,... | collective-permute-start | bytes 786440 | tf_op jit(solution)/shard_map/ppermute | solution.py:102
  70.8 0.7 collective-permute-start.15
  71.5 2.0 %fusion = f32[256,1344]{0,1:T(8,128)S(1)} fusion(f32[256,1344]{0,1:T(8,128)S(1)} %fusion.30, f32[256,1344]{0,1:T(8,128)S(1)} %fusion.38, bf16[1,1344,1024]{2,1,0:T(8,128)(2,1)S(1)} %copy-done, bf16[128,1024]{1,0:T(8,128)(2,1)} %collective-permute-done.7, bf16[128,1024]{1,0:T(8,128)(2,1)} %collective-permute-done.6), kind=kOutput, calls=%fused_computation.1 | convolution fusion | flops 706379776 | bytes 7405568 | tf_op jit(solution)/shard_map/dot_general | solution.py:17
  73.6 0.1 collective-permute-start.10
  73.8 9.9 %collective-permute-done.16 = bf16[128,1024]{1,0:T(8,128)(2,1)S(1)} collective-permute-done((bf16[128,1024]{1,0:T(8,128)(2,1)S(1)}, bf16[128,1024]{1,0:T(8,128)(2,1)S(1)}, u32[]{:S(2)}, u32[]{:S(2)}) %collective-permute-start.16) | collective-permute-done | bytes 262176 | tf_op jit(solution)/shard_map/ppermute | solution.py:102
  83.7 1.3 %collective-permute-start.17 = (bf16[128,1024]{1,0:T(8,128)(2,1)S(1)}, bf16[128,1024]{1,0:T(8,128)(2,1)S(1)}, u32[]{:S(2)}, u32[]{:S(2)}) collective-permute-start(bf16[128,1024]{1,0:T(8,128)(2,1)S(1)} %broadcast_select_fusion), channel_id=1, source_target_pairs={{4,6},{2,0},{5,7},{3,1},{12,14},{10,8},{13,15},{11,9},{20,22},{18,... | collective-permute-start | bytes 786440 | tf_op jit(solution)/shard_map/ppermute | solution.py:161
  85.0 0.5 fusion.26
  85.5 0.5 fusion.34
  86.0 0.9 fusion.23
  87.0 0.1 collective-permute-start.20
  87.1 5.5 %collective-permute-done.17 = bf16[128,1024]{1,0:T(8,128)(2,1)S(1)} collective-permute-done((bf16[128,1024]{1,0:T(8,128)(2,1)S(1)}, bf16[128,1024]{1,0:T(8,128)(2,1)S(1)}, u32[]{:S(2)}, u32[]{:S(2)}) %collective-permute-start.17) | collective-permute-done | bytes 262176 | tf_op jit(solution)/shard_map/ppermute | solution.py:161
  92.6 0.5 fusion.28
  93.2 0.5 fusion.36
  93.7 0.9 fusion.17
  94.7 0.1 add_convert_fusion
  94.9 2.5 %collective-permute-start.11 = (bf16[256,672]{0,1:T(8,128)(2,1)S(1)}, bf16[256,672]{0,1:T(8,128)(2,1)S(1)}, u32[]{:S(2)}, u32[]{:S(2)}) collective-permute-start(bf16[256,672]{0,1:T(8,128)(2,1)S(1)} %add_convert_fusion), channel_id=1, source_target_pairs={{8,0},{16,8},{24,16},{0,24},{9,1},{17,9},{25,17},{1,25},{10,2},{18... | collective-permute-start | bytes 1032200 | tf_op jit(solution)/shard_map/ppermute | solution.py:107
  97.4 1.2 %collective-permute-start.19 = (bf16[128,672]{0,1:T(8,128)(2,1)S(1)}, bf16[128,672]{0,1:T(8,128)(2,1)S(1)}, u32[]{:S(2)}, u32[]{:S(2)}) collective-permute-start(bf16[128,672]{0,1:T(8,128)(2,1)S(1)} %add_convert_fusion.3), channel_id=1, source_target_pairs={{8,0},{16,8},{24,16},{0,24},{9,1},{17,9},{25,17},{1,25},{10,2},{18... | collective-permute-start | bytes 516104 | tf_op jit(solution)/shard_map/ppermute | solution.py:107
  98.8 0.8 collective-permute-start.21
  99.6 6.2 %collective-permute-done.11 = bf16[256,672]{0,1:T(8,128)(2,1)S(1)} collective-permute-done((bf16[256,672]{0,1:T(8,128)(2,1)S(1)}, bf16[256,672]{0,1:T(8,128)(2,1)S(1)}, u32[]{:S(2)}, u32[]{:S(2)}) %collective-permute-start.11) | collective-permute-done | bytes 344096 | tf_op jit(solution)/shard_map/ppermute | solution.py:107
  105.8 3.7 %collective-permute-done.19 = bf16[128,672]{0,1:T(8,128)(2,1)S(1)} collective-permute-done((bf16[128,672]{0,1:T(8,128)(2,1)S(1)}, bf16[128,672]{0,1:T(8,128)(2,1)S(1)}, u32[]{:S(2)}, u32[]{:S(2)}) %collective-permute-start.19) | collective-permute-done | bytes 172064 | tf_op jit(solution)/shard_map/ppermute | solution.py:107
  109.5 0.1 fusion.50
  109.5 3.2 %collective-permute-done.21 = bf16[128,672]{0,1:T(8,128)(2,1)S(1)} collective-permute-done((bf16[128,672]{0,1:T(8,128)(2,1)S(1)}, bf16[128,672]{0,1:T(8,128)(2,1)S(1)}, u32[]{:S(2)}, u32[]{:S(2)}) %collective-permute-start.21) | collective-permute-done | bytes 172064 | tf_op jit(solution)/shard_map/ppermute | solution.py:107
  112.8 0.8 copy-done.13
  113.6 0.7 fusion.48
  (45 shorter events, 0.6 us)
Async XLA Ops:
  0.0 47.7 %copy-start = (bf16[1,1344,1024]{2,1,0:T(8,128)(2,1)S(1)}, bf16[1,1344,1024]{2,1,0:T(8,128)(2,1)}, u32[]{:S(2)}) copy-start(bf16[1,1344,1024]{2,1,0:T(8,128)(2,1)} %param.12) | copy-start | bytes 8257540
  1.0 12.7 %collective-permute-start = (bf16[48,1024]{1,0:T(8,128)(2,1)S(1)}, bf16[48,1024]{1,0:T(8,128)(2,1)S(1)}, u32[]{:S(2)}, u32[]{:S(2)}) collective-permute-start(bf16[48,1024]{1,0:T(8,128)(2,1)S(1)} %fusion.62), channel_id=1, source_target_pairs={{0,4},{2,6},{1,5},{3,7},{8,12},{10,14},{9,13},{11,15},{16,20},{18,... | collective-permute-start | bytes 294920 | tf_op jit(solution)/shard_map/ppermute | solution.py:102
  7.9 8.8 %collective-permute-start.1 = (bf16[128,1024]{1,0:T(8,128)(2,1)S(1)}, bf16[128,1024]{1,0:T(8,128)(2,1)S(1)}, u32[]{:S(2)}, u32[]{:S(2)}) collective-permute-start(bf16[128,1024]{1,0:T(8,128)(2,1)S(1)} %pad_maximum_fusion.refs_2_), channel_id=1, source_target_pairs={{0,2},{2,4},{4,6},{1,3},{3,5},{5,7},{8,10},{10,12},{12,14},{9,11},... | collective-permute-start | bytes 786440 | tf_op jit(solution)/shard_map/ppermute | solution.py:102
  11.4 0.7 copy-start.1
  13.7 0.6 copy-start.7
  16.7 0.7 copy-start.5
  17.4 0.9 copy-start.2
  18.3 0.9 copy-start.3
  19.3 0.9 copy-start.4
  20.2 0.9 copy-start.6
  21.2 0.9 copy-start.8
  25.0 17.5 %collective-permute-start.2 = (bf16[128,1024]{1,0:T(8,128)(2,1)}, bf16[128,1024]{1,0:T(8,128)(2,1)}, u32[]{:S(2)}, u32[]{:S(2)}) collective-permute-start(bf16[128,1024]{1,0:T(8,128)(2,1)} %get-tuple-element.11), channel_id=1, source_target_pairs={{2,0},{4,2},{6,4},{3,1},{5,3},{7,5},{10,8},{12,10},{14,12},{11,9},... | collective-permute-start | bytes 786440 | tf_op jit(solution)/shard_map/ppermute | solution.py:102
  26.3 16.2 %collective-permute-start.3 = (bf16[48,1024]{1,0:T(8,128)(2,1)}, bf16[48,1024]{1,0:T(8,128)(2,1)}, u32[]{:S(2)}, u32[]{:S(2)}) collective-permute-start(bf16[48,1024]{1,0:T(8,128)(2,1)} %get-tuple-element.12), channel_id=1, source_target_pairs={{4,0},{6,2},{5,1},{7,3},{12,8},{14,10},{13,9},{15,11},{20,16},{22,... | collective-permute-start | bytes 294920 | tf_op jit(solution)/shard_map/ppermute | solution.py:102
  27.6 25.5 %collective-permute-start.7 = (bf16[128,1024]{1,0:T(8,128)(2,1)S(1)}, bf16[128,1024]{1,0:T(8,128)(2,1)}, u32[]{:S(2)}, u32[]{:S(2)}) collective-permute-start(bf16[128,1024]{1,0:T(8,128)(2,1)S(1)} %get-tuple-element.9), channel_id=1, source_target_pairs={{2,0},{4,2},{6,4},{3,1},{5,3},{7,5},{10,8},{12,10},{14,12},{11,9},... | collective-permute-start | bytes 786440 | tf_op jit(solution)/shard_map/ppermute | solution.py:102
  28.9 25.5 %collective-permute-start.6 = (bf16[128,1024]{1,0:T(8,128)(2,1)S(1)}, bf16[128,1024]{1,0:T(8,128)(2,1)}, u32[]{:S(2)}, u32[]{:S(2)}) collective-permute-start(bf16[128,1024]{1,0:T(8,128)(2,1)S(1)} %get-tuple-element.9), channel_id=1, source_target_pairs={{0,2},{2,4},{4,6},{1,3},{3,5},{5,7},{8,10},{10,12},{12,14},{9,11},... | collective-permute-start | bytes 786440 | tf_op jit(solution)/shard_map/ppermute | solution.py:102
  44.3 2.0 %copy-start.10 = (bf16[1,1344,512]{2,1,0:T(8,128)(2,1)S(1)}, bf16[1,1344,512]{2,1,0:T(8,128)(2,1)}, u32[]{:S(2)}) copy-start(bf16[1,1344,512]{2,1,0:T(8,128)(2,1)} %param.13) | copy-start | bytes 4128772
  48.7 0.8 copy-start.12
  50.2 4.9 %collective-permute-start.4 = (bf16[128,672]{0,1:T(8,128)(2,1)}, bf16[128,672]{0,1:T(8,128)(2,1)S(1)}, u32[]{:S(2)}, u32[]{:S(2)}) collective-permute-start(bf16[128,672]{0,1:T(8,128)(2,1)} %select_convert_fusion.3), channel_id=1, source_target_pairs={{1,0},{0,1},{3,2},{2,3},{5,4},{4,5},{7,6},{6,7},{9,8},{8,9},{11,10... | collective-permute-start | bytes 516104 | tf_op jit(solution)/shard_map/ppermute | solution.py:107
  50.2 8.5 %collective-permute-start.8 = (bf16[128,1024]{1,0:T(8,128)(2,1)}, bf16[128,1024]{1,0:T(8,128)(2,1)S(1)}, u32[]{:S(2)}, u32[]{:S(2)}) collective-permute-start(bf16[128,1024]{1,0:T(8,128)(2,1)} %add_convert_fusion.1), channel_id=1, source_target_pairs={{0,2},{2,4},{4,6},{1,3},{3,5},{5,7},{8,10},{10,12},{12,14},{9,11},... | collective-permute-start | bytes 786440 | tf_op jit(solution)/shard_map/ppermute | solution.py:102
  51.6 11.4 %copy-start.9 = (bf16[1,1344,512]{2,1,0:T(8,128)(2,1)S(1)}, bf16[1,1344,512]{2,1,0:T(8,128)(2,1)}, u32[]{:S(2)}) copy-start(bf16[1,1344,512]{2,1,0:T(8,128)(2,1)} %param.14) | copy-start | bytes 4128772
  51.6 11.3 %collective-permute-start.9 = (bf16[128,1024]{1,0:T(8,128)(2,1)}, bf16[128,1024]{1,0:T(8,128)(2,1)S(1)}, u32[]{:S(2)}, u32[]{:S(2)}) collective-permute-start(bf16[128,1024]{1,0:T(8,128)(2,1)} %add_convert_fusion.1), channel_id=1, source_target_pairs={{2,0},{4,2},{6,4},{3,1},{5,3},{7,5},{10,8},{12,10},{14,12},{11,9},... | collective-permute-start | bytes 786440 | tf_op jit(solution)/shard_map/ppermute | solution.py:102
  53.1 15.1 %collective-permute-start.13 = (bf16[128,1024]{1,0:T(8,128)(2,1)}, bf16[128,1024]{1,0:T(8,128)(2,1)S(1)}, u32[]{:S(2)}, u32[]{:S(2)}) collective-permute-start(bf16[128,1024]{1,0:T(8,128)(2,1)} %collective-permute-done.7), channel_id=1, source_target_pairs={{2,0},{4,2},{3,1},{5,3},{10,8},{12,10},{11,9},{13,11},{18,16},{20,... | collective-permute-start | bytes 786440 | tf_op jit(solution)/shard_map/ppermute | solution.py:102
  54.4 13.8 %collective-permute-start.12 = (bf16[128,1024]{1,0:T(8,128)(2,1)}, bf16[128,1024]{1,0:T(8,128)(2,1)S(1)}, u32[]{:S(2)}, u32[]{:S(2)}) collective-permute-start(bf16[128,1024]{1,0:T(8,128)(2,1)} %collective-permute-done.6), channel_id=1, source_target_pairs={{2,4},{4,6},{3,5},{5,7},{10,12},{12,14},{11,13},{13,15},{18,20},{2... | collective-permute-start | bytes 786440 | tf_op jit(solution)/shard_map/ppermute | solution.py:102
  56.2 17.4 %collective-permute-start.5 = (bf16[128,672]{0,1:T(8,128)(2,1)S(1)}, bf16[128,672]{0,1:T(8,128)(2,1)S(1)}, u32[]{:S(2)}, u32[]{:S(2)}) collective-permute-start(bf16[128,672]{0,1:T(8,128)(2,1)S(1)} %add_convert_fusion.4), channel_id=1, source_target_pairs={{8,0},{16,8},{24,16},{0,24},{9,1},{17,9},{25,17},{1,25},{10,2},{18... | collective-permute-start | bytes 516104 | tf_op jit(solution)/shard_map/ppermute | solution.py:107
  63.0 1.3 %copy-start.11 = (bf16[1,1344,512]{2,1,0:T(8,128)(2,1)S(1)}, bf16[1,1344,512]{2,1,0:T(8,128)(2,1)}, u32[]{:S(2)}) copy-start(bf16[1,1344,512]{2,1,0:T(8,128)(2,1)} %param.13) | copy-start | bytes 4128772
  68.2 25.5 %collective-permute-start.14 = (bf16[128,1024]{1,0:T(8,128)(2,1)S(1)}, bf16[128,1024]{1,0:T(8,128)(2,1)S(1)}, u32[]{:S(2)}, u32[]{:S(2)}) collective-permute-start(bf16[128,1024]{1,0:T(8,128)(2,1)S(1)} %broadcast_select_fusion.1), channel_id=1, source_target_pairs={{4,6},{2,0},{5,7},{3,1},{12,14},{10,8},{13,15},{11,9},{20,22},{18,... | collective-permute-start | bytes 786440 | tf_op jit(solution)/shard_map/ppermute | solution.py:161
  69.5 14.1 %collective-permute-start.16 = (bf16[128,1024]{1,0:T(8,128)(2,1)S(1)}, bf16[128,1024]{1,0:T(8,128)(2,1)S(1)}, u32[]{:S(2)}, u32[]{:S(2)}) collective-permute-start(bf16[128,1024]{1,0:T(8,128)(2,1)S(1)} %collective-permute-done.9), channel_id=1, source_target_pairs={{2,0},{4,2},{3,1},{5,3},{10,8},{12,10},{11,9},{13,11},{18,16},{20,... | collective-permute-start | bytes 786440 | tf_op jit(solution)/shard_map/ppermute | solution.py:102
  70.8 12.8 %collective-permute-start.15 = (bf16[128,1024]{1,0:T(8,128)(2,1)S(1)}, bf16[128,1024]{1,0:T(8,128)(2,1)S(1)}, u32[]{:S(2)}, u32[]{:S(2)}) collective-permute-start(bf16[128,1024]{1,0:T(8,128)(2,1)S(1)} %collective-permute-done.8), channel_id=1, source_target_pairs={{2,4},{4,6},{3,5},{5,7},{10,12},{12,14},{11,13},{13,15},{18,20},{2... | collective-permute-start | bytes 786440 | tf_op jit(solution)/shard_map/ppermute | solution.py:102
  73.6 21.2 %collective-permute-start.10 = (bf16[256,672]{0,1:T(8,128)(2,1)S(1)}, bf16[256,672]{0,1:T(8,128)(2,1)S(1)}, u32[]{:S(2)}, u32[]{:S(2)}) collective-permute-start(bf16[256,672]{0,1:T(8,128)(2,1)S(1)} %select_convert_fusion), channel_id=1, source_target_pairs={{1,0},{0,1},{3,2},{2,3},{5,4},{4,5},{7,6},{6,7},{9,8},{8,9},{11,10... | collective-permute-start | bytes 1032200 | tf_op jit(solution)/shard_map/ppermute | solution.py:107
  83.7 8.9 %collective-permute-start.17 = (bf16[128,1024]{1,0:T(8,128)(2,1)S(1)}, bf16[128,1024]{1,0:T(8,128)(2,1)S(1)}, u32[]{:S(2)}, u32[]{:S(2)}) collective-permute-start(bf16[128,1024]{1,0:T(8,128)(2,1)S(1)} %broadcast_select_fusion), channel_id=1, source_target_pairs={{4,6},{2,0},{5,7},{3,1},{12,14},{10,8},{13,15},{11,9},{20,22},{18,... | collective-permute-start | bytes 786440 | tf_op jit(solution)/shard_map/ppermute | solution.py:161
  87.0 11.7 %collective-permute-start.20 = (bf16[128,672]{0,1:T(8,128)(2,1)S(1)}, bf16[128,672]{0,1:T(8,128)(2,1)S(1)}, u32[]{:S(2)}, u32[]{:S(2)}) collective-permute-start(bf16[128,672]{0,1:T(8,128)(2,1)S(1)} %select_convert_fusion.1), channel_id=1, source_target_pairs={{1,0},{0,1},{3,2},{2,3},{5,4},{4,5},{7,6},{6,7},{9,8},{8,9},{11,10... | collective-permute-start | bytes 516104 | tf_op jit(solution)/shard_map/ppermute | solution.py:107
  94.6 2.7 %collective-permute-start.18 = (bf16[128,672]{0,1:T(8,128)(2,1)S(1)}, bf16[128,672]{0,1:T(8,128)(2,1)S(1)}, u32[]{:S(2)}, u32[]{:S(2)}) collective-permute-start(bf16[128,672]{0,1:T(8,128)(2,1)S(1)} %select_convert_fusion.2), channel_id=1, source_target_pairs={{1,0},{0,1},{3,2},{2,3},{5,4},{4,5},{7,6},{6,7},{9,8},{8,9},{11,10... | collective-permute-start | bytes 516104 | tf_op jit(solution)/shard_map/ppermute | solution.py:107
  94.9 10.9 %collective-permute-start.11 = (bf16[256,672]{0,1:T(8,128)(2,1)S(1)}, bf16[256,672]{0,1:T(8,128)(2,1)S(1)}, u32[]{:S(2)}, u32[]{:S(2)}) collective-permute-start(bf16[256,672]{0,1:T(8,128)(2,1)S(1)} %add_convert_fusion), channel_id=1, source_target_pairs={{8,0},{16,8},{24,16},{0,24},{9,1},{17,9},{25,17},{1,25},{10,2},{18... | collective-permute-start | bytes 1032200 | tf_op jit(solution)/shard_map/ppermute | solution.py:107
  97.4 12.0 %collective-permute-start.19 = (bf16[128,672]{0,1:T(8,128)(2,1)S(1)}, bf16[128,672]{0,1:T(8,128)(2,1)S(1)}, u32[]{:S(2)}, u32[]{:S(2)}) collective-permute-start(bf16[128,672]{0,1:T(8,128)(2,1)S(1)} %add_convert_fusion.3), channel_id=1, source_target_pairs={{8,0},{16,8},{24,16},{0,24},{9,1},{17,9},{25,17},{1,25},{10,2},{18... | collective-permute-start | bytes 516104 | tf_op jit(solution)/shard_map/ppermute | solution.py:107
  98.8 14.0 %collective-permute-start.21 = (bf16[128,672]{0,1:T(8,128)(2,1)S(1)}, bf16[128,672]{0,1:T(8,128)(2,1)S(1)}, u32[]{:S(2)}, u32[]{:S(2)}) collective-permute-start(bf16[128,672]{0,1:T(8,128)(2,1)S(1)} %add_convert_fusion.2), channel_id=1, source_target_pairs={{8,0},{16,8},{24,16},{0,24},{9,1},{17,9},{25,17},{1,25},{10,2},{18... | collective-permute-start | bytes 516104 | tf_op jit(solution)/shard_map/ppermute | solution.py:107
  112.8 0.8 copy-start.13

commit v2 on v1

--- a/solution.py
+++ b/solution.py
@@ -82,15 +82,100 @@
     return pl.pallas_call(
         functools.partial(attention_kernel, kv_heads, group_width, halo_rows),
         out_shape=outs,
-        in_specs=[whole] * (4 + len(halos)),
+        in_specs=[pl.BlockSpec()] * 2 + [whole] * (2 + len(halos)),
         out_specs=[whole] * len(outs),
-        compiler_params=pltpu.CompilerParams(vmem_limit_bytes=32 * 1024 * 1024),
+        compiler_params=pltpu.CompilerParams(vmem_limit_bytes=8 * 1024 * 1024),
         cost_estimate=pl.CostEstimate(
             flops=12 * rows * span * query_cols,
             bytes_accessed=4 * rows * query_cols * 2,
             transcendentals=rows * span * kv_heads * group_width,
         ),
     )(query, grad, kv, bias, *halos)
+
+
+def join_kernel(query_ref, kv_ref, *refs):
+    *part_refs, joined_ref, total_ref = refs
+    rows = kv_ref.shape[0]
+    query_cols = query_ref.shape[1]
+    joined_ref[:, :query_cols] = query_ref[...]
+    total = kv_ref[...]
+    for part_ref in part_refs:
+        size = part_ref.shape[0]
+        part = part_ref[...].astype(jnp.float32)
+        if size < rows:
+            part = jnp.concatenate(
+                [jnp.zeros((rows - size, part.shape[1]), jnp.float32), part], axis=0
+            )
+        total = total + part
+    total = total.astype(jnp.bfloat16)
+    joined_ref[:, query_cols:] = total
+    total_ref[...] = total
+
+
+def join(query_part, kv_part, returned):
+    rows, query_cols = query_part.shape
+    kv_cols = kv_part.shape[1]
+    whole = pl.BlockSpec(memory_space=pltpu.VMEM)
+    return pl.pallas_call(
+        join_kernel,
+        out_shape=[
+            jax.ShapeDtypeStruct((rows, query_cols + kv_cols), jnp.bfloat16),
+            jax.ShapeDtypeStruct((rows, kv_cols), jnp.bfloat16),
+        ],
+        in_specs=[whole] * (2 + len(returned)),
+        out_specs=[whole] * 2,
+        compiler_params=pltpu.CompilerParams(vmem_limit_bytes=8 * 1024 * 1024),
+        cost_estimate=pl.CostEstimate(flops=1, bytes_accessed=1, transcendentals=0),
+    )(query_part, kv_part, *returned)
+
+
+def project_kernel(pieces, tile, core_ref, *refs):
+    flat_refs, (query_weight, key_weight, value_weight) = refs[: sum(pieces)], refs[-6:-3]
+    full_ref, give_ref, block_ref = refs[-3:]
+    row, at = 0, 0
+    for count in pieces:
+        column = 0
+        for ref in flat_refs[at : at + count]:
+            block_ref[row : row + ref.shape[0], column : column + ref.shape[1]] = ref[...]
+            column += ref.shape[1]
+        at += count
+        row += flat_refs[at - 1].shape[0]
+    query_cols, kv_cols = query_weight.shape[1], key_weight.shape[1]
+
+    def step(i, carry):
+        at = pl.ds(pl.multiple_of(i * tile, 16), tile)
+        full_ref[at, :] = (
+            dot(query_weight[at, :], block_ref[:, :query_cols], 1, 1)
+            + dot(key_weight[at, :], block_ref[:, query_cols : query_cols + kv_cols], 1, 1)
+            + dot(value_weight[at, :], block_ref[:, query_cols + kv_cols :], 1, 1)
+        )
+        return carry
+
+    lax.fori_loop(0, full_ref.shape[0] // tile, step, 0)
+    half = give_ref.shape[0]
+    other = pl.multiple_of((1 - core_ref[0]) * half, 8)
+    give_ref[...] = full_ref[pl.ds(other, half), :].astype(jnp.bfloat16)
+
+
+def project(blocks, weights, core):
+    width = weights[0].shape[0]
+    rows = sum(block[0].shape[0] for block in blocks)
+    cols = sum(weight.shape[1] for weight in weights)
+    tile = max(t for t in range(16, 449, 16) if width % t == 0)
+    flat = [piece for block in blocks for piece in block]
+    whole = pl.BlockSpec(memory_space=pltpu.VMEM)
+    return pl.pallas_call(
+        functools.partial(project_kernel, [len(block) for block in blocks], tile),
+        out_shape=[
+            jax.ShapeDtypeStruct((width, rows), jnp.float32),
+            jax.ShapeDtypeStruct((width // 2, rows), jnp.bfloat16),
+        ],
+        in_specs=[pl.BlockSpec(memory_space=pltpu.SMEM)] + [whole] * (len(flat) + 3),
+        out_specs=[whole] * 2,
+        scratch_shapes=[pltpu.VMEM((rows, cols), jnp.bfloat16)],
+        compiler_params=pltpu.CompilerParams(vmem_limit_bytes=8 * 1024 * 1024),
+        cost_estimate=pl.CostEstimate(flops=1, bytes_accessed=1, transcendentals=0),
+    )(core, *flat, *weights)
 
 
 def moved(block, axis, by, first=0):
@@ -100,6 +185,10 @@
     else:
         sources = range(-by, size - first)
     return lax.ppermute(block, axis, [(i, i + by) for i in sources])
+
+
+def after(arrays, *others):
+    return lax.optimization_barrier((*arrays, *others))[: len(arrays)]
 
 
 def passed_along(block, axis, distance):
@@ -123,12 +212,13 @@
     kv_cols = key_row_matrix.shape[2]
     shards = lax.axis_size("seq")
     place = lax.axis_index("seq")
-    core = lax.axis_index("mp")
     back = min(WINDOW, tokens // 3) - 1
     halo_rows = []
     while sum(halo_rows) < back and len(halo_rows) < shards - 1:
         halo_rows.append(min(rows, -(-(back - sum(halo_rows)) // 16) * 16))
-    kv = jnp.concatenate([key_row_matrix[0], value_row_matrix[0]], axis=1)
+    kv = lax.optimization_barrier(
+        jnp.concatenate([key_row_matrix[0], value_row_matrix[0]], axis=1)
+    )
     halos = [moved(kv[rows - size :], "seq", d) for d, size in enumerate(halo_rows, 1)]
     reach = sum(halo_rows)
     first_row = place * rows
@@ -146,63 +236,74 @@
     grad_query, grad_kv, *grad_halos = attention_backward(
         query_rows[0], out_grad[0], kv, bias, halos[::-1]
     )
-    for d, part in enumerate(grad_halos[::-1], 1):
-        part = moved(part, "seq", -d).astype(jnp.float32)
-        grad_kv = grad_kv + jnp.pad(part, ((rows - part.shape[0], 0), (0, 0)))
-    grad_kv = grad_kv.astype(jnp.bfloat16)
-
-    def chain(piece):
-        up, down = piece, piece
-        arrived = []
-        for step in range(1, shards):
-            if 2 * step > shards + 1:
-                both = [(i, i + 1) for i in range(step - 1, shards - 1)]
-                both += [(i, i - 1) for i in range(1, shards - step + 1)]
-                up = down = lax.ppermute(up, "seq", both)
-                arrived.append([up])
-                continue
-            up = moved(up, "seq", 1, step - 1)
+    returned = [moved(part, "seq", -d) for d, part in enumerate(grad_halos[::-1], 1)]
+    query_up = moved(grad_query, "seq", 1)
+    held, *returned = after((grad_query, *returned), query_up)
+    own, kv_up = join(held, grad_kv, returned)
+    down = own
+    weights = (w_query[0], key_weight[0], value_weight[0])
+    core = lax.axis_index("mp").astype(jnp.int32)
+
+    def halves_summed(blocks):
+        full, give = project(blocks, weights, core[None])
+        half = give.shape[0]
+        keep = lax.dynamic_slice_in_dim(full, core * half, half, 0)
+        got = passed_along(give, "mp", 1)
+        return give, (keep + got.astype(jnp.float32)).astype(jnp.bfloat16)
+
+    results, waiting = [], [[own]]
+    for step in range(1, shards):
+        if 2 * step > shards + 1:
+            both = [(i, i + 1) for i in range(step - 1, shards - 1)]
+            both += [(i, i - 1) for i in range(1, shards - step + 1)]
+            down = lax.ppermute(down, "seq", both)
+            arrived = [[down]]
+            early = None
+        else:
+            if step > 1:
+                query_up = moved(query_up, "seq", 1, step - 1)
+            kv_up = moved(kv_up, "seq", 1, step - 1)
             down = moved(down, "seq", -1, step - 1)
+            arrived = [[query_up, kv_up], [down]]
+            early = kv_up if step == 1 else query_up
             if 2 * step >= shards:
-                up = down = jnp.where(place >= step, up, down)
-                arrived.append([up])
-            else:
-                arrived.append([up, down])
-        return arrived
-
-    def finished(query_part, kv_part):
-        partial = (
-            dot(query_part, w_query[0], 1, 1)
-            + dot(kv_part[:, :kv_cols], key_weight[0], 1, 1)
-            + dot(kv_part[:, kv_cols:], value_weight[0], 1, 1)
-        )
-        half = partial.shape[1] // 2
-        low, high = partial[:, :half], partial[:, half:]
-        keep = jnp.where(core == 0, low, high)
-        give = jnp.where(core == 0, high, low).astype(jnp.bfloat16)
-        got = passed_along(give, "mp", 1)
-        total = (keep + got.astype(jnp.float32)).astype(jnp.bfloat16)
-        return passed_along(total, "section", -1)
-
-    query_steps, kv_steps = chain(grad_query), chain(grad_kv)
-    results = [[finished(grad_query, grad_kv)]]
-    for query_parts, kv_parts in zip(query_steps, kv_steps):
-        if len(query_parts) == 1:
-            results.append([finished(query_parts[0], kv_parts[0])])
-        else:
-            joined = finished(
-                jnp.concatenate(query_parts, axis=0), jnp.concatenate(kv_parts, axis=0)
-            )
-            results.append([joined[:rows], joined[rows:]])
-    upstream = jnp.zeros((tokens, results[0][0].shape[1]), jnp.bfloat16)
+                up = jnp.concatenate([query_up, kv_up], axis=1)
+                down = jnp.where(place >= step, up, down)
+                arrived = [[down]]
+        others = [] if early is None else [early]
+        if step == 2:
+            others.append(total)
+        elif step > 2:
+            others += [results[step - 3], total]
+        if others:
+            waiting = [after(tuple(block), *others) for block in waiting]
+        give, total = halves_summed(waiting)
+        if 2 * step <= shards + 1:
+            (down,) = after((down,), give)
+        results.append(passed_along(total, "section", -1))
+        waiting = arrived
+        if 2 * step >= shards:
+            waiting = [[down]]
+    last = tuple(waiting[0])
+    if shards > 1:
+        last = after(last, total, *results[:-1])
+    total = halves_summed([last, *waiting[1:]])[1]
+    if shards > 1:
+        (total,) = after((total,), results[-1])
+    results.append(passed_along(total, "section", -1))
+    results = [
+        [block[:, i * rows : (i + 1) * rows] for i in range(block.shape[1] // rows)]
+        for block in results
+    ]
+    upstream = jnp.zeros((results[0][0].shape[0], tokens), jnp.bfloat16)
     for s in range(shards):
         behind = results[s][0]
         ahead = results[(shards - s) % shards][-1]
         block = jnp.where(place >= s, behind, ahead)
         upstream = lax.dynamic_update_slice_in_dim(
-            upstream, block, ((place - s) % shards) * rows, 0
+            upstream, block, ((place - s) % shards) * rows, 1
         )
-    return upstream[None]
+    return upstream.T[None]
 
 
 def solution(mesh):

time: 115 us -> 109 us (0.948)
  matrix products: 11.3 us -> 0 us
  Pallas kernels: 2.92 us -> 12.9 us
  waiting for transfers between devices: 45.8 us -> 40.9 us
  other arithmetic: 6.9 us -> 3.81 us
  starting transfers between devices: 36.2 us -> 39.1 us
    dot_general x12 -> x0, matrix products: 11.3 us -> none  [dot(): lax.dot_general(left, right, (((left_dim,), (right_dim,)), ((), ())), pre...]
    pallas_call x0 -> x5, Pallas kernels: none -> 10.6 us  [the longest x4 9.85 us: project(): pl.pallas_call(functools.partial(project_kernel, [len(block) for block in...]
    ppermute x12 -> x10, waiting for transfers between devices: 27.1 us -> 16.9 us  [moved(): return lax.ppermute(block, axis, [(i, i + by) for i in sources])]
    ppermute x8, waiting for transfers between devices: 13.1 us -> 17.1 us  [passed_along(): lax.ppermute(block, axis, [((i - distance) % len(devices), i) for i in de...]
    convert_element_type x9 -> x4, other arithmetic: 3.97 us -> 1.27 us  [halves_summed(): return (give, (keep + got.astype(jnp.float32)).astype(jnp.bfloat16))]
    ppermute x8, starting transfers between devices: 7.29 us -> 9.71 us  [passed_along(): lax.ppermute(block, axis, [((i - distance) % len(devices), i) for i in de...]
    ppermute x12 -> x10, starting transfers between devices: 26.3 us -> 28.1 us  [moved(): return lax.ppermute(block, axis, [(i, i + by) for i in sources])]
    ppermute x2 -> x1, waiting for transfers between devices: 5.55 us -> 6.87 us  [per_device(): down = lax.ppermute(down, 'seq', both)]
  transfers between devices with their start and end apart: 22 -> 19, of which waited for: 9 -> 8; matrix products, arithmetic and copies ran while one was open for 16% -> 4% of each run, Pallas kernels for 0% -> 7%
where the time goes in v2:
time: 109 us; the launch traced here: 107 us
  waiting for transfers between devices  40.9 us (38%)
  starting transfers between devices  39.1 us (36%)
  Pallas kernels  12.9 us (12%)
  local copies, waits for them, and re-layouts  10.5 us (10%)
  other arithmetic  3.81 us (3%)
    ppermute x10, starting transfers between devices, moved(): return lax.ppermute(block, axis, [(i, i + by) for i in sources])  28.1 us
    ppermute x8, waiting for transfers between devices, passed_along(): lax.ppermute(block, axis, [((i - distance) % len(devices), i) for i in de...  17.1 us
    ppermute x10, waiting for transfers between devices, moved(): return lax.ppermute(block, axis, [(i, i + by) for i in sources])  16.9 us
    pallas_call x4, Pallas kernels, project(): pl.pallas_call(functools.partial(project_kernel, [len(block) for block in...  9.85 us
    ppermute x8, starting transfers between devices, passed_along(): lax.ppermute(block, axis, [((i - distance) % len(devices), i) for i in de...  9.71 us
    unnamed x26, local copies, waits for them, and re-layouts  8.97 us
    ppermute x1, waiting for transfers between devices, per_device(): down = lax.ppermute(down, 'seq', both)  6.87 us
    pallas_call x1, Pallas kernels, attention_backward(): pl.pallas_call(functools.partial(attention_kernel, kv_heads, group_width,...  2.23 us
  transfers between devices with their start and end apart: 19, of which 8 were waited for; matrix products, arithmetic and copies ran while one was open for 4% of the time, Pallas kernels for 7%

profile of v2, /device:TPU:0, one launch (start us, length us, event | category | flops | bytes accessed | tf_op | source)
XLA Modules:
  0.0 107.5 jit_solution(1076432249012911181)
XLA Ops:
  0.0 1.0 pad_maximum_fusion.refs_2_
  1.0 4.9 %collective-permute-start.1 = (bf16[128,1024]{1,0:T(8,128)(2,1)S(1)}, bf16[128,1024]{1,0:T(8,128)(2,1)S(1)}, u32[]{:S(2)}, u32[]{:S(2)}) collective-permute-start(bf16[128,1024]{1,0:T(8,128)(2,1)S(1)} %pad_maximum_fusion.refs_2_), channel_id=1, source_target_pairs={{0,2},{2,4},{4,6},{1,3},{3,5},{5,7},{8,10},{10,12},{12,14},{9,11},... | collective-permute-start | bytes 786440 | tf_op jit(solution)/shard_map/ppermute | solution.py:187
  6.0 4.5 %collective-permute-start = (bf16[48,1024]{1,0:T(8,128)(2,1)S(1)}, bf16[48,1024]{1,0:T(8,128)(2,1)S(1)}, u32[]{:S(2)}, u32[]{:S(2)}) collective-permute-start(bf16[48,1024]{1,0:T(8,128)(2,1)S(1)} %slice.12), channel_id=1, source_target_pairs={{0,4},{2,6},{1,5},{3,7},{8,12},{10,14},{9,13},{11,15},{16,20},{18,... | collective-permute-start | bytes 294920 | tf_op jit(solution)/shard_map/ppermute | solution.py:187
  10.5 0.8 pad_dynamic-slice_fusion
  11.2 0.7 fusion.7
  11.9 0.1 fusion.6.refs_3_
  12.0 1.6 %collective-permute-done.refs_4_ = bf16[48,1024]{1,0:T(8,128)(2,1)S(1)} collective-permute-done((bf16[48,1024]{1,0:T(8,128)(2,1)S(1)}, bf16[48,1024]{1,0:T(8,128)(2,1)S(1)}, u32[]{:S(2)}, u32[]{:S(2)}) %collective-permute-start) | collective-permute-done | bytes 98336 | tf_op jit(solution)/shard_map/ppermute | solution.py:187
  13.6 0.0 collective-permute-done.1.refs_5_
  13.6 0.9 copy-done.8
  14.6 0.9 copy-done.9
  15.5 2.2 %shard_map.82 = (bf16[128,1024]{1,0:T(8,128)(2,1)S(1)}, f32[128,1024]{1,0:T(8,128)S(1)}, bf16[48,1024]{1,0:T(8,128)(2,1)S(1)}, bf16[128,1024]{1,0:T(8,128)(2,1)S(1)}) custom-call(bf16[128,1024]{1,0:T(8,128)(2,1)S(1)} %bitcast.26, bf16[128,1024]{1,0:T(8,128)(2,1)S(1)} %bitcast.27, bf16[128,1024]{1,0:T(8,128)(2,1)S(1)} %pad_maximum_fusion.refs_2_, ...), custom_call_target="tpu_custom_call" | custom-call | flops 478150656 | bytes 1048576 | tf_op jit(solution)/shard_map/pallas_call | solution.py:82
  17.8 5.6 %collective-permute-start.4 = (bf16[128,1024]{1,0:T(8,128)(2,1)S(1)}, bf16[128,1024]{1,0:T(8,128)(2,1)S(1)}, u32[]{:S(2)}, u32[]{:S(2)}) collective-permute-start(bf16[128,1024]{1,0:T(8,128)(2,1)S(1)} %get-tuple-element.34.query_ref), channel_id=1, source_target_pairs={{0,2},{2,4},{4,6},{1,3},{3,5},{5,7},{8,10},{10,12},{12,14},{9,11},... | collective-permute-start | bytes 786440 | tf_op jit(solution)/shard_map/ppermute | solution.py:187
  23.3 1.3 %collective-permute-start.2 = (bf16[128,1024]{1,0:T(8,128)(2,1)S(1)}, bf16[128,1024]{1,0:T(8,128)(2,1)S(1)}, u32[]{:S(2)}, u32[]{:S(2)}) collective-permute-start(bf16[128,1024]{1,0:T(8,128)(2,1)S(1)} %get-tuple-element.32), channel_id=1, source_target_pairs={{2,0},{4,2},{6,4},{3,1},{5,3},{7,5},{10,8},{12,10},{14,12},{11,9},... | collective-permute-start | bytes 786440 | tf_op jit(solution)/shard_map/ppermute | solution.py:187
  24.6 1.3 %collective-permute-start.3 = (bf16[48,1024]{1,0:T(8,128)(2,1)S(1)}, bf16[48,1024]{1,0:T(8,128)(2,1)S(1)}, u32[]{:S(2)}, u32[]{:S(2)}) collective-permute-start(bf16[48,1024]{1,0:T(8,128)(2,1)S(1)} %get-tuple-element.33), channel_id=1, source_target_pairs={{4,0},{6,2},{5,1},{7,3},{12,8},{14,10},{13,9},{15,11},{20,16},{22,... | collective-permute-start | bytes 294920 | tf_op jit(solution)/shard_map/ppermute | solution.py:187
  25.9 11.7 %collective-permute-done.3.refs_1_ = bf16[48,1024]{1,0:T(8,128)(2,1)S(1)} collective-permute-done((bf16[48,1024]{1,0:T(8,128)(2,1)S(1)}, bf16[48,1024]{1,0:T(8,128)(2,1)S(1)}, u32[]{:S(2)}, u32[]{:S(2)}) %collective-permute-start.3) | collective-permute-done | bytes 98336 | tf_op jit(solution)/shard_map/ppermute | solution.py:187
  37.7 0.0 collective-permute-done.4.refs_0_
  37.7 0.0 collective-permute-done.2.refs_0_
  37.7 0.8 shard_map.83
  38.5 1.3 %collective-permute-start.9 = (bf16[128,2048]{1,0:T(8,128)(2,1)S(1)}, bf16[128,2048]{1,0:T(8,128)(2,1)}, u32[]{:S(2)}, u32[]{:S(2)}) collective-permute-start(bf16[128,2048]{1,0:T(8,128)(2,1)S(1)} %get-tuple-element.40.refs_0_), channel_id=1, source_target_pairs={{2,0},{4,2},{6,4},{3,1},{5,3},{7,5},{10,8},{12,10},{14,12},{11,9},... | collective-permute-start | bytes 1572872 | tf_op jit(solution)/shard_map/ppermute | solution.py:187
  39.8 5.2 %collective-permute-start.5 = (bf16[128,1024]{1,0:T(8,128)(2,1)}, bf16[128,1024]{1,0:T(8,128)(2,1)}, u32[]{:S(2)}, u32[]{:S(2)}) collective-permute-start(bf16[128,1024]{1,0:T(8,128)(2,1)} %get-tuple-element.39), channel_id=1, source_target_pairs={{0,2},{2,4},{4,6},{1,3},{3,5},{5,7},{8,10},{10,12},{12,14},{9,11},... | collective-permute-start | bytes 786440 | tf_op jit(solution)/shard_map/ppermute | solution.py:187
  45.0 3.5 %collective-permute-done.5.refs_1_ = bf16[128,1024]{1,0:T(8,128)(2,1)} collective-permute-done((bf16[128,1024]{1,0:T(8,128)(2,1)}, bf16[128,1024]{1,0:T(8,128)(2,1)}, u32[]{:S(2)}, u32[]{:S(2)}) %collective-permute-start.5) | collective-permute-done | bytes 262176 | tf_op jit(solution)/shard_map/ppermute | solution.py:187
  48.5 1.3 %copy-done.1 = bf16[1,1344,512]{2,1,0:T(8,128)(2,1)S(1)} copy-done((bf16[1,1344,512]{2,1,0:T(8,128)(2,1)S(1)}, bf16[1,1344,512]{2,1,0:T(8,128)(2,1)}, u32[]{:S(2)}) %copy-start.1) | copy-done | bytes 1376280
  49.8 1.3 %copy-done.4 = bf16[1,1344,512]{2,1,0:T(8,128)(2,1)S(1)} copy-done((bf16[1,1344,512]{2,1,0:T(8,128)(2,1)S(1)}, bf16[1,1344,512]{2,1,0:T(8,128)(2,1)}, u32[]{:S(2)}) %copy-start.4) | copy-done | bytes 1376280
  51.2 2.6 %shard_map.84 = (f32[1344,128]{1,0:T(8,128)S(1)}, bf16[672,128]{1,0:T(8,128)(2,1)}) custom-call(s32[1]{0:T(128)} %bitcast.core_ref, bf16[128,2048]{1,0:T(8,128)(2,1)S(1)} %get-tuple-element.40.refs_0_, bf16[1344,1024]{1,0:T(8,128)(2,1)S(1)} %bitcast.14, bf16[1344,512]{1,0:T(8,128)(2,1)S(1)} %bitcast.18, bf16[1344,512]{1,0:T(8,128)(2,1)S(1)} %bitcast.22), custom_call_target="tpu_custom_call" | custom-call | flops 1 | bytes 1 | tf_op jit(solution)/shard_map/pallas_call | solution.py:167
  53.8 0.8 copy-done.7
  54.7 0.0 collective-permute-done.9.refs_2_
  54.7 1.3 %collective-permute-start.13 = (bf16[128,2048]{1,0:T(8,128)(2,1)}, bf16[128,2048]{1,0:T(8,128)(2,1)S(1)}, u32[]{:S(2)}, u32[]{:S(2)}) collective-permute-start(bf16[128,2048]{1,0:T(8,128)(2,1)} %collective-permute-done.9.refs_2_), channel_id=1, source_target_pairs={{2,0},{4,2},{3,1},{5,3},{10,8},{12,10},{11,9},{13,11},{18,16},{20,... | collective-permute-start | bytes 1572872 | tf_op jit(solution)/shard_map/ppermute | solution.py:187
  56.0 0.1 collective-permute-start.6
  56.0 1.4 %collective-permute-start.8 = (bf16[128,1024]{1,0:T(8,128)(2,1)S(1)}, bf16[128,1024]{1,0:T(8,128)(2,1)}, u32[]{:S(2)}, u32[]{:S(2)}) collective-permute-start(bf16[128,1024]{1,0:T(8,128)(2,1)S(1)} %collective-permute-done.4.refs_0_), channel_id=1, source_target_pairs={{2,4},{4,6},{3,5},{5,7},{10,12},{12,14},{11,13},{13,15},{18,20},{2... | collective-permute-start | bytes 786440 | tf_op jit(solution)/shard_map/ppermute | solution.py:187
  57.4 1.4 %collective-permute-start.12 = (bf16[128,1024]{1,0:T(8,128)(2,1)}, bf16[128,1024]{1,0:T(8,128)(2,1)}, u32[]{:S(2)}, u32[]{:S(2)}) collective-permute-start(bf16[128,1024]{1,0:T(8,128)(2,1)} %collective-permute-done.5.refs_1_), channel_id=1, source_target_pairs={{2,4},{4,6},{3,5},{5,7},{10,12},{12,14},{11,13},{13,15},{18,20},{2... | collective-permute-start | bytes 786440 | tf_op jit(solution)/shard_map/ppermute | solution.py:187
  58.8 0.0 collective-permute-done.6
  58.8 1.1 %add_convert_fusion.3 = bf16[672,128]{1,0:T(8,128)(2,1)S(1)} fusion(bf16[672,128]{1,0:T(8,128)(2,1)} %collective-permute-done.6, f32[1344,128]{1,0:T(8,128)} %copy-done.7, s32[]{:T(128)S(6)} %select_n.76), kind=kLoop, calls=%fused_computation.4 | loop fusion | flops 258048 | bytes 688132 | tf_op jit(solution)/shard_map/convert_element_type | solution.py:252
  59.9 2.5 %collective-permute-start.7 = (bf16[672,128]{1,0:T(8,128)(2,1)S(1)}, bf16[672,128]{1,0:T(8,128)(2,1)S(1)}, u32[]{:S(2)}, u32[]{:S(2)}) collective-permute-start(bf16[672,128]{1,0:T(8,128)(2,1)S(1)} %add_convert_fusion.3), channel_id=1, source_target_pairs={{8,0},{16,8},{24,16},{0,24},{9,1},{17,9},{25,17},{1,25},{10,2},{18... | collective-permute-start | bytes 516104 | tf_op jit(solution)/shard_map/ppermute | solution.py:196
  62.4 0.0 collective-permute-done.8
  62.4 1.3 %copy-done.2 = bf16[1,1344,512]{2,1,0:T(8,128)(2,1)S(1)} copy-done((bf16[1,1344,512]{2,1,0:T(8,128)(2,1)S(1)}, bf16[1,1344,512]{2,1,0:T(8,128)(2,1)}, u32[]{:S(2)}) %copy-start.2) | copy-done | bytes 1376280
  63.7 1.3 %copy-done.5 = bf16[1,1344,512]{2,1,0:T(8,128)(2,1)S(1)} copy-done((bf16[1,1344,512]{2,1,0:T(8,128)(2,1)S(1)}, bf16[1,1344,512]{2,1,0:T(8,128)(2,1)}, u32[]{:S(2)}) %copy-start.5) | copy-done | bytes 1376280
  65.1 3.3 %shard_map.85 = (f32[1344,256]{1,0:T(8,128)S(1)}, bf16[672,256]{1,0:T(8,128)(2,1)S(1)}) custom-call(s32[1]{0:T(128)} %bitcast.core_ref, bf16[128,1024]{1,0:T(8,128)(2,1)S(1)} %collective-permute-done.4.refs_0_, bf16[128,1024]{1,0:T(8,128)(2,1)} %collective-permute-done.5.refs_1_, bf16[128,2048]{1,0:T(8,128)(2,1)} %collective-permute-done.9.refs_2_, ...), custom_call_target="tpu_custom_call" | custom-call | flops 1 | bytes 1 | tf_op jit(solution)/shard_map/pallas_call | solution.py:167
  68.3 0.0 copy-start.3
  68.3 0.0 copy-start.6
  68.4 0.3 collective-permute-start.10
  68.6 0.0 collective-permute-done.12
  68.6 0.0 collective-permute-done.13
  68.6 1.3 %maximum_select_fusion.refs_0_ = bf16[128,2048]{1,0:T(8,128)(2,1)S(1)} fusion(bf16[128,2048]{1,0:T(8,128)(2,1)S(1)} %collective-permute-done.13, bf16[128,1024]{1,0:T(8,128)(2,1)} %collective-permute-done.12, bf16[128,1024]{1,0:T(8,128)(2,1)} %collective-permute-done.8, pred[]{:T(512)S(6)} %ge.20), kind=kLoop, calls=%fused_computation.1 | loop fusion | flops 1310720 | bytes 1572865 | tf_op jit(solution)/shard_map/jit(_where)/select_n | solution.py:271
  69.9 1.3 %collective-permute-start.14 = (bf16[128,2048]{1,0:T(8,128)(2,1)S(1)}, bf16[128,2048]{1,0:T(8,128)(2,1)S(1)}, u32[]{:S(2)}, u32[]{:S(2)}) collective-permute-start(bf16[128,2048]{1,0:T(8,128)(2,1)S(1)} %maximum_select_fusion.refs_0_), channel_id=1, source_target_pairs={{4,6},{2,0},{5,7},{3,1},{12,14},{10,8},{13,15},{11,9},{20,22},{18,... | collective-permute-start | bytes 1572872 | tf_op jit(solution)/shard_map/ppermute | solution.py:259
  71.2 0.0 collective-permute-done.10
  71.2 0.1 add_convert_fusion
  71.4 0.0 copy-start.11
  71.4 2.0 %shard_map.86 = (f32[1344,128]{1,0:T(8,128)S(1)}, bf16[672,128]{1,0:T(8,128)(2,1)S(1)}) custom-call(s32[1]{0:T(128)} %bitcast.core_ref, bf16[128,2048]{1,0:T(8,128)(2,1)S(1)} %maximum_select_fusion.refs_0_, bf16[1344,1024]{1,0:T(8,128)(2,1)S(1)} %bitcast.16, bf16[1344,512]{1,0:T(8,128)(2,1)S(1)} %bitcast.20, bf16[1344,512]{1,0:T(8,128)(2,1)S(1)} %bitcast.24), custom_call_target="tpu_custom_call" | custom-call | flops 1 | bytes 1 | tf_op jit(solution)/shard_map/pallas_call | solution.py:167
  73.4 0.4 collective-permute-start.15
  73.8 0.5 collective-permute-start.11
  74.3 0.5 collective-permute-done.15
  74.9 9.0 %collective-permute-done.11 = bf16[672,256]{1,0:T(8,128)(2,1)S(1)} collective-permute-done((bf16[672,256]{1,0:T(8,128)(2,1)S(1)}, bf16[672,256]{1,0:T(8,128)(2,1)S(1)}, u32[]{:S(2)}, u32[]{:S(2)}) %collective-permute-start.11) | collective-permute-done | bytes 344096 | tf_op jit(solution)/shard_map/ppermute | solution.py:196
  83.9 6.9 %collective-permute-done.14.refs_0_ = bf16[128,2048]{1,0:T(8,128)(2,1)S(1)} collective-permute-done((bf16[128,2048]{1,0:T(8,128)(2,1)S(1)}, bf16[128,2048]{1,0:T(8,128)(2,1)S(1)}, u32[]{:S(2)}, u32[]{:S(2)}) %collective-permute-start.14) | collective-permute-done | bytes 524320 | tf_op jit(solution)/shard_map/ppermute | solution.py:259
  90.8 2.0 %shard_map.87 = (f32[1344,128]{1,0:T(8,128)S(1)}, bf16[672,128]{1,0:T(8,128)(2,1)S(1)}) custom-call(s32[1]{0:T(128)} %bitcast.core_ref, bf16[128,2048]{1,0:T(8,128)(2,1)S(1)} %collective-permute-done.14.refs_0_, bf16[1344,1024]{1,0:T(8,128)(2,1)S(1)} %bitcast.17, bf16[1344,512]{1,0:T(8,128)(2,1)S(1)} %bitcast.21, bf16[1344,512]{1,0:T(8,128)(2,1)S(1)} %bitcast.25), custom_call_target="tpu_custom_call" | custom-call | flops 1 | bytes 1 | tf_op jit(solution)/shard_map/pallas_call | solution.py:167
  92.8 0.0 copy-start.12
  92.8 0.1 collective-permute-start.16
  92.9 2.5 %collective-permute-start.17 = (bf16[672,128]{1,0:T(8,128)(2,1)S(1)}, bf16[672,128]{1,0:T(8,128)(2,1)S(1)}, u32[]{:S(2)}, u32[]{:S(2)}) collective-permute-start(bf16[672,128]{1,0:T(8,128)(2,1)S(1)} %add_convert_fusion.2), channel_id=1, source_target_pairs={{8,0},{16,8},{24,16},{0,24},{9,1},{17,9},{25,17},{1,25},{10,2},{18... | collective-permute-start | bytes 516104 | tf_op jit(solution)/shard_map/ppermute | solution.py:196
  95.4 4.2 %collective-permute-done.17 = bf16[672,128]{1,0:T(8,128)(2,1)S(1)} collective-permute-done((bf16[672,128]{1,0:T(8,128)(2,1)S(1)}, bf16[672,128]{1,0:T(8,128)(2,1)S(1)}, u32[]{:S(2)}, u32[]{:S(2)}) %collective-permute-start.17) | collective-permute-done | bytes 172064 | tf_op jit(solution)/shard_map/ppermute | solution.py:196
  99.6 3.3 %collective-permute-start.18 = (bf16[672,128]{1,0:T(8,128)(2,1)S(1)}, bf16[672,128]{1,0:T(8,128)(2,1)S(1)}, u32[]{:S(2)}, u32[]{:S(2)}) collective-permute-start(bf16[672,128]{1,0:T(8,128)(2,1)S(1)} %add_convert_fusion.1), channel_id=1, source_target_pairs={{8,0},{16,8},{24,16},{0,24},{9,1},{17,9},{25,17},{1,25},{10,2},{18... | collective-permute-start | bytes 516104 | tf_op jit(solution)/shard_map/ppermute | solution.py:196
  103.1 3.3 %collective-permute-done.18 = bf16[672,128]{1,0:T(8,128)(2,1)S(1)} collective-permute-done((bf16[672,128]{1,0:T(8,128)(2,1)S(1)}, bf16[672,128]{1,0:T(8,128)(2,1)S(1)}, u32[]{:S(2)}, u32[]{:S(2)}) %collective-permute-start.18) | collective-permute-done | bytes 172064 | tf_op jit(solution)/shard_map/ppermute | solution.py:196
  106.4 0.1 fusion.1
  106.6 0.1 fusion
  106.6 0.0 copy-start.10
  106.7 0.8 copy-done.10
  (22 shorter events, 0.3 us)
Async XLA Ops:
  1.0 12.6 %collective-permute-start.1 = (bf16[128,1024]{1,0:T(8,128)(2,1)S(1)}, bf16[128,1024]{1,0:T(8,128)(2,1)S(1)}, u32[]{:S(2)}, u32[]{:S(2)}) collective-permute-start(bf16[128,1024]{1,0:T(8,128)(2,1)S(1)} %pad_maximum_fusion.refs_2_), channel_id=1, source_target_pairs={{0,2},{2,4},{4,6},{1,3},{3,5},{5,7},{8,10},{10,12},{12,14},{9,11},... | collective-permute-start | bytes 786440 | tf_op jit(solution)/shard_map/ppermute | solution.py:187
  6.0 7.7 %collective-permute-start = (bf16[48,1024]{1,0:T(8,128)(2,1)S(1)}, bf16[48,1024]{1,0:T(8,128)(2,1)S(1)}, u32[]{:S(2)}, u32[]{:S(2)}) collective-permute-start(bf16[48,1024]{1,0:T(8,128)(2,1)S(1)} %slice.12), channel_id=1, source_target_pairs={{0,4},{2,6},{1,5},{3,7},{8,12},{10,14},{9,13},{11,15},{16,20},{18,... | collective-permute-start | bytes 294920 | tf_op jit(solution)/shard_map/ppermute | solution.py:187
  13.6 1.0 copy-start.8
  14.6 0.9 copy-start.9
  15.5 33.0 %copy-start = (bf16[1,1344,1024]{2,1,0:T(8,128)(2,1)S(1)}, bf16[1,1344,1024]{2,1,0:T(8,128)(2,1)}, u32[]{:S(2)}) copy-start(bf16[1,1344,1024]{2,1,0:T(8,128)(2,1)} %param.12) | copy-start | bytes 8257540
  17.8 19.9 %collective-permute-start.4 = (bf16[128,1024]{1,0:T(8,128)(2,1)S(1)}, bf16[128,1024]{1,0:T(8,128)(2,1)S(1)}, u32[]{:S(2)}, u32[]{:S(2)}) collective-permute-start(bf16[128,1024]{1,0:T(8,128)(2,1)S(1)} %get-tuple-element.34.query_ref), channel_id=1, source_target_pairs={{0,2},{2,4},{4,6},{1,3},{3,5},{5,7},{8,10},{10,12},{12,14},{9,11},... | collective-permute-start | bytes 786440 | tf_op jit(solution)/shard_map/ppermute | solution.py:187
  23.3 14.3 %collective-permute-start.2 = (bf16[128,1024]{1,0:T(8,128)(2,1)S(1)}, bf16[128,1024]{1,0:T(8,128)(2,1)S(1)}, u32[]{:S(2)}, u32[]{:S(2)}) collective-permute-start(bf16[128,1024]{1,0:T(8,128)(2,1)S(1)} %get-tuple-element.32), channel_id=1, source_target_pairs={{2,0},{4,2},{6,4},{3,1},{5,3},{7,5},{10,8},{12,10},{14,12},{11,9},... | collective-permute-start | bytes 786440 | tf_op jit(solution)/shard_map/ppermute | solution.py:187
  24.6 13.0 %collective-permute-start.3 = (bf16[48,1024]{1,0:T(8,128)(2,1)S(1)}, bf16[48,1024]{1,0:T(8,128)(2,1)S(1)}, u32[]{:S(2)}, u32[]{:S(2)}) collective-permute-start(bf16[48,1024]{1,0:T(8,128)(2,1)S(1)} %get-tuple-element.33), channel_id=1, source_target_pairs={{4,0},{6,2},{5,1},{7,3},{12,8},{14,10},{13,9},{15,11},{20,16},{22,... | collective-permute-start | bytes 294920 | tf_op jit(solution)/shard_map/ppermute | solution.py:187
  38.5 16.2 %collective-permute-start.9 = (bf16[128,2048]{1,0:T(8,128)(2,1)S(1)}, bf16[128,2048]{1,0:T(8,128)(2,1)}, u32[]{:S(2)}, u32[]{:S(2)}) collective-permute-start(bf16[128,2048]{1,0:T(8,128)(2,1)S(1)} %get-tuple-element.40.refs_0_), channel_id=1, source_target_pairs={{2,0},{4,2},{6,4},{3,1},{5,3},{7,5},{10,8},{12,10},{14,12},{11,9},... | collective-permute-start | bytes 1572872 | tf_op jit(solution)/shard_map/ppermute | solution.py:187
  39.8 8.7 %collective-permute-start.5 = (bf16[128,1024]{1,0:T(8,128)(2,1)}, bf16[128,1024]{1,0:T(8,128)(2,1)}, u32[]{:S(2)}, u32[]{:S(2)}) collective-permute-start(bf16[128,1024]{1,0:T(8,128)(2,1)} %get-tuple-element.39), channel_id=1, source_target_pairs={{0,2},{2,4},{4,6},{1,3},{3,5},{5,7},{8,10},{10,12},{12,14},{9,11},... | collective-permute-start | bytes 786440 | tf_op jit(solution)/shard_map/ppermute | solution.py:187
  48.5 1.3 %copy-start.1 = (bf16[1,1344,512]{2,1,0:T(8,128)(2,1)S(1)}, bf16[1,1344,512]{2,1,0:T(8,128)(2,1)}, u32[]{:S(2)}) copy-start(bf16[1,1344,512]{2,1,0:T(8,128)(2,1)} %param.13) | copy-start | bytes 4128772
  49.8 1.3 %copy-start.4 = (bf16[1,1344,512]{2,1,0:T(8,128)(2,1)S(1)}, bf16[1,1344,512]{2,1,0:T(8,128)(2,1)}, u32[]{:S(2)}) copy-start(bf16[1,1344,512]{2,1,0:T(8,128)(2,1)} %param.14) | copy-start | bytes 4128772
  53.8 0.8 copy-start.7
  54.7 14.0 %collective-permute-start.13 = (bf16[128,2048]{1,0:T(8,128)(2,1)}, bf16[128,2048]{1,0:T(8,128)(2,1)S(1)}, u32[]{:S(2)}, u32[]{:S(2)}) collective-permute-start(bf16[128,2048]{1,0:T(8,128)(2,1)} %collective-permute-done.9.refs_2_), channel_id=1, source_target_pairs={{2,0},{4,2},{3,1},{5,3},{10,8},{12,10},{11,9},{13,11},{18,16},{20,... | collective-permute-start | bytes 1572872 | tf_op jit(solution)/shard_map/ppermute | solution.py:187
  56.0 2.8 %collective-permute-start.6 = (bf16[672,128]{1,0:T(8,128)(2,1)}, bf16[672,128]{1,0:T(8,128)(2,1)}, u32[]{:S(2)}, u32[]{:S(2)}) collective-permute-start(bf16[672,128]{1,0:T(8,128)(2,1)} %get-tuple-element.42), channel_id=1, source_target_pairs={{1,0},{0,1},{3,2},{2,3},{5,4},{4,5},{7,6},{6,7},{9,8},{8,9},{11,10... | collective-permute-start | bytes 516104 | tf_op jit(solution)/shard_map/ppermute | solution.py:196
  56.0 6.3 %collective-permute-start.8 = (bf16[128,1024]{1,0:T(8,128)(2,1)S(1)}, bf16[128,1024]{1,0:T(8,128)(2,1)}, u32[]{:S(2)}, u32[]{:S(2)}) collective-permute-start(bf16[128,1024]{1,0:T(8,128)(2,1)S(1)} %collective-permute-done.4.refs_0_), channel_id=1, source_target_pairs={{2,4},{4,6},{3,5},{5,7},{10,12},{12,14},{11,13},{13,15},{18,20},{2... | collective-permute-start | bytes 786440 | tf_op jit(solution)/shard_map/ppermute | solution.py:187
  57.4 11.2 %collective-permute-start.12 = (bf16[128,1024]{1,0:T(8,128)(2,1)}, bf16[128,1024]{1,0:T(8,128)(2,1)}, u32[]{:S(2)}, u32[]{:S(2)}) collective-permute-start(bf16[128,1024]{1,0:T(8,128)(2,1)} %collective-permute-done.5.refs_1_), channel_id=1, source_target_pairs={{2,4},{4,6},{3,5},{5,7},{10,12},{12,14},{11,13},{13,15},{18,20},{2... | collective-permute-start | bytes 786440 | tf_op jit(solution)/shard_map/ppermute | solution.py:187
  59.9 11.4 %collective-permute-start.7 = (bf16[672,128]{1,0:T(8,128)(2,1)S(1)}, bf16[672,128]{1,0:T(8,128)(2,1)S(1)}, u32[]{:S(2)}, u32[]{:S(2)}) collective-permute-start(bf16[672,128]{1,0:T(8,128)(2,1)S(1)} %add_convert_fusion.3), channel_id=1, source_target_pairs={{8,0},{16,8},{24,16},{0,24},{9,1},{17,9},{25,17},{1,25},{10,2},{18... | collective-permute-start | bytes 516104 | tf_op jit(solution)/shard_map/ppermute | solution.py:196
  62.4 1.3 %copy-start.2 = (bf16[1,1344,512]{2,1,0:T(8,128)(2,1)S(1)}, bf16[1,1344,512]{2,1,0:T(8,128)(2,1)}, u32[]{:S(2)}) copy-start(bf16[1,1344,512]{2,1,0:T(8,128)(2,1)} %param.13) | copy-start | bytes 4128772
  63.7 1.3 %copy-start.5 = (bf16[1,1344,512]{2,1,0:T(8,128)(2,1)S(1)}, bf16[1,1344,512]{2,1,0:T(8,128)(2,1)}, u32[]{:S(2)}) copy-start(bf16[1,1344,512]{2,1,0:T(8,128)(2,1)} %param.14) | copy-start | bytes 4128772
  68.3 3.0 %copy-start.3 = (bf16[1,1344,512]{2,1,0:T(8,128)(2,1)S(1)}, bf16[1,1344,512]{2,1,0:T(8,128)(2,1)}, u32[]{:S(2)}) copy-start(bf16[1,1344,512]{2,1,0:T(8,128)(2,1)} %param.13) | copy-start | bytes 4128772
  68.3 3.0 %copy-start.6 = (bf16[1,1344,512]{2,1,0:T(8,128)(2,1)S(1)}, bf16[1,1344,512]{2,1,0:T(8,128)(2,1)}, u32[]{:S(2)}) copy-start(bf16[1,1344,512]{2,1,0:T(8,128)(2,1)} %param.14) | copy-start | bytes 4128772
  68.4 2.9 %collective-permute-start.10 = (bf16[672,256]{1,0:T(8,128)(2,1)S(1)}, bf16[672,256]{1,0:T(8,128)(2,1)S(1)}, u32[]{:S(2)}, u32[]{:S(2)}) collective-permute-start(bf16[672,256]{1,0:T(8,128)(2,1)S(1)} %get-tuple-element.47), channel_id=1, source_target_pairs={{1,0},{0,1},{3,2},{2,3},{5,4},{4,5},{7,6},{6,7},{9,8},{8,9},{11,10... | collective-permute-start | bytes 1032200 | tf_op jit(solution)/shard_map/ppermute | solution.py:196
  69.9 20.9 %collective-permute-start.14 = (bf16[128,2048]{1,0:T(8,128)(2,1)S(1)}, bf16[128,2048]{1,0:T(8,128)(2,1)S(1)}, u32[]{:S(2)}, u32[]{:S(2)}) collective-permute-start(bf16[128,2048]{1,0:T(8,128)(2,1)S(1)} %maximum_select_fusion.refs_0_), channel_id=1, source_target_pairs={{4,6},{2,0},{5,7},{3,1},{12,14},{10,8},{13,15},{11,9},{20,22},{18,... | collective-permute-start | bytes 1572872 | tf_op jit(solution)/shard_map/ppermute | solution.py:259
  71.4 2.0 %copy-start.11 = (bf16[672,128]{1,0:T(8,128)(2,1)}, bf16[672,128]{1,0:T(8,128)(2,1)S(1)}, u32[]{:S(2)}) copy-start(bf16[672,128]{1,0:T(8,128)(2,1)S(1)} %collective-permute-done.7) | copy-start | bytes 516100
  73.4 1.5 %collective-permute-start.15 = (bf16[672,128]{1,0:T(8,128)(2,1)S(1)}, bf16[672,128]{1,0:T(8,128)(2,1)S(1)}, u32[]{:S(2)}, u32[]{:S(2)}) collective-permute-start(bf16[672,128]{1,0:T(8,128)(2,1)S(1)} %get-tuple-element.52), channel_id=1, source_target_pairs={{1,0},{0,1},{3,2},{2,3},{5,4},{4,5},{7,6},{6,7},{9,8},{8,9},{11,10... | collective-permute-start | bytes 516104 | tf_op jit(solution)/shard_map/ppermute | solution.py:196
  73.8 10.1 %collective-permute-start.11 = (bf16[672,256]{1,0:T(8,128)(2,1)S(1)}, bf16[672,256]{1,0:T(8,128)(2,1)S(1)}, u32[]{:S(2)}, u32[]{:S(2)}) collective-permute-start(bf16[672,256]{1,0:T(8,128)(2,1)S(1)} %add_convert_fusion), channel_id=1, source_target_pairs={{8,0},{16,8},{24,16},{0,24},{9,1},{17,9},{25,17},{1,25},{10,2},{18... | collective-permute-start | bytes 1032200 | tf_op jit(solution)/shard_map/ppermute | solution.py:196
  92.8 10.3 %copy-start.12 = (bf16[672,128]{1,0:T(8,128)(2,1)S(1)}, bf16[672,128]{1,0:T(8,128)(2,1)}, u32[]{:S(2)}) copy-start(bf16[672,128]{1,0:T(8,128)(2,1)} %copy-done.11) | copy-start | bytes 516100
  92.8 2.6 %collective-permute-start.16 = (bf16[672,128]{1,0:T(8,128)(2,1)S(1)}, bf16[672,128]{1,0:T(8,128)(2,1)S(1)}, u32[]{:S(2)}, u32[]{:S(2)}) collective-permute-start(bf16[672,128]{1,0:T(8,128)(2,1)S(1)} %get-tuple-element.55), channel_id=1, source_target_pairs={{1,0},{0,1},{3,2},{2,3},{5,4},{4,5},{7,6},{6,7},{9,8},{8,9},{11,10... | collective-permute-start | bytes 516104 | tf_op jit(solution)/shard_map/ppermute | solution.py:196
  92.9 6.8 %collective-permute-start.17 = (bf16[672,128]{1,0:T(8,128)(2,1)S(1)}, bf16[672,128]{1,0:T(8,128)(2,1)S(1)}, u32[]{:S(2)}, u32[]{:S(2)}) collective-permute-start(bf16[672,128]{1,0:T(8,128)(2,1)S(1)} %add_convert_fusion.2), channel_id=1, source_target_pairs={{8,0},{16,8},{24,16},{0,24},{9,1},{17,9},{25,17},{1,25},{10,2},{18... | collective-permute-start | bytes 516104 | tf_op jit(solution)/shard_map/ppermute | solution.py:196
  99.6 6.8 %collective-permute-start.18 = (bf16[672,128]{1,0:T(8,128)(2,1)S(1)}, bf16[672,128]{1,0:T(8,128)(2,1)S(1)}, u32[]{:S(2)}, u32[]{:S(2)}) collective-permute-start(bf16[672,128]{1,0:T(8,128)(2,1)S(1)} %add_convert_fusion.1), channel_id=1, source_target_pairs={{8,0},{16,8},{24,16},{0,24},{9,1},{17,9},{25,17},{1,25},{10,2},{18... | collective-permute-start | bytes 516104 | tf_op jit(solution)/shard_map/ppermute | solution.py:196
  106.6 0.8 copy-start.10

commit v3 on v2

--- a/solution.py
+++ b/solution.py
@@ -22,24 +22,42 @@
     )
 
 
+def stack_kernel(kv_heads, group_width, query_ref, grad_ref, query_out, grad_out):
+    rows = query_ref.shape[0]
+    for head in range(kv_heads * group_width):
+        cols = slice(head * HEAD_WIDTH, (head + 1) * HEAD_WIDTH)
+        query_out[head * rows : (head + 1) * rows, :] = query_ref[:, cols]
+        grad_out[head * rows : (head + 1) * rows, :] = grad_ref[:, cols]
+
+
+def stack(query, grad, kv_heads, group_width):
+    rows, query_cols = query.shape
+    whole = pl.BlockSpec(memory_space=pltpu.VMEM)
+    shape = jax.ShapeDtypeStruct((rows * kv_heads * group_width, HEAD_WIDTH), jnp.bfloat16)
+    return pl.pallas_call(
+        functools.partial(stack_kernel, kv_heads, group_width),
+        out_shape=[shape] * 2,
+        in_specs=[whole] * 2,
+        out_specs=[whole] * 2,
+        compiler_params=pltpu.CompilerParams(vmem_limit_bytes=8 * 1024 * 1024),
+        cost_estimate=pl.CostEstimate(flops=1, bytes_accessed=1, transcendentals=0),
+    )(query, grad)
+
+
 def attention_kernel(kv_heads, group_width, halo_rows, *refs):
     halo_count = len(halo_rows)
     query_ref, grad_ref, kv_ref, bias_ref = refs[:4]
     halo_refs = refs[4 : 4 + halo_count]
     grad_query_ref, grad_kv_ref = refs[4 + halo_count : 6 + halo_count]
     grad_halo_refs = refs[6 + halo_count :]
-    rows = query_ref.shape[0]
+    rows = kv_ref.shape[0]
     kv_cols = kv_heads * HEAD_WIDTH
     scaling = 1.0 / math.sqrt(HEAD_WIDTH)
     bias = jnp.concatenate([bias_ref[...]] * group_width, axis=1)
     for group in range(kv_heads):
         heads = [group * group_width + member for member in range(group_width)]
-        query = jnp.concatenate(
-            [query_ref[:, h * HEAD_WIDTH : (h + 1) * HEAD_WIDTH] for h in heads], axis=0
-        )
-        grad = jnp.concatenate(
-            [grad_ref[:, h * HEAD_WIDTH : (h + 1) * HEAD_WIDTH] for h in heads], axis=0
-        )
+        stacked = slice(heads[0] * rows, (heads[-1] + 1) * rows)
+        query, grad = query_ref[stacked, :], grad_ref[stacked, :]
         key_cols = slice(group * HEAD_WIDTH, (group + 1) * HEAD_WIDTH)
         value_cols = slice(kv_cols + group * HEAD_WIDTH, kv_cols + (group + 1) * HEAD_WIDTH)
         blocks = [*halo_refs, kv_ref]
@@ -67,10 +85,10 @@
 
 
 def attention_backward(query, grad, kv, bias, halos):
-    rows, query_cols = query.shape
-    kv_cols = kv.shape[1] // 2
+    rows, kv_cols = kv.shape[0], kv.shape[1] // 2
     kv_heads = kv_cols // HEAD_WIDTH
-    group_width = query_cols // kv_cols
+    group_width = query.shape[0] // (rows * kv_heads)
+    query_cols = kv_heads * group_width * HEAD_WIDTH
     halo_rows = [halo.shape[0] for halo in halos]
     span = bias.shape[0]
     whole = pl.BlockSpec(memory_space=pltpu.VMEM)
@@ -82,7 +100,7 @@
     return pl.pallas_call(
         functools.partial(attention_kernel, kv_heads, group_width, halo_rows),
         out_shape=outs,
-        in_specs=[pl.BlockSpec()] * 2 + [whole] * (2 + len(halos)),
+        in_specs=[whole] * (4 + len(halos)),
         out_specs=[whole] * len(outs),
         compiler_params=pltpu.CompilerParams(vmem_limit_bytes=8 * 1024 * 1024),
         cost_estimate=pl.CostEstimate(
@@ -94,7 +112,7 @@
 
 
 def join_kernel(query_ref, kv_ref, *refs):
-    *part_refs, joined_ref, total_ref = refs
+    *part_refs, joined_ref = refs
     rows = kv_ref.shape[0]
     query_cols = query_ref.shape[1]
     joined_ref[:, :query_cols] = query_ref[...]
@@ -107,9 +125,7 @@
                 [jnp.zeros((rows - size, part.shape[1]), jnp.float32), part], axis=0
             )
         total = total + part
-    total = total.astype(jnp.bfloat16)
-    joined_ref[:, query_cols:] = total
-    total_ref[...] = total
+    joined_ref[:, query_cols:] = total.astype(jnp.bfloat16)
 
 
 def join(query_part, kv_part, returned):
@@ -118,12 +134,9 @@
     whole = pl.BlockSpec(memory_space=pltpu.VMEM)
     return pl.pallas_call(
         join_kernel,
-        out_shape=[
-            jax.ShapeDtypeStruct((rows, query_cols + kv_cols), jnp.bfloat16),
-            jax.ShapeDtypeStruct((rows, kv_cols), jnp.bfloat16),
-        ],
+        out_shape=jax.ShapeDtypeStruct((rows, query_cols + kv_cols), jnp.bfloat16),
         in_specs=[whole] * (2 + len(returned)),
-        out_specs=[whole] * 2,
+        out_specs=whole,
         compiler_params=pltpu.CompilerParams(vmem_limit_bytes=8 * 1024 * 1024),
         cost_estimate=pl.CostEstimate(flops=1, bytes_accessed=1, transcendentals=0),
     )(query_part, kv_part, *returned)
@@ -174,17 +187,20 @@
         out_specs=[whole] * 2,
         scratch_shapes=[pltpu.VMEM((rows, cols), jnp.bfloat16)],
         compiler_params=pltpu.CompilerParams(vmem_limit_bytes=8 * 1024 * 1024),
-        cost_estimate=pl.CostEstimate(flops=1, bytes_accessed=1, transcendentals=0),
+        cost_estimate=pl.CostEstimate(
+            flops=2 * rows * width * cols,
+            bytes_accessed=2 * width * cols + 6 * width * rows,
+            transcendentals=0,
+        ),
     )(core, *flat, *weights)
 
 
-def moved(block, axis, by, first=0):
+def swapped(block, axis, first):
     size = lax.axis_size(axis)
-    if by > 0:
-        sources = range(first, size - by)
-    else:
-        sources = range(-by, size - first)
-    return lax.ppermute(block, axis, [(i, i + by) for i in sources])
+    target = list(range(size))
+    for i in range(first, size - 1, 2):
+        target[i], target[i + 1] = i + 1, i
+    return lax.ppermute(block, axis, list(enumerate(target)))
 
 
 def after(arrays, *others):
@@ -219,7 +235,7 @@
     kv = lax.optimization_barrier(
         jnp.concatenate([key_row_matrix[0], value_row_matrix[0]], axis=1)
     )
-    halos = [moved(kv[rows - size :], "seq", d) for d, size in enumerate(halo_rows, 1)]
+    halos = [passed_along(kv[rows - size :], "seq", d) for d, size in enumerate(halo_rows, 1)]
     reach = sum(halo_rows)
     first_row = place * rows
     key_docs = lax.dynamic_slice_in_dim(
@@ -233,68 +249,56 @@
     )
     allowed = (query_docs[None, :] == key_docs[:, None]) & (offset >= 0) & (offset < WINDOW)
     bias = jnp.where(allowed, 0.0, MASKED).astype(jnp.float32)
+    kv_heads = kv_cols // HEAD_WIDTH
+    query_stack, grad_stack = stack(
+        *after((query_rows[0], out_grad[0]), kv), kv_heads, query_rows.shape[2] // kv_cols
+    )
     grad_query, grad_kv, *grad_halos = attention_backward(
-        query_rows[0], out_grad[0], kv, bias, halos[::-1]
-    )
-    returned = [moved(part, "seq", -d) for d, part in enumerate(grad_halos[::-1], 1)]
-    query_up = moved(grad_query, "seq", 1)
-    held, *returned = after((grad_query, *returned), query_up)
-    own, kv_up = join(held, grad_kv, returned)
-    down = own
+        query_stack, grad_stack, kv, bias, halos[::-1]
+    )
+    returned = [passed_along(part, "seq", -d) for d, part in enumerate(grad_halos[::-1], 1)]
+    own = join(grad_query, grad_kv, returned)
     weights = (w_query[0], key_weight[0], value_weight[0])
     core = lax.axis_index("mp").astype(jnp.int32)
 
     def halves_summed(blocks):
-        full, give = project(blocks, weights, core[None])
+        full, give = project([(block,) for block in blocks], weights, core[None])
         half = give.shape[0]
         keep = lax.dynamic_slice_in_dim(full, core * half, half, 0)
         got = passed_along(give, "mp", 1)
         return give, (keep + got.astype(jnp.float32)).astype(jnp.bfloat16)
 
-    results, waiting = [], [[own]]
+    even = place % 2 == 0
+    results, waiting = [], [own]
+    by_first, by_second = own, own
     for step in range(1, shards):
-        if 2 * step > shards + 1:
-            both = [(i, i + 1) for i in range(step - 1, shards - 1)]
-            both += [(i, i - 1) for i in range(1, shards - step + 1)]
-            down = lax.ppermute(down, "seq", both)
-            arrived = [[down]]
-            early = None
+        came_first = swapped(by_first, "seq", 0)
+        last = step == shards - 1 and shards % 2 == 0
+        came_second = came_first if last else swapped(by_second, "seq", 1)
+        if step == 2:
+            waiting = after(waiting, total)
+        elif step > 2:
+            waiting = after(waiting, total, results[step - 3])
+        give, total = halves_summed(waiting)
+        if step < shards - 1:
+            came_first, came_second = after((came_first, came_second), give)
+        results.append(passed_along(total, "section", -1))
+        by_first, by_second = came_second, came_first
+        if last:
+            waiting = [came_first]
+        elif 2 * step < shards:
+            waiting = [came_first, came_second]
         else:
-            if step > 1:
-                query_up = moved(query_up, "seq", 1, step - 1)
-            kv_up = moved(kv_up, "seq", 1, step - 1)
-            down = moved(down, "seq", -1, step - 1)
-            arrived = [[query_up, kv_up], [down]]
-            early = kv_up if step == 1 else query_up
-            if 2 * step >= shards:
-                up = jnp.concatenate([query_up, kv_up], axis=1)
-                down = jnp.where(place >= step, up, down)
-                arrived = [[down]]
-        others = [] if early is None else [early]
-        if step == 2:
-            others.append(total)
-        elif step > 2:
-            others += [results[step - 3], total]
-        if others:
-            waiting = [after(tuple(block), *others) for block in waiting]
-        give, total = halves_summed(waiting)
-        if 2 * step <= shards + 1:
-            (down,) = after((down,), give)
-        results.append(passed_along(total, "section", -1))
-        waiting = arrived
-        if 2 * step >= shards:
-            waiting = [[down]]
-    last = tuple(waiting[0])
+            waiting = [jnp.where(even == (place >= step), came_second, came_first)]
     if shards > 1:
-        last = after(last, total, *results[:-1])
-    total = halves_summed([last, *waiting[1:]])[1]
-    if shards > 1:
-        (total,) = after((total,), results[-1])
-    results.append(passed_along(total, "section", -1))
-    results = [
-        [block[:, i * rows : (i + 1) * rows] for i in range(block.shape[1] // rows)]
-        for block in results
-    ]
+        waiting = after(waiting, *results)
+    results.append(passed_along(halves_summed(waiting)[1], "section", -1))
+    for step, block in enumerate(results):
+        if block.shape[1] == rows:
+            results[step] = [block]
+        else:
+            first, second = block[:, :rows], block[:, rows:]
+            results[step] = [jnp.where(even, second, first), jnp.where(even, first, second)]
     upstream = jnp.zeros((results[0][0].shape[0], tokens), jnp.bfloat16)
     for s in range(shards):
         behind = results[s][0]

time: 109 us -> 102 us (0.936)
  starting transfers between devices: 39.1 us -> 33.9 us
  waiting for transfers between devices: 40.9 us -> 38.3 us
  other arithmetic: 3.81 us -> 5.57 us
  Pallas kernels: 12.9 us -> 11.7 us
  local copies, waits for them, and re-layouts: 10.5 us -> 11.6 us
    ppermute x11 -> x5, waiting for transfers between devices: 23.7 us -> 5.71 us  [swapped(): return lax.ppermute(block, axis, list(enumerate(target)))]
    ppermute x8 -> x12, waiting for transfers between devices: 17.1 us -> 32.6 us  [passed_along(): lax.ppermute(block, axis, [((i - distance) % len(devices), i) for i in de...]
    ppermute x11 -> x5, starting transfers between devices: 29.4 us -> 17.5 us  [swapped(): return lax.ppermute(block, axis, list(enumerate(target)))]
    ppermute x8 -> x12, starting transfers between devices: 9.71 us -> 16.4 us  [passed_along(): lax.ppermute(block, axis, [((i - distance) % len(devices), i) for i in de...]
    convert_element_type x4, other arithmetic: 1.27 us -> 3.18 us  [halves_summed(): return (give, (keep + got.astype(jnp.float32)).astype(jnp.bfloat16))]
    unnamed x26 -> x28, local copies, waits for them, and re-layouts: 8.97 us -> 10 us
  transfers between devices with their start and end apart: 19 -> 17, of which waited for: 8 -> 9; matrix products, arithmetic and copies ran while one was open for 4% -> 6% of each run, Pallas kernels for 7% -> 2%
where the time goes in v3:
time: 102 us; the launch traced here: 101 us
  waiting for transfers between devices  38.3 us (38%)
  starting transfers between devices  33.9 us (33%)
  Pallas kernels  11.7 us (11%)
  local copies, waits for them, and re-layouts  11.6 us (11%)
  other arithmetic  5.57 us (5%)
    ppermute x12, waiting for transfers between devices, passed_along(): lax.ppermute(block, axis, [((i - distance) % len(devices), i) for i in de...  32.6 us
    ppermute x5, starting transfers between devices, swapped(): return lax.ppermute(block, axis, list(enumerate(target)))  17.5 us
    ppermute x12, starting transfers between devices, passed_along(): lax.ppermute(block, axis, [((i - distance) % len(devices), i) for i in de...  16.4 us
    unnamed x28, local copies, waits for them, and re-layouts  10 us
    pallas_call x4, Pallas kernels, project(): pl.pallas_call(functools.partial(project_kernel, [len(block) for block in...  9.25 us
    ppermute x5, waiting for transfers between devices, swapped(): return lax.ppermute(block, axis, list(enumerate(target)))  5.71 us
    convert_element_type x4, other arithmetic, halves_summed(): return (give, (keep + got.astype(jnp.float32)).astype(jnp.bfloat16))  3.18 us
    pallas_call x1, Pallas kernels, attention_backward(): pl.pallas_call(functools.partial(attention_kernel, kv_heads, group_width,...  2.24 us
  transfers between devices with their start and end apart: 17, of which 9 were waited for; matrix products, arithmetic and copies ran while one was open for 6% of the time, Pallas kernels for 2%

profile of v3, /device:TPU:0, one launch (start us, length us, event | category | flops | bytes accessed | tf_op | source)
XLA Modules:
  0.0 101.3 jit_solution(3265277398518756026)
XLA Ops:
  0.0 1.0 pad_maximum_fusion.refs_2_
  1.0 3.1 %collective-permute-start.1 = (bf16[128,1024]{1,0:T(8,128)(2,1)S(1)}, bf16[128,1024]{1,0:T(8,128)(2,1)S(1)}, u32[]{:S(2)}, u32[]{:S(2)}) collective-permute-start(bf16[128,1024]{1,0:T(8,128)(2,1)S(1)} %pad_maximum_fusion.refs_2_), channel_id=1, source_target_pairs={{6,0},{0,2},{2,4},{4,6},{7,1},{1,3},{3,5},{5,7},{14,8},{8,10},{10,... | collective-permute-start | bytes 786440 | tf_op jit(solution)/shard_map/ppermute | solution.py:212
  4.1 2.6 %collective-permute-start = (bf16[48,1024]{1,0:T(8,128)(2,1)S(1)}, bf16[48,1024]{1,0:T(8,128)(2,1)S(1)}, u32[]{:S(2)}, u32[]{:S(2)}) collective-permute-start(bf16[48,1024]{1,0:T(8,128)(2,1)S(1)} %slice.12), channel_id=1, source_target_pairs={{4,0},{6,2},{0,4},{2,6},{5,1},{7,3},{1,5},{3,7},{12,8},{14,10},{8,... | collective-permute-start | bytes 294920 | tf_op jit(solution)/shard_map/ppermute | solution.py:212
  6.7 0.8 pad_dynamic-slice_fusion
  7.5 0.7 fusion.5
  8.1 0.1 fusion.4.refs_3_
  8.3 0.0 copy-start.8
  8.3 0.9 copy-done.8
  9.2 0.9 copy-done.9
  10.2 0.1 shard_map.82
  10.3 6.4 %collective-permute-done.refs_4_ = bf16[48,1024]{1,0:T(8,128)(2,1)S(1)} collective-permute-done((bf16[48,1024]{1,0:T(8,128)(2,1)S(1)}, bf16[48,1024]{1,0:T(8,128)(2,1)S(1)}, u32[]{:S(2)}, u32[]{:S(2)}) %collective-permute-start) | collective-permute-done | bytes 98336 | tf_op jit(solution)/shard_map/ppermute | solution.py:212
  16.6 0.0 collective-permute-done.1.refs_5_
  16.6 2.2 %shard_map.83 = (bf16[128,1024]{1,0:T(8,128)(2,1)S(1)}, f32[128,1024]{1,0:T(8,128)S(1)}, bf16[48,1024]{1,0:T(8,128)(2,1)S(1)}, bf16[128,1024]{1,0:T(8,128)(2,1)S(1)}) custom-call(bf16[1024,128]{1,0:T(8,128)(2,1)S(1)} %get-tuple-element.31.refs_0_, bf16[1024,128]{1,0:T(8,128)(2,1)S(1)} %get-tuple-element.32.refs_1_, ...), custom_call_target="tpu_custom_call" | custom-call | flops 478150656 | bytes 1048576 | tf_op jit(solution)/shard_map/pallas_call | solution.py:100
  18.9 1.7 %collective-permute-start.2 = (bf16[128,1024]{1,0:T(8,128)(2,1)S(1)}, bf16[128,1024]{1,0:T(8,128)(2,1)S(1)}, u32[]{:S(2)}, u32[]{:S(2)}) collective-permute-start(bf16[128,1024]{1,0:T(8,128)(2,1)S(1)} %get-tuple-element.35), channel_id=1, source_target_pairs={{2,0},{4,2},{6,4},{0,6},{3,1},{5,3},{7,5},{1,7},{10,8},{12,10},{14... | collective-permute-start | bytes 786440 | tf_op jit(solution)/shard_map/ppermute | solution.py:212
  20.5 0.0 collective-permute-start.3
  20.5 8.7 %collective-permute-done.3.refs_1_ = bf16[48,1024]{1,0:T(8,128)(2,1)S(1)} collective-permute-done((bf16[48,1024]{1,0:T(8,128)(2,1)S(1)}, bf16[48,1024]{1,0:T(8,128)(2,1)S(1)}, u32[]{:S(2)}, u32[]{:S(2)}) %collective-permute-start.3) | collective-permute-done | bytes 98336 | tf_op jit(solution)/shard_map/ppermute | solution.py:212
  29.3 0.0 collective-permute-done.2.refs_0_
  29.3 0.1 shard_map.84.refs_0_
  29.3 1.4 %collective-permute-start.6 = (bf16[128,2048]{1,0:T(8,128)(2,1)S(1)}, bf16[128,2048]{1,0:T(8,128)(2,1)}, u32[]{:S(2)}, u32[]{:S(2)}) collective-permute-start(bf16[128,2048]{1,0:T(8,128)(2,1)S(1)} %shard_map.84.refs_0_), channel_id=1, source_target_pairs={{0,2},{2,0},{4,6},{6,4},{1,3},{3,1},{5,7},{7,5},{8,10},{10,8},{12,... | collective-permute-start | bytes 1572872 | tf_op jit(solution)/shard_map/ppermute | solution.py:203
  30.8 1.4 %collective-permute-start.7 = (bf16[128,2048]{1,0:T(8,128)(2,1)S(1)}, bf16[128,2048]{1,0:T(8,128)(2,1)}, u32[]{:S(2)}, u32[]{:S(2)}) collective-permute-start(bf16[128,2048]{1,0:T(8,128)(2,1)S(1)} %shard_map.84.refs_0_), channel_id=1, source_target_pairs={{0,0},{2,4},{4,2},{6,6},{1,1},{3,5},{5,3},{7,7},{8,8},{10,12},{12,... | collective-permute-start | bytes 1572872 | tf_op jit(solution)/shard_map/ppermute | solution.py:203
  32.2 1.3 %copy-done.1 = bf16[1,1344,512]{2,1,0:T(8,128)(2,1)S(1)} copy-done((bf16[1,1344,512]{2,1,0:T(8,128)(2,1)S(1)}, bf16[1,1344,512]{2,1,0:T(8,128)(2,1)}, u32[]{:S(2)}) %copy-start.1) | copy-done | bytes 1376280
  33.6 1.3 %copy-done.4 = bf16[1,1344,512]{2,1,0:T(8,128)(2,1)S(1)} copy-done((bf16[1,1344,512]{2,1,0:T(8,128)(2,1)S(1)}, bf16[1,1344,512]{2,1,0:T(8,128)(2,1)}, u32[]{:S(2)}) %copy-start.4) | copy-done | bytes 1376280
  34.9 2.0 %shard_map.85 = (f32[1344,128]{1,0:T(8,128)S(1)}, bf16[672,128]{1,0:T(8,128)(2,1)S(1)}) custom-call(s32[1]{0:T(128)} %bitcast.core_ref, bf16[128,2048]{1,0:T(8,128)(2,1)S(1)} %shard_map.84.refs_0_, bf16[1344,1024]{1,0:T(8,128)(2,1)S(1)} %bitcast.14, bf16[1344,512]{1,0:T(8,128)(2,1)S(1)} %bitcast.18, bf16[1344,512]{1,0:T(8,128)(2,1)S(1)} %bitcast.22), custom_call_target="tpu_custom_call" | custom-call | flops 704643072 | bytes 6537216 | tf_op jit(solution)/shard_map/pallas_call | solution.py:180
  36.9 0.0 copy-start.10
  36.9 0.8 copy-done.10
  37.7 0.0 collective-permute-start.4
  37.7 1.5 %collective-permute-done.4 = bf16[672,128]{1,0:T(8,128)(2,1)} collective-permute-done((bf16[672,128]{1,0:T(8,128)(2,1)S(1)}, bf16[672,128]{1,0:T(8,128)(2,1)}, u32[]{:S(2)}, u32[]{:S(2)}) %collective-permute-start.4) | collective-permute-done | bytes 172064 | tf_op jit(solution)/shard_map/ppermute | solution.py:212
  39.3 1.8 %add_convert_fusion.3 = bf16[672,128]{1,0:T(8,128)(2,1)} fusion(bf16[672,128]{1,0:T(8,128)(2,1)} %collective-permute-done.4, f32[1344,128]{1,0:T(8,128)} %copy-done.10, s32[]{:T(128)S(6)} %select_n.90), kind=kLoop, calls=%fused_computation.4 | loop fusion | flops 258048 | bytes 688132 | tf_op jit(solution)/shard_map/convert_element_type | solution.py:269
  41.1 1.9 %collective-permute-done.6.refs_0_ = bf16[128,2048]{1,0:T(8,128)(2,1)} collective-permute-done((bf16[128,2048]{1,0:T(8,128)(2,1)S(1)}, bf16[128,2048]{1,0:T(8,128)(2,1)}, u32[]{:S(2)}, u32[]{:S(2)}) %collective-permute-start.6) | collective-permute-done | bytes 524320 | tf_op jit(solution)/shard_map/ppermute | solution.py:203
  43.0 0.0 collective-permute-done.7.refs_1_
  43.0 1.3 %copy-done.2 = bf16[1,1344,512]{2,1,0:T(8,128)(2,1)S(1)} copy-done((bf16[1,1344,512]{2,1,0:T(8,128)(2,1)S(1)}, bf16[1,1344,512]{2,1,0:T(8,128)(2,1)}, u32[]{:S(2)}) %copy-start.2) | copy-done | bytes 1376280
  44.3 1.3 %copy-done.5 = bf16[1,1344,512]{2,1,0:T(8,128)(2,1)S(1)} copy-done((bf16[1,1344,512]{2,1,0:T(8,128)(2,1)S(1)}, bf16[1,1344,512]{2,1,0:T(8,128)(2,1)}, u32[]{:S(2)}) %copy-start.5) | copy-done | bytes 1376280
  45.7 3.3 %shard_map.86 = (f32[1344,256]{1,0:T(8,128)S(1)}, bf16[672,256]{1,0:T(8,128)(2,1)S(1)}) custom-call(s32[1]{0:T(128)} %bitcast.core_ref, bf16[128,2048]{1,0:T(8,128)(2,1)} %collective-permute-done.6.refs_0_, bf16[128,2048]{1,0:T(8,128)(2,1)} %collective-permute-done.7.refs_1_, bf16[1344,1024]{1,0:T(8,128)(2,1)S(1)} %bitcast.15, ...), custom_call_target="tpu_custom_call" | custom-call | flops 1409286144 | bytes 7569408 | tf_op jit(solution)/shard_map/pallas_call | solution.py:180
  49.0 1.1 %copy-done.7 = f32[1344,256]{1,0:T(8,128)} copy-done((f32[1344,256]{1,0:T(8,128)}, f32[1344,256]{1,0:T(8,128)S(1)}, u32[]{:S(2)}) %copy-start.7) | copy-done | bytes 1376280
  50.1 0.0 collective-permute-start.8
  50.1 5.6 %collective-permute-start.10 = (bf16[128,2048]{1,0:T(8,128)(2,1)}, bf16[128,2048]{1,0:T(8,128)(2,1)}, u32[]{:S(2)}, u32[]{:S(2)}) collective-permute-start(bf16[128,2048]{1,0:T(8,128)(2,1)} %collective-permute-done.7.refs_1_), channel_id=1, source_target_pairs={{0,2},{2,0},{4,6},{6,4},{1,3},{3,1},{5,7},{7,5},{8,10},{10,8},{12,... | collective-permute-start | bytes 1572872 | tf_op jit(solution)/shard_map/ppermute | solution.py:203
  55.7 5.4 %collective-permute-start.11 = (bf16[128,2048]{1,0:T(8,128)(2,1)}, bf16[128,2048]{1,0:T(8,128)(2,1)}, u32[]{:S(2)}, u32[]{:S(2)}) collective-permute-start(bf16[128,2048]{1,0:T(8,128)(2,1)} %collective-permute-done.6.refs_0_), channel_id=1, source_target_pairs={{0,0},{2,4},{4,2},{6,6},{1,1},{3,5},{5,3},{7,7},{8,8},{10,12},{12,... | collective-permute-start | bytes 1572872 | tf_op jit(solution)/shard_map/ppermute | solution.py:203
  61.0 2.4 %collective-permute-start.5 = (bf16[672,128]{1,0:T(8,128)(2,1)}, bf16[672,128]{1,0:T(8,128)(2,1)S(1)}, u32[]{:S(2)}, u32[]{:S(2)}) collective-permute-start(bf16[672,128]{1,0:T(8,128)(2,1)} %add_convert_fusion.3), channel_id=1, source_target_pairs={{8,0},{16,8},{24,16},{0,24},{9,1},{17,9},{25,17},{1,25},{10,2},{18... | collective-permute-start | bytes 516104 | tf_op jit(solution)/shard_map/ppermute | solution.py:212
  63.5 0.0 collective-permute-done.8
  63.5 1.3 %add_convert_fusion = bf16[672,256]{1,0:T(8,128)(2,1)S(1)} fusion(bf16[672,256]{1,0:T(8,128)(2,1)S(1)} %collective-permute-done.8, f32[1344,256]{1,0:T(8,128)} %copy-done.7, s32[]{:T(128)S(6)} %select_n.90), kind=kLoop, calls=%fused_computation | loop fusion | flops 516096 | bytes 1376260 | tf_op jit(solution)/shard_map/convert_element_type | solution.py:269
  64.8 3.8 %collective-permute-done.10 = bf16[128,2048]{1,0:T(8,128)(2,1)} collective-permute-done((bf16[128,2048]{1,0:T(8,128)(2,1)}, bf16[128,2048]{1,0:T(8,128)(2,1)}, u32[]{:S(2)}, u32[]{:S(2)}) %collective-permute-start.10) | collective-permute-done | bytes 524320 | tf_op jit(solution)/shard_map/ppermute | solution.py:203
  68.6 0.0 collective-permute-done.11
  68.6 1.1 %broadcast_select_fusion.refs_0_ = bf16[128,2048]{1,0:T(8,128)(2,1)S(1)} fusion(bf16[128,2048]{1,0:T(8,128)(2,1)} %collective-permute-done.11, bf16[128,2048]{1,0:T(8,128)(2,1)} %collective-permute-done.10, pred[]{:T(512)S(6)} %eq.32), kind=kLoop, calls=%fused_computation.1 | loop fusion | flops 262144 | bytes 1572865 | tf_op jit(solution)/shard_map/jit(_where)/select_n | solution.py:292
  69.7 0.0 collective-permute-done.5
  69.7 0.0 copy-start.12
  69.7 2.0 %shard_map.87 = (f32[1344,128]{1,0:T(8,128)S(1)}, bf16[672,128]{1,0:T(8,128)(2,1)S(1)}) custom-call(s32[1]{0:T(128)} %bitcast.core_ref, bf16[128,2048]{1,0:T(8,128)(2,1)S(1)} %broadcast_select_fusion.refs_0_, bf16[1344,1024]{1,0:T(8,128)(2,1)S(1)} %bitcast.16, bf16[1344,512]{1,0:T(8,128)(2,1)S(1)} %bitcast.20, bf16[1344,512]{1,0:T(8,128)(2,1)S(1)} %bitcast.24), custom_call_target="tpu_custom_call" | custom-call | flops 704643072 | bytes 6537216 | tf_op jit(solution)/shard_map/pallas_call | solution.py:180
  71.7 0.1 collective-permute-start.13
  71.8 3.7 %collective-permute-start.12 = (bf16[128,2048]{1,0:T(8,128)(2,1)}, bf16[128,2048]{1,0:T(8,128)(2,1)S(1)}, u32[]{:S(2)}, u32[]{:S(2)}) collective-permute-start(bf16[128,2048]{1,0:T(8,128)(2,1)} %collective-permute-done.11), channel_id=1, source_target_pairs={{0,2},{2,0},{4,6},{6,4},{1,3},{3,1},{5,7},{7,5},{8,10},{10,8},{12,... | collective-permute-start | bytes 1572872 | tf_op jit(solution)/shard_map/ppermute | solution.py:203
  75.5 2.4 %collective-permute-start.9 = (bf16[672,256]{1,0:T(8,128)(2,1)S(1)}, bf16[672,256]{1,0:T(8,128)(2,1)S(1)}, u32[]{:S(2)}, u32[]{:S(2)}) collective-permute-start(bf16[672,256]{1,0:T(8,128)(2,1)S(1)} %add_convert_fusion), channel_id=1, source_target_pairs={{8,0},{16,8},{24,16},{0,24},{9,1},{17,9},{25,17},{1,25},{10,2},{18... | collective-permute-start | bytes 1032200 | tf_op jit(solution)/shard_map/ppermute | solution.py:212
  77.9 0.0 collective-permute-done.13
  78.0 0.6 collective-permute-start.14
  78.6 7.8 %collective-permute-done.9 = bf16[672,256]{1,0:T(8,128)(2,1)S(1)} collective-permute-done((bf16[672,256]{1,0:T(8,128)(2,1)S(1)}, bf16[672,256]{1,0:T(8,128)(2,1)S(1)}, u32[]{:S(2)}, u32[]{:S(2)}) %collective-permute-start.9) | collective-permute-done | bytes 344096 | tf_op jit(solution)/shard_map/ppermute | solution.py:212
  86.4 2.9 %collective-permute-done.14 = bf16[672,128]{1,0:T(8,128)(2,1)S(1)} collective-permute-done((bf16[672,128]{1,0:T(8,128)(2,1)S(1)}, bf16[672,128]{1,0:T(8,128)(2,1)S(1)}, u32[]{:S(2)}, u32[]{:S(2)}) %collective-permute-start.14) | collective-permute-done | bytes 172064 | tf_op jit(solution)/shard_map/ppermute | solution.py:212
  89.3 0.0 collective-permute-done.12.refs_0_
  89.3 2.0 %shard_map.88 = (f32[1344,128]{1,0:T(8,128)S(1)}, bf16[672,128]{1,0:T(8,128)(2,1)S(1)}) custom-call(s32[1]{0:T(128)} %bitcast.core_ref, bf16[128,2048]{1,0:T(8,128)(2,1)S(1)} %collective-permute-done.12.refs_0_, bf16[1344,1024]{1,0:T(8,128)(2,1)S(1)} %bitcast.17, bf16[1344,512]{1,0:T(8,128)(2,1)S(1)} %bitcast.21, bf16[1344,512]{1,0:T(8,128)(2,1)S(1)} %bitcast.25), custom_call_target="tpu_custom_call" | custom-call | flops 704643072 | bytes 6537216 | tf_op jit(solution)/shard_map/pallas_call | solution.py:180
  91.3 0.0 copy-start.13
  91.3 0.1 collective-permute-start.15
  91.4 1.4 %collective-permute-done.15 = bf16[672,128]{1,0:T(8,128)(2,1)S(1)} collective-permute-done((bf16[672,128]{1,0:T(8,128)(2,1)S(1)}, bf16[672,128]{1,0:T(8,128)(2,1)S(1)}, u32[]{:S(2)}, u32[]{:S(2)}) %collective-permute-start.15) | collective-permute-done | bytes 172064 | tf_op jit(solution)/shard_map/ppermute | solution.py:212
  92.8 3.4 %collective-permute-start.16 = (bf16[672,128]{1,0:T(8,128)(2,1)S(1)}, bf16[672,128]{1,0:T(8,128)(2,1)S(1)}, u32[]{:S(2)}, u32[]{:S(2)}) collective-permute-start(bf16[672,128]{1,0:T(8,128)(2,1)S(1)} %add_convert_fusion.1), channel_id=1, source_target_pairs={{8,0},{16,8},{24,16},{0,24},{9,1},{17,9},{25,17},{1,25},{10,2},{18... | collective-permute-start | bytes 516104 | tf_op jit(solution)/shard_map/ppermute | solution.py:212
  96.3 3.8 %collective-permute-done.16 = bf16[672,128]{1,0:T(8,128)(2,1)S(1)} collective-permute-done((bf16[672,128]{1,0:T(8,128)(2,1)S(1)}, bf16[672,128]{1,0:T(8,128)(2,1)S(1)}, u32[]{:S(2)}, u32[]{:S(2)}) %collective-permute-start.16) | collective-permute-done | bytes 172064 | tf_op jit(solution)/shard_map/ppermute | solution.py:212
  100.2 0.1 select_dynamic-update-slice_fusion.1
  100.3 0.1 select_dynamic-update-slice_fusion
  100.4 0.0 copy-start.11
  100.4 0.8 copy-done.11
  (21 shorter events, 0.3 us)
Async XLA Ops:
  1.0 15.6 %collective-permute-start.1 = (bf16[128,1024]{1,0:T(8,128)(2,1)S(1)}, bf16[128,1024]{1,0:T(8,128)(2,1)S(1)}, u32[]{:S(2)}, u32[]{:S(2)}) collective-permute-start(bf16[128,1024]{1,0:T(8,128)(2,1)S(1)} %pad_maximum_fusion.refs_2_), channel_id=1, source_target_pairs={{6,0},{0,2},{2,4},{4,6},{7,1},{1,3},{3,5},{5,7},{14,8},{8,10},{10,... | collective-permute-start | bytes 786440 | tf_op jit(solution)/shard_map/ppermute | solution.py:212
  4.1 12.5 %collective-permute-start = (bf16[48,1024]{1,0:T(8,128)(2,1)S(1)}, bf16[48,1024]{1,0:T(8,128)(2,1)S(1)}, u32[]{:S(2)}, u32[]{:S(2)}) collective-permute-start(bf16[48,1024]{1,0:T(8,128)(2,1)S(1)} %slice.12), channel_id=1, source_target_pairs={{4,0},{6,2},{0,4},{2,6},{5,1},{7,3},{1,5},{3,7},{12,8},{14,10},{8,... | collective-permute-start | bytes 294920 | tf_op jit(solution)/shard_map/ppermute | solution.py:212
  8.3 1.0 copy-start.8
  9.2 0.9 copy-start.9
  16.6 15.6 %copy-start = (bf16[1,1344,1024]{2,1,0:T(8,128)(2,1)S(1)}, bf16[1,1344,1024]{2,1,0:T(8,128)(2,1)}, u32[]{:S(2)}) copy-start(bf16[1,1344,1024]{2,1,0:T(8,128)(2,1)} %param.12) | copy-start | bytes 8257540
  18.9 10.4 %collective-permute-start.2 = (bf16[128,1024]{1,0:T(8,128)(2,1)S(1)}, bf16[128,1024]{1,0:T(8,128)(2,1)S(1)}, u32[]{:S(2)}, u32[]{:S(2)}) collective-permute-start(bf16[128,1024]{1,0:T(8,128)(2,1)S(1)} %get-tuple-element.35), channel_id=1, source_target_pairs={{2,0},{4,2},{6,4},{0,6},{3,1},{5,3},{7,5},{1,7},{10,8},{12,10},{14... | collective-permute-start | bytes 786440 | tf_op jit(solution)/shard_map/ppermute | solution.py:212
  20.5 8.7 %collective-permute-start.3 = (bf16[48,1024]{1,0:T(8,128)(2,1)S(1)}, bf16[48,1024]{1,0:T(8,128)(2,1)S(1)}, u32[]{:S(2)}, u32[]{:S(2)}) collective-permute-start(bf16[48,1024]{1,0:T(8,128)(2,1)S(1)} %get-tuple-element.36), channel_id=1, source_target_pairs={{4,0},{6,2},{0,4},{2,6},{5,1},{7,3},{1,5},{3,7},{12,8},{14,10},{8,... | collective-permute-start | bytes 294920 | tf_op jit(solution)/shard_map/ppermute | solution.py:212
  29.3 13.7 %collective-permute-start.6 = (bf16[128,2048]{1,0:T(8,128)(2,1)S(1)}, bf16[128,2048]{1,0:T(8,128)(2,1)}, u32[]{:S(2)}, u32[]{:S(2)}) collective-permute-start(bf16[128,2048]{1,0:T(8,128)(2,1)S(1)} %shard_map.84.refs_0_), channel_id=1, source_target_pairs={{0,2},{2,0},{4,6},{6,4},{1,3},{3,1},{5,7},{7,5},{8,10},{10,8},{12,... | collective-permute-start | bytes 1572872 | tf_op jit(solution)/shard_map/ppermute | solution.py:203
  30.8 12.2 %collective-permute-start.7 = (bf16[128,2048]{1,0:T(8,128)(2,1)S(1)}, bf16[128,2048]{1,0:T(8,128)(2,1)}, u32[]{:S(2)}, u32[]{:S(2)}) collective-permute-start(bf16[128,2048]{1,0:T(8,128)(2,1)S(1)} %shard_map.84.refs_0_), channel_id=1, source_target_pairs={{0,0},{2,4},{4,2},{6,6},{1,1},{3,5},{5,3},{7,7},{8,8},{10,12},{12,... | collective-permute-start | bytes 1572872 | tf_op jit(solution)/shard_map/ppermute | solution.py:203
  32.2 1.3 %copy-start.1 = (bf16[1,1344,512]{2,1,0:T(8,128)(2,1)S(1)}, bf16[1,1344,512]{2,1,0:T(8,128)(2,1)}, u32[]{:S(2)}) copy-start(bf16[1,1344,512]{2,1,0:T(8,128)(2,1)} %param.13) | copy-start | bytes 4128772
  33.6 1.3 %copy-start.4 = (bf16[1,1344,512]{2,1,0:T(8,128)(2,1)S(1)}, bf16[1,1344,512]{2,1,0:T(8,128)(2,1)}, u32[]{:S(2)}) copy-start(bf16[1,1344,512]{2,1,0:T(8,128)(2,1)} %param.14) | copy-start | bytes 4128772
  36.9 0.8 copy-start.10
  37.7 1.5 %collective-permute-start.4 = (bf16[672,128]{1,0:T(8,128)(2,1)S(1)}, bf16[672,128]{1,0:T(8,128)(2,1)}, u32[]{:S(2)}, u32[]{:S(2)}) collective-permute-start(bf16[672,128]{1,0:T(8,128)(2,1)S(1)} %get-tuple-element.38), channel_id=1, source_target_pairs={{1,0},{0,1},{3,2},{2,3},{5,4},{4,5},{7,6},{6,7},{9,8},{8,9},{11,10... | collective-permute-start | bytes 516104 | tf_op jit(solution)/shard_map/ppermute | solution.py:212
  43.0 1.3 %copy-start.2 = (bf16[1,1344,512]{2,1,0:T(8,128)(2,1)S(1)}, bf16[1,1344,512]{2,1,0:T(8,128)(2,1)}, u32[]{:S(2)}) copy-start(bf16[1,1344,512]{2,1,0:T(8,128)(2,1)} %param.13) | copy-start | bytes 4128772
  44.3 1.3 %copy-start.5 = (bf16[1,1344,512]{2,1,0:T(8,128)(2,1)S(1)}, bf16[1,1344,512]{2,1,0:T(8,128)(2,1)}, u32[]{:S(2)}) copy-start(bf16[1,1344,512]{2,1,0:T(8,128)(2,1)} %param.14) | copy-start | bytes 4128772
  49.0 1.1 %copy-start.7 = (f32[1344,256]{1,0:T(8,128)}, f32[1344,256]{1,0:T(8,128)S(1)}, u32[]{:S(2)}) copy-start(f32[1344,256]{1,0:T(8,128)S(1)} %get-tuple-element.43) | copy-start | bytes 4128772
  50.1 13.4 %collective-permute-start.8 = (bf16[672,256]{1,0:T(8,128)(2,1)S(1)}, bf16[672,256]{1,0:T(8,128)(2,1)S(1)}, u32[]{:S(2)}, u32[]{:S(2)}) collective-permute-start(bf16[672,256]{1,0:T(8,128)(2,1)S(1)} %get-tuple-element.44), channel_id=1, source_target_pairs={{1,0},{0,1},{3,2},{2,3},{5,4},{4,5},{7,6},{6,7},{9,8},{8,9},{11,10... | collective-permute-start | bytes 1032200 | tf_op jit(solution)/shard_map/ppermute | solution.py:212
  50.1 18.5 %collective-permute-start.10 = (bf16[128,2048]{1,0:T(8,128)(2,1)}, bf16[128,2048]{1,0:T(8,128)(2,1)}, u32[]{:S(2)}, u32[]{:S(2)}) collective-permute-start(bf16[128,2048]{1,0:T(8,128)(2,1)} %collective-permute-done.7.refs_1_), channel_id=1, source_target_pairs={{0,2},{2,0},{4,6},{6,4},{1,3},{3,1},{5,7},{7,5},{8,10},{10,8},{12,... | collective-permute-start | bytes 1572872 | tf_op jit(solution)/shard_map/ppermute | solution.py:203
  55.7 12.9 %collective-permute-start.11 = (bf16[128,2048]{1,0:T(8,128)(2,1)}, bf16[128,2048]{1,0:T(8,128)(2,1)}, u32[]{:S(2)}, u32[]{:S(2)}) collective-permute-start(bf16[128,2048]{1,0:T(8,128)(2,1)} %collective-permute-done.6.refs_0_), channel_id=1, source_target_pairs={{0,0},{2,4},{4,2},{6,6},{1,1},{3,5},{5,3},{7,7},{8,8},{10,12},{12,... | collective-permute-start | bytes 1572872 | tf_op jit(solution)/shard_map/ppermute | solution.py:203
  61.0 8.6 %collective-permute-start.5 = (bf16[672,128]{1,0:T(8,128)(2,1)}, bf16[672,128]{1,0:T(8,128)(2,1)S(1)}, u32[]{:S(2)}, u32[]{:S(2)}) collective-permute-start(bf16[672,128]{1,0:T(8,128)(2,1)} %add_convert_fusion.3), channel_id=1, source_target_pairs={{8,0},{16,8},{24,16},{0,24},{9,1},{17,9},{25,17},{1,25},{10,2},{18... | collective-permute-start | bytes 516104 | tf_op jit(solution)/shard_map/ppermute | solution.py:212
  63.5 6.2 %copy-start.3 = (bf16[1,1344,512]{2,1,0:T(8,128)(2,1)S(1)}, bf16[1,1344,512]{2,1,0:T(8,128)(2,1)}, u32[]{:S(2)}) copy-start(bf16[1,1344,512]{2,1,0:T(8,128)(2,1)} %param.13) | copy-start | bytes 4128772
  63.5 6.2 %copy-start.6 = (bf16[1,1344,512]{2,1,0:T(8,128)(2,1)S(1)}, bf16[1,1344,512]{2,1,0:T(8,128)(2,1)}, u32[]{:S(2)}) copy-start(bf16[1,1344,512]{2,1,0:T(8,128)(2,1)} %param.14) | copy-start | bytes 4128772
  69.7 2.0 %copy-start.12 = (bf16[672,128]{1,0:T(8,128)(2,1)}, bf16[672,128]{1,0:T(8,128)(2,1)S(1)}, u32[]{:S(2)}) copy-start(bf16[672,128]{1,0:T(8,128)(2,1)S(1)} %collective-permute-done.5) | copy-start | bytes 516100
  71.7 6.2 %collective-permute-start.13 = (bf16[672,128]{1,0:T(8,128)(2,1)S(1)}, bf16[672,128]{1,0:T(8,128)(2,1)S(1)}, u32[]{:S(2)}, u32[]{:S(2)}) collective-permute-start(bf16[672,128]{1,0:T(8,128)(2,1)S(1)} %get-tuple-element.49), channel_id=1, source_target_pairs={{1,0},{0,1},{3,2},{2,3},{5,4},{4,5},{7,6},{6,7},{9,8},{8,9},{11,10... | collective-permute-start | bytes 516104 | tf_op jit(solution)/shard_map/ppermute | solution.py:212
  71.8 17.5 %collective-permute-start.12 = (bf16[128,2048]{1,0:T(8,128)(2,1)}, bf16[128,2048]{1,0:T(8,128)(2,1)S(1)}, u32[]{:S(2)}, u32[]{:S(2)}) collective-permute-start(bf16[128,2048]{1,0:T(8,128)(2,1)} %collective-permute-done.11), channel_id=1, source_target_pairs={{0,2},{2,0},{4,6},{6,4},{1,3},{3,1},{5,7},{7,5},{8,10},{10,8},{12,... | collective-permute-start | bytes 1572872 | tf_op jit(solution)/shard_map/ppermute | solution.py:203
  75.5 10.9 %collective-permute-start.9 = (bf16[672,256]{1,0:T(8,128)(2,1)S(1)}, bf16[672,256]{1,0:T(8,128)(2,1)S(1)}, u32[]{:S(2)}, u32[]{:S(2)}) collective-permute-start(bf16[672,256]{1,0:T(8,128)(2,1)S(1)} %add_convert_fusion), channel_id=1, source_target_pairs={{8,0},{16,8},{24,16},{0,24},{9,1},{17,9},{25,17},{1,25},{10,2},{18... | collective-permute-start | bytes 1032200 | tf_op jit(solution)/shard_map/ppermute | solution.py:212
  78.0 11.3 %collective-permute-start.14 = (bf16[672,128]{1,0:T(8,128)(2,1)S(1)}, bf16[672,128]{1,0:T(8,128)(2,1)S(1)}, u32[]{:S(2)}, u32[]{:S(2)}) collective-permute-start(bf16[672,128]{1,0:T(8,128)(2,1)S(1)} %add_convert_fusion.2), channel_id=1, source_target_pairs={{8,0},{16,8},{24,16},{0,24},{9,1},{17,9},{25,17},{1,25},{10,2},{18... | collective-permute-start | bytes 516104 | tf_op jit(solution)/shard_map/ppermute | solution.py:212
  91.3 5.0 %copy-start.13 = (bf16[672,128]{1,0:T(8,128)(2,1)S(1)}, bf16[672,128]{1,0:T(8,128)(2,1)}, u32[]{:S(2)}) copy-start(bf16[672,128]{1,0:T(8,128)(2,1)} %copy-done.12) | copy-start | bytes 516100
  91.3 1.5 %collective-permute-start.15 = (bf16[672,128]{1,0:T(8,128)(2,1)S(1)}, bf16[672,128]{1,0:T(8,128)(2,1)S(1)}, u32[]{:S(2)}, u32[]{:S(2)}) collective-permute-start(bf16[672,128]{1,0:T(8,128)(2,1)S(1)} %get-tuple-element.52), channel_id=1, source_target_pairs={{1,0},{0,1},{3,2},{2,3},{5,4},{4,5},{7,6},{6,7},{9,8},{8,9},{11,10... | collective-permute-start | bytes 516104 | tf_op jit(solution)/shard_map/ppermute | solution.py:212
  92.8 7.3 %collective-permute-start.16 = (bf16[672,128]{1,0:T(8,128)(2,1)S(1)}, bf16[672,128]{1,0:T(8,128)(2,1)S(1)}, u32[]{:S(2)}, u32[]{:S(2)}) collective-permute-start(bf16[672,128]{1,0:T(8,128)(2,1)S(1)} %add_convert_fusion.1), channel_id=1, source_target_pairs={{8,0},{16,8},{24,16},{0,24},{9,1},{17,9},{25,17},{1,25},{10,2},{18... | collective-permute-start | bytes 516104 | tf_op jit(solution)/shard_map/ppermute | solution.py:212
  100.4 0.8 copy-start.11

commit v4 on v3

--- a/solution.py
+++ b/solution.py
@@ -111,11 +111,9 @@
     )(query, grad, kv, bias, *halos)
 
 
-def join_kernel(query_ref, kv_ref, *refs):
-    *part_refs, joined_ref = refs
+def join_kernel(kv_ref, *refs):
+    *part_refs, total_ref = refs
     rows = kv_ref.shape[0]
-    query_cols = query_ref.shape[1]
-    joined_ref[:, :query_cols] = query_ref[...]
     total = kv_ref[...]
     for part_ref in part_refs:
         size = part_ref.shape[0]
@@ -125,35 +123,39 @@
                 [jnp.zeros((rows - size, part.shape[1]), jnp.float32), part], axis=0
             )
         total = total + part
-    joined_ref[:, query_cols:] = total.astype(jnp.bfloat16)
-
-
-def join(query_part, kv_part, returned):
-    rows, query_cols = query_part.shape
-    kv_cols = kv_part.shape[1]
+    total_ref[...] = total.astype(jnp.bfloat16)
+
+
+def join(kv_part, returned):
     whole = pl.BlockSpec(memory_space=pltpu.VMEM)
     return pl.pallas_call(
         join_kernel,
-        out_shape=jax.ShapeDtypeStruct((rows, query_cols + kv_cols), jnp.bfloat16),
-        in_specs=[whole] * (2 + len(returned)),
+        out_shape=jax.ShapeDtypeStruct(kv_part.shape, jnp.bfloat16),
+        in_specs=[whole] * (1 + len(returned)),
         out_specs=whole,
         compiler_params=pltpu.CompilerParams(vmem_limit_bytes=8 * 1024 * 1024),
         cost_estimate=pl.CostEstimate(flops=1, bytes_accessed=1, transcendentals=0),
-    )(query_part, kv_part, *returned)
-
-
-def project_kernel(pieces, tile, core_ref, *refs):
-    flat_refs, (query_weight, key_weight, value_weight) = refs[: sum(pieces)], refs[-6:-3]
-    full_ref, give_ref, block_ref = refs[-3:]
-    row, at = 0, 0
-    for count in pieces:
-        column = 0
-        for ref in flat_refs[at : at + count]:
-            block_ref[row : row + ref.shape[0], column : column + ref.shape[1]] = ref[...]
-            column += ref.shape[1]
-        at += count
-        row += flat_refs[at - 1].shape[0]
-    query_cols, kv_cols = query_weight.shape[1], key_weight.shape[1]
+    )(kv_part, *returned)
+
+
+def project_kernel(blocks, chosen, tile, scalar_ref, *refs):
+    flat_refs, weight_refs = refs[: 2 * blocks], refs[2 * blocks : 2 * blocks + 3]
+    full_ref, give_ref, block_ref = refs[2 * blocks + 3 :]
+    query_cols = flat_refs[0].shape[1]
+    kv_cols = flat_refs[1].shape[1] // 2
+
+    def take(block, row):
+        rows = flat_refs[2 * block].shape[0]
+        block_ref[row : row + rows, :query_cols] = flat_refs[2 * block][...]
+        block_ref[row : row + rows, query_cols:] = flat_refs[2 * block + 1][...]
+
+    if chosen:
+        for block in range(blocks):
+            pl.when(scalar_ref[1] == block)(functools.partial(take, block, 0))
+    else:
+        for block in range(blocks):
+            take(block, block * flat_refs[0].shape[0])
+    query_weight, key_weight, value_weight = weight_refs
 
     def step(i, carry):
         at = pl.ds(pl.multiple_of(i * tile, 16), tile)
@@ -166,24 +168,26 @@
 
     lax.fori_loop(0, full_ref.shape[0] // tile, step, 0)
     half = give_ref.shape[0]
-    other = pl.multiple_of((1 - core_ref[0]) * half, 8)
+    other = pl.multiple_of((1 - scalar_ref[0]) * half, 8)
     give_ref[...] = full_ref[pl.ds(other, half), :].astype(jnp.bfloat16)
 
 
-def project(blocks, weights, core):
+def project(blocks, weights, core, choice=None):
     width = weights[0].shape[0]
-    rows = sum(block[0].shape[0] for block in blocks)
+    rows = blocks[0][0].shape[0] * (len(blocks) if choice is None else 1)
     cols = sum(weight.shape[1] for weight in weights)
     tile = max(t for t in range(16, 449, 16) if width % t == 0)
     flat = [piece for block in blocks for piece in block]
+    scalars = jnp.stack([core, core if choice is None else choice])
     whole = pl.BlockSpec(memory_space=pltpu.VMEM)
     return pl.pallas_call(
-        functools.partial(project_kernel, [len(block) for block in blocks], tile),
+        functools.partial(project_kernel, len(blocks), choice is not None, tile),
         out_shape=[
             jax.ShapeDtypeStruct((width, rows), jnp.float32),
             jax.ShapeDtypeStruct((width // 2, rows), jnp.bfloat16),
         ],
-        in_specs=[pl.BlockSpec(memory_space=pltpu.SMEM)] + [whole] * (len(flat) + 3),
+        in_specs=[pl.BlockSpec(memory_space=pltpu.SMEM)]
+        + [whole] * (len(flat) + 3),
         out_specs=[whole] * 2,
         scratch_shapes=[pltpu.VMEM((rows, cols), jnp.bfloat16)],
         compiler_params=pltpu.CompilerParams(vmem_limit_bytes=8 * 1024 * 1024),
@@ -192,15 +196,14 @@
             bytes_accessed=2 * width * cols + 6 * width * rows,
             transcendentals=0,
         ),
-    )(core, *flat, *weights)
+    )(scalars, *flat, *weights)
 
 
 def swapped(block, axis, first):
-    size = lax.axis_size(axis)
-    target = list(range(size))
-    for i in range(first, size - 1, 2):
-        target[i], target[i + 1] = i + 1, i
-    return lax.ppermute(block, axis, list(enumerate(target)))
+    pairs = []
+    for i in range(first, lax.axis_size(axis) - 1, 2):
+        pairs += [(i, i + 1), (i + 1, i)]
+    return lax.ppermute(block, axis, pairs)
 
 
 def after(arrays, *others):
@@ -257,42 +260,67 @@
         query_stack, grad_stack, kv, bias, halos[::-1]
     )
     returned = [passed_along(part, "seq", -d) for d, part in enumerate(grad_halos[::-1], 1)]
-    own = join(grad_query, grad_kv, returned)
     weights = (w_query[0], key_weight[0], value_weight[0])
     core = lax.axis_index("mp").astype(jnp.int32)
-
-    def halves_summed(blocks):
-        full, give = project([(block,) for block in blocks], weights, core[None])
+    even = place % 2 == 0
+
+    def halves_summed(blocks, choice, late):
+        full, give = project(blocks, weights, core, choice)
         half = give.shape[0]
         keep = lax.dynamic_slice_in_dim(full, core * half, half, 0)
-        got = passed_along(give, "mp", 1)
-        return give, (keep + got.astype(jnp.float32)).astype(jnp.bfloat16)
-
-    even = place % 2 == 0
-    results, waiting = [], [own]
-    by_first, by_second = own, own
+        got = jnp.concatenate(
+            [
+                passed_along(give[:, i : i + rows], "mp", 1)
+                for i in range(0, give.shape[1], rows)
+            ],
+            axis=1,
+        )
+        (got,) = after((got,), *late)
+        return (keep + got.astype(jnp.float32)).astype(jnp.bfloat16)
+
+    def swap(pair, step):
+        last = step == shards - 1 and shards % 2 == 0
+        first = swapped(pair[0], "seq", 0)
+        second = first if last else swapped(pair[1], "seq", 1)
+        return second, first
+
+    query_steps = [(grad_query, grad_query)]
+    if shards > 1:
+        query_steps.append(swap(query_steps[0], 1))
+        grad_kv, *returned = after((grad_kv, *returned), *query_steps[1])
+    kv_own = join(grad_kv, returned)
+    kv_steps = [(kv_own, kv_own)]
+    results, total = [], None
+
+    def product(step, *gates):
+        choice = None
+        if step == 0 or (step == shards - 1 and shards % 2 == 0):
+            blocks = [(query_steps[step][1], kv_steps[step][1])]
+        else:
+            blocks = list(zip(query_steps[step][::-1], kv_steps[step][::-1]))
+            if 2 * step >= shards:
+                choice = (even == (place >= step)).astype(jnp.int32)
+        earlier = [*gates, *results[-2:-1]]
+        if step:
+            earlier.append(total)
+        if earlier:
+            blocks = [after(block, *earlier) for block in blocks]
+        late = kv_steps[step + 1] if 1 < step < shards - 1 else ()
+        summed = halves_summed(blocks, choice, late)
+        results.append(passed_along(summed, "section", -1))
+        return summed
+
+    def gate(step):
+        arrived = [*kv_steps[step], *query_steps[step + 1]]
+        (rows_out,) = after((kv_steps[step][1][:16, :HEAD_WIDTH],), *arrived)
+        return passed_along(rows_out, "mp", 1)
+
     for step in range(1, shards):
-        came_first = swapped(by_first, "seq", 0)
-        last = step == shards - 1 and shards % 2 == 0
-        came_second = came_first if last else swapped(by_second, "seq", 1)
-        if step == 2:
-            waiting = after(waiting, total)
-        elif step > 2:
-            waiting = after(waiting, total, results[step - 3])
-        give, total = halves_summed(waiting)
-        if step < shards - 1:
-            came_first, came_second = after((came_first, came_second), give)
-        results.append(passed_along(total, "section", -1))
-        by_first, by_second = came_second, came_first
-        if last:
-            waiting = [came_first]
-        elif 2 * step < shards:
-            waiting = [came_first, came_second]
-        else:
-            waiting = [jnp.where(even == (place >= step), came_second, came_first)]
-    if shards > 1:
-        waiting = after(waiting, *results)
-    results.append(passed_along(halves_summed(waiting)[1], "section", -1))
+        kv_steps.append(swap(kv_steps[step - 1], step))
+        if step + 1 < shards:
+            query_steps.append(swap(query_steps[step], step + 1))
+        total = product(step - 1, gate(step - 1))
+    total = product(shards - 1)
     for step, block in enumerate(results):
         if block.shape[1] == rows:
             results[step] = [block]

time: 102 us -> 118 us (1.16)
  local copies, waits for them, and re-layouts: 11.6 us -> 18.6 us
  waiting for transfers between devices: 38.3 us -> 44.1 us
  Pallas kernels: 11.7 us -> 16.5 us
  starting transfers between devices: 33.9 us -> 32 us
    unnamed x28 -> x50, local copies, waits for them, and re-layouts: 10 us -> 16.3 us
    ppermute x12 -> x15, waiting for transfers between devices: 32.6 us -> 37.6 us  [passed_along(): lax.ppermute(block, axis, [((i - distance) % len(devices), i) for i in de...]
    pallas_call x5, Pallas kernels: 9.33 us -> 13.4 us  [the longest x4 12.5 us: project(): pl.pallas_call(functools.partial(project_kernel, len(blocks), choice is n...]
    ppermute x5 -> x10, starting transfers between devices: 17.5 us -> 13.9 us  [swapped(): return lax.ppermute(block, axis, pairs)]
    ppermute x12 -> x15, starting transfers between devices: 16.4 us -> 18 us  [passed_along(): lax.ppermute(block, axis, [((i - distance) % len(devices), i) for i in de...]
    ppermute x5 -> x10, waiting for transfers between devices: 5.71 us -> 6.51 us  [swapped(): return lax.ppermute(block, axis, pairs)]
  transfers between devices with their start and end apart: 17 -> 25, of which waited for: 9 -> 10; matrix products, arithmetic and copies ran while one was open for 6% -> 5% of each run, Pallas kernels for 2% -> 6%
where the time goes in v4:
time: 118 us; the launch traced here: 117 us
  waiting for transfers between devices  44.1 us (37%)
  starting transfers between devices  32 us (27%)
  local copies, waits for them, and re-layouts  18.6 us (16%)
  Pallas kernels  16.5 us (14%)
  other arithmetic  5.5 us (5%)
    ppermute x15, waiting for transfers between devices, passed_along(): lax.ppermute(block, axis, [((i - distance) % len(devices), i) for i in de...  37.6 us
    ppermute x15, starting transfers between devices, passed_along(): lax.ppermute(block, axis, [((i - distance) % len(devices), i) for i in de...  18 us
    unnamed x50, local copies, waits for them, and re-layouts  16.3 us
    ppermute x10, starting transfers between devices, swapped(): return lax.ppermute(block, axis, pairs)  13.9 us
    pallas_call x4, Pallas kernels, project(): pl.pallas_call(functools.partial(project_kernel, len(blocks), choice is n...  12.5 us
    ppermute x10, waiting for transfers between devices, swapped(): return lax.ppermute(block, axis, pairs)  6.51 us
    convert_element_type x4, other arithmetic, halves_summed(): return (keep + got.astype(jnp.float32)).astype(jnp.bfloat16)  3.03 us
    pallas_call x1, Pallas kernels, attention_backward(): pl.pallas_call(functools.partial(attention_kernel, kv_heads, group_width,...  2.99 us
  transfers between devices with their start and end apart: 25, of which 10 were waited for; matrix products, arithmetic and copies ran while one was open for 5% of the time, Pallas kernels for 6%

profile of v4, /device:TPU:0, one launch (start us, length us, event | category | flops | bytes accessed | tf_op | source)
XLA Modules:
  0.0 117.0 jit_solution(9713827140500908435)
XLA Ops:
  0.0 1.0 pad_maximum_fusion.1.refs_2_
  1.0 3.1 %collective-permute-start.1 = (bf16[128,1024]{1,0:T(8,128)(2,1)S(1)}, bf16[128,1024]{1,0:T(8,128)(2,1)S(1)}, u32[]{:S(2)}, u32[]{:S(2)}) collective-permute-start(bf16[128,1024]{1,0:T(8,128)(2,1)S(1)} %pad_maximum_fusion.1.refs_2_), channel_id=1, source_target_pairs={{6,0},{0,2},{2,4},{4,6},{7,1},{1,3},{3,5},{5,7},{14,8},{8,10},{10,... | collective-permute-start | bytes 786440 | tf_op jit(solution)/shard_map/ppermute | solution.py:215
  4.1 2.6 %collective-permute-start = (bf16[48,1024]{1,0:T(8,128)(2,1)S(1)}, bf16[48,1024]{1,0:T(8,128)(2,1)S(1)}, u32[]{:S(2)}, u32[]{:S(2)}) collective-permute-start(bf16[48,1024]{1,0:T(8,128)(2,1)S(1)} %slice.29), channel_id=1, source_target_pairs={{4,0},{6,2},{0,4},{2,6},{5,1},{7,3},{1,5},{3,7},{12,8},{14,10},{8,... | collective-permute-start | bytes 294920 | tf_op jit(solution)/shard_map/ppermute | solution.py:215
  6.7 0.8 pad_dynamic-slice_fusion
  7.5 0.7 fusion.5
  8.1 0.1 fusion.4.refs_3_
  8.3 0.9 copy-done.9
  9.2 0.9 copy-done.10
  10.2 0.1 shard_map.82
  10.3 6.4 %collective-permute-done.refs_4_ = bf16[48,1024]{1,0:T(8,128)(2,1)S(1)} collective-permute-done((bf16[48,1024]{1,0:T(8,128)(2,1)S(1)}, bf16[48,1024]{1,0:T(8,128)(2,1)S(1)}, u32[]{:S(2)}, u32[]{:S(2)}) %collective-permute-start) | collective-permute-done | bytes 98336 | tf_op jit(solution)/shard_map/ppermute | solution.py:215
  16.6 0.6 copy-done.18
  17.3 0.7 copy-done.16
  18.0 0.9 copy-done.17
  18.9 0.9 copy-done.19
  19.8 3.0 %shard_map.83 = (bf16[128,1024]{1,0:T(8,128)(2,1)}, f32[128,1024]{1,0:T(8,128)S(1)}, bf16[48,1024]{1,0:T(8,128)(2,1)}, bf16[128,1024]{1,0:T(8,128)(2,1)}) custom-call(bf16[1024,128]{1,0:T(8,128)(2,1)S(1)} %get-tuple-element.41.refs_0_, bf16[1024,128]{1,0:T(8,128)(2,1)S(1)} %get-tuple-element.42.refs_1_, bf16[128,1024]{1,0:T(8,128)(2,1)S(1)} %pad_maximum_fusion.1.refs_2_, ...), custom_call_target="tpu_custom_call" | custom-call | flops 478150656 | bytes 1048576 | tf_op jit(solution)/shard_map/pallas_call | solution.py:100
  22.8 1.4 %collective-permute-start.4 = (bf16[128,1024]{1,0:T(8,128)(2,1)}, bf16[128,1024]{1,0:T(8,128)(2,1)}, u32[]{:S(2)}, u32[]{:S(2)}) collective-permute-start(bf16[128,1024]{1,0:T(8,128)(2,1)} %get-tuple-element.50.refs_0_), channel_id=1, source_target_pairs={{2,4},{4,2},{3,5},{5,3},{10,12},{12,10},{11,13},{13,11},{18,20},{2... | collective-permute-start | bytes 786440 | tf_op jit(solution)/shard_map/ppermute | solution.py:206
  24.2 0.7 collective-permute-start.5
  24.9 1.6 %collective-permute-start.2 = (bf16[128,1024]{1,0:T(8,128)(2,1)}, bf16[128,1024]{1,0:T(8,128)(2,1)S(1)}, u32[]{:S(2)}, u32[]{:S(2)}) collective-permute-start(bf16[128,1024]{1,0:T(8,128)(2,1)} %get-tuple-element.45), channel_id=1, source_target_pairs={{2,0},{4,2},{6,4},{0,6},{3,1},{5,3},{7,5},{1,7},{10,8},{12,10},{14... | collective-permute-start | bytes 786440 | tf_op jit(solution)/shard_map/ppermute | solution.py:215
  26.5 1.2 collective-permute-start.3
  27.7 13.2 %collective-permute-done.3.refs_1_ = bf16[48,1024]{1,0:T(8,128)(2,1)} collective-permute-done((bf16[48,1024]{1,0:T(8,128)(2,1)}, bf16[48,1024]{1,0:T(8,128)(2,1)}, u32[]{:S(2)}, u32[]{:S(2)}) %collective-permute-start.3) | collective-permute-done | bytes 98336 | tf_op jit(solution)/shard_map/ppermute | solution.py:215
  40.9 0.7 copy-done.11
  41.6 0.9 copy-done.12
  42.5 1.0 shard_map.84.refs_1_
  43.5 1.4 %collective-permute-start.9 = (bf16[128,1024]{1,0:T(8,128)(2,1)S(1)}, bf16[128,1024]{1,0:T(8,128)(2,1)}, u32[]{:S(2)}, u32[]{:S(2)}) collective-permute-start(bf16[128,1024]{1,0:T(8,128)(2,1)S(1)} %shard_map.84.refs_1_), channel_id=1, source_target_pairs={{2,4},{4,2},{3,5},{5,3},{10,12},{12,10},{11,13},{13,11},{18,20},{2... | collective-permute-start | bytes 786440 | tf_op jit(solution)/shard_map/ppermute | solution.py:206
  44.9 2.2 %collective-permute-start.8 = (bf16[128,1024]{1,0:T(8,128)(2,1)S(1)}, bf16[128,1024]{1,0:T(8,128)(2,1)S(1)}, u32[]{:S(2)}, u32[]{:S(2)}) collective-permute-start(bf16[128,1024]{1,0:T(8,128)(2,1)S(1)} %shard_map.84.refs_1_), channel_id=1, source_target_pairs={{0,2},{2,0},{4,6},{6,4},{1,3},{3,1},{5,7},{7,5},{8,10},{10,8},{12,... | collective-permute-start | bytes 786440 | tf_op jit(solution)/shard_map/ppermute | solution.py:206
  47.0 0.7 collective-permute-start.10
  47.7 2.9 %collective-permute-start.11 = (bf16[128,1024]{1,0:T(8,128)(2,1)}, bf16[128,1024]{1,0:T(8,128)(2,1)}, u32[]{:S(2)}, u32[]{:S(2)}) collective-permute-start(bf16[128,1024]{1,0:T(8,128)(2,1)} %collective-permute-done.4.refs_2_), channel_id=1, source_target_pairs={{0,2},{2,0},{4,6},{6,4},{1,3},{3,1},{5,7},{7,5},{8,10},{10,8},{12,... | collective-permute-start | bytes 786440 | tf_op jit(solution)/shard_map/ppermute | solution.py:206
  50.7 1.3 %copy-done.1 = bf16[1,1344,512]{2,1,0:T(8,128)(2,1)S(1)} copy-done((bf16[1,1344,512]{2,1,0:T(8,128)(2,1)S(1)}, bf16[1,1344,512]{2,1,0:T(8,128)(2,1)}, u32[]{:S(2)}) %copy-start.1) | copy-done | bytes 1376280
  52.0 1.3 %copy-done.4 = bf16[1,1344,512]{2,1,0:T(8,128)(2,1)S(1)} copy-done((bf16[1,1344,512]{2,1,0:T(8,128)(2,1)S(1)}, bf16[1,1344,512]{2,1,0:T(8,128)(2,1)}, u32[]{:S(2)}) %copy-start.4) | copy-done | bytes 1376280
  53.4 3.6 %shard_map.85 = (f32[1344,128]{1,0:T(8,128)S(1)}, bf16[672,128]{1,0:T(8,128)(2,1)}) custom-call(s32[2]{0:T(128)S(1)} %pad_add_fusion.scalar_ref, bf16[128,1024]{1,0:T(8,128)(2,1)} %get-tuple-element.50.refs_0_, bf16[128,1024]{1,0:T(8,128)(2,1)S(1)} %shard_map.84.refs_1_, bf16[1344,1024]{1,0:T(8,128)(2,1)S(1)} %bitcast.15, bf16[1344,512]{1,0:T(8,128)(2,1)S(1)} %bitcast.19, ...), custom_call_target="tpu_custom_call" | custom-call | flops 704643072 | bytes 6537216 | tf_op jit(solution)/shard_map/pallas_call | solution.py:183
  57.0 0.8 copy-done.15
  57.8 1.7 %collective-permute-done.6 = bf16[672,128]{1,0:T(8,128)(2,1)} collective-permute-done((bf16[672,128]{1,0:T(8,128)(2,1)}, bf16[672,128]{1,0:T(8,128)(2,1)}, u32[]{:S(2)}, u32[]{:S(2)}) %collective-permute-start.6) | collective-permute-done | bytes 172064 | tf_op jit(solution)/shard_map/ppermute | solution.py:215
  59.6 0.2 collective-permute-start.12
  59.8 1.8 %add_convert_fusion.3 = bf16[672,128]{1,0:T(8,128)(2,1)} fusion(bf16[672,128]{1,0:T(8,128)(2,1)} %collective-permute-done.6, f32[1344,128]{1,0:T(8,128)} %copy-done.15, s32[]{:T(128)S(6)} %select_n.82), kind=kLoop, calls=%fused_computation.4 | loop fusion | flops 258048 | bytes 688132 | tf_op jit(solution)/shard_map/convert_element_type | solution.py:279
  61.6 1.3 %copy-done.2 = bf16[1,1344,512]{2,1,0:T(8,128)(2,1)S(1)} copy-done((bf16[1,1344,512]{2,1,0:T(8,128)(2,1)S(1)}, bf16[1,1344,512]{2,1,0:T(8,128)(2,1)}, u32[]{:S(2)}) %copy-start.2) | copy-done | bytes 1376280
  62.9 1.3 %copy-done.5 = bf16[1,1344,512]{2,1,0:T(8,128)(2,1)S(1)} copy-done((bf16[1,1344,512]{2,1,0:T(8,128)(2,1)S(1)}, bf16[1,1344,512]{2,1,0:T(8,128)(2,1)}, u32[]{:S(2)}) %copy-start.5) | copy-done | bytes 1376280
  64.3 3.3 %shard_map.86 = (f32[1344,256]{1,0:T(8,128)S(1)}, bf16[672,256]{1,0:T(8,128)(2,1)S(1)}) custom-call(s32[2]{0:T(128)S(1)} %pad_add_fusion.scalar_ref, bf16[128,1024]{1,0:T(8,128)(2,1)} %collective-permute-done.5.refs_0_, bf16[128,1024]{1,0:T(8,128)(2,1)S(1)} %collective-permute-done.8.refs_1_, bf16[128,1024]{1,0:T(8,128)(2,1)} %collective-permute-done.4.refs_2_, ...), custom_call_target="tpu_custom_call" | custom-call | flops 1409286144 | bytes 7569408 | tf_op jit(solution)/shard_map/pallas_call | solution.py:183
  67.5 1.1 copy-done.8
  68.6 0.7 fusion.6
  69.4 0.4 collective-permute-start.13
  69.8 0.1 collective-permute-start.14
  69.9 1.4 %collective-permute-start.17 = (bf16[128,1024]{1,0:T(8,128)(2,1)S(1)}, bf16[128,1024]{1,0:T(8,128)(2,1)}, u32[]{:S(2)}, u32[]{:S(2)}) collective-permute-start(bf16[128,1024]{1,0:T(8,128)(2,1)S(1)} %collective-permute-done.8.refs_1_), channel_id=1, source_target_pairs={{2,4},{4,2},{3,5},{5,3},{10,12},{12,10},{11,13},{13,11},{18,20},{2... | collective-permute-start | bytes 786440 | tf_op jit(solution)/shard_map/ppermute | solution.py:206
  71.3 3.1 %collective-permute-start.16 = (bf16[128,1024]{1,0:T(8,128)(2,1)}, bf16[128,1024]{1,0:T(8,128)(2,1)S(1)}, u32[]{:S(2)}, u32[]{:S(2)}) collective-permute-start(bf16[128,1024]{1,0:T(8,128)(2,1)} %copy-done.13), channel_id=1, source_target_pairs={{0,2},{2,0},{4,6},{6,4},{1,3},{3,1},{5,7},{7,5},{8,10},{10,8},{12,... | collective-permute-start | bytes 786440 | tf_op jit(solution)/shard_map/ppermute | solution.py:206
  74.5 2.4 %collective-permute-start.7 = (bf16[672,128]{1,0:T(8,128)(2,1)}, bf16[672,128]{1,0:T(8,128)(2,1)S(1)}, u32[]{:S(2)}, u32[]{:S(2)}) collective-permute-start(bf16[672,128]{1,0:T(8,128)(2,1)} %add_convert_fusion.3), channel_id=1, source_target_pairs={{8,0},{16,8},{24,16},{0,24},{9,1},{17,9},{25,17},{1,25},{10,2},{18... | collective-permute-start | bytes 516104 | tf_op jit(solution)/shard_map/ppermute | solution.py:215
  76.9 1.0 pad_maximum_fusion
  78.0 1.3 %collective-permute-done.19.refs_1_ = bf16[128,1024]{1,0:T(8,128)(2,1)S(1)} collective-permute-done((bf16[128,1024]{1,0:T(8,128)(2,1)}, bf16[128,1024]{1,0:T(8,128)(2,1)S(1)}, u32[]{:S(2)}, u32[]{:S(2)}) %collective-permute-start.19) | collective-permute-done | bytes 262176 | tf_op jit(solution)/shard_map/ppermute | solution.py:206
  79.3 5.0 %collective-permute-done.16.refs_0_ = bf16[128,1024]{1,0:T(8,128)(2,1)S(1)} collective-permute-done((bf16[128,1024]{1,0:T(8,128)(2,1)}, bf16[128,1024]{1,0:T(8,128)(2,1)S(1)}, u32[]{:S(2)}, u32[]{:S(2)}) %collective-permute-start.16) | collective-permute-done | bytes 262176 | tf_op jit(solution)/shard_map/ppermute | solution.py:206
  84.3 0.3 collective-permute-start.18
  84.6 1.2 %add_convert_fusion = bf16[672,256]{1,0:T(8,128)(2,1)S(1)} fusion(bf16[672,256]{1,0:T(8,128)(2,1)S(1)} %pad_maximum_fusion, f32[1344,256]{1,0:T(8,128)} %copy-done.8, s32[]{:T(128)S(6)} %select_n.82), kind=kLoop, calls=%fused_computation | loop fusion | flops 516096 | bytes 1376260 | tf_op jit(solution)/shard_map/convert_element_type | solution.py:279
  85.8 1.4 %copy-done.6 = bf16[1,1344,512]{2,1,0:T(8,128)(2,1)S(1)} copy-done((bf16[1,1344,512]{2,1,0:T(8,128)(2,1)S(1)}, bf16[1,1344,512]{2,1,0:T(8,128)(2,1)}, u32[]{:S(2)}) %copy-start.6) | copy-done | bytes 1376280
  87.2 3.1 %shard_map.87 = (f32[1344,128]{1,0:T(8,128)S(1)}, bf16[672,128]{1,0:T(8,128)(2,1)S(1)}) custom-call(s32[2]{0:T(128)S(1)} %pad_add_fusion.1.scalar_ref, bf16[128,1024]{1,0:T(8,128)(2,1)} %collective-permute-done.11.refs_0_, bf16[128,1024]{1,0:T(8,128)(2,1)S(1)} %collective-permute-done.19.refs_1_, bf16[128,1024]{1,0:T(8,128)(2,1)S(1)} %copy-done.14, ...), custom_call_target="tpu_custom_call" | custom-call | flops 704643072 | bytes 6537216 | tf_op jit(solution)/shard_map/pallas_call | solution.py:183
  90.3 0.3 collective-permute-start.21
  90.6 2.5 %collective-permute-start.15 = (bf16[672,256]{1,0:T(8,128)(2,1)S(1)}, bf16[672,256]{1,0:T(8,128)(2,1)S(1)}, u32[]{:S(2)}, u32[]{:S(2)}) collective-permute-start(bf16[672,256]{1,0:T(8,128)(2,1)S(1)} %add_convert_fusion), channel_id=1, source_target_pairs={{8,0},{16,8},{24,16},{0,24},{9,1},{17,9},{25,17},{1,25},{10,2},{18... | collective-permute-start | bytes 1032200 | tf_op jit(solution)/shard_map/ppermute | solution.py:215
  93.1 0.1 collective-permute-done.18.refs_1_
  93.3 7.6 %collective-permute-done.15 = bf16[672,256]{1,0:T(8,128)(2,1)S(1)} collective-permute-done((bf16[672,256]{1,0:T(8,128)(2,1)S(1)}, bf16[672,256]{1,0:T(8,128)(2,1)S(1)}, u32[]{:S(2)}, u32[]{:S(2)}) %collective-permute-start.15) | collective-permute-done | bytes 344096 | tf_op jit(solution)/shard_map/ppermute | solution.py:215
  100.9 2.5 %shard_map.88 = (f32[1344,128]{1,0:T(8,128)S(1)}, bf16[672,128]{1,0:T(8,128)(2,1)S(1)}) custom-call(s32[2]{0:T(128)S(1)} %pad_add_fusion.scalar_ref, bf16[128,1024]{1,0:T(8,128)(2,1)S(1)} %collective-permute-done.16.refs_0_, bf16[128,1024]{1,0:T(8,128)(2,1)S(1)} %collective-permute-done.18.refs_1_, bf16[1344,1024]{1,0:T(8,128)(2,1)S(1)} %bitcast.18, ...), custom_call_target="tpu_custom_call" | custom-call | flops 704643072 | bytes 6537216 | tf_op jit(solution)/shard_map/pallas_call | solution.py:183
  103.5 1.4 %collective-permute-done.22 = bf16[672,128]{1,0:T(8,128)(2,1)S(1)} collective-permute-done((bf16[672,128]{1,0:T(8,128)(2,1)S(1)}, bf16[672,128]{1,0:T(8,128)(2,1)S(1)}, u32[]{:S(2)}, u32[]{:S(2)}) %collective-permute-start.22) | collective-permute-done | bytes 172064 | tf_op jit(solution)/shard_map/ppermute | solution.py:215
  105.0 3.4 %collective-permute-start.23 = (bf16[672,128]{1,0:T(8,128)(2,1)S(1)}, bf16[672,128]{1,0:T(8,128)(2,1)S(1)}, u32[]{:S(2)}, u32[]{:S(2)}) collective-permute-start(bf16[672,128]{1,0:T(8,128)(2,1)S(1)} %add_convert_fusion.1), channel_id=1, source_target_pairs={{8,0},{16,8},{24,16},{0,24},{9,1},{17,9},{25,17},{1,25},{10,2},{18... | collective-permute-start | bytes 516104 | tf_op jit(solution)/shard_map/ppermute | solution.py:215
  108.5 0.2 collective-permute-start.24
  108.6 4.5 %collective-permute-done.23 = bf16[672,128]{1,0:T(8,128)(2,1)S(1)} collective-permute-done((bf16[672,128]{1,0:T(8,128)(2,1)S(1)}, bf16[672,128]{1,0:T(8,128)(2,1)S(1)}, u32[]{:S(2)}, u32[]{:S(2)}) %collective-permute-start.23) | collective-permute-done | bytes 172064 | tf_op jit(solution)/shard_map/ppermute | solution.py:215
  113.1 0.1 select_dynamic-update-slice_fusion.1
  113.2 2.8 %collective-permute-done.24 = bf16[672,128]{1,0:T(8,128)(2,1)S(1)} collective-permute-done((bf16[672,128]{1,0:T(8,128)(2,1)S(1)}, bf16[672,128]{1,0:T(8,128)(2,1)S(1)}, u32[]{:S(2)}, u32[]{:S(2)}) %collective-permute-start.24) | collective-permute-done | bytes 172064 | tf_op jit(solution)/shard_map/ppermute | solution.py:215
  116.0 0.1 select_dynamic-update-slice_fusion
  116.2 0.8 copy-done.22
  (64 shorter events, 0.6 us)
Async XLA Ops:
  1.0 16.3 %collective-permute-start.1 = (bf16[128,1024]{1,0:T(8,128)(2,1)S(1)}, bf16[128,1024]{1,0:T(8,128)(2,1)S(1)}, u32[]{:S(2)}, u32[]{:S(2)}) collective-permute-start(bf16[128,1024]{1,0:T(8,128)(2,1)S(1)} %pad_maximum_fusion.1.refs_2_), channel_id=1, source_target_pairs={{6,0},{0,2},{2,4},{4,6},{7,1},{1,3},{3,5},{5,7},{14,8},{8,10},{10,... | collective-permute-start | bytes 786440 | tf_op jit(solution)/shard_map/ppermute | solution.py:215
  4.1 12.5 %collective-permute-start = (bf16[48,1024]{1,0:T(8,128)(2,1)S(1)}, bf16[48,1024]{1,0:T(8,128)(2,1)S(1)}, u32[]{:S(2)}, u32[]{:S(2)}) collective-permute-start(bf16[48,1024]{1,0:T(8,128)(2,1)S(1)} %slice.29), channel_id=1, source_target_pairs={{4,0},{6,2},{0,4},{2,6},{5,1},{7,3},{1,5},{3,7},{12,8},{14,10},{8,... | collective-permute-start | bytes 294920 | tf_op jit(solution)/shard_map/ppermute | solution.py:215
  8.3 1.0 copy-start.9
  9.2 0.9 copy-start.10
  16.6 0.6 copy-start.18
  17.3 0.7 copy-start.16
  18.0 0.9 copy-start.17
  18.9 0.9 copy-start.19
  19.8 30.9 %copy-start = (bf16[1,1344,1024]{2,1,0:T(8,128)(2,1)S(1)}, bf16[1,1344,1024]{2,1,0:T(8,128)(2,1)}, u32[]{:S(2)}) copy-start(bf16[1,1344,1024]{2,1,0:T(8,128)(2,1)} %param.12) | copy-start | bytes 8257540
  22.8 18.1 %collective-permute-start.4 = (bf16[128,1024]{1,0:T(8,128)(2,1)}, bf16[128,1024]{1,0:T(8,128)(2,1)}, u32[]{:S(2)}, u32[]{:S(2)}) collective-permute-start(bf16[128,1024]{1,0:T(8,128)(2,1)} %get-tuple-element.50.refs_0_), channel_id=1, source_target_pairs={{2,4},{4,2},{3,5},{5,3},{10,12},{12,10},{11,13},{13,11},{18,20},{2... | collective-permute-start | bytes 786440 | tf_op jit(solution)/shard_map/ppermute | solution.py:206
  24.2 16.7 %collective-permute-start.5 = (bf16[128,1024]{1,0:T(8,128)(2,1)}, bf16[128,1024]{1,0:T(8,128)(2,1)}, u32[]{:S(2)}, u32[]{:S(2)}) collective-permute-start(bf16[128,1024]{1,0:T(8,128)(2,1)} %get-tuple-element.50.refs_0_), channel_id=1, source_target_pairs={{0,2},{2,0},{4,6},{6,4},{1,3},{3,1},{5,7},{7,5},{8,10},{10,8},{12,... | collective-permute-start | bytes 786440 | tf_op jit(solution)/shard_map/ppermute | solution.py:206
  24.9 16.0 %collective-permute-start.2 = (bf16[128,1024]{1,0:T(8,128)(2,1)}, bf16[128,1024]{1,0:T(8,128)(2,1)S(1)}, u32[]{:S(2)}, u32[]{:S(2)}) collective-permute-start(bf16[128,1024]{1,0:T(8,128)(2,1)} %get-tuple-element.45), channel_id=1, source_target_pairs={{2,0},{4,2},{6,4},{0,6},{3,1},{5,3},{7,5},{1,7},{10,8},{12,10},{14... | collective-permute-start | bytes 786440 | tf_op jit(solution)/shard_map/ppermute | solution.py:215
  26.5 14.4 %collective-permute-start.3 = (bf16[48,1024]{1,0:T(8,128)(2,1)}, bf16[48,1024]{1,0:T(8,128)(2,1)}, u32[]{:S(2)}, u32[]{:S(2)}) collective-permute-start(bf16[48,1024]{1,0:T(8,128)(2,1)} %get-tuple-element.46), channel_id=1, source_target_pairs={{4,0},{6,2},{0,4},{2,6},{5,1},{7,3},{1,5},{3,7},{12,8},{14,10},{8,... | collective-permute-start | bytes 294920 | tf_op jit(solution)/shard_map/ppermute | solution.py:215
  40.9 0.7 copy-start.11
  41.6 0.9 copy-start.12
  43.5 16.1 %collective-permute-start.9 = (bf16[128,1024]{1,0:T(8,128)(2,1)S(1)}, bf16[128,1024]{1,0:T(8,128)(2,1)}, u32[]{:S(2)}, u32[]{:S(2)}) collective-permute-start(bf16[128,1024]{1,0:T(8,128)(2,1)S(1)} %shard_map.84.refs_1_), channel_id=1, source_target_pairs={{2,4},{4,2},{3,5},{5,3},{10,12},{12,10},{11,13},{13,11},{18,20},{2... | collective-permute-start | bytes 786440 | tf_op jit(solution)/shard_map/ppermute | solution.py:206
  44.9 14.7 %collective-permute-start.8 = (bf16[128,1024]{1,0:T(8,128)(2,1)S(1)}, bf16[128,1024]{1,0:T(8,128)(2,1)S(1)}, u32[]{:S(2)}, u32[]{:S(2)}) collective-permute-start(bf16[128,1024]{1,0:T(8,128)(2,1)S(1)} %shard_map.84.refs_1_), channel_id=1, source_target_pairs={{0,2},{2,0},{4,6},{6,4},{1,3},{3,1},{5,7},{7,5},{8,10},{10,8},{12,... | collective-permute-start | bytes 786440 | tf_op jit(solution)/shard_map/ppermute | solution.py:206
  47.0 12.5 %collective-permute-start.10 = (bf16[128,1024]{1,0:T(8,128)(2,1)}, bf16[128,1024]{1,0:T(8,128)(2,1)S(1)}, u32[]{:S(2)}, u32[]{:S(2)}) collective-permute-start(bf16[128,1024]{1,0:T(8,128)(2,1)} %collective-permute-done.5.refs_0_), channel_id=1, source_target_pairs={{2,4},{4,2},{3,5},{5,3},{10,12},{12,10},{11,13},{13,11},{18,20},{2... | collective-permute-start | bytes 786440 | tf_op jit(solution)/shard_map/ppermute | solution.py:206
  47.7 11.9 %collective-permute-start.11 = (bf16[128,1024]{1,0:T(8,128)(2,1)}, bf16[128,1024]{1,0:T(8,128)(2,1)}, u32[]{:S(2)}, u32[]{:S(2)}) collective-permute-start(bf16[128,1024]{1,0:T(8,128)(2,1)} %collective-permute-done.4.refs_2_), channel_id=1, source_target_pairs={{0,2},{2,0},{4,6},{6,4},{1,3},{3,1},{5,7},{7,5},{8,10},{10,8},{12,... | collective-permute-start | bytes 786440 | tf_op jit(solution)/shard_map/ppermute | solution.py:206
  50.7 1.3 %copy-start.1 = (bf16[1,1344,512]{2,1,0:T(8,128)(2,1)S(1)}, bf16[1,1344,512]{2,1,0:T(8,128)(2,1)}, u32[]{:S(2)}) copy-start(bf16[1,1344,512]{2,1,0:T(8,128)(2,1)} %param.13) | copy-start | bytes 4128772
  52.0 1.3 %copy-start.4 = (bf16[1,1344,512]{2,1,0:T(8,128)(2,1)S(1)}, bf16[1,1344,512]{2,1,0:T(8,128)(2,1)}, u32[]{:S(2)}) copy-start(bf16[1,1344,512]{2,1,0:T(8,128)(2,1)} %param.14) | copy-start | bytes 4128772
  57.0 0.8 copy-start.15
  57.8 1.7 %collective-permute-start.6 = (bf16[672,128]{1,0:T(8,128)(2,1)}, bf16[672,128]{1,0:T(8,128)(2,1)}, u32[]{:S(2)}, u32[]{:S(2)}) collective-permute-start(bf16[672,128]{1,0:T(8,128)(2,1)} %get-tuple-element.53), channel_id=1, source_target_pairs={{1,0},{0,1},{3,2},{2,3},{5,4},{4,5},{7,6},{6,7},{9,8},{8,9},{11,10... | collective-permute-start | bytes 516104 | tf_op jit(solution)/shard_map/ppermute | solution.py:215
  59.6 10.4 %copy-start.13 = (bf16[128,1024]{1,0:T(8,128)(2,1)}, bf16[128,1024]{1,0:T(8,128)(2,1)S(1)}, u32[]{:S(2)}) copy-start(bf16[128,1024]{1,0:T(8,128)(2,1)S(1)} %collective-permute-done.10.refs_2_) | copy-start | bytes 786436
  59.6 2.0 %collective-permute-start.12 = (bf16[16,128]{1,0:T(8,128)(2,1)S(1)}, bf16[16,128]{1,0:T(8,128)(2,1)S(1)}, u32[]{:S(2)}, u32[]{:S(2)}) collective-permute-start(bf16[16,128]{1,0:T(8,128)(2,1)S(1)} %slice.30), channel_id=1, source_target_pairs={{1,0},{0,1},{3,2},{2,3},{5,4},{4,5},{7,6},{6,7},{9,8},{8,9},{11,10... | collective-permute-start | bytes 12296 | tf_op jit(solution)/shard_map/ppermute | solution.py:215
  61.6 1.3 %copy-start.2 = (bf16[1,1344,512]{2,1,0:T(8,128)(2,1)S(1)}, bf16[1,1344,512]{2,1,0:T(8,128)(2,1)}, u32[]{:S(2)}) copy-start(bf16[1,1344,512]{2,1,0:T(8,128)(2,1)} %param.13) | copy-start | bytes 4128772
  62.9 1.3 %copy-start.5 = (bf16[1,1344,512]{2,1,0:T(8,128)(2,1)S(1)}, bf16[1,1344,512]{2,1,0:T(8,128)(2,1)}, u32[]{:S(2)}) copy-start(bf16[1,1344,512]{2,1,0:T(8,128)(2,1)} %param.14) | copy-start | bytes 4128772
  67.5 1.1 copy-start.8
  69.4 5.1 %collective-permute-start.13 = (bf16[672,128]{1,0:T(8,128)(2,1)}, bf16[672,128]{1,0:T(8,128)(2,1)}, u32[]{:S(2)}, u32[]{:S(2)}) collective-permute-start(bf16[672,128]{1,0:T(8,128)(2,1)} %get-tuple-element.73), channel_id=1, source_target_pairs={{1,0},{0,1},{3,2},{2,3},{5,4},{4,5},{7,6},{6,7},{9,8},{8,9},{11,10... | collective-permute-start | bytes 516104 | tf_op jit(solution)/shard_map/ppermute | solution.py:215
  69.8 7.2 %collective-permute-start.14 = (bf16[672,128]{1,0:T(8,128)(2,1)}, bf16[672,128]{1,0:T(8,128)(2,1)}, u32[]{:S(2)}, u32[]{:S(2)}) collective-permute-start(bf16[672,128]{1,0:T(8,128)(2,1)} %get-tuple-element.74), channel_id=1, source_target_pairs={{1,0},{0,1},{3,2},{2,3},{5,4},{4,5},{7,6},{6,7},{9,8},{8,9},{11,10... | collective-permute-start | bytes 516104 | tf_op jit(solution)/shard_map/ppermute | solution.py:215
  69.9 9.3 %collective-permute-start.19 = (bf16[128,1024]{1,0:T(8,128)(2,1)}, bf16[128,1024]{1,0:T(8,128)(2,1)S(1)}, u32[]{:S(2)}, u32[]{:S(2)}) collective-permute-start(bf16[128,1024]{1,0:T(8,128)(2,1)} %collective-permute-done.9.refs_3_), channel_id=1, source_target_pairs={{0,2},{2,0},{4,6},{6,4},{1,3},{3,1},{5,7},{7,5},{8,10},{10,8},{12,... | collective-permute-start | bytes 786440 | tf_op jit(solution)/shard_map/ppermute | solution.py:206
  69.9 9.3 %collective-permute-start.17 = (bf16[128,1024]{1,0:T(8,128)(2,1)S(1)}, bf16[128,1024]{1,0:T(8,128)(2,1)}, u32[]{:S(2)}, u32[]{:S(2)}) collective-permute-start(bf16[128,1024]{1,0:T(8,128)(2,1)S(1)} %collective-permute-done.8.refs_1_), channel_id=1, source_target_pairs={{2,4},{4,2},{3,5},{5,3},{10,12},{12,10},{11,13},{13,11},{18,20},{2... | collective-permute-start | bytes 786440 | tf_op jit(solution)/shard_map/ppermute | solution.py:206
  71.3 13.0 %collective-permute-start.16 = (bf16[128,1024]{1,0:T(8,128)(2,1)}, bf16[128,1024]{1,0:T(8,128)(2,1)S(1)}, u32[]{:S(2)}, u32[]{:S(2)}) collective-permute-start(bf16[128,1024]{1,0:T(8,128)(2,1)} %copy-done.13), channel_id=1, source_target_pairs={{0,2},{2,0},{4,6},{6,4},{1,3},{3,1},{5,7},{7,5},{8,10},{10,8},{12,... | collective-permute-start | bytes 786440 | tf_op jit(solution)/shard_map/ppermute | solution.py:206
  74.4 11.4 %copy-start.3 = (bf16[1,1344,512]{2,1,0:T(8,128)(2,1)S(1)}, bf16[1,1344,512]{2,1,0:T(8,128)(2,1)}, u32[]{:S(2)}) copy-start(bf16[1,1344,512]{2,1,0:T(8,128)(2,1)} %param.13) | copy-start | bytes 4128772
  74.4 11.4 %copy-start.14 = (bf16[128,1024]{1,0:T(8,128)(2,1)S(1)}, bf16[128,1024]{1,0:T(8,128)(2,1)}, u32[]{:S(2)}) copy-start(bf16[128,1024]{1,0:T(8,128)(2,1)} %copy-done.13) | copy-start | bytes 786436
  74.5 11.3 %collective-permute-start.7 = (bf16[672,128]{1,0:T(8,128)(2,1)}, bf16[672,128]{1,0:T(8,128)(2,1)S(1)}, u32[]{:S(2)}, u32[]{:S(2)}) collective-permute-start(bf16[672,128]{1,0:T(8,128)(2,1)} %add_convert_fusion.3), channel_id=1, source_target_pairs={{8,0},{16,8},{24,16},{0,24},{9,1},{17,9},{25,17},{1,25},{10,2},{18... | collective-permute-start | bytes 516104 | tf_op jit(solution)/shard_map/ppermute | solution.py:215
  84.3 1.5 %collective-permute-start.20 = (bf16[16,128]{1,0:T(8,128)(2,1)S(1)}, bf16[16,128]{1,0:T(8,128)(2,1)S(1)}, u32[]{:S(2)}, u32[]{:S(2)}) collective-permute-start(bf16[16,128]{1,0:T(8,128)(2,1)S(1)} %slice.33), channel_id=1, source_target_pairs={{1,0},{0,1},{3,2},{2,3},{5,4},{4,5},{7,6},{6,7},{9,8},{8,9},{11,10... | collective-permute-start | bytes 12296 | tf_op jit(solution)/shard_map/ppermute | solution.py:215
  84.3 8.9 %collective-permute-start.18 = (bf16[128,1024]{1,0:T(8,128)(2,1)}, bf16[128,1024]{1,0:T(8,128)(2,1)S(1)}, u32[]{:S(2)}, u32[]{:S(2)}) collective-permute-start(bf16[128,1024]{1,0:T(8,128)(2,1)} %collective-permute-done.17.refs_3_), channel_id=1, source_target_pairs={{0,2},{2,0},{4,6},{6,4},{1,3},{3,1},{5,7},{7,5},{8,10},{10,8},{12,... | collective-permute-start | bytes 786440 | tf_op jit(solution)/shard_map/ppermute | solution.py:206
  85.8 4.6 %copy-start.23 = (bf16[672,128]{1,0:T(8,128)(2,1)}, bf16[672,128]{1,0:T(8,128)(2,1)S(1)}, u32[]{:S(2)}) copy-start(bf16[672,128]{1,0:T(8,128)(2,1)S(1)} %collective-permute-done.7) | copy-start | bytes 516100
  85.8 1.4 %copy-start.6 = (bf16[1,1344,512]{2,1,0:T(8,128)(2,1)S(1)}, bf16[1,1344,512]{2,1,0:T(8,128)(2,1)}, u32[]{:S(2)}) copy-start(bf16[1,1344,512]{2,1,0:T(8,128)(2,1)} %param.14) | copy-start | bytes 4128772
  87.2 13.7 %copy-start.7 = (bf16[1,1344,512]{2,1,0:T(8,128)(2,1)S(1)}, bf16[1,1344,512]{2,1,0:T(8,128)(2,1)}, u32[]{:S(2)}) copy-start(bf16[1,1344,512]{2,1,0:T(8,128)(2,1)} %param.14) | copy-start | bytes 4128772
  90.3 2.7 %collective-permute-start.21 = (bf16[672,128]{1,0:T(8,128)(2,1)S(1)}, bf16[672,128]{1,0:T(8,128)(2,1)S(1)}, u32[]{:S(2)}, u32[]{:S(2)}) collective-permute-start(bf16[672,128]{1,0:T(8,128)(2,1)S(1)} %get-tuple-element.67), channel_id=1, source_target_pairs={{1,0},{0,1},{3,2},{2,3},{5,4},{4,5},{7,6},{6,7},{9,8},{8,9},{11,10... | collective-permute-start | bytes 516104 | tf_op jit(solution)/shard_map/ppermute | solution.py:215
  90.6 10.3 %collective-permute-start.15 = (bf16[672,256]{1,0:T(8,128)(2,1)S(1)}, bf16[672,256]{1,0:T(8,128)(2,1)S(1)}, u32[]{:S(2)}, u32[]{:S(2)}) collective-permute-start(bf16[672,256]{1,0:T(8,128)(2,1)S(1)} %add_convert_fusion), channel_id=1, source_target_pairs={{8,0},{16,8},{24,16},{0,24},{9,1},{17,9},{25,17},{1,25},{10,2},{18... | collective-permute-start | bytes 1032200 | tf_op jit(solution)/shard_map/ppermute | solution.py:215
  100.9 2.5 %copy-start.20 = (bf16[672,256]{1,0:T(8,128)(2,1)}, bf16[672,256]{1,0:T(8,128)(2,1)S(1)}, u32[]{:S(2)}) copy-start(bf16[672,256]{1,0:T(8,128)(2,1)S(1)} %collective-permute-done.15) | copy-start | bytes 1032196
  103.4 5.0 %copy-start.24 = (bf16[672,128]{1,0:T(8,128)(2,1)S(1)}, bf16[672,128]{1,0:T(8,128)(2,1)}, u32[]{:S(2)}) copy-start(bf16[672,128]{1,0:T(8,128)(2,1)} %copy-done.23) | copy-start | bytes 516100
  103.4 9.7 %copy-start.21 = (bf16[672,256]{1,0:T(8,128)(2,1)S(1)}, bf16[672,256]{1,0:T(8,128)(2,1)}, u32[]{:S(2)}) copy-start(bf16[672,256]{1,0:T(8,128)(2,1)} %copy-done.20) | copy-start | bytes 1032196
  103.5 1.5 %collective-permute-start.22 = (bf16[672,128]{1,0:T(8,128)(2,1)S(1)}, bf16[672,128]{1,0:T(8,128)(2,1)S(1)}, u32[]{:S(2)}, u32[]{:S(2)}) collective-permute-start(bf16[672,128]{1,0:T(8,128)(2,1)S(1)} %get-tuple-element.72), channel_id=1, source_target_pairs={{1,0},{0,1},{3,2},{2,3},{5,4},{4,5},{7,6},{6,7},{9,8},{8,9},{11,10... | collective-permute-start | bytes 516104 | tf_op jit(solution)/shard_map/ppermute | solution.py:215
  105.0 8.1 %collective-permute-start.23 = (bf16[672,128]{1,0:T(8,128)(2,1)S(1)}, bf16[672,128]{1,0:T(8,128)(2,1)S(1)}, u32[]{:S(2)}, u32[]{:S(2)}) collective-permute-start(bf16[672,128]{1,0:T(8,128)(2,1)S(1)} %add_convert_fusion.1), channel_id=1, source_target_pairs={{8,0},{16,8},{24,16},{0,24},{9,1},{17,9},{25,17},{1,25},{10,2},{18... | collective-permute-start | bytes 516104 | tf_op jit(solution)/shard_map/ppermute | solution.py:215
  108.5 7.5 %collective-permute-start.24 = (bf16[672,128]{1,0:T(8,128)(2,1)S(1)}, bf16[672,128]{1,0:T(8,128)(2,1)S(1)}, u32[]{:S(2)}, u32[]{:S(2)}) collective-permute-start(bf16[672,128]{1,0:T(8,128)(2,1)S(1)} %add_convert_fusion.2), channel_id=1, source_target_pairs={{8,0},{16,8},{24,16},{0,24},{9,1},{17,9},{25,17},{1,25},{10,2},{18... | collective-permute-start | bytes 516104 | tf_op jit(solution)/shard_map/ppermute | solution.py:215
  116.1 0.8 copy-start.22

commit v5 on v3

--- a/solution.py
+++ b/solution.py
@@ -196,11 +196,10 @@
 
 
 def swapped(block, axis, first):
-    size = lax.axis_size(axis)
-    target = list(range(size))
-    for i in range(first, size - 1, 2):
-        target[i], target[i + 1] = i + 1, i
-    return lax.ppermute(block, axis, list(enumerate(target)))
+    pairs = []
+    for i in range(first, lax.axis_size(axis) - 1, 2):
+        pairs += [(i, i + 1), (i + 1, i)]
+    return lax.ppermute(block, axis, pairs)
 
 
 def after(arrays, *others):
@@ -261,12 +260,17 @@
     weights = (w_query[0], key_weight[0], value_weight[0])
     core = lax.axis_index("mp").astype(jnp.int32)
 
-    def halves_summed(blocks):
+    def halves_summed(blocks, *late):
         full, give = project([(block,) for block in blocks], weights, core[None])
         half = give.shape[0]
         keep = lax.dynamic_slice_in_dim(full, core * half, half, 0)
-        got = passed_along(give, "mp", 1)
-        return give, (keep + got.astype(jnp.float32)).astype(jnp.bfloat16)
+        sums = []
+        for i in range(0, give.shape[1], rows):
+            got = passed_along(give[:, i : i + rows], "mp", 1)
+            if late:
+                (got,) = after((got,), *late)
+            sums.append((keep[:, i : i + rows] + got.astype(jnp.float32)).astype(jnp.bfloat16))
+        return jnp.concatenate(sums, axis=1)
 
     even = place % 2 == 0
     results, waiting = [], [own]
@@ -275,13 +279,9 @@
         came_first = swapped(by_first, "seq", 0)
         last = step == shards - 1 and shards % 2 == 0
         came_second = came_first if last else swapped(by_second, "seq", 1)
-        if step == 2:
-            waiting = after(waiting, total)
-        elif step > 2:
-            waiting = after(waiting, total, results[step - 3])
-        give, total = halves_summed(waiting)
-        if step < shards - 1:
-            came_first, came_second = after((came_first, came_second), give)
+        if step > 1:
+            waiting = after(waiting, total, *(results[-2:] if 2 * step > shards else ()))
+        total = halves_summed(waiting, *((came_first, came_second) if step > 1 else ()))
         results.append(passed_along(total, "section", -1))
         by_first, by_second = came_second, came_first
         if last:
@@ -291,8 +291,8 @@
         else:
             waiting = [jnp.where(even == (place >= step), came_second, came_first)]
     if shards > 1:
-        waiting = after(waiting, *results)
-    results.append(passed_along(halves_summed(waiting)[1], "section", -1))
+        waiting = after(waiting, total)
+    results.append(passed_along(halves_summed(waiting), "section", -1))
     for step, block in enumerate(results):
         if block.shape[1] == rows:
             results[step] = [block]

time: 102 us -> 95.2 us (0.933)
  starting transfers between devices: 33.9 us -> 29 us
  waiting for transfers between devices: 38.3 us -> 35.9 us
    ppermute x5, starting transfers between devices: 17.5 us -> 13.9 us  [swapped(): return lax.ppermute(block, axis, pairs)]
    ppermute x5, waiting for transfers between devices: 5.71 us -> 4.12 us  [swapped(): return lax.ppermute(block, axis, pairs)]
    ppermute x12 -> x13, starting transfers between devices: 16.4 us -> 15.1 us  [passed_along(): lax.ppermute(block, axis, [((i - distance) % len(devices), i) for i in de...]
    ppermute x12 -> x13, waiting for transfers between devices: 32.6 us -> 31.8 us  [passed_along(): lax.ppermute(block, axis, [((i - distance) % len(devices), i) for i in de...]
    unnamed x28 -> x30, local copies, waits for them, and re-layouts: 10 us -> 10.1 us
  transfers between devices with their start and end apart: 17 -> 18, of which waited for: 9 -> 11; matrix products, arithmetic and copies ran while one was open for 6% -> 7% of each run, Pallas kernels for 2% -> 8%
where the time goes in v5:
time: 95.2 us; the launch traced here: 94.7 us
  waiting for transfers between devices  35.9 us (38%)
  starting transfers between devices  29 us (30%)
  local copies, waits for them, and re-layouts  12.4 us (13%)
  Pallas kernels  11.7 us (12%)
  other arithmetic  5.56 us (6%)
    ppermute x13, waiting for transfers between devices, passed_along(): lax.ppermute(block, axis, [((i - distance) % len(devices), i) for i in de...  31.8 us
    ppermute x13, starting transfers between devices, passed_along(): lax.ppermute(block, axis, [((i - distance) % len(devices), i) for i in de...  15.1 us
    ppermute x5, starting transfers between devices, swapped(): return lax.ppermute(block, axis, pairs)  13.9 us
    unnamed x30, local copies, waits for them, and re-layouts  10.1 us
    pallas_call x4, Pallas kernels, project(): pl.pallas_call(functools.partial(project_kernel, [len(block) for block in...  9.26 us
    ppermute x5, waiting for transfers between devices, swapped(): return lax.ppermute(block, axis, pairs)  4.12 us
    convert_element_type x4, other arithmetic, halves_summed(): (keep[:, i:i + rows] + got.astype(jnp.float32)).astype(jnp.bfloat16)  3.14 us
    pallas_call x1, Pallas kernels, attention_backward(): pl.pallas_call(functools.partial(attention_kernel, kv_heads, group_width,...  2.24 us
  transfers between devices with their start and end apart: 18, of which 11 were waited for; matrix products, arithmetic and copies ran while one was open for 7% of the time, Pallas kernels for 8%

profile of v5, /device:TPU:0, one launch (start us, length us, event | category | flops | bytes accessed | tf_op | source)
XLA Modules:
  0.0 94.7 jit_solution(17189068314672928779)
XLA Ops:
  0.0 1.0 %pad_maximum_fusion.1.refs_2_ = bf16[128,1024]{1,0:T(8,128)(2,1)S(1)} fusion(bf16[128,512]{1,0:T(8,128)(2,1)} %bitcast.28, bf16[128,512]{1,0:T(8,128)(2,1)} %bitcast.29), kind=kLoop, calls=%fused_computation.9 | loop fusion | flops 524288 | bytes 524288 | tf_op jit(solution)/shard_map/concatenate | solution.py:235
  1.0 3.1 %collective-permute-start.1 = (bf16[128,1024]{1,0:T(8,128)(2,1)S(1)}, bf16[128,1024]{1,0:T(8,128)(2,1)S(1)}, u32[]{:S(2)}, u32[]{:S(2)}) collective-permute-start(bf16[128,1024]{1,0:T(8,128)(2,1)S(1)} %pad_maximum_fusion.1.refs_2_), channel_id=1, source_target_pairs={{6,0},{0,2},{2,4},{4,6},{7,1},{1,3},{3,5},{5,7},{14,8},{8,10},{10,... | collective-permute-start | bytes 786440 | tf_op jit(solution)/shard_map/ppermute | solution.py:211
  4.1 2.6 %collective-permute-start = (bf16[48,1024]{1,0:T(8,128)(2,1)S(1)}, bf16[48,1024]{1,0:T(8,128)(2,1)S(1)}, u32[]{:S(2)}, u32[]{:S(2)}) collective-permute-start(bf16[48,1024]{1,0:T(8,128)(2,1)S(1)} %slice.28), channel_id=1, source_target_pairs={{4,0},{6,2},{0,4},{2,6},{5,1},{7,3},{1,5},{3,7},{12,8},{14,10},{8,... | collective-permute-start | bytes 294920 | tf_op jit(solution)/shard_map/ppermute | solution.py:211
  6.7 0.8 pad_dynamic-slice_fusion
  7.5 0.7 fusion.7
  8.1 0.1 fusion.6.refs_3_
  8.3 0.0 copy-start.8
  8.3 0.9 copy-done.8
  9.2 0.9 %copy-done.9 = bf16[1,128,1024]{2,1,0:T(8,128)(2,1)S(1)} copy-done((bf16[1,128,1024]{2,1,0:T(8,128)(2,1)S(1)}, bf16[1,128,1024]{2,1,0:T(8,128)(2,1)}, u32[]{:S(2)}) %copy-start.9) | copy-done | bytes 262168
  10.2 0.1 shard_map.82
  10.3 6.4 %collective-permute-done.refs_4_ = bf16[48,1024]{1,0:T(8,128)(2,1)S(1)} collective-permute-done((bf16[48,1024]{1,0:T(8,128)(2,1)S(1)}, bf16[48,1024]{1,0:T(8,128)(2,1)S(1)}, u32[]{:S(2)}, u32[]{:S(2)}) %collective-permute-start) | collective-permute-done | bytes 98336 | tf_op jit(solution)/shard_map/ppermute | solution.py:211
  16.6 0.0 collective-permute-done.1.refs_5_
  16.6 2.2 %shard_map.83 = (bf16[128,1024]{1,0:T(8,128)(2,1)S(1)}, f32[128,1024]{1,0:T(8,128)S(1)}, bf16[48,1024]{1,0:T(8,128)(2,1)S(1)}, bf16[128,1024]{1,0:T(8,128)(2,1)S(1)}) custom-call(bf16[1024,128]{1,0:T(8,128)(2,1)S(1)} %get-tuple-element.30.refs_0_, bf16[1024,128]{1,0:T(8,128)(2,1)S(1)} %get-tuple-element.31.refs_1_, ...), custom_call_target="tpu_custom_call" | custom-call | flops 478150656 | bytes 1048576 | tf_op jit(solution)/shard_map/pallas_call | solution.py:100
  18.9 1.7 %collective-permute-start.2 = (bf16[128,1024]{1,0:T(8,128)(2,1)S(1)}, bf16[128,1024]{1,0:T(8,128)(2,1)S(1)}, u32[]{:S(2)}, u32[]{:S(2)}) collective-permute-start(bf16[128,1024]{1,0:T(8,128)(2,1)S(1)} %get-tuple-element.34), channel_id=1, source_target_pairs={{2,0},{4,2},{6,4},{0,6},{3,1},{5,3},{7,5},{1,7},{10,8},{12,10},{14... | collective-permute-start | bytes 786440 | tf_op jit(solution)/shard_map/ppermute | solution.py:211
  20.5 0.0 collective-permute-start.3
  20.5 8.7 %collective-permute-done.3.refs_1_ = bf16[48,1024]{1,0:T(8,128)(2,1)S(1)} collective-permute-done((bf16[48,1024]{1,0:T(8,128)(2,1)S(1)}, bf16[48,1024]{1,0:T(8,128)(2,1)S(1)}, u32[]{:S(2)}, u32[]{:S(2)}) %collective-permute-start.3) | collective-permute-done | bytes 98336 | tf_op jit(solution)/shard_map/ppermute | solution.py:211
  29.3 0.0 collective-permute-done.2.refs_0_
  29.3 0.1 shard_map.84.refs_0_
  29.3 1.4 %collective-permute-start.6 = (bf16[128,2048]{1,0:T(8,128)(2,1)S(1)}, bf16[128,2048]{1,0:T(8,128)(2,1)}, u32[]{:S(2)}, u32[]{:S(2)}) collective-permute-start(bf16[128,2048]{1,0:T(8,128)(2,1)S(1)} %shard_map.84.refs_0_), channel_id=1, source_target_pairs={{0,2},{2,0},{4,6},{6,4},{1,3},{3,1},{5,7},{7,5},{8,10},{10,8},{12,... | collective-permute-start | bytes 1572872 | tf_op jit(solution)/shard_map/ppermute | solution.py:202
  30.8 1.5 %collective-permute-start.7 = (bf16[128,2048]{1,0:T(8,128)(2,1)S(1)}, bf16[128,2048]{1,0:T(8,128)(2,1)}, u32[]{:S(2)}, u32[]{:S(2)}) collective-permute-start(bf16[128,2048]{1,0:T(8,128)(2,1)S(1)} %shard_map.84.refs_0_), channel_id=1, source_target_pairs={{2,4},{4,2},{3,5},{5,3},{10,12},{12,10},{11,13},{13,11},{18,20},{2... | collective-permute-start | bytes 1572872 | tf_op jit(solution)/shard_map/ppermute | solution.py:202
  32.2 1.3 %copy-done.1 = bf16[1,1344,512]{2,1,0:T(8,128)(2,1)S(1)} copy-done((bf16[1,1344,512]{2,1,0:T(8,128)(2,1)S(1)}, bf16[1,1344,512]{2,1,0:T(8,128)(2,1)}, u32[]{:S(2)}) %copy-start.1) | copy-done | bytes 1376280
  33.6 1.3 %copy-done.4 = bf16[1,1344,512]{2,1,0:T(8,128)(2,1)S(1)} copy-done((bf16[1,1344,512]{2,1,0:T(8,128)(2,1)S(1)}, bf16[1,1344,512]{2,1,0:T(8,128)(2,1)}, u32[]{:S(2)}) %copy-start.4) | copy-done | bytes 1376280
  34.9 2.0 %shard_map.85 = (f32[1344,128]{1,0:T(8,128)S(1)}, bf16[672,128]{1,0:T(8,128)(2,1)S(1)}) custom-call(s32[1]{0:T(128)} %bitcast.core_ref, bf16[128,2048]{1,0:T(8,128)(2,1)S(1)} %shard_map.84.refs_0_, bf16[1344,1024]{1,0:T(8,128)(2,1)S(1)} %bitcast.14, bf16[1344,512]{1,0:T(8,128)(2,1)S(1)} %bitcast.18, bf16[1344,512]{1,0:T(8,128)(2,1)S(1)} %bitcast.22), custom_call_target="tpu_custom_call" | custom-call | flops 704643072 | bytes 6537216 | tf_op jit(solution)/shard_map/pallas_call | solution.py:180
  36.9 0.0 copy-start.10
  36.9 0.8 copy-done.10
  37.8 0.0 collective-permute-start.4
  37.8 1.5 %collective-permute-done.4 = bf16[672,128]{1,0:T(8,128)(2,1)} collective-permute-done((bf16[672,128]{1,0:T(8,128)(2,1)S(1)}, bf16[672,128]{1,0:T(8,128)(2,1)}, u32[]{:S(2)}, u32[]{:S(2)}) %collective-permute-start.4) | collective-permute-done | bytes 172064 | tf_op jit(solution)/shard_map/ppermute | solution.py:211
  39.3 1.8 %add_convert_fusion.2 = bf16[672,128]{1,0:T(8,128)(2,1)} fusion(bf16[672,128]{1,0:T(8,128)(2,1)} %collective-permute-done.4, f32[1344,128]{1,0:T(8,128)} %copy-done.10, s32[]{:T(128)S(6)} %select_n.90), kind=kLoop, calls=%fused_computation.8 | loop fusion | flops 258048 | bytes 688132 | tf_op jit(solution)/shard_map/convert_element_type | solution.py:272
  41.1 1.9 %collective-permute-done.6.refs_0_ = bf16[128,2048]{1,0:T(8,128)(2,1)} collective-permute-done((bf16[128,2048]{1,0:T(8,128)(2,1)S(1)}, bf16[128,2048]{1,0:T(8,128)(2,1)}, u32[]{:S(2)}, u32[]{:S(2)}) %collective-permute-start.6) | collective-permute-done | bytes 524320 | tf_op jit(solution)/shard_map/ppermute | solution.py:202
  43.0 0.7 collective-permute-start.10
  43.7 8.6 %collective-permute-start.9 = (bf16[128,2048]{1,0:T(8,128)(2,1)}, bf16[128,2048]{1,0:T(8,128)(2,1)}, u32[]{:S(2)}, u32[]{:S(2)}) collective-permute-start(bf16[128,2048]{1,0:T(8,128)(2,1)} %collective-permute-done.7.refs_1_), channel_id=1, source_target_pairs={{0,2},{2,0},{4,6},{6,4},{1,3},{3,1},{5,7},{7,5},{8,10},{10,8},{12,... | collective-permute-start | bytes 1572872 | tf_op jit(solution)/shard_map/ppermute | solution.py:202
  52.2 1.3 %copy-done.2 = bf16[1,1344,512]{2,1,0:T(8,128)(2,1)S(1)} copy-done((bf16[1,1344,512]{2,1,0:T(8,128)(2,1)S(1)}, bf16[1,1344,512]{2,1,0:T(8,128)(2,1)}, u32[]{:S(2)}) %copy-start.2) | copy-done | bytes 1376280
  53.6 1.3 %copy-done.5 = bf16[1,1344,512]{2,1,0:T(8,128)(2,1)S(1)} copy-done((bf16[1,1344,512]{2,1,0:T(8,128)(2,1)S(1)}, bf16[1,1344,512]{2,1,0:T(8,128)(2,1)}, u32[]{:S(2)}) %copy-start.5) | copy-done | bytes 1376280
  54.9 3.3 %shard_map.86 = (f32[1344,256]{1,0:T(8,128)S(1)}, bf16[672,256]{1,0:T(8,128)(2,1)S(1)}) custom-call(s32[1]{0:T(128)} %bitcast.core_ref, bf16[128,2048]{1,0:T(8,128)(2,1)} %collective-permute-done.6.refs_0_, bf16[128,2048]{1,0:T(8,128)(2,1)} %collective-permute-done.7.refs_1_, bf16[1344,1024]{1,0:T(8,128)(2,1)S(1)} %bitcast.15, ...), custom_call_target="tpu_custom_call" | custom-call | flops 1409286144 | bytes 7569408 | tf_op jit(solution)/shard_map/pallas_call | solution.py:180
  58.3 1.1 %copy-done.7 = f32[1344,256]{1,0:T(8,128)} copy-done((f32[1344,256]{1,0:T(8,128)}, f32[1344,256]{1,0:T(8,128)S(1)}, u32[]{:S(2)}) %copy-start.7) | copy-done | bytes 1376280
  59.4 0.7 fusion.8
  60.1 0.5 collective-permute-start.8
  60.6 2.4 %collective-permute-start.5 = (bf16[672,128]{1,0:T(8,128)(2,1)}, bf16[672,128]{1,0:T(8,128)(2,1)S(1)}, u32[]{:S(2)}, u32[]{:S(2)}) collective-permute-start(bf16[672,128]{1,0:T(8,128)(2,1)} %add_convert_fusion.2), channel_id=1, source_target_pairs={{8,0},{16,8},{24,16},{0,24},{9,1},{17,9},{25,17},{1,25},{10,2},{18... | collective-permute-start | bytes 516104 | tf_op jit(solution)/shard_map/ppermute | solution.py:211
  63.1 0.0 collective-permute-done.11
  63.1 0.0 collective-permute-done.10
  63.1 0.1 collective-permute-done.9
  63.2 0.0 collective-permute-done.8
  63.2 1.3 %fusion.1 = (bf16[672,128]{1,0:T(8,128)(2,1)S(1)}, bf16[672,128]{1,0:T(8,128)(2,1)S(1)}) fusion(f32[1344,256]{1,0:T(8,128)} %copy-done.7, s32[]{:T(128)S(6)} %select_n.90, bf16[672,128]{1,0:T(8,128)(2,1)} %collective-permute-done.8, bf16[672,128]{1,0:T(8,128)(2,1)S(1)} %collective-permute-done.11, s32[]{:T(128)S(6)} %add.92), kind=kLoop, calls=%fused_computation.4 | loop fusion | flops 516096 | bytes 1376264 | tf_op jit(solution)/shard_map/convert_element_type | solution.py:272
  64.5 0.0 copy-start.3
  64.6 2.5 %collective-permute-start.12 = (bf16[672,256]{1,0:T(8,128)(2,1)S(1)}, bf16[672,256]{1,0:T(8,128)(2,1)S(1)}, u32[]{:S(2)}, u32[]{:S(2)}) collective-permute-start(bf16[672,256]{1,0:T(8,128)(2,1)S(1)} %pad_maximum_fusion), channel_id=1, source_target_pairs={{8,0},{16,8},{24,16},{0,24},{9,1},{17,9},{25,17},{1,25},{10,2},{18... | collective-permute-start | bytes 1032200 | tf_op jit(solution)/shard_map/ppermute | solution.py:211
  67.1 1.7 %collective-permute-start.13 = (bf16[128,2048]{1,0:T(8,128)(2,1)}, bf16[128,2048]{1,0:T(8,128)(2,1)S(1)}, u32[]{:S(2)}, u32[]{:S(2)}) collective-permute-start(bf16[128,2048]{1,0:T(8,128)(2,1)} %copy-done.12), channel_id=1, source_target_pairs={{0,2},{2,0},{4,6},{6,4},{1,3},{3,1},{5,7},{7,5},{8,10},{10,8},{12,... | collective-permute-start | bytes 1572872 | tf_op jit(solution)/shard_map/ppermute | solution.py:202
  68.8 1.1 %broadcast_select_fusion.refs_0_ = bf16[128,2048]{1,0:T(8,128)(2,1)S(1)} fusion(bf16[128,2048]{1,0:T(8,128)(2,1)} %copy-done.12, bf16[128,2048]{1,0:T(8,128)(2,1)} %collective-permute-done.9, pred[]{:T(512)S(6)} %eq.32), kind=kLoop, calls=%fused_computation | loop fusion | flops 262144 | bytes 1572865 | tf_op jit(solution)/shard_map/jit(_where)/select_n | solution.py:292
  69.9 0.0 collective-permute-done.5
  70.0 4.5 %collective-permute-done.12 = bf16[672,256]{1,0:T(8,128)(2,1)S(1)} collective-permute-done((bf16[672,256]{1,0:T(8,128)(2,1)S(1)}, bf16[672,256]{1,0:T(8,128)(2,1)S(1)}, u32[]{:S(2)}, u32[]{:S(2)}) %collective-permute-start.12) | collective-permute-done | bytes 344096 | tf_op jit(solution)/shard_map/ppermute | solution.py:211
  74.5 2.0 %shard_map.87 = (f32[1344,128]{1,0:T(8,128)S(1)}, bf16[672,128]{1,0:T(8,128)(2,1)S(1)}) custom-call(s32[1]{0:T(128)} %bitcast.core_ref, bf16[128,2048]{1,0:T(8,128)(2,1)S(1)} %broadcast_select_fusion.refs_0_, bf16[1344,1024]{1,0:T(8,128)(2,1)S(1)} %bitcast.16, bf16[1344,512]{1,0:T(8,128)(2,1)S(1)} %bitcast.20, bf16[1344,512]{1,0:T(8,128)(2,1)S(1)} %bitcast.24), custom_call_target="tpu_custom_call" | custom-call | flops 704643072 | bytes 6537216 | tf_op jit(solution)/shard_map/pallas_call | solution.py:180
  76.5 0.1 collective-permute-start.14
  76.6 1.4 %collective-permute-done.14 = bf16[672,128]{1,0:T(8,128)(2,1)S(1)} collective-permute-done((bf16[672,128]{1,0:T(8,128)(2,1)S(1)}, bf16[672,128]{1,0:T(8,128)(2,1)S(1)}, u32[]{:S(2)}, u32[]{:S(2)}) %collective-permute-start.14) | collective-permute-done | bytes 172064 | tf_op jit(solution)/shard_map/ppermute | solution.py:211
  78.0 2.1 %collective-permute-done.13.refs_0_ = bf16[128,2048]{1,0:T(8,128)(2,1)S(1)} collective-permute-done((bf16[128,2048]{1,0:T(8,128)(2,1)}, bf16[128,2048]{1,0:T(8,128)(2,1)S(1)}, u32[]{:S(2)}, u32[]{:S(2)}) %collective-permute-start.13) | collective-permute-done | bytes 524320 | tf_op jit(solution)/shard_map/ppermute | solution.py:202
  80.1 2.0 %shard_map.88 = (f32[1344,128]{1,0:T(8,128)S(1)}, bf16[672,128]{1,0:T(8,128)(2,1)S(1)}) custom-call(s32[1]{0:T(128)} %bitcast.core_ref, bf16[128,2048]{1,0:T(8,128)(2,1)S(1)} %collective-permute-done.13.refs_0_, bf16[1344,1024]{1,0:T(8,128)(2,1)S(1)} %bitcast.17, bf16[1344,512]{1,0:T(8,128)(2,1)S(1)} %bitcast.21, bf16[1344,512]{1,0:T(8,128)(2,1)S(1)} %bitcast.25), custom_call_target="tpu_custom_call" | custom-call | flops 704643072 | bytes 6537216 | tf_op jit(solution)/shard_map/pallas_call | solution.py:180
  82.1 0.1 collective-permute-start.15
  82.1 1.4 %collective-permute-done.15 = bf16[672,128]{1,0:T(8,128)(2,1)S(1)} collective-permute-done((bf16[672,128]{1,0:T(8,128)(2,1)S(1)}, bf16[672,128]{1,0:T(8,128)(2,1)S(1)}, u32[]{:S(2)}, u32[]{:S(2)}) %collective-permute-start.15) | collective-permute-done | bytes 172064 | tf_op jit(solution)/shard_map/ppermute | solution.py:211
  83.6 1.4 %collective-permute-start.16 = (bf16[672,128]{1,0:T(8,128)(2,1)S(1)}, bf16[672,128]{1,0:T(8,128)(2,1)S(1)}, u32[]{:S(2)}, u32[]{:S(2)}) collective-permute-start(bf16[672,128]{1,0:T(8,128)(2,1)S(1)} %add_convert_fusion), channel_id=1, source_target_pairs={{8,0},{16,8},{24,16},{0,24},{9,1},{17,9},{25,17},{1,25},{10,2},{18... | collective-permute-start | bytes 516104 | tf_op jit(solution)/shard_map/ppermute | solution.py:211
  85.0 0.7 collective-permute-start.17
  85.8 5.1 %collective-permute-done.16 = bf16[672,128]{1,0:T(8,128)(2,1)S(1)} collective-permute-done((bf16[672,128]{1,0:T(8,128)(2,1)S(1)}, bf16[672,128]{1,0:T(8,128)(2,1)S(1)}, u32[]{:S(2)}, u32[]{:S(2)}) %collective-permute-start.16) | collective-permute-done | bytes 172064 | tf_op jit(solution)/shard_map/ppermute | solution.py:211
  90.8 0.1 select_dynamic-update-slice_fusion.1
  90.9 2.8 %collective-permute-done.17 = bf16[672,128]{1,0:T(8,128)(2,1)S(1)} collective-permute-done((bf16[672,128]{1,0:T(8,128)(2,1)S(1)}, bf16[672,128]{1,0:T(8,128)(2,1)S(1)}, u32[]{:S(2)}, u32[]{:S(2)}) %collective-permute-start.17) | collective-permute-done | bytes 172064 | tf_op jit(solution)/shard_map/ppermute | solution.py:211
  93.8 0.1 select_dynamic-update-slice_fusion
  93.9 0.0 copy-start.11
  93.9 0.8 copy-done.11
  (27 shorter events, 0.3 us)
Async XLA Ops:
  1.0 15.6 %collective-permute-start.1 = (bf16[128,1024]{1,0:T(8,128)(2,1)S(1)}, bf16[128,1024]{1,0:T(8,128)(2,1)S(1)}, u32[]{:S(2)}, u32[]{:S(2)}) collective-permute-start(bf16[128,1024]{1,0:T(8,128)(2,1)S(1)} %pad_maximum_fusion.1.refs_2_), channel_id=1, source_target_pairs={{6,0},{0,2},{2,4},{4,6},{7,1},{1,3},{3,5},{5,7},{14,8},{8,10},{10,... | collective-permute-start | bytes 786440 | tf_op jit(solution)/shard_map/ppermute | solution.py:211
  4.1 12.5 %collective-permute-start = (bf16[48,1024]{1,0:T(8,128)(2,1)S(1)}, bf16[48,1024]{1,0:T(8,128)(2,1)S(1)}, u32[]{:S(2)}, u32[]{:S(2)}) collective-permute-start(bf16[48,1024]{1,0:T(8,128)(2,1)S(1)} %slice.28), channel_id=1, source_target_pairs={{4,0},{6,2},{0,4},{2,6},{5,1},{7,3},{1,5},{3,7},{12,8},{14,10},{8,... | collective-permute-start | bytes 294920 | tf_op jit(solution)/shard_map/ppermute | solution.py:211
  8.3 1.0 %copy-start.8 = (bf16[1,128,1024]{2,1,0:T(8,128)(2,1)S(1)}, bf16[1,128,1024]{2,1,0:T(8,128)(2,1)}, u32[]{:S(2)}) copy-start(bf16[1,128,1024]{2,1,0:T(8,128)(2,1)} %param.8) | copy-start | bytes 786436
  9.2 0.9 %copy-start.9 = (bf16[1,128,1024]{2,1,0:T(8,128)(2,1)S(1)}, bf16[1,128,1024]{2,1,0:T(8,128)(2,1)}, u32[]{:S(2)}) copy-start(bf16[1,128,1024]{2,1,0:T(8,128)(2,1)} %param.11) | copy-start | bytes 786436
  16.6 15.6 %copy-start = (bf16[1,1344,1024]{2,1,0:T(8,128)(2,1)S(1)}, bf16[1,1344,1024]{2,1,0:T(8,128)(2,1)}, u32[]{:S(2)}) copy-start(bf16[1,1344,1024]{2,1,0:T(8,128)(2,1)} %param.12) | copy-start | bytes 8257540
  18.9 10.4 %collective-permute-start.2 = (bf16[128,1024]{1,0:T(8,128)(2,1)S(1)}, bf16[128,1024]{1,0:T(8,128)(2,1)S(1)}, u32[]{:S(2)}, u32[]{:S(2)}) collective-permute-start(bf16[128,1024]{1,0:T(8,128)(2,1)S(1)} %get-tuple-element.34), channel_id=1, source_target_pairs={{2,0},{4,2},{6,4},{0,6},{3,1},{5,3},{7,5},{1,7},{10,8},{12,10},{14... | collective-permute-start | bytes 786440 | tf_op jit(solution)/shard_map/ppermute | solution.py:211
  20.5 8.7 %collective-permute-start.3 = (bf16[48,1024]{1,0:T(8,128)(2,1)S(1)}, bf16[48,1024]{1,0:T(8,128)(2,1)S(1)}, u32[]{:S(2)}, u32[]{:S(2)}) collective-permute-start(bf16[48,1024]{1,0:T(8,128)(2,1)S(1)} %get-tuple-element.35), channel_id=1, source_target_pairs={{4,0},{6,2},{0,4},{2,6},{5,1},{7,3},{1,5},{3,7},{12,8},{14,10},{8,... | collective-permute-start | bytes 294920 | tf_op jit(solution)/shard_map/ppermute | solution.py:211
  29.3 13.7 %collective-permute-start.6 = (bf16[128,2048]{1,0:T(8,128)(2,1)S(1)}, bf16[128,2048]{1,0:T(8,128)(2,1)}, u32[]{:S(2)}, u32[]{:S(2)}) collective-permute-start(bf16[128,2048]{1,0:T(8,128)(2,1)S(1)} %shard_map.84.refs_0_), channel_id=1, source_target_pairs={{0,2},{2,0},{4,6},{6,4},{1,3},{3,1},{5,7},{7,5},{8,10},{10,8},{12,... | collective-permute-start | bytes 1572872 | tf_op jit(solution)/shard_map/ppermute | solution.py:202
  30.8 12.2 %collective-permute-start.7 = (bf16[128,2048]{1,0:T(8,128)(2,1)S(1)}, bf16[128,2048]{1,0:T(8,128)(2,1)}, u32[]{:S(2)}, u32[]{:S(2)}) collective-permute-start(bf16[128,2048]{1,0:T(8,128)(2,1)S(1)} %shard_map.84.refs_0_), channel_id=1, source_target_pairs={{2,4},{4,2},{3,5},{5,3},{10,12},{12,10},{11,13},{13,11},{18,20},{2... | collective-permute-start | bytes 1572872 | tf_op jit(solution)/shard_map/ppermute | solution.py:202
  32.2 1.3 %copy-start.1 = (bf16[1,1344,512]{2,1,0:T(8,128)(2,1)S(1)}, bf16[1,1344,512]{2,1,0:T(8,128)(2,1)}, u32[]{:S(2)}) copy-start(bf16[1,1344,512]{2,1,0:T(8,128)(2,1)} %param.13) | copy-start | bytes 4128772
  33.6 1.3 %copy-start.4 = (bf16[1,1344,512]{2,1,0:T(8,128)(2,1)S(1)}, bf16[1,1344,512]{2,1,0:T(8,128)(2,1)}, u32[]{:S(2)}) copy-start(bf16[1,1344,512]{2,1,0:T(8,128)(2,1)} %param.14) | copy-start | bytes 4128772
  36.9 0.8 copy-start.10
  37.8 1.5 %collective-permute-start.4 = (bf16[672,128]{1,0:T(8,128)(2,1)S(1)}, bf16[672,128]{1,0:T(8,128)(2,1)}, u32[]{:S(2)}, u32[]{:S(2)}) collective-permute-start(bf16[672,128]{1,0:T(8,128)(2,1)S(1)} %get-tuple-element.37), channel_id=1, source_target_pairs={{1,0},{0,1},{3,2},{2,3},{5,4},{4,5},{7,6},{6,7},{9,8},{8,9},{11,10... | collective-permute-start | bytes 516104 | tf_op jit(solution)/shard_map/ppermute | solution.py:211
  43.0 20.1 %collective-permute-start.10 = (bf16[128,2048]{1,0:T(8,128)(2,1)}, bf16[128,2048]{1,0:T(8,128)(2,1)S(1)}, u32[]{:S(2)}, u32[]{:S(2)}) collective-permute-start(bf16[128,2048]{1,0:T(8,128)(2,1)} %collective-permute-done.6.refs_0_), channel_id=1, source_target_pairs={{2,4},{4,2},{3,5},{5,3},{10,12},{12,10},{11,13},{13,11},{18,20},{2... | collective-permute-start | bytes 1572872 | tf_op jit(solution)/shard_map/ppermute | solution.py:202
  43.7 19.5 %collective-permute-start.9 = (bf16[128,2048]{1,0:T(8,128)(2,1)}, bf16[128,2048]{1,0:T(8,128)(2,1)}, u32[]{:S(2)}, u32[]{:S(2)}) collective-permute-start(bf16[128,2048]{1,0:T(8,128)(2,1)} %collective-permute-done.7.refs_1_), channel_id=1, source_target_pairs={{0,2},{2,0},{4,6},{6,4},{1,3},{3,1},{5,7},{7,5},{8,10},{10,8},{12,... | collective-permute-start | bytes 1572872 | tf_op jit(solution)/shard_map/ppermute | solution.py:202
  52.2 1.3 %copy-start.2 = (bf16[1,1344,512]{2,1,0:T(8,128)(2,1)S(1)}, bf16[1,1344,512]{2,1,0:T(8,128)(2,1)}, u32[]{:S(2)}) copy-start(bf16[1,1344,512]{2,1,0:T(8,128)(2,1)} %param.13) | copy-start | bytes 4128772
  53.6 1.3 %copy-start.5 = (bf16[1,1344,512]{2,1,0:T(8,128)(2,1)S(1)}, bf16[1,1344,512]{2,1,0:T(8,128)(2,1)}, u32[]{:S(2)}) copy-start(bf16[1,1344,512]{2,1,0:T(8,128)(2,1)} %param.14) | copy-start | bytes 4128772
  58.3 1.1 %copy-start.7 = (f32[1344,256]{1,0:T(8,128)}, f32[1344,256]{1,0:T(8,128)S(1)}, u32[]{:S(2)}) copy-start(f32[1344,256]{1,0:T(8,128)S(1)} %get-tuple-element.40) | copy-start | bytes 4128772
  60.1 3.0 %collective-permute-start.11 = (bf16[672,128]{1,0:T(8,128)(2,1)}, bf16[672,128]{1,0:T(8,128)(2,1)S(1)}, u32[]{:S(2)}, u32[]{:S(2)}) collective-permute-start(bf16[672,128]{1,0:T(8,128)(2,1)} %get-tuple-element.54), channel_id=1, source_target_pairs={{1,0},{0,1},{3,2},{2,3},{5,4},{4,5},{7,6},{6,7},{9,8},{8,9},{11,10... | collective-permute-start | bytes 516104 | tf_op jit(solution)/shard_map/ppermute | solution.py:211
  60.1 3.1 %collective-permute-start.8 = (bf16[672,128]{1,0:T(8,128)(2,1)}, bf16[672,128]{1,0:T(8,128)(2,1)}, u32[]{:S(2)}, u32[]{:S(2)}) collective-permute-start(bf16[672,128]{1,0:T(8,128)(2,1)} %get-tuple-element.53), channel_id=1, source_target_pairs={{1,0},{0,1},{3,2},{2,3},{5,4},{4,5},{7,6},{6,7},{9,8},{8,9},{11,10... | collective-permute-start | bytes 516104 | tf_op jit(solution)/shard_map/ppermute | solution.py:211
  60.6 9.3 %collective-permute-start.5 = (bf16[672,128]{1,0:T(8,128)(2,1)}, bf16[672,128]{1,0:T(8,128)(2,1)S(1)}, u32[]{:S(2)}, u32[]{:S(2)}) collective-permute-start(bf16[672,128]{1,0:T(8,128)(2,1)} %add_convert_fusion.2), channel_id=1, source_target_pairs={{8,0},{16,8},{24,16},{0,24},{9,1},{17,9},{25,17},{1,25},{10,2},{18... | collective-permute-start | bytes 516104 | tf_op jit(solution)/shard_map/ppermute | solution.py:211
  63.1 1.5 %copy-start.12 = (bf16[128,2048]{1,0:T(8,128)(2,1)}, bf16[128,2048]{1,0:T(8,128)(2,1)S(1)}, u32[]{:S(2)}) copy-start(bf16[128,2048]{1,0:T(8,128)(2,1)S(1)} %collective-permute-done.10) | copy-start | bytes 1572868
  63.2 11.3 %copy-start.6 = (bf16[1,1344,512]{2,1,0:T(8,128)(2,1)S(1)}, bf16[1,1344,512]{2,1,0:T(8,128)(2,1)}, u32[]{:S(2)}) copy-start(bf16[1,1344,512]{2,1,0:T(8,128)(2,1)} %param.14) | copy-start | bytes 4128772
  64.5 10.0 %copy-start.3 = (bf16[1,1344,512]{2,1,0:T(8,128)(2,1)S(1)}, bf16[1,1344,512]{2,1,0:T(8,128)(2,1)}, u32[]{:S(2)}) copy-start(bf16[1,1344,512]{2,1,0:T(8,128)(2,1)} %param.13) | copy-start | bytes 4128772
  64.6 9.9 %collective-permute-start.12 = (bf16[672,256]{1,0:T(8,128)(2,1)S(1)}, bf16[672,256]{1,0:T(8,128)(2,1)S(1)}, u32[]{:S(2)}, u32[]{:S(2)}) collective-permute-start(bf16[672,256]{1,0:T(8,128)(2,1)S(1)} %pad_maximum_fusion), channel_id=1, source_target_pairs={{8,0},{16,8},{24,16},{0,24},{9,1},{17,9},{25,17},{1,25},{10,2},{18... | collective-permute-start | bytes 1032200 | tf_op jit(solution)/shard_map/ppermute | solution.py:211
  67.1 12.9 %collective-permute-start.13 = (bf16[128,2048]{1,0:T(8,128)(2,1)}, bf16[128,2048]{1,0:T(8,128)(2,1)S(1)}, u32[]{:S(2)}, u32[]{:S(2)}) collective-permute-start(bf16[128,2048]{1,0:T(8,128)(2,1)} %copy-done.12), channel_id=1, source_target_pairs={{0,2},{2,0},{4,6},{6,4},{1,3},{3,1},{5,7},{7,5},{8,10},{10,8},{12,... | collective-permute-start | bytes 1572872 | tf_op jit(solution)/shard_map/ppermute | solution.py:202
  70.0 6.5 %copy-start.13 = (bf16[672,128]{1,0:T(8,128)(2,1)}, bf16[672,128]{1,0:T(8,128)(2,1)S(1)}, u32[]{:S(2)}) copy-start(bf16[672,128]{1,0:T(8,128)(2,1)S(1)} %collective-permute-done.5) | copy-start | bytes 516100
  76.5 1.5 %collective-permute-start.14 = (bf16[672,128]{1,0:T(8,128)(2,1)S(1)}, bf16[672,128]{1,0:T(8,128)(2,1)S(1)}, u32[]{:S(2)}, u32[]{:S(2)}) collective-permute-start(bf16[672,128]{1,0:T(8,128)(2,1)S(1)} %get-tuple-element.46), channel_id=1, source_target_pairs={{1,0},{0,1},{3,2},{2,3},{5,4},{4,5},{7,6},{6,7},{9,8},{8,9},{11,10... | collective-permute-start | bytes 516104 | tf_op jit(solution)/shard_map/ppermute | solution.py:211
  82.1 2.9 %copy-start.14 = (bf16[672,128]{1,0:T(8,128)(2,1)S(1)}, bf16[672,128]{1,0:T(8,128)(2,1)}, u32[]{:S(2)}) copy-start(bf16[672,128]{1,0:T(8,128)(2,1)} %copy-done.13) | copy-start | bytes 516100
  82.1 1.5 %collective-permute-start.15 = (bf16[672,128]{1,0:T(8,128)(2,1)S(1)}, bf16[672,128]{1,0:T(8,128)(2,1)S(1)}, u32[]{:S(2)}, u32[]{:S(2)}) collective-permute-start(bf16[672,128]{1,0:T(8,128)(2,1)S(1)} %get-tuple-element.50), channel_id=1, source_target_pairs={{1,0},{0,1},{3,2},{2,3},{5,4},{4,5},{7,6},{6,7},{9,8},{8,9},{11,10... | collective-permute-start | bytes 516104 | tf_op jit(solution)/shard_map/ppermute | solution.py:211
  83.6 7.3 %collective-permute-start.16 = (bf16[672,128]{1,0:T(8,128)(2,1)S(1)}, bf16[672,128]{1,0:T(8,128)(2,1)S(1)}, u32[]{:S(2)}, u32[]{:S(2)}) collective-permute-start(bf16[672,128]{1,0:T(8,128)(2,1)S(1)} %add_convert_fusion), channel_id=1, source_target_pairs={{8,0},{16,8},{24,16},{0,24},{9,1},{17,9},{25,17},{1,25},{10,2},{18... | collective-permute-start | bytes 516104 | tf_op jit(solution)/shard_map/ppermute | solution.py:211
  85.0 8.7 %collective-permute-start.17 = (bf16[672,128]{1,0:T(8,128)(2,1)S(1)}, bf16[672,128]{1,0:T(8,128)(2,1)S(1)}, u32[]{:S(2)}, u32[]{:S(2)}) collective-permute-start(bf16[672,128]{1,0:T(8,128)(2,1)S(1)} %add_convert_fusion.1), channel_id=1, source_target_pairs={{8,0},{16,8},{24,16},{0,24},{9,1},{17,9},{25,17},{1,25},{10,2},{18... | collective-permute-start | bytes 516104 | tf_op jit(solution)/shard_map/ppermute | solution.py:211
  93.9 0.8 copy-start.11

commit v6 on v5

--- a/solution.py
+++ b/solution.py
@@ -143,8 +143,10 @@
 
 
 def project_kernel(pieces, tile, core_ref, *refs):
-    flat_refs, (query_weight, key_weight, value_weight) = refs[: sum(pieces)], refs[-6:-3]
-    full_ref, give_ref, block_ref = refs[-3:]
+    count = len(pieces)
+    flat_refs, (query_weight, key_weight, value_weight) = refs[: sum(pieces)], refs[sum(pieces) :][:3]
+    keep_refs, give_refs = refs[-2 * count - 2 : -count - 2], refs[-count - 2 : -2]
+    full_ref, block_ref = refs[-2:]
     row, at = 0, 0
     for count in pieces:
         column = 0
@@ -165,27 +167,33 @@
         return carry
 
     lax.fori_loop(0, full_ref.shape[0] // tile, step, 0)
-    half = give_ref.shape[0]
-    other = pl.multiple_of((1 - core_ref[0]) * half, 8)
-    give_ref[...] = full_ref[pl.ds(other, half), :].astype(jnp.bfloat16)
+    half, rows = give_refs[0].shape
+    own = pl.ds(pl.multiple_of(core_ref[0] * half, 8), half)
+    other = pl.ds(pl.multiple_of((1 - core_ref[0]) * half, 8), half)
+    for i, (keep_ref, give_ref) in enumerate(zip(keep_refs, give_refs)):
+        cols = slice(i * rows, (i + 1) * rows)
+        keep_ref[...] = full_ref[own, cols]
+        give_ref[...] = full_ref[other, cols].astype(jnp.bfloat16)
 
 
 def project(blocks, weights, core):
     width = weights[0].shape[0]
     rows = sum(block[0].shape[0] for block in blocks)
+    half = (width // 2, rows // len(blocks))
     cols = sum(weight.shape[1] for weight in weights)
     tile = max(t for t in range(16, 449, 16) if width % t == 0)
     flat = [piece for block in blocks for piece in block]
     whole = pl.BlockSpec(memory_space=pltpu.VMEM)
     return pl.pallas_call(
         functools.partial(project_kernel, [len(block) for block in blocks], tile),
-        out_shape=[
-            jax.ShapeDtypeStruct((width, rows), jnp.float32),
-            jax.ShapeDtypeStruct((width // 2, rows), jnp.bfloat16),
+        out_shape=[jax.ShapeDtypeStruct(half, jnp.float32)] * len(blocks)
+        + [jax.ShapeDtypeStruct(half, jnp.bfloat16)] * len(blocks),
+        in_specs=[pl.BlockSpec(memory_space=pltpu.SMEM)] + [whole] * (len(flat) + 3),
+        out_specs=[whole] * (2 * len(blocks)),
+        scratch_shapes=[
+            pltpu.VMEM((width, rows), jnp.float32),
+            pltpu.VMEM((rows, cols), jnp.bfloat16),
         ],
-        in_specs=[pl.BlockSpec(memory_space=pltpu.SMEM)] + [whole] * (len(flat) + 3),
-        out_specs=[whole] * 2,
-        scratch_shapes=[pltpu.VMEM((rows, cols), jnp.bfloat16)],
         compiler_params=pltpu.CompilerParams(vmem_limit_bytes=8 * 1024 * 1024),
         cost_estimate=pl.CostEstimate(
             flops=2 * rows * width * cols,
@@ -193,6 +201,11 @@
             transcendentals=0,
         ),
     )(core, *flat, *weights)
+
+
+def moved(block, axis, by):
+    size = lax.axis_size(axis)
+    return lax.ppermute(block, axis, [(i, i + by) for i in range(size) if 0 <= i + by < size])
 
 
 def swapped(block, axis, first):
@@ -234,7 +247,7 @@
     kv = lax.optimization_barrier(
         jnp.concatenate([key_row_matrix[0], value_row_matrix[0]], axis=1)
     )
-    halos = [passed_along(kv[rows - size :], "seq", d) for d, size in enumerate(halo_rows, 1)]
+    halos = [moved(kv[rows - size :], "seq", d) for d, size in enumerate(halo_rows, 1)]
     reach = sum(halo_rows)
     first_row = place * rows
     key_docs = lax.dynamic_slice_in_dim(
@@ -255,21 +268,19 @@
     grad_query, grad_kv, *grad_halos = attention_backward(
         query_stack, grad_stack, kv, bias, halos[::-1]
     )
-    returned = [passed_along(part, "seq", -d) for d, part in enumerate(grad_halos[::-1], 1)]
+    returned = [moved(part, "seq", -d) for d, part in enumerate(grad_halos[::-1], 1)]
     own = join(grad_query, grad_kv, returned)
     weights = (w_query[0], key_weight[0], value_weight[0])
     core = lax.axis_index("mp").astype(jnp.int32)
 
     def halves_summed(blocks, *late):
-        full, give = project([(block,) for block in blocks], weights, core[None])
-        half = give.shape[0]
-        keep = lax.dynamic_slice_in_dim(full, core * half, half, 0)
+        halves = project([(block,) for block in blocks], weights, core[None])
         sums = []
-        for i in range(0, give.shape[1], rows):
-            got = passed_along(give[:, i : i + rows], "mp", 1)
+        for keep, give in zip(halves[: len(blocks)], halves[len(blocks) :]):
+            got = passed_along(give, "mp", 1)
             if late:
                 (got,) = after((got,), *late)
-            sums.append((keep[:, i : i + rows] + got.astype(jnp.float32)).astype(jnp.bfloat16))
+            sums.append((keep + got.astype(jnp.float32)).astype(jnp.bfloat16))
         return jnp.concatenate(sums, axis=1)
 
     even = place % 2 == 0
@@ -280,14 +291,17 @@
         last = step == shards - 1 and shards % 2 == 0
         came_second = came_first if last else swapped(by_second, "seq", 1)
         if step > 1:
-            waiting = after(waiting, total, *(results[-2:] if 2 * step > shards else ()))
-        total = halves_summed(waiting, *((came_first, came_second) if step > 1 else ()))
+            waiting = after(waiting, total, *results[-2:-1])
+        late = (came_second, came_first) if step > 1 else ()
+        if step > 2:
+            late += (results[-1],)
+        total = halves_summed(waiting, *late)
         results.append(passed_along(total, "section", -1))
         by_first, by_second = came_second, came_first
         if last:
             waiting = [came_first]
         elif 2 * step < shards:
-            waiting = [came_first, came_second]
+            waiting = [came_second, came_first]
         else:
             waiting = [jnp.where(even == (place >= step), came_second, came_first)]
     if shards > 1:
@@ -297,7 +311,7 @@
         if block.shape[1] == rows:
             results[step] = [block]
         else:
-            first, second = block[:, :rows], block[:, rows:]
+            second, first = block[:, :rows], block[:, rows:]
             results[step] = [jnp.where(even, second, first), jnp.where(even, first, second)]
     upstream = jnp.zeros((results[0][0].shape[0], tokens), jnp.bfloat16)
     for s in range(shards):

time: 95.2 us -> 90.1 us (0.946)
  local copies, waits for them, and re-layouts: 12.4 us -> 7.02 us
  waiting for transfers between devices: 35.9 us -> 32.5 us
  starting transfers between devices: 29 us -> 31.9 us
    ppermute x13 -> x9, waiting for transfers between devices: 31.8 us -> 10.7 us  [passed_along(): lax.ppermute(block, axis, [((i - distance) % len(devices), i) for i in de...]
    ppermute x0 -> x4, waiting for transfers between devices: none -> 13.3 us  [moved(): lax.ppermute(block, axis, [(i, i + by) for i in range(size) if 0 <= i + b...]
    ppermute x0 -> x4, starting transfers between devices: none -> 12 us  [moved(): lax.ppermute(block, axis, [(i, i + by) for i in range(size) if 0 <= i + b...]
    ppermute x13 -> x9, starting transfers between devices: 15.1 us -> 7.79 us  [passed_along(): lax.ppermute(block, axis, [((i - distance) % len(devices), i) for i in de...]
    unnamed x30 -> x24, local copies, waits for them, and re-layouts: 10.1 us -> 5.45 us
    ppermute x5, waiting for transfers between devices: 4.12 us -> 8.44 us  [swapped(): return lax.ppermute(block, axis, pairs)]
    ppermute x5, starting transfers between devices: 13.9 us -> 12.1 us  [swapped(): return lax.ppermute(block, axis, pairs)]
    convert_element_type x4 -> x5, other arithmetic: 3.14 us -> 2.87 us  [halves_summed(): sums.append((keep + got.astype(jnp.float32)).astype(jnp.bfloat16))]
  transfers between devices with their start and end apart: 18 -> 18, of which waited for: 11 -> 8; matrix products, arithmetic and copies ran while one was open for 7% -> 6% of each run, Pallas kernels for 8% -> 9%
where the time goes in v6:
time: 90.1 us; the launch traced here: 89.6 us
  waiting for transfers between devices  32.5 us (36%)
  starting transfers between devices  31.9 us (35%)
  Pallas kernels  12.6 us (14%)
  local copies, waits for them, and re-layouts  7.02 us (8%)
  other arithmetic  5.3 us (6%)
    ppermute x4, waiting for transfers between devices, moved(): lax.ppermute(block, axis, [(i, i + by) for i in range(size) if 0 <= i + b...  13.3 us
    ppermute x5, starting transfers between devices, swapped(): return lax.ppermute(block, axis, pairs)  12.1 us
    ppermute x4, starting transfers between devices, moved(): lax.ppermute(block, axis, [(i, i + by) for i in range(size) if 0 <= i + b...  12 us
    ppermute x9, waiting for transfers between devices, passed_along(): lax.ppermute(block, axis, [((i - distance) % len(devices), i) for i in de...  10.7 us
    pallas_call x4, Pallas kernels, project(): pl.pallas_call(functools.partial(project_kernel, [len(block) for block in...  10.1 us
    ppermute x5, waiting for transfers between devices, swapped(): return lax.ppermute(block, axis, pairs)  8.44 us
    ppermute x9, starting transfers between devices, passed_along(): lax.ppermute(block, axis, [((i - distance) % len(devices), i) for i in de...  7.79 us
    unnamed x24, local copies, waits for them, and re-layouts  5.45 us
  transfers between devices with their start and end apart: 18, of which 8 were waited for; matrix products, arithmetic and copies ran while one was open for 6% of the time, Pallas kernels for 9%

profile of v6, /device:TPU:0, one launch (start us, length us, event | category | flops | bytes accessed | tf_op | source)
XLA Modules:
  0.0 89.6 jit_solution(11028312993963933680)
XLA Ops:
  0.0 1.0 %pad_maximum_fusion.1.refs_2_ = bf16[128,1024]{1,0:T(8,128)(2,1)S(1)} fusion(bf16[128,512]{1,0:T(8,128)(2,1)} %bitcast.28, bf16[128,512]{1,0:T(8,128)(2,1)} %bitcast.29), kind=kLoop, calls=%fused_computation.7 | loop fusion | flops 524288 | bytes 524288 | tf_op jit(solution)/shard_map/concatenate | solution.py:248
  1.0 4.9 %collective-permute-start.1 = (bf16[128,1024]{1,0:T(8,128)(2,1)S(1)}, bf16[128,1024]{1,0:T(8,128)(2,1)S(1)}, u32[]{:S(2)}, u32[]{:S(2)}) collective-permute-start(bf16[128,1024]{1,0:T(8,128)(2,1)S(1)} %pad_maximum_fusion.1.refs_2_), channel_id=1, source_target_pairs={{0,2},{2,4},{4,6},{1,3},{3,5},{5,7},{8,10},{10,12},{12,14},{9,11},... | collective-permute-start | bytes 786440 | tf_op jit(solution)/shard_map/ppermute | solution.py:208
  6.0 4.5 %collective-permute-start = (bf16[48,1024]{1,0:T(8,128)(2,1)S(1)}, bf16[48,1024]{1,0:T(8,128)(2,1)S(1)}, u32[]{:S(2)}, u32[]{:S(2)}) collective-permute-start(bf16[48,1024]{1,0:T(8,128)(2,1)S(1)} %slice.12), channel_id=1, source_target_pairs={{0,4},{2,6},{1,5},{3,7},{8,12},{10,14},{9,13},{11,15},{16,20},{18,... | collective-permute-start | bytes 294920 | tf_op jit(solution)/shard_map/ppermute | solution.py:208
  10.5 0.8 pad_dynamic-slice_fusion
  11.2 0.7 fusion.5
  11.9 0.1 fusion.4.refs_3_
  12.0 0.0 copy-start.7
  12.0 0.9 %copy-done.7 = bf16[1,128,1024]{2,1,0:T(8,128)(2,1)S(1)} copy-done((bf16[1,128,1024]{2,1,0:T(8,128)(2,1)S(1)}, bf16[1,128,1024]{2,1,0:T(8,128)(2,1)}, u32[]{:S(2)}) %copy-start.7) | copy-done | bytes 262168
  13.0 0.9 %copy-done.8 = bf16[1,128,1024]{2,1,0:T(8,128)(2,1)S(1)} copy-done((bf16[1,128,1024]{2,1,0:T(8,128)(2,1)S(1)}, bf16[1,128,1024]{2,1,0:T(8,128)(2,1)}, u32[]{:S(2)}) %copy-start.8) | copy-done | bytes 262168
  13.9 0.1 shard_map.82
  14.0 0.0 collective-permute-done.refs_4_
  14.0 0.0 collective-permute-done.1.refs_5_
  14.0 0.0 copy-start
  14.0 2.2 %shard_map.83 = (bf16[128,1024]{1,0:T(8,128)(2,1)S(1)}, f32[128,1024]{1,0:T(8,128)S(1)}, bf16[48,1024]{1,0:T(8,128)(2,1)S(1)}, bf16[128,1024]{1,0:T(8,128)(2,1)S(1)}) custom-call(bf16[1024,128]{1,0:T(8,128)(2,1)S(1)} %get-tuple-element.32.refs_0_, bf16[1024,128]{1,0:T(8,128)(2,1)S(1)} %get-tuple-element.33.refs_1_, ...), custom_call_target="tpu_custom_call" | custom-call | flops 478150656 | bytes 1048576 | tf_op jit(solution)/shard_map/pallas_call | solution.py:100
  16.3 1.3 %collective-permute-start.2 = (bf16[128,1024]{1,0:T(8,128)(2,1)S(1)}, bf16[128,1024]{1,0:T(8,128)(2,1)S(1)}, u32[]{:S(2)}, u32[]{:S(2)}) collective-permute-start(bf16[128,1024]{1,0:T(8,128)(2,1)S(1)} %get-tuple-element.36), channel_id=1, source_target_pairs={{2,0},{4,2},{6,4},{3,1},{5,3},{7,5},{10,8},{12,10},{14,12},{11,9},... | collective-permute-start | bytes 786440 | tf_op jit(solution)/shard_map/ppermute | solution.py:208
  17.6 1.3 %collective-permute-start.3 = (bf16[48,1024]{1,0:T(8,128)(2,1)S(1)}, bf16[48,1024]{1,0:T(8,128)(2,1)S(1)}, u32[]{:S(2)}, u32[]{:S(2)}) collective-permute-start(bf16[48,1024]{1,0:T(8,128)(2,1)S(1)} %get-tuple-element.37), channel_id=1, source_target_pairs={{4,0},{6,2},{5,1},{7,3},{12,8},{14,10},{13,9},{15,11},{20,16},{22,... | collective-permute-start | bytes 294920 | tf_op jit(solution)/shard_map/ppermute | solution.py:208
  18.9 13.3 %collective-permute-done.3.refs_1_ = bf16[48,1024]{1,0:T(8,128)(2,1)S(1)} collective-permute-done((bf16[48,1024]{1,0:T(8,128)(2,1)S(1)}, bf16[48,1024]{1,0:T(8,128)(2,1)S(1)}, u32[]{:S(2)}, u32[]{:S(2)}) %collective-permute-start.3) | collective-permute-done | bytes 98336 | tf_op jit(solution)/shard_map/ppermute | solution.py:208
  32.2 0.0 collective-permute-done.2.refs_0_
  32.2 0.1 shard_map.84.refs_0_
  32.3 1.5 %collective-permute-start.6 = (bf16[128,2048]{1,0:T(8,128)(2,1)S(1)}, bf16[128,2048]{1,0:T(8,128)(2,1)}, u32[]{:S(2)}, u32[]{:S(2)}) collective-permute-start(bf16[128,2048]{1,0:T(8,128)(2,1)S(1)} %shard_map.84.refs_0_), channel_id=1, source_target_pairs={{2,4},{4,2},{3,5},{5,3},{10,12},{12,10},{11,13},{13,11},{18,20},{2... | collective-permute-start | bytes 1572872 | tf_op jit(solution)/shard_map/ppermute | solution.py:215
  33.8 0.6 collective-permute-start.7
  34.4 1.3 %copy-done.1 = bf16[1,1344,512]{2,1,0:T(8,128)(2,1)S(1)} copy-done((bf16[1,1344,512]{2,1,0:T(8,128)(2,1)S(1)}, bf16[1,1344,512]{2,1,0:T(8,128)(2,1)}, u32[]{:S(2)}) %copy-start.1) | copy-done | bytes 1376280
  35.8 1.3 %copy-done.4 = bf16[1,1344,512]{2,1,0:T(8,128)(2,1)S(1)} copy-done((bf16[1,1344,512]{2,1,0:T(8,128)(2,1)S(1)}, bf16[1,1344,512]{2,1,0:T(8,128)(2,1)}, u32[]{:S(2)}) %copy-start.4) | copy-done | bytes 1376280
  37.1 2.0 %shard_map.85 = (f32[672,128]{1,0:T(8,128)S(1)}, bf16[672,128]{1,0:T(8,128)(2,1)S(1)}) custom-call(s32[1]{0:T(128)} %bitcast.core_ref, bf16[128,2048]{1,0:T(8,128)(2,1)S(1)} %shard_map.84.refs_0_, bf16[1344,1024]{1,0:T(8,128)(2,1)S(1)} %bitcast.14, bf16[1344,512]{1,0:T(8,128)(2,1)S(1)} %bitcast.18, bf16[1344,512]{1,0:T(8,128)(2,1)S(1)} %bitcast.22), custom_call_target="tpu_custom_call" | custom-call | flops 704643072 | bytes 6537216 | tf_op jit(solution)/shard_map/pallas_call | solution.py:187
  39.1 0.1 collective-permute-start.4
  39.2 0.0 collective-permute-done.6.refs_0_
  39.2 5.7 %collective-permute-start.10 = (bf16[128,2048]{1,0:T(8,128)(2,1)}, bf16[128,2048]{1,0:T(8,128)(2,1)}, u32[]{:S(2)}, u32[]{:S(2)}) collective-permute-start(bf16[128,2048]{1,0:T(8,128)(2,1)} %collective-permute-done.6.refs_0_), channel_id=1, source_target_pairs={{0,2},{2,0},{4,6},{6,4},{1,3},{3,1},{5,7},{7,5},{8,10},{10,8},{12,... | collective-permute-start | bytes 1572872 | tf_op jit(solution)/shard_map/ppermute | solution.py:215
  45.0 1.2 %collective-permute-done.7.refs_1_ = bf16[128,2048]{1,0:T(8,128)(2,1)} collective-permute-done((bf16[128,2048]{1,0:T(8,128)(2,1)S(1)}, bf16[128,2048]{1,0:T(8,128)(2,1)}, u32[]{:S(2)}, u32[]{:S(2)}) %collective-permute-start.7) | collective-permute-done | bytes 524320 | tf_op jit(solution)/shard_map/ppermute | solution.py:215
  46.1 1.4 %collective-permute-start.9 = (bf16[128,2048]{1,0:T(8,128)(2,1)}, bf16[128,2048]{1,0:T(8,128)(2,1)}, u32[]{:S(2)}, u32[]{:S(2)}) collective-permute-start(bf16[128,2048]{1,0:T(8,128)(2,1)} %collective-permute-done.7.refs_1_), channel_id=1, source_target_pairs={{2,4},{4,2},{3,5},{5,3},{10,12},{12,10},{11,13},{13,11},{18,20},{2... | collective-permute-start | bytes 1572872 | tf_op jit(solution)/shard_map/ppermute | solution.py:215
  47.6 0.0 collective-permute-done.4
  47.6 0.7 add_convert_fusion.4
  48.3 4.1 %shard_map.86 = (f32[672,128]{1,0:T(8,128)S(1)}, f32[672,128]{1,0:T(8,128)S(1)}, bf16[672,128]{1,0:T(8,128)(2,1)}, bf16[672,128]{1,0:T(8,128)(2,1)}) custom-call(s32[1]{0:T(128)} %bitcast.core_ref, bf16[128,2048]{1,0:T(8,128)(2,1)} %collective-permute-done.6.refs_0_, bf16[128,2048]{1,0:T(8,128)(2,1)} %collective-permute-done.7.refs_1_, ...), custom_call_target="tpu_custom_call" | custom-call | flops 1409286144 | bytes 7569408 | tf_op jit(solution)/shard_map/pallas_call | solution.py:187
  52.4 0.5 collective-permute-start.11
  52.9 2.5 %collective-permute-start.5 = (bf16[672,128]{1,0:T(8,128)(2,1)}, bf16[672,128]{1,0:T(8,128)(2,1)S(1)}, u32[]{:S(2)}, u32[]{:S(2)}) collective-permute-start(bf16[672,128]{1,0:T(8,128)(2,1)} %add_convert_fusion.4), channel_id=1, source_target_pairs={{8,0},{16,8},{24,16},{0,24},{9,1},{17,9},{25,17},{1,25},{10,2},{18... | collective-permute-start | bytes 516104 | tf_op jit(solution)/shard_map/ppermute | solution.py:224
  55.4 0.0 collective-permute-done.8
  55.4 0.2 collective-permute-done.10
  55.7 0.0 collective-permute-done.9
  55.7 0.0 collective-permute-done.11
  55.7 1.0 %add_convert_fusion.3 = bf16[672,128]{1,0:T(8,128)(2,1)S(1)} fusion(f32[672,128]{1,0:T(8,128)S(1)} %get-tuple-element.42, bf16[672,128]{1,0:T(8,128)(2,1)} %collective-permute-done.8), kind=kLoop, calls=%fused_computation.5 | loop fusion | flops 258048 | bytes 688128 | tf_op jit(solution)/shard_map/convert_element_type | solution.py:283
  56.6 0.0 copy-start.3
  56.6 0.0 copy-start.6
  56.6 1.1 %add_convert_fusion.2 = bf16[672,128]{1,0:T(8,128)(2,1)S(1)} fusion(f32[672,128]{1,0:T(8,128)S(1)} %get-tuple-element.45, bf16[672,128]{1,0:T(8,128)(2,1)} %collective-permute-done.11), kind=kLoop, calls=%fused_computation.4 | loop fusion | flops 258048 | bytes 688128 | tf_op jit(solution)/shard_map/convert_element_type | solution.py:283
  57.8 2.5 %collective-permute-start.12 = (bf16[672,256]{1,0:T(8,128)(2,1)S(1)}, bf16[672,256]{1,0:T(8,128)(2,1)S(1)}, u32[]{:S(2)}, u32[]{:S(2)}) collective-permute-start(bf16[672,256]{1,0:T(8,128)(2,1)S(1)} %pad_maximum_fusion), channel_id=1, source_target_pairs={{8,0},{16,8},{24,16},{0,24},{9,1},{17,9},{25,17},{1,25},{10,2},{18... | collective-permute-start | bytes 1032200 | tf_op jit(solution)/shard_map/ppermute | solution.py:224
  60.3 2.9 %collective-permute-start.13 = (bf16[128,2048]{1,0:T(8,128)(2,1)}, bf16[128,2048]{1,0:T(8,128)(2,1)S(1)}, u32[]{:S(2)}, u32[]{:S(2)}) collective-permute-start(bf16[128,2048]{1,0:T(8,128)(2,1)} %collective-permute-done.9), channel_id=1, source_target_pairs={{0,2},{2,0},{4,6},{6,4},{1,3},{3,1},{5,7},{7,5},{8,10},{10,8},{12,... | collective-permute-start | bytes 1572872 | tf_op jit(solution)/shard_map/ppermute | solution.py:215
  63.2 1.1 %broadcast_select_fusion.refs_0_ = bf16[128,2048]{1,0:T(8,128)(2,1)S(1)} fusion(bf16[128,2048]{1,0:T(8,128)(2,1)} %collective-permute-done.9, bf16[128,2048]{1,0:T(8,128)(2,1)} %collective-permute-done.10, pred[]{:T(512)S(6)} %eq.32), kind=kLoop, calls=%fused_computation | loop fusion | flops 262144 | bytes 1572865 | tf_op jit(solution)/shard_map/jit(_where)/select_n | solution.py:306
  64.3 0.0 copy-start.10
  64.3 2.0 %shard_map.87 = (f32[672,128]{1,0:T(8,128)S(1)}, bf16[672,128]{1,0:T(8,128)(2,1)S(1)}) custom-call(s32[1]{0:T(128)} %bitcast.core_ref, bf16[128,2048]{1,0:T(8,128)(2,1)S(1)} %broadcast_select_fusion.refs_0_, bf16[1344,1024]{1,0:T(8,128)(2,1)S(1)} %bitcast.16, bf16[1344,512]{1,0:T(8,128)(2,1)S(1)} %bitcast.20, bf16[1344,512]{1,0:T(8,128)(2,1)S(1)} %bitcast.24), custom_call_target="tpu_custom_call" | custom-call | flops 704643072 | bytes 6537216 | tf_op jit(solution)/shard_map/pallas_call | solution.py:187
  66.4 0.1 collective-permute-start.14
  66.4 1.4 %collective-permute-done.14 = bf16[672,128]{1,0:T(8,128)(2,1)S(1)} collective-permute-done((bf16[672,128]{1,0:T(8,128)(2,1)S(1)}, bf16[672,128]{1,0:T(8,128)(2,1)S(1)}, u32[]{:S(2)}, u32[]{:S(2)}) %collective-permute-start.14) | collective-permute-done | bytes 172064 | tf_op jit(solution)/shard_map/ppermute | solution.py:224
  67.8 7.0 %collective-permute-done.13.refs_0_ = bf16[128,2048]{1,0:T(8,128)(2,1)S(1)} collective-permute-done((bf16[128,2048]{1,0:T(8,128)(2,1)}, bf16[128,2048]{1,0:T(8,128)(2,1)S(1)}, u32[]{:S(2)}, u32[]{:S(2)}) %collective-permute-start.13) | collective-permute-done | bytes 524320 | tf_op jit(solution)/shard_map/ppermute | solution.py:215
  74.8 0.1 add_convert_fusion.1
  74.9 2.0 %shard_map.88 = (f32[672,128]{1,0:T(8,128)S(1)}, bf16[672,128]{1,0:T(8,128)(2,1)S(1)}) custom-call(s32[1]{0:T(128)} %bitcast.core_ref, bf16[128,2048]{1,0:T(8,128)(2,1)S(1)} %collective-permute-done.13.refs_0_, bf16[1344,1024]{1,0:T(8,128)(2,1)S(1)} %bitcast.17, bf16[1344,512]{1,0:T(8,128)(2,1)S(1)} %bitcast.21, bf16[1344,512]{1,0:T(8,128)(2,1)S(1)} %bitcast.25), custom_call_target="tpu_custom_call" | custom-call | flops 704643072 | bytes 6537216 | tf_op jit(solution)/shard_map/pallas_call | solution.py:187
  76.9 0.0 copy-start.11
  76.9 0.1 collective-permute-start.15
  77.0 1.4 %collective-permute-done.15 = bf16[672,128]{1,0:T(8,128)(2,1)S(1)} collective-permute-done((bf16[672,128]{1,0:T(8,128)(2,1)S(1)}, bf16[672,128]{1,0:T(8,128)(2,1)S(1)}, u32[]{:S(2)}, u32[]{:S(2)}) %collective-permute-start.15) | collective-permute-done | bytes 172064 | tf_op jit(solution)/shard_map/ppermute | solution.py:224
  78.4 0.1 add_convert_fusion
  78.5 0.6 collective-permute-start.16
  79.2 1.5 %collective-permute-start.17 = (bf16[672,128]{1,0:T(8,128)(2,1)S(1)}, bf16[672,128]{1,0:T(8,128)(2,1)S(1)}, u32[]{:S(2)}, u32[]{:S(2)}) collective-permute-start(bf16[672,128]{1,0:T(8,128)(2,1)S(1)} %add_convert_fusion.1), channel_id=1, source_target_pairs={{8,0},{16,8},{24,16},{0,24},{9,1},{17,9},{25,17},{1,25},{10,2},{18... | collective-permute-start | bytes 516104 | tf_op jit(solution)/shard_map/ppermute | solution.py:224
  80.7 5.1 %collective-permute-done.16 = bf16[672,128]{1,0:T(8,128)(2,1)S(1)} collective-permute-done((bf16[672,128]{1,0:T(8,128)(2,1)S(1)}, bf16[672,128]{1,0:T(8,128)(2,1)S(1)}, u32[]{:S(2)}, u32[]{:S(2)}) %collective-permute-start.16) | collective-permute-done | bytes 172064 | tf_op jit(solution)/shard_map/ppermute | solution.py:224
  85.7 0.1 select_dynamic-update-slice_fusion.1
  85.8 2.8 %collective-permute-done.17 = bf16[672,128]{1,0:T(8,128)(2,1)S(1)} collective-permute-done((bf16[672,128]{1,0:T(8,128)(2,1)S(1)}, bf16[672,128]{1,0:T(8,128)(2,1)S(1)}, u32[]{:S(2)}, u32[]{:S(2)}) %collective-permute-start.17) | collective-permute-done | bytes 172064 | tf_op jit(solution)/shard_map/ppermute | solution.py:224
  88.7 0.1 select_dynamic-update-slice_fusion
  88.8 0.0 copy-start.9
  88.8 0.8 copy-done.9
  (21 shorter events, 0.2 us)
Async XLA Ops:
  1.0 13.0 %collective-permute-start.1 = (bf16[128,1024]{1,0:T(8,128)(2,1)S(1)}, bf16[128,1024]{1,0:T(8,128)(2,1)S(1)}, u32[]{:S(2)}, u32[]{:S(2)}) collective-permute-start(bf16[128,1024]{1,0:T(8,128)(2,1)S(1)} %pad_maximum_fusion.1.refs_2_), channel_id=1, source_target_pairs={{0,2},{2,4},{4,6},{1,3},{3,5},{5,7},{8,10},{10,12},{12,14},{9,11},... | collective-permute-start | bytes 786440 | tf_op jit(solution)/shard_map/ppermute | solution.py:208
  6.0 8.1 %collective-permute-start = (bf16[48,1024]{1,0:T(8,128)(2,1)S(1)}, bf16[48,1024]{1,0:T(8,128)(2,1)S(1)}, u32[]{:S(2)}, u32[]{:S(2)}) collective-permute-start(bf16[48,1024]{1,0:T(8,128)(2,1)S(1)} %slice.12), channel_id=1, source_target_pairs={{0,4},{2,6},{1,5},{3,7},{8,12},{10,14},{9,13},{11,15},{16,20},{18,... | collective-permute-start | bytes 294920 | tf_op jit(solution)/shard_map/ppermute | solution.py:208
  12.0 1.0 %copy-start.7 = (bf16[1,128,1024]{2,1,0:T(8,128)(2,1)S(1)}, bf16[1,128,1024]{2,1,0:T(8,128)(2,1)}, u32[]{:S(2)}) copy-start(bf16[1,128,1024]{2,1,0:T(8,128)(2,1)} %param.8) | copy-start | bytes 786436
  13.0 0.9 %copy-start.8 = (bf16[1,128,1024]{2,1,0:T(8,128)(2,1)S(1)}, bf16[1,128,1024]{2,1,0:T(8,128)(2,1)}, u32[]{:S(2)}) copy-start(bf16[1,128,1024]{2,1,0:T(8,128)(2,1)} %param.11) | copy-start | bytes 786436
  14.0 20.4 %copy-start = (bf16[1,1344,1024]{2,1,0:T(8,128)(2,1)S(1)}, bf16[1,1344,1024]{2,1,0:T(8,128)(2,1)}, u32[]{:S(2)}) copy-start(bf16[1,1344,1024]{2,1,0:T(8,128)(2,1)} %param.12) | copy-start | bytes 8257540
  16.3 15.9 %collective-permute-start.2 = (bf16[128,1024]{1,0:T(8,128)(2,1)S(1)}, bf16[128,1024]{1,0:T(8,128)(2,1)S(1)}, u32[]{:S(2)}, u32[]{:S(2)}) collective-permute-start(bf16[128,1024]{1,0:T(8,128)(2,1)S(1)} %get-tuple-element.36), channel_id=1, source_target_pairs={{2,0},{4,2},{6,4},{3,1},{5,3},{7,5},{10,8},{12,10},{14,12},{11,9},... | collective-permute-start | bytes 786440 | tf_op jit(solution)/shard_map/ppermute | solution.py:208
  17.6 14.6 %collective-permute-start.3 = (bf16[48,1024]{1,0:T(8,128)(2,1)S(1)}, bf16[48,1024]{1,0:T(8,128)(2,1)S(1)}, u32[]{:S(2)}, u32[]{:S(2)}) collective-permute-start(bf16[48,1024]{1,0:T(8,128)(2,1)S(1)} %get-tuple-element.37), channel_id=1, source_target_pairs={{4,0},{6,2},{5,1},{7,3},{12,8},{14,10},{13,9},{15,11},{20,16},{22,... | collective-permute-start | bytes 294920 | tf_op jit(solution)/shard_map/ppermute | solution.py:208
  32.3 6.9 %collective-permute-start.6 = (bf16[128,2048]{1,0:T(8,128)(2,1)S(1)}, bf16[128,2048]{1,0:T(8,128)(2,1)}, u32[]{:S(2)}, u32[]{:S(2)}) collective-permute-start(bf16[128,2048]{1,0:T(8,128)(2,1)S(1)} %shard_map.84.refs_0_), channel_id=1, source_target_pairs={{2,4},{4,2},{3,5},{5,3},{10,12},{12,10},{11,13},{13,11},{18,20},{2... | collective-permute-start | bytes 1572872 | tf_op jit(solution)/shard_map/ppermute | solution.py:215
  33.8 12.4 %collective-permute-start.7 = (bf16[128,2048]{1,0:T(8,128)(2,1)S(1)}, bf16[128,2048]{1,0:T(8,128)(2,1)}, u32[]{:S(2)}, u32[]{:S(2)}) collective-permute-start(bf16[128,2048]{1,0:T(8,128)(2,1)S(1)} %shard_map.84.refs_0_), channel_id=1, source_target_pairs={{0,2},{2,0},{4,6},{6,4},{1,3},{3,1},{5,7},{7,5},{8,10},{10,8},{12,... | collective-permute-start | bytes 1572872 | tf_op jit(solution)/shard_map/ppermute | solution.py:215
  34.4 1.3 %copy-start.1 = (bf16[1,1344,512]{2,1,0:T(8,128)(2,1)S(1)}, bf16[1,1344,512]{2,1,0:T(8,128)(2,1)}, u32[]{:S(2)}) copy-start(bf16[1,1344,512]{2,1,0:T(8,128)(2,1)} %param.13) | copy-start | bytes 4128772
  35.8 1.3 %copy-start.4 = (bf16[1,1344,512]{2,1,0:T(8,128)(2,1)S(1)}, bf16[1,1344,512]{2,1,0:T(8,128)(2,1)}, u32[]{:S(2)}) copy-start(bf16[1,1344,512]{2,1,0:T(8,128)(2,1)} %param.14) | copy-start | bytes 4128772
  37.1 11.2 %copy-start.2 = (bf16[1,1344,512]{2,1,0:T(8,128)(2,1)S(1)}, bf16[1,1344,512]{2,1,0:T(8,128)(2,1)}, u32[]{:S(2)}) copy-start(bf16[1,1344,512]{2,1,0:T(8,128)(2,1)} %param.13) | copy-start | bytes 4128772
  37.1 11.2 %copy-start.5 = (bf16[1,1344,512]{2,1,0:T(8,128)(2,1)S(1)}, bf16[1,1344,512]{2,1,0:T(8,128)(2,1)}, u32[]{:S(2)}) copy-start(bf16[1,1344,512]{2,1,0:T(8,128)(2,1)} %param.14) | copy-start | bytes 4128772
  39.1 8.5 %collective-permute-start.4 = (bf16[672,128]{1,0:T(8,128)(2,1)S(1)}, bf16[672,128]{1,0:T(8,128)(2,1)S(1)}, u32[]{:S(2)}, u32[]{:S(2)}) collective-permute-start(bf16[672,128]{1,0:T(8,128)(2,1)S(1)} %get-tuple-element.39), channel_id=1, source_target_pairs={{1,0},{0,1},{3,2},{2,3},{5,4},{4,5},{7,6},{6,7},{9,8},{8,9},{11,10... | collective-permute-start | bytes 516104 | tf_op jit(solution)/shard_map/ppermute | solution.py:224
  39.2 16.4 %collective-permute-start.10 = (bf16[128,2048]{1,0:T(8,128)(2,1)}, bf16[128,2048]{1,0:T(8,128)(2,1)}, u32[]{:S(2)}, u32[]{:S(2)}) collective-permute-start(bf16[128,2048]{1,0:T(8,128)(2,1)} %collective-permute-done.6.refs_0_), channel_id=1, source_target_pairs={{0,2},{2,0},{4,6},{6,4},{1,3},{3,1},{5,7},{7,5},{8,10},{10,8},{12,... | collective-permute-start | bytes 1572872 | tf_op jit(solution)/shard_map/ppermute | solution.py:215
  46.1 9.5 %collective-permute-start.9 = (bf16[128,2048]{1,0:T(8,128)(2,1)}, bf16[128,2048]{1,0:T(8,128)(2,1)}, u32[]{:S(2)}, u32[]{:S(2)}) collective-permute-start(bf16[128,2048]{1,0:T(8,128)(2,1)} %collective-permute-done.7.refs_1_), channel_id=1, source_target_pairs={{2,4},{4,2},{3,5},{5,3},{10,12},{12,10},{11,13},{13,11},{18,20},{2... | collective-permute-start | bytes 1572872 | tf_op jit(solution)/shard_map/ppermute | solution.py:215
  52.4 3.0 %collective-permute-start.8 = (bf16[672,128]{1,0:T(8,128)(2,1)}, bf16[672,128]{1,0:T(8,128)(2,1)}, u32[]{:S(2)}, u32[]{:S(2)}) collective-permute-start(bf16[672,128]{1,0:T(8,128)(2,1)} %get-tuple-element.43), channel_id=1, source_target_pairs={{1,0},{0,1},{3,2},{2,3},{5,4},{4,5},{7,6},{6,7},{9,8},{8,9},{11,10... | collective-permute-start | bytes 516104 | tf_op jit(solution)/shard_map/ppermute | solution.py:224
  52.4 3.2 %collective-permute-start.11 = (bf16[672,128]{1,0:T(8,128)(2,1)}, bf16[672,128]{1,0:T(8,128)(2,1)}, u32[]{:S(2)}, u32[]{:S(2)}) collective-permute-start(bf16[672,128]{1,0:T(8,128)(2,1)} %get-tuple-element.46), channel_id=1, source_target_pairs={{1,0},{0,1},{3,2},{2,3},{5,4},{4,5},{7,6},{6,7},{9,8},{8,9},{11,10... | collective-permute-start | bytes 516104 | tf_op jit(solution)/shard_map/ppermute | solution.py:224
  52.9 11.3 %collective-permute-start.5 = (bf16[672,128]{1,0:T(8,128)(2,1)}, bf16[672,128]{1,0:T(8,128)(2,1)S(1)}, u32[]{:S(2)}, u32[]{:S(2)}) collective-permute-start(bf16[672,128]{1,0:T(8,128)(2,1)} %add_convert_fusion.4), channel_id=1, source_target_pairs={{8,0},{16,8},{24,16},{0,24},{9,1},{17,9},{25,17},{1,25},{10,2},{18... | collective-permute-start | bytes 516104 | tf_op jit(solution)/shard_map/ppermute | solution.py:224
  56.6 7.7 %copy-start.3 = (bf16[1,1344,512]{2,1,0:T(8,128)(2,1)S(1)}, bf16[1,1344,512]{2,1,0:T(8,128)(2,1)}, u32[]{:S(2)}) copy-start(bf16[1,1344,512]{2,1,0:T(8,128)(2,1)} %param.13) | copy-start | bytes 4128772
  56.6 7.7 %copy-start.6 = (bf16[1,1344,512]{2,1,0:T(8,128)(2,1)S(1)}, bf16[1,1344,512]{2,1,0:T(8,128)(2,1)}, u32[]{:S(2)}) copy-start(bf16[1,1344,512]{2,1,0:T(8,128)(2,1)} %param.14) | copy-start | bytes 4128772
  57.8 10.0 %collective-permute-start.12 = (bf16[672,256]{1,0:T(8,128)(2,1)S(1)}, bf16[672,256]{1,0:T(8,128)(2,1)S(1)}, u32[]{:S(2)}, u32[]{:S(2)}) collective-permute-start(bf16[672,256]{1,0:T(8,128)(2,1)S(1)} %pad_maximum_fusion), channel_id=1, source_target_pairs={{8,0},{16,8},{24,16},{0,24},{9,1},{17,9},{25,17},{1,25},{10,2},{18... | collective-permute-start | bytes 1032200 | tf_op jit(solution)/shard_map/ppermute | solution.py:224
  60.3 14.5 %collective-permute-start.13 = (bf16[128,2048]{1,0:T(8,128)(2,1)}, bf16[128,2048]{1,0:T(8,128)(2,1)S(1)}, u32[]{:S(2)}, u32[]{:S(2)}) collective-permute-start(bf16[128,2048]{1,0:T(8,128)(2,1)} %collective-permute-done.9), channel_id=1, source_target_pairs={{0,2},{2,0},{4,6},{6,4},{1,3},{3,1},{5,7},{7,5},{8,10},{10,8},{12,... | collective-permute-start | bytes 1572872 | tf_op jit(solution)/shard_map/ppermute | solution.py:215
  64.3 2.0 %copy-start.10 = (bf16[672,128]{1,0:T(8,128)(2,1)}, bf16[672,128]{1,0:T(8,128)(2,1)S(1)}, u32[]{:S(2)}) copy-start(bf16[672,128]{1,0:T(8,128)(2,1)S(1)} %collective-permute-done.5) | copy-start | bytes 516100
  66.4 1.5 %collective-permute-start.14 = (bf16[672,128]{1,0:T(8,128)(2,1)S(1)}, bf16[672,128]{1,0:T(8,128)(2,1)S(1)}, u32[]{:S(2)}, u32[]{:S(2)}) collective-permute-start(bf16[672,128]{1,0:T(8,128)(2,1)S(1)} %get-tuple-element.50), channel_id=1, source_target_pairs={{1,0},{0,1},{3,2},{2,3},{5,4},{4,5},{7,6},{6,7},{9,8},{8,9},{11,10... | collective-permute-start | bytes 516104 | tf_op jit(solution)/shard_map/ppermute | solution.py:224
  76.9 2.2 %copy-start.11 = (bf16[672,128]{1,0:T(8,128)(2,1)S(1)}, bf16[672,128]{1,0:T(8,128)(2,1)}, u32[]{:S(2)}) copy-start(bf16[672,128]{1,0:T(8,128)(2,1)} %copy-done.10) | copy-start | bytes 516100
  76.9 1.5 %collective-permute-start.15 = (bf16[672,128]{1,0:T(8,128)(2,1)S(1)}, bf16[672,128]{1,0:T(8,128)(2,1)S(1)}, u32[]{:S(2)}, u32[]{:S(2)}) collective-permute-start(bf16[672,128]{1,0:T(8,128)(2,1)S(1)} %get-tuple-element.54), channel_id=1, source_target_pairs={{1,0},{0,1},{3,2},{2,3},{5,4},{4,5},{7,6},{6,7},{9,8},{8,9},{11,10... | collective-permute-start | bytes 516104 | tf_op jit(solution)/shard_map/ppermute | solution.py:224
  78.5 7.3 %collective-permute-start.16 = (bf16[672,128]{1,0:T(8,128)(2,1)S(1)}, bf16[672,128]{1,0:T(8,128)(2,1)S(1)}, u32[]{:S(2)}, u32[]{:S(2)}) collective-permute-start(bf16[672,128]{1,0:T(8,128)(2,1)S(1)} %add_convert_fusion), channel_id=1, source_target_pairs={{8,0},{16,8},{24,16},{0,24},{9,1},{17,9},{25,17},{1,25},{10,2},{18... | collective-permute-start | bytes 516104 | tf_op jit(solution)/shard_map/ppermute | solution.py:224
  79.2 9.4 %collective-permute-start.17 = (bf16[672,128]{1,0:T(8,128)(2,1)S(1)}, bf16[672,128]{1,0:T(8,128)(2,1)S(1)}, u32[]{:S(2)}, u32[]{:S(2)}) collective-permute-start(bf16[672,128]{1,0:T(8,128)(2,1)S(1)} %add_convert_fusion.1), channel_id=1, source_target_pairs={{8,0},{16,8},{24,16},{0,24},{9,1},{17,9},{25,17},{1,25},{10,2},{18... | collective-permute-start | bytes 516104 | tf_op jit(solution)/shard_map/ppermute | solution.py:224
  88.8 0.8 copy-start.9

commit v7 on v6

--- a/solution.py
+++ b/solution.py
@@ -281,7 +281,7 @@
             if late:
                 (got,) = after((got,), *late)
             sums.append((keep + got.astype(jnp.float32)).astype(jnp.bfloat16))
-        return jnp.concatenate(sums, axis=1)
+        return sums
 
     even = place % 2 == 0
     results, waiting = [], [own]
@@ -291,27 +291,24 @@
         last = step == shards - 1 and shards % 2 == 0
         came_second = came_first if last else swapped(by_second, "seq", 1)
         if step > 1:
-            waiting = after(waiting, total, *results[-2:-1])
-        late = (came_second, came_first) if step > 1 else ()
-        if step > 2:
-            late += (results[-1],)
-        total = halves_summed(waiting, *late)
-        results.append(passed_along(total, "section", -1))
+            waiting = after(waiting, *sums, *(results[-2] if step > 2 else ()))
+        late = (came_first, came_second) if step > 1 else ()
+        sums = halves_summed(waiting, *late, *(results[-1] if step > 2 else ()))
+        results.append([passed_along(block, "section", -1) for block in sums])
         by_first, by_second = came_second, came_first
         if last:
             waiting = [came_first]
         elif 2 * step < shards:
-            waiting = [came_second, came_first]
+            waiting = [came_first, came_second]
         else:
             waiting = [jnp.where(even == (place >= step), came_second, came_first)]
     if shards > 1:
-        waiting = after(waiting, total)
-    results.append(passed_along(halves_summed(waiting), "section", -1))
-    for step, block in enumerate(results):
-        if block.shape[1] == rows:
-            results[step] = [block]
-        else:
-            second, first = block[:, :rows], block[:, rows:]
+        waiting = after(waiting, *sums)
+    sums = halves_summed(waiting, *(results[-1] if shards > 1 else ()))
+    results.append([passed_along(block, "section", -1) for block in sums])
+    for step, blocks in enumerate(results):
+        if len(blocks) > 1:
+            first, second = blocks
             results[step] = [jnp.where(even, second, first), jnp.where(even, first, second)]
     upstream = jnp.zeros((results[0][0].shape[0], tokens), jnp.bfloat16)
     for s in range(shards):

time: 90.1 us -> 92.6 us (1.028)
  waiting for transfers between devices: 32.5 us -> 36.3 us
  other arithmetic: 5.3 us -> 4.2 us
    ppermute x5, starting transfers between devices: 12.1 us -> 6.32 us  [swapped(): return lax.ppermute(block, axis, pairs)]
    ppermute x9 -> x10, starting transfers between devices: 7.79 us -> 12.8 us  [passed_along(): lax.ppermute(block, axis, [((i - distance) % len(devices), i) for i in de...]
    ppermute x9 -> x10, waiting for transfers between devices: 10.7 us -> 15 us  [passed_along(): lax.ppermute(block, axis, [((i - distance) % len(devices), i) for i in de...]
    convert_element_type x5, other arithmetic: 2.87 us -> 1.81 us  [halves_summed(): sums.append((keep + got.astype(jnp.float32)).astype(jnp.bfloat16))]
    unnamed x24 -> x26, local copies, waits for them, and re-layouts: 5.45 us -> 6.12 us
  transfers between devices with their start and end apart: 18 -> 19, of which waited for: 8 -> 7; matrix products, arithmetic and copies ran while one was open for 6% -> 5% of each run, Pallas kernels for 9% -> 9%
where the time goes in v7:
time: 92.6 us; the launch traced here: 92.1 us
  waiting for transfers between devices  36.3 us (39%)
  starting transfers between devices  31.1 us (34%)
  Pallas kernels  12.5 us (13%)
  local copies, waits for them, and re-layouts  7.69 us (8%)
  other arithmetic  4.2 us (5%)
    ppermute x10, waiting for transfers between devices, passed_along(): lax.ppermute(block, axis, [((i - distance) % len(devices), i) for i in de...  15 us
    ppermute x4, waiting for transfers between devices, moved(): lax.ppermute(block, axis, [(i, i + by) for i in range(size) if 0 <= i + b...  13.4 us
    ppermute x10, starting transfers between devices, passed_along(): lax.ppermute(block, axis, [((i - distance) % len(devices), i) for i in de...  12.8 us
    ppermute x4, starting transfers between devices, moved(): lax.ppermute(block, axis, [(i, i + by) for i in range(size) if 0 <= i + b...  12 us
    pallas_call x4, Pallas kernels, project(): pl.pallas_call(functools.partial(project_kernel, [len(block) for block in...  10.1 us
    ppermute x5, waiting for transfers between devices, swapped(): return lax.ppermute(block, axis, pairs)  7.89 us
    ppermute x5, starting transfers between devices, swapped(): return lax.ppermute(block, axis, pairs)  6.32 us
    unnamed x26, local copies, waits for them, and re-layouts  6.12 us
  transfers between devices with their start and end apart: 19, of which 7 were waited for; matrix products, arithmetic and copies ran while one was open for 5% of the time, Pallas kernels for 9%

profile of v7, /device:TPU:0, one launch (start us, length us, event | category | flops | bytes accessed | tf_op | source)
XLA Modules:
  0.0 92.1 jit_solution(31250628893381626)
XLA Ops:
  0.0 1.0 %pad_maximum_fusion.refs_2_ = bf16[128,1024]{1,0:T(8,128)(2,1)S(1)} fusion(bf16[128,512]{1,0:T(8,128)(2,1)} %bitcast.28, bf16[128,512]{1,0:T(8,128)(2,1)} %bitcast.29), kind=kLoop, calls=%fused_computation.6 | loop fusion | flops 524288 | bytes 524288 | tf_op jit(solution)/shard_map/concatenate | solution.py:248
  1.0 4.9 %collective-permute-start.1 = (bf16[128,1024]{1,0:T(8,128)(2,1)S(1)}, bf16[128,1024]{1,0:T(8,128)(2,1)S(1)}, u32[]{:S(2)}, u32[]{:S(2)}) collective-permute-start(bf16[128,1024]{1,0:T(8,128)(2,1)S(1)} %pad_maximum_fusion.refs_2_), channel_id=1, source_target_pairs={{0,2},{2,4},{4,6},{1,3},{3,5},{5,7},{8,10},{10,12},{12,14},{9,11},... | collective-permute-start | bytes 786440 | tf_op jit(solution)/shard_map/ppermute | solution.py:208
  6.0 4.5 %collective-permute-start = (bf16[48,1024]{1,0:T(8,128)(2,1)S(1)}, bf16[48,1024]{1,0:T(8,128)(2,1)S(1)}, u32[]{:S(2)}, u32[]{:S(2)}) collective-permute-start(bf16[48,1024]{1,0:T(8,128)(2,1)S(1)} %slice.4), channel_id=1, source_target_pairs={{0,4},{2,6},{1,5},{3,7},{8,12},{10,14},{9,13},{11,15},{16,20},{18,... | collective-permute-start | bytes 294920 | tf_op jit(solution)/shard_map/ppermute | solution.py:208
  10.5 0.8 pad_dynamic-slice_fusion
  11.2 0.7 fusion.5
  11.9 0.1 fusion.4.refs_3_
  12.0 0.0 copy-start.7
  12.0 0.9 %copy-done.7 = bf16[1,128,1024]{2,1,0:T(8,128)(2,1)S(1)} copy-done((bf16[1,128,1024]{2,1,0:T(8,128)(2,1)S(1)}, bf16[1,128,1024]{2,1,0:T(8,128)(2,1)}, u32[]{:S(2)}) %copy-start.7) | copy-done | bytes 262168
  13.0 0.9 %copy-done.8 = bf16[1,128,1024]{2,1,0:T(8,128)(2,1)S(1)} copy-done((bf16[1,128,1024]{2,1,0:T(8,128)(2,1)S(1)}, bf16[1,128,1024]{2,1,0:T(8,128)(2,1)}, u32[]{:S(2)}) %copy-start.8) | copy-done | bytes 262168
  13.9 0.1 shard_map.82
  14.0 0.0 collective-permute-done.refs_4_
  14.0 0.0 collective-permute-done.1.refs_5_
  14.0 0.0 copy-start
  14.0 2.2 %shard_map.83 = (bf16[128,1024]{1,0:T(8,128)(2,1)S(1)}, f32[128,1024]{1,0:T(8,128)S(1)}, bf16[48,1024]{1,0:T(8,128)(2,1)S(1)}, bf16[128,1024]{1,0:T(8,128)(2,1)S(1)}) custom-call(bf16[1024,128]{1,0:T(8,128)(2,1)S(1)} %get-tuple-element.33.refs_0_, bf16[1024,128]{1,0:T(8,128)(2,1)S(1)} %get-tuple-element.34.refs_1_, ...), custom_call_target="tpu_custom_call" | custom-call | flops 478150656 | bytes 1048576 | tf_op jit(solution)/shard_map/pallas_call | solution.py:100
  16.3 1.3 %collective-permute-start.2 = (bf16[128,1024]{1,0:T(8,128)(2,1)S(1)}, bf16[128,1024]{1,0:T(8,128)(2,1)S(1)}, u32[]{:S(2)}, u32[]{:S(2)}) collective-permute-start(bf16[128,1024]{1,0:T(8,128)(2,1)S(1)} %get-tuple-element.37), channel_id=1, source_target_pairs={{2,0},{4,2},{6,4},{3,1},{5,3},{7,5},{10,8},{12,10},{14,12},{11,9},... | collective-permute-start | bytes 786440 | tf_op jit(solution)/shard_map/ppermute | solution.py:208
  17.6 1.3 %collective-permute-start.3 = (bf16[48,1024]{1,0:T(8,128)(2,1)S(1)}, bf16[48,1024]{1,0:T(8,128)(2,1)S(1)}, u32[]{:S(2)}, u32[]{:S(2)}) collective-permute-start(bf16[48,1024]{1,0:T(8,128)(2,1)S(1)} %get-tuple-element.38), channel_id=1, source_target_pairs={{4,0},{6,2},{5,1},{7,3},{12,8},{14,10},{13,9},{15,11},{20,16},{22,... | collective-permute-start | bytes 294920 | tf_op jit(solution)/shard_map/ppermute | solution.py:208
  18.9 13.4 %collective-permute-done.3.refs_1_ = bf16[48,1024]{1,0:T(8,128)(2,1)S(1)} collective-permute-done((bf16[48,1024]{1,0:T(8,128)(2,1)S(1)}, bf16[48,1024]{1,0:T(8,128)(2,1)S(1)}, u32[]{:S(2)}, u32[]{:S(2)}) %collective-permute-start.3) | collective-permute-done | bytes 98336 | tf_op jit(solution)/shard_map/ppermute | solution.py:208
  32.3 0.1 shard_map.84.refs_0_
  32.4 0.1 collective-permute-start.6
  32.5 1.5 %collective-permute-start.7 = (bf16[128,2048]{1,0:T(8,128)(2,1)S(1)}, bf16[128,2048]{1,0:T(8,128)(2,1)}, u32[]{:S(2)}, u32[]{:S(2)}) collective-permute-start(bf16[128,2048]{1,0:T(8,128)(2,1)S(1)} %shard_map.84.refs_0_), channel_id=1, source_target_pairs={{2,4},{4,2},{3,5},{5,3},{10,12},{12,10},{11,13},{13,11},{18,20},{2... | collective-permute-start | bytes 1572872 | tf_op jit(solution)/shard_map/ppermute | solution.py:215
  33.9 1.3 %copy-done.1 = bf16[1,1344,512]{2,1,0:T(8,128)(2,1)S(1)} copy-done((bf16[1,1344,512]{2,1,0:T(8,128)(2,1)S(1)}, bf16[1,1344,512]{2,1,0:T(8,128)(2,1)}, u32[]{:S(2)}) %copy-start.1) | copy-done | bytes 1376280
  35.3 1.3 %copy-done.4 = bf16[1,1344,512]{2,1,0:T(8,128)(2,1)S(1)} copy-done((bf16[1,1344,512]{2,1,0:T(8,128)(2,1)S(1)}, bf16[1,1344,512]{2,1,0:T(8,128)(2,1)}, u32[]{:S(2)}) %copy-start.4) | copy-done | bytes 1376280
  36.6 2.0 %shard_map.85 = (f32[672,128]{1,0:T(8,128)S(1)}, bf16[672,128]{1,0:T(8,128)(2,1)S(1)}) custom-call(s32[1]{0:T(128)} %bitcast.core_ref, bf16[128,2048]{1,0:T(8,128)(2,1)S(1)} %shard_map.84.refs_0_, bf16[1344,1024]{1,0:T(8,128)(2,1)S(1)} %bitcast.14, bf16[1344,512]{1,0:T(8,128)(2,1)S(1)} %bitcast.18, bf16[1344,512]{1,0:T(8,128)(2,1)S(1)} %bitcast.22), custom_call_target="tpu_custom_call" | custom-call | flops 704643072 | bytes 6537216 | tf_op jit(solution)/shard_map/pallas_call | solution.py:187
  38.6 0.1 collective-permute-start.4
  38.7 4.9 %collective-permute-done.6.refs_0_ = bf16[128,2048]{1,0:T(8,128)(2,1)} collective-permute-done((bf16[128,2048]{1,0:T(8,128)(2,1)S(1)}, bf16[128,2048]{1,0:T(8,128)(2,1)}, u32[]{:S(2)}, u32[]{:S(2)}) %collective-permute-start.6) | collective-permute-done | bytes 524320 | tf_op jit(solution)/shard_map/ppermute | solution.py:215
  43.6 1.4 %collective-permute-start.10 = (bf16[128,2048]{1,0:T(8,128)(2,1)}, bf16[128,2048]{1,0:T(8,128)(2,1)}, u32[]{:S(2)}, u32[]{:S(2)}) collective-permute-start(bf16[128,2048]{1,0:T(8,128)(2,1)} %collective-permute-done.6.refs_0_), channel_id=1, source_target_pairs={{2,4},{4,2},{3,5},{5,3},{10,12},{12,10},{11,13},{13,11},{18,20},{2... | collective-permute-start | bytes 1572872 | tf_op jit(solution)/shard_map/ppermute | solution.py:215
  45.0 0.0 collective-permute-done.7.refs_1_
  45.0 1.6 %collective-permute-start.9 = (bf16[128,2048]{1,0:T(8,128)(2,1)}, bf16[128,2048]{1,0:T(8,128)(2,1)}, u32[]{:S(2)}, u32[]{:S(2)}) collective-permute-start(bf16[128,2048]{1,0:T(8,128)(2,1)} %collective-permute-done.7.refs_1_), channel_id=1, source_target_pairs={{0,2},{2,0},{4,6},{6,4},{1,3},{3,1},{5,7},{7,5},{8,10},{10,8},{12,... | collective-permute-start | bytes 1572872 | tf_op jit(solution)/shard_map/ppermute | solution.py:215
  46.6 0.0 collective-permute-done.4
  46.6 0.7 add_convert_fusion.4
  47.3 4.1 %shard_map.86 = (f32[672,128]{1,0:T(8,128)S(1)}, f32[672,128]{1,0:T(8,128)S(1)}, bf16[672,128]{1,0:T(8,128)(2,1)S(1)}, bf16[672,128]{1,0:T(8,128)(2,1)}) custom-call(s32[1]{0:T(128)} %bitcast.core_ref, bf16[128,2048]{1,0:T(8,128)(2,1)} %collective-permute-done.6.refs_0_, bf16[128,2048]{1,0:T(8,128)(2,1)} %collective-permute-done.7.refs_1_, ...), custom_call_target="tpu_custom_call" | custom-call | flops 1409286144 | bytes 7569408 | tf_op jit(solution)/shard_map/pallas_call | solution.py:187
  51.4 0.7 copy-done.9
  52.1 0.0 collective-permute-start.8
  52.1 2.5 %collective-permute-start.5 = (bf16[672,128]{1,0:T(8,128)(2,1)}, bf16[672,128]{1,0:T(8,128)(2,1)S(1)}, u32[]{:S(2)}, u32[]{:S(2)}) collective-permute-start(bf16[672,128]{1,0:T(8,128)(2,1)} %add_convert_fusion.4), channel_id=1, source_target_pairs={{8,0},{16,8},{24,16},{0,24},{9,1},{17,9},{25,17},{1,25},{10,2},{18... | collective-permute-start | bytes 516104 | tf_op jit(solution)/shard_map/ppermute | solution.py:224
  54.6 0.2 collective-permute-start.12
  54.8 0.0 collective-permute-done.8
  54.8 0.0 collective-permute-done.10
  54.8 3.0 %collective-permute-done.9 = bf16[128,2048]{1,0:T(8,128)(2,1)} collective-permute-done((bf16[128,2048]{1,0:T(8,128)(2,1)}, bf16[128,2048]{1,0:T(8,128)(2,1)}, u32[]{:S(2)}, u32[]{:S(2)}) %collective-permute-start.9) | collective-permute-done | bytes 524320 | tf_op jit(solution)/shard_map/ppermute | solution.py:215
  57.8 1.7 %collective-permute-start.14 = (bf16[128,2048]{1,0:T(8,128)(2,1)}, bf16[128,2048]{1,0:T(8,128)(2,1)S(1)}, u32[]{:S(2)}, u32[]{:S(2)}) collective-permute-start(bf16[128,2048]{1,0:T(8,128)(2,1)} %collective-permute-done.10), channel_id=1, source_target_pairs={{0,2},{2,0},{4,6},{6,4},{1,3},{3,1},{5,7},{7,5},{8,10},{10,8},{12,... | collective-permute-start | bytes 1572872 | tf_op jit(solution)/shard_map/ppermute | solution.py:215
  59.5 1.1 %broadcast_select_fusion.refs_0_ = bf16[128,2048]{1,0:T(8,128)(2,1)S(1)} fusion(bf16[128,2048]{1,0:T(8,128)(2,1)} %collective-permute-done.10, bf16[128,2048]{1,0:T(8,128)(2,1)} %collective-permute-done.9, pred[]{:T(512)S(6)} %eq.32), kind=kLoop, calls=%fused_computation | loop fusion | flops 262144 | bytes 1572865 | tf_op jit(solution)/shard_map/jit(_where)/select_n | solution.py:304
  60.6 1.0 %add_convert_fusion.3 = bf16[672,128]{1,0:T(8,128)(2,1)S(1)} fusion(f32[672,128]{1,0:T(8,128)S(1)} %get-tuple-element.43, bf16[672,128]{1,0:T(8,128)(2,1)} %collective-permute-done.8), kind=kLoop, calls=%fused_computation.4 | loop fusion | flops 258048 | bytes 688128 | tf_op jit(solution)/shard_map/convert_element_type | solution.py:283
  61.7 0.0 copy-start.11
  61.7 2.0 %shard_map.87 = (f32[672,128]{1,0:T(8,128)S(1)}, bf16[672,128]{1,0:T(8,128)(2,1)S(1)}) custom-call(s32[1]{0:T(128)} %bitcast.core_ref, bf16[128,2048]{1,0:T(8,128)(2,1)S(1)} %broadcast_select_fusion.refs_0_, bf16[1344,1024]{1,0:T(8,128)(2,1)S(1)} %bitcast.16, bf16[1344,512]{1,0:T(8,128)(2,1)S(1)} %bitcast.20, bf16[1344,512]{1,0:T(8,128)(2,1)S(1)} %bitcast.24), custom_call_target="tpu_custom_call" | custom-call | flops 704643072 | bytes 6537216 | tf_op jit(solution)/shard_map/pallas_call | solution.py:187
  63.7 0.1 collective-permute-start.15
  63.8 2.5 %collective-permute-start.11 = (bf16[672,128]{1,0:T(8,128)(2,1)S(1)}, bf16[672,128]{1,0:T(8,128)(2,1)S(1)}, u32[]{:S(2)}, u32[]{:S(2)}) collective-permute-start(bf16[672,128]{1,0:T(8,128)(2,1)S(1)} %add_convert_fusion.3), channel_id=1, source_target_pairs={{8,0},{16,8},{24,16},{0,24},{9,1},{17,9},{25,17},{1,25},{10,2},{18... | collective-permute-start | bytes 516104 | tf_op jit(solution)/shard_map/ppermute | solution.py:224
  66.3 0.5 collective-permute-start.13
  66.8 0.0 collective-permute-done.15
  66.8 4.2 %collective-permute-done.11 = bf16[672,128]{1,0:T(8,128)(2,1)S(1)} collective-permute-done((bf16[672,128]{1,0:T(8,128)(2,1)S(1)}, bf16[672,128]{1,0:T(8,128)(2,1)S(1)}, u32[]{:S(2)}, u32[]{:S(2)}) %collective-permute-start.11) | collective-permute-done | bytes 172064 | tf_op jit(solution)/shard_map/ppermute | solution.py:224
  71.0 3.2 %collective-permute-done.13 = bf16[672,128]{1,0:T(8,128)(2,1)S(1)} collective-permute-done((bf16[672,128]{1,0:T(8,128)(2,1)S(1)}, bf16[672,128]{1,0:T(8,128)(2,1)S(1)}, u32[]{:S(2)}, u32[]{:S(2)}) %collective-permute-start.13) | collective-permute-done | bytes 172064 | tf_op jit(solution)/shard_map/ppermute | solution.py:224
  74.3 0.0 collective-permute-done.14.refs_0_
  74.3 0.1 add_convert_fusion.1
  74.3 2.0 %shard_map.88 = (f32[672,128]{1,0:T(8,128)S(1)}, bf16[672,128]{1,0:T(8,128)(2,1)S(1)}) custom-call(s32[1]{0:T(128)} %bitcast.core_ref, bf16[128,2048]{1,0:T(8,128)(2,1)S(1)} %collective-permute-done.14.refs_0_, bf16[1344,1024]{1,0:T(8,128)(2,1)S(1)} %bitcast.17, bf16[1344,512]{1,0:T(8,128)(2,1)S(1)} %bitcast.21, bf16[1344,512]{1,0:T(8,128)(2,1)S(1)} %bitcast.25), custom_call_target="tpu_custom_call" | custom-call | flops 704643072 | bytes 6537216 | tf_op jit(solution)/shard_map/pallas_call | solution.py:187
  76.3 0.0 copy-start.12
  76.3 0.1 collective-permute-start.16
  76.4 3.4 %collective-permute-start.17 = (bf16[672,128]{1,0:T(8,128)(2,1)S(1)}, bf16[672,128]{1,0:T(8,128)(2,1)S(1)}, u32[]{:S(2)}, u32[]{:S(2)}) collective-permute-start(bf16[672,128]{1,0:T(8,128)(2,1)S(1)} %add_convert_fusion.1), channel_id=1, source_target_pairs={{8,0},{16,8},{24,16},{0,24},{9,1},{17,9},{25,17},{1,25},{10,2},{18... | collective-permute-start | bytes 516104 | tf_op jit(solution)/shard_map/ppermute | solution.py:224
  79.8 0.0 collective-permute-done.16
  79.8 4.2 %collective-permute-done.17 = bf16[672,128]{1,0:T(8,128)(2,1)S(1)} collective-permute-done((bf16[672,128]{1,0:T(8,128)(2,1)S(1)}, bf16[672,128]{1,0:T(8,128)(2,1)S(1)}, u32[]{:S(2)}, u32[]{:S(2)}) %collective-permute-start.17) | collective-permute-done | bytes 172064 | tf_op jit(solution)/shard_map/ppermute | solution.py:224
  84.1 0.1 add_convert_fusion
  84.1 3.4 %collective-permute-start.18 = (bf16[672,128]{1,0:T(8,128)(2,1)S(1)}, bf16[672,128]{1,0:T(8,128)(2,1)S(1)}, u32[]{:S(2)}, u32[]{:S(2)}) collective-permute-start(bf16[672,128]{1,0:T(8,128)(2,1)S(1)} %add_convert_fusion), channel_id=1, source_target_pairs={{8,0},{16,8},{24,16},{0,24},{9,1},{17,9},{25,17},{1,25},{10,2},{18... | collective-permute-start | bytes 516104 | tf_op jit(solution)/shard_map/ppermute | solution.py:224
  87.7 3.3 %collective-permute-done.18 = bf16[672,128]{1,0:T(8,128)(2,1)S(1)} collective-permute-done((bf16[672,128]{1,0:T(8,128)(2,1)S(1)}, bf16[672,128]{1,0:T(8,128)(2,1)S(1)}, u32[]{:S(2)}, u32[]{:S(2)}) %collective-permute-start.18) | collective-permute-done | bytes 172064 | tf_op jit(solution)/shard_map/ppermute | solution.py:224
  91.0 0.1 select_dynamic-update-slice_fusion.1
  91.2 0.1 select_dynamic-update-slice_fusion
  91.3 0.0 copy-start.10
  91.3 0.8 copy-done.10
  (24 shorter events, 0.2 us)
Async XLA Ops:
  1.0 13.0 %collective-permute-start.1 = (bf16[128,1024]{1,0:T(8,128)(2,1)S(1)}, bf16[128,1024]{1,0:T(8,128)(2,1)S(1)}, u32[]{:S(2)}, u32[]{:S(2)}) collective-permute-start(bf16[128,1024]{1,0:T(8,128)(2,1)S(1)} %pad_maximum_fusion.refs_2_), channel_id=1, source_target_pairs={{0,2},{2,4},{4,6},{1,3},{3,5},{5,7},{8,10},{10,12},{12,14},{9,11},... | collective-permute-start | bytes 786440 | tf_op jit(solution)/shard_map/ppermute | solution.py:208
  6.0 8.1 %collective-permute-start = (bf16[48,1024]{1,0:T(8,128)(2,1)S(1)}, bf16[48,1024]{1,0:T(8,128)(2,1)S(1)}, u32[]{:S(2)}, u32[]{:S(2)}) collective-permute-start(bf16[48,1024]{1,0:T(8,128)(2,1)S(1)} %slice.4), channel_id=1, source_target_pairs={{0,4},{2,6},{1,5},{3,7},{8,12},{10,14},{9,13},{11,15},{16,20},{18,... | collective-permute-start | bytes 294920 | tf_op jit(solution)/shard_map/ppermute | solution.py:208
  12.0 1.0 %copy-start.7 = (bf16[1,128,1024]{2,1,0:T(8,128)(2,1)S(1)}, bf16[1,128,1024]{2,1,0:T(8,128)(2,1)}, u32[]{:S(2)}) copy-start(bf16[1,128,1024]{2,1,0:T(8,128)(2,1)} %param.8) | copy-start | bytes 786436
  13.0 0.9 %copy-start.8 = (bf16[1,128,1024]{2,1,0:T(8,128)(2,1)S(1)}, bf16[1,128,1024]{2,1,0:T(8,128)(2,1)}, u32[]{:S(2)}) copy-start(bf16[1,128,1024]{2,1,0:T(8,128)(2,1)} %param.11) | copy-start | bytes 786436
  14.0 19.9 %copy-start = (bf16[1,1344,1024]{2,1,0:T(8,128)(2,1)S(1)}, bf16[1,1344,1024]{2,1,0:T(8,128)(2,1)}, u32[]{:S(2)}) copy-start(bf16[1,1344,1024]{2,1,0:T(8,128)(2,1)} %param.12) | copy-start | bytes 8257540
  16.3 16.0 %collective-permute-start.2 = (bf16[128,1024]{1,0:T(8,128)(2,1)S(1)}, bf16[128,1024]{1,0:T(8,128)(2,1)S(1)}, u32[]{:S(2)}, u32[]{:S(2)}) collective-permute-start(bf16[128,1024]{1,0:T(8,128)(2,1)S(1)} %get-tuple-element.37), channel_id=1, source_target_pairs={{2,0},{4,2},{6,4},{3,1},{5,3},{7,5},{10,8},{12,10},{14,12},{11,9},... | collective-permute-start | bytes 786440 | tf_op jit(solution)/shard_map/ppermute | solution.py:208
  17.6 14.7 %collective-permute-start.3 = (bf16[48,1024]{1,0:T(8,128)(2,1)S(1)}, bf16[48,1024]{1,0:T(8,128)(2,1)S(1)}, u32[]{:S(2)}, u32[]{:S(2)}) collective-permute-start(bf16[48,1024]{1,0:T(8,128)(2,1)S(1)} %get-tuple-element.38), channel_id=1, source_target_pairs={{4,0},{6,2},{5,1},{7,3},{12,8},{14,10},{13,9},{15,11},{20,16},{22,... | collective-permute-start | bytes 294920 | tf_op jit(solution)/shard_map/ppermute | solution.py:208
  32.4 11.2 %collective-permute-start.6 = (bf16[128,2048]{1,0:T(8,128)(2,1)S(1)}, bf16[128,2048]{1,0:T(8,128)(2,1)}, u32[]{:S(2)}, u32[]{:S(2)}) collective-permute-start(bf16[128,2048]{1,0:T(8,128)(2,1)S(1)} %shard_map.84.refs_0_), channel_id=1, source_target_pairs={{0,2},{2,0},{4,6},{6,4},{1,3},{3,1},{5,7},{7,5},{8,10},{10,8},{12,... | collective-permute-start | bytes 1572872 | tf_op jit(solution)/shard_map/ppermute | solution.py:215
  32.5 12.6 %collective-permute-start.7 = (bf16[128,2048]{1,0:T(8,128)(2,1)S(1)}, bf16[128,2048]{1,0:T(8,128)(2,1)}, u32[]{:S(2)}, u32[]{:S(2)}) collective-permute-start(bf16[128,2048]{1,0:T(8,128)(2,1)S(1)} %shard_map.84.refs_0_), channel_id=1, source_target_pairs={{2,4},{4,2},{3,5},{5,3},{10,12},{12,10},{11,13},{13,11},{18,20},{2... | collective-permute-start | bytes 1572872 | tf_op jit(solution)/shard_map/ppermute | solution.py:215
  33.9 1.3 %copy-start.1 = (bf16[1,1344,512]{2,1,0:T(8,128)(2,1)S(1)}, bf16[1,1344,512]{2,1,0:T(8,128)(2,1)}, u32[]{:S(2)}) copy-start(bf16[1,1344,512]{2,1,0:T(8,128)(2,1)} %param.13) | copy-start | bytes 4128772
  35.3 1.3 %copy-start.4 = (bf16[1,1344,512]{2,1,0:T(8,128)(2,1)S(1)}, bf16[1,1344,512]{2,1,0:T(8,128)(2,1)}, u32[]{:S(2)}) copy-start(bf16[1,1344,512]{2,1,0:T(8,128)(2,1)} %param.14) | copy-start | bytes 4128772
  36.6 10.7 %copy-start.2 = (bf16[1,1344,512]{2,1,0:T(8,128)(2,1)S(1)}, bf16[1,1344,512]{2,1,0:T(8,128)(2,1)}, u32[]{:S(2)}) copy-start(bf16[1,1344,512]{2,1,0:T(8,128)(2,1)} %param.13) | copy-start | bytes 4128772
  36.6 10.7 %copy-start.5 = (bf16[1,1344,512]{2,1,0:T(8,128)(2,1)S(1)}, bf16[1,1344,512]{2,1,0:T(8,128)(2,1)}, u32[]{:S(2)}) copy-start(bf16[1,1344,512]{2,1,0:T(8,128)(2,1)} %param.14) | copy-start | bytes 4128772
  38.6 8.0 %collective-permute-start.4 = (bf16[672,128]{1,0:T(8,128)(2,1)S(1)}, bf16[672,128]{1,0:T(8,128)(2,1)S(1)}, u32[]{:S(2)}, u32[]{:S(2)}) collective-permute-start(bf16[672,128]{1,0:T(8,128)(2,1)S(1)} %get-tuple-element.40), channel_id=1, source_target_pairs={{1,0},{0,1},{3,2},{2,3},{5,4},{4,5},{7,6},{6,7},{9,8},{8,9},{11,10... | collective-permute-start | bytes 516104 | tf_op jit(solution)/shard_map/ppermute | solution.py:224
  43.6 11.2 %collective-permute-start.10 = (bf16[128,2048]{1,0:T(8,128)(2,1)}, bf16[128,2048]{1,0:T(8,128)(2,1)}, u32[]{:S(2)}, u32[]{:S(2)}) collective-permute-start(bf16[128,2048]{1,0:T(8,128)(2,1)} %collective-permute-done.6.refs_0_), channel_id=1, source_target_pairs={{2,4},{4,2},{3,5},{5,3},{10,12},{12,10},{11,13},{13,11},{18,20},{2... | collective-permute-start | bytes 1572872 | tf_op jit(solution)/shard_map/ppermute | solution.py:215
  45.0 12.8 %collective-permute-start.9 = (bf16[128,2048]{1,0:T(8,128)(2,1)}, bf16[128,2048]{1,0:T(8,128)(2,1)}, u32[]{:S(2)}, u32[]{:S(2)}) collective-permute-start(bf16[128,2048]{1,0:T(8,128)(2,1)} %collective-permute-done.7.refs_1_), channel_id=1, source_target_pairs={{0,2},{2,0},{4,6},{6,4},{1,3},{3,1},{5,7},{7,5},{8,10},{10,8},{12,... | collective-permute-start | bytes 1572872 | tf_op jit(solution)/shard_map/ppermute | solution.py:215
  51.4 0.7 copy-start.9
  52.1 2.7 %collective-permute-start.8 = (bf16[672,128]{1,0:T(8,128)(2,1)}, bf16[672,128]{1,0:T(8,128)(2,1)}, u32[]{:S(2)}, u32[]{:S(2)}) collective-permute-start(bf16[672,128]{1,0:T(8,128)(2,1)} %get-tuple-element.44), channel_id=1, source_target_pairs={{1,0},{0,1},{3,2},{2,3},{5,4},{4,5},{7,6},{6,7},{9,8},{8,9},{11,10... | collective-permute-start | bytes 516104 | tf_op jit(solution)/shard_map/ppermute | solution.py:224
  52.1 9.6 %collective-permute-start.5 = (bf16[672,128]{1,0:T(8,128)(2,1)}, bf16[672,128]{1,0:T(8,128)(2,1)S(1)}, u32[]{:S(2)}, u32[]{:S(2)}) collective-permute-start(bf16[672,128]{1,0:T(8,128)(2,1)} %add_convert_fusion.4), channel_id=1, source_target_pairs={{8,0},{16,8},{24,16},{0,24},{9,1},{17,9},{25,17},{1,25},{10,2},{18... | collective-permute-start | bytes 516104 | tf_op jit(solution)/shard_map/ppermute | solution.py:224
  54.6 7.1 %copy-start.3 = (bf16[1,1344,512]{2,1,0:T(8,128)(2,1)S(1)}, bf16[1,1344,512]{2,1,0:T(8,128)(2,1)}, u32[]{:S(2)}) copy-start(bf16[1,1344,512]{2,1,0:T(8,128)(2,1)} %param.13) | copy-start | bytes 4128772
  54.6 7.1 %copy-start.6 = (bf16[1,1344,512]{2,1,0:T(8,128)(2,1)S(1)}, bf16[1,1344,512]{2,1,0:T(8,128)(2,1)}, u32[]{:S(2)}) copy-start(bf16[1,1344,512]{2,1,0:T(8,128)(2,1)} %param.14) | copy-start | bytes 4128772
  54.6 7.0 %collective-permute-start.12 = (bf16[672,128]{1,0:T(8,128)(2,1)}, bf16[672,128]{1,0:T(8,128)(2,1)S(1)}, u32[]{:S(2)}, u32[]{:S(2)}) collective-permute-start(bf16[672,128]{1,0:T(8,128)(2,1)} %copy-done.9), channel_id=1, source_target_pairs={{1,0},{0,1},{3,2},{2,3},{5,4},{4,5},{7,6},{6,7},{9,8},{8,9},{11,10... | collective-permute-start | bytes 516104 | tf_op jit(solution)/shard_map/ppermute | solution.py:224
  57.8 16.5 %collective-permute-start.14 = (bf16[128,2048]{1,0:T(8,128)(2,1)}, bf16[128,2048]{1,0:T(8,128)(2,1)S(1)}, u32[]{:S(2)}, u32[]{:S(2)}) collective-permute-start(bf16[128,2048]{1,0:T(8,128)(2,1)} %collective-permute-done.10), channel_id=1, source_target_pairs={{0,2},{2,0},{4,6},{6,4},{1,3},{3,1},{5,7},{7,5},{8,10},{10,8},{12,... | collective-permute-start | bytes 1572872 | tf_op jit(solution)/shard_map/ppermute | solution.py:215
  61.7 2.0 %copy-start.11 = (bf16[672,128]{1,0:T(8,128)(2,1)}, bf16[672,128]{1,0:T(8,128)(2,1)S(1)}, u32[]{:S(2)}) copy-start(bf16[672,128]{1,0:T(8,128)(2,1)S(1)} %collective-permute-done.5) | copy-start | bytes 516100
  63.7 3.1 %collective-permute-start.15 = (bf16[672,128]{1,0:T(8,128)(2,1)S(1)}, bf16[672,128]{1,0:T(8,128)(2,1)S(1)}, u32[]{:S(2)}, u32[]{:S(2)}) collective-permute-start(bf16[672,128]{1,0:T(8,128)(2,1)S(1)} %get-tuple-element.51), channel_id=1, source_target_pairs={{1,0},{0,1},{3,2},{2,3},{5,4},{4,5},{7,6},{6,7},{9,8},{8,9},{11,10... | collective-permute-start | bytes 516104 | tf_op jit(solution)/shard_map/ppermute | solution.py:224
  63.8 7.2 %collective-permute-start.11 = (bf16[672,128]{1,0:T(8,128)(2,1)S(1)}, bf16[672,128]{1,0:T(8,128)(2,1)S(1)}, u32[]{:S(2)}, u32[]{:S(2)}) collective-permute-start(bf16[672,128]{1,0:T(8,128)(2,1)S(1)} %add_convert_fusion.3), channel_id=1, source_target_pairs={{8,0},{16,8},{24,16},{0,24},{9,1},{17,9},{25,17},{1,25},{10,2},{18... | collective-permute-start | bytes 516104 | tf_op jit(solution)/shard_map/ppermute | solution.py:224
  66.3 8.0 %collective-permute-start.13 = (bf16[672,128]{1,0:T(8,128)(2,1)S(1)}, bf16[672,128]{1,0:T(8,128)(2,1)S(1)}, u32[]{:S(2)}, u32[]{:S(2)}) collective-permute-start(bf16[672,128]{1,0:T(8,128)(2,1)S(1)} %add_convert_fusion.2), channel_id=1, source_target_pairs={{8,0},{16,8},{24,16},{0,24},{9,1},{17,9},{25,17},{1,25},{10,2},{18... | collective-permute-start | bytes 516104 | tf_op jit(solution)/shard_map/ppermute | solution.py:224
  76.3 11.3 %copy-start.12 = (bf16[672,128]{1,0:T(8,128)(2,1)S(1)}, bf16[672,128]{1,0:T(8,128)(2,1)}, u32[]{:S(2)}) copy-start(bf16[672,128]{1,0:T(8,128)(2,1)} %copy-done.11) | copy-start | bytes 516100
  76.3 3.5 %collective-permute-start.16 = (bf16[672,128]{1,0:T(8,128)(2,1)S(1)}, bf16[672,128]{1,0:T(8,128)(2,1)S(1)}, u32[]{:S(2)}, u32[]{:S(2)}) collective-permute-start(bf16[672,128]{1,0:T(8,128)(2,1)S(1)} %get-tuple-element.55), channel_id=1, source_target_pairs={{1,0},{0,1},{3,2},{2,3},{5,4},{4,5},{7,6},{6,7},{9,8},{8,9},{11,10... | collective-permute-start | bytes 516104 | tf_op jit(solution)/shard_map/ppermute | solution.py:224
  76.4 7.6 %collective-permute-start.17 = (bf16[672,128]{1,0:T(8,128)(2,1)S(1)}, bf16[672,128]{1,0:T(8,128)(2,1)S(1)}, u32[]{:S(2)}, u32[]{:S(2)}) collective-permute-start(bf16[672,128]{1,0:T(8,128)(2,1)S(1)} %add_convert_fusion.1), channel_id=1, source_target_pairs={{8,0},{16,8},{24,16},{0,24},{9,1},{17,9},{25,17},{1,25},{10,2},{18... | collective-permute-start | bytes 516104 | tf_op jit(solution)/shard_map/ppermute | solution.py:224
  84.1 6.9 %collective-permute-start.18 = (bf16[672,128]{1,0:T(8,128)(2,1)S(1)}, bf16[672,128]{1,0:T(8,128)(2,1)S(1)}, u32[]{:S(2)}, u32[]{:S(2)}) collective-permute-start(bf16[672,128]{1,0:T(8,128)(2,1)S(1)} %add_convert_fusion), channel_id=1, source_target_pairs={{8,0},{16,8},{24,16},{0,24},{9,1},{17,9},{25,17},{1,25},{10,2},{18... | collective-permute-start | bytes 516104 | tf_op jit(solution)/shard_map/ppermute | solution.py:224
  91.3 0.8 copy-start.10

commit v8 on v7

--- a/solution.py
+++ b/solution.py
@@ -273,10 +273,12 @@
     weights = (w_query[0], key_weight[0], value_weight[0])
     core = lax.axis_index("mp").astype(jnp.int32)
 
-    def halves_summed(blocks, *late):
+    def halves_summed(blocks, late, before=()):
         halves = project([(block,) for block in blocks], weights, core[None])
         sums = []
         for keep, give in zip(halves[: len(blocks)], halves[len(blocks) :]):
+            if before:
+                (give,) = after((give,), *before)
             got = passed_along(give, "mp", 1)
             if late:
                 (got,) = after((got,), *late)
@@ -293,7 +295,7 @@
         if step > 1:
             waiting = after(waiting, *sums, *(results[-2] if step > 2 else ()))
         late = (came_first, came_second) if step > 1 else ()
-        sums = halves_summed(waiting, *late, *(results[-1] if step > 2 else ()))
+        sums = halves_summed(waiting, late)
         results.append([passed_along(block, "section", -1) for block in sums])
         by_first, by_second = came_second, came_first
         if last:
@@ -304,7 +306,7 @@
             waiting = [jnp.where(even == (place >= step), came_second, came_first)]
     if shards > 1:
         waiting = after(waiting, *sums)
-    sums = halves_summed(waiting, *(results[-1] if shards > 1 else ()))
+    sums = halves_summed(waiting, (), results[-2] if shards > 2 else ())
     results.append([passed_along(block, "section", -1) for block in sums])
     for step, blocks in enumerate(results):
         if len(blocks) > 1:

time: 92.6 us -> 88.2 us (0.952)
  starting transfers between devices: 31.1 us -> 27.8 us
  waiting for transfers between devices: 36.3 us -> 35.3 us
    ppermute x10, waiting for transfers between devices: 15 us -> 11.2 us  [passed_along(): lax.ppermute(block, axis, [((i - distance) % len(devices), i) for i in de...]
    ppermute x10, starting transfers between devices: 12.8 us -> 9.42 us  [passed_along(): lax.ppermute(block, axis, [((i - distance) % len(devices), i) for i in de...]
    ppermute x5, waiting for transfers between devices: 7.89 us -> 10.7 us  [swapped(): return lax.ppermute(block, axis, pairs)]
  transfers between devices with their start and end apart: 19 -> 19, of which waited for: 7 -> 8; matrix products, arithmetic and copies ran while one was open for 5% -> 5% of each run, Pallas kernels for 9% -> 12%
where the time goes in v8:
time: 88.2 us; the launch traced here: 87.7 us
  waiting for transfers between devices  35.3 us (40%)
  starting transfers between devices  27.8 us (32%)
  Pallas kernels  12.5 us (14%)
  local copies, waits for them, and re-layouts  7.69 us (9%)
  other arithmetic  4.19 us (5%)
    ppermute x4, waiting for transfers between devices, moved(): lax.ppermute(block, axis, [(i, i + by) for i in range(size) if 0 <= i + b...  13.4 us
    ppermute x4, starting transfers between devices, moved(): lax.ppermute(block, axis, [(i, i + by) for i in range(size) if 0 <= i + b...  12 us
    ppermute x10, waiting for transfers between devices, passed_along(): lax.ppermute(block, axis, [((i - distance) % len(devices), i) for i in de...  11.2 us
    ppermute x5, waiting for transfers between devices, swapped(): return lax.ppermute(block, axis, pairs)  10.7 us
    pallas_call x4, Pallas kernels, project(): pl.pallas_call(functools.partial(project_kernel, [len(block) for block in...  10.1 us
    ppermute x10, starting transfers between devices, passed_along(): lax.ppermute(block, axis, [((i - distance) % len(devices), i) for i in de...  9.42 us
    ppermute x5, starting transfers between devices, swapped(): return lax.ppermute(block, axis, pairs)  6.32 us
    unnamed x26, local copies, waits for them, and re-layouts  6.12 us
  transfers between devices with their start and end apart: 19, of which 8 were waited for; matrix products, arithmetic and copies ran while one was open for 5% of the time, Pallas kernels for 12%

profile of v8, /device:TPU:0, one launch (start us, length us, event | category | flops | bytes accessed | tf_op | source)
XLA Modules:
  0.0 87.7 jit_solution(4543300751266549995)
XLA Ops:
  0.0 1.0 %pad_maximum_fusion.refs_2_ = bf16[128,1024]{1,0:T(8,128)(2,1)S(1)} fusion(bf16[128,512]{1,0:T(8,128)(2,1)} %bitcast.28, bf16[128,512]{1,0:T(8,128)(2,1)} %bitcast.29), kind=kLoop, calls=%fused_computation.6 | loop fusion | flops 524288 | bytes 524288 | tf_op jit(solution)/shard_map/concatenate | solution.py:248
  1.0 4.9 %collective-permute-start.1 = (bf16[128,1024]{1,0:T(8,128)(2,1)S(1)}, bf16[128,1024]{1,0:T(8,128)(2,1)S(1)}, u32[]{:S(2)}, u32[]{:S(2)}) collective-permute-start(bf16[128,1024]{1,0:T(8,128)(2,1)S(1)} %pad_maximum_fusion.refs_2_), channel_id=1, source_target_pairs={{0,2},{2,4},{4,6},{1,3},{3,5},{5,7},{8,10},{10,12},{12,14},{9,11},... | collective-permute-start | bytes 786440 | tf_op jit(solution)/shard_map/ppermute | solution.py:208
  6.0 4.5 %collective-permute-start = (bf16[48,1024]{1,0:T(8,128)(2,1)S(1)}, bf16[48,1024]{1,0:T(8,128)(2,1)S(1)}, u32[]{:S(2)}, u32[]{:S(2)}) collective-permute-start(bf16[48,1024]{1,0:T(8,128)(2,1)S(1)} %slice.4), channel_id=1, source_target_pairs={{0,4},{2,6},{1,5},{3,7},{8,12},{10,14},{9,13},{11,15},{16,20},{18,... | collective-permute-start | bytes 294920 | tf_op jit(solution)/shard_map/ppermute | solution.py:208
  10.5 0.8 pad_dynamic-slice_fusion
  11.2 0.7 fusion.5
  11.9 0.1 fusion.4.refs_3_
  12.0 0.0 copy-start.7
  12.0 0.9 %copy-done.7 = bf16[1,128,1024]{2,1,0:T(8,128)(2,1)S(1)} copy-done((bf16[1,128,1024]{2,1,0:T(8,128)(2,1)S(1)}, bf16[1,128,1024]{2,1,0:T(8,128)(2,1)}, u32[]{:S(2)}) %copy-start.7) | copy-done | bytes 262168
  13.0 0.9 %copy-done.8 = bf16[1,128,1024]{2,1,0:T(8,128)(2,1)S(1)} copy-done((bf16[1,128,1024]{2,1,0:T(8,128)(2,1)S(1)}, bf16[1,128,1024]{2,1,0:T(8,128)(2,1)}, u32[]{:S(2)}) %copy-start.8) | copy-done | bytes 262168
  13.9 0.1 shard_map.82
  14.0 0.0 collective-permute-done.refs_4_
  14.0 0.0 collective-permute-done.1.refs_5_
  14.0 0.0 copy-start
  14.0 2.2 %shard_map.83 = (bf16[128,1024]{1,0:T(8,128)(2,1)S(1)}, f32[128,1024]{1,0:T(8,128)S(1)}, bf16[48,1024]{1,0:T(8,128)(2,1)S(1)}, bf16[128,1024]{1,0:T(8,128)(2,1)S(1)}) custom-call(bf16[1024,128]{1,0:T(8,128)(2,1)S(1)} %get-tuple-element.33.refs_0_, bf16[1024,128]{1,0:T(8,128)(2,1)S(1)} %get-tuple-element.34.refs_1_, ...), custom_call_target="tpu_custom_call" | custom-call | flops 478150656 | bytes 1048576 | tf_op jit(solution)/shard_map/pallas_call | solution.py:100
  16.3 1.3 %collective-permute-start.2 = (bf16[128,1024]{1,0:T(8,128)(2,1)S(1)}, bf16[128,1024]{1,0:T(8,128)(2,1)S(1)}, u32[]{:S(2)}, u32[]{:S(2)}) collective-permute-start(bf16[128,1024]{1,0:T(8,128)(2,1)S(1)} %get-tuple-element.37), channel_id=1, source_target_pairs={{2,0},{4,2},{6,4},{3,1},{5,3},{7,5},{10,8},{12,10},{14,12},{11,9},... | collective-permute-start | bytes 786440 | tf_op jit(solution)/shard_map/ppermute | solution.py:208
  17.6 1.3 %collective-permute-start.3 = (bf16[48,1024]{1,0:T(8,128)(2,1)S(1)}, bf16[48,1024]{1,0:T(8,128)(2,1)S(1)}, u32[]{:S(2)}, u32[]{:S(2)}) collective-permute-start(bf16[48,1024]{1,0:T(8,128)(2,1)S(1)} %get-tuple-element.38), channel_id=1, source_target_pairs={{4,0},{6,2},{5,1},{7,3},{12,8},{14,10},{13,9},{15,11},{20,16},{22,... | collective-permute-start | bytes 294920 | tf_op jit(solution)/shard_map/ppermute | solution.py:208
  18.9 13.4 %collective-permute-done.3.refs_1_ = bf16[48,1024]{1,0:T(8,128)(2,1)S(1)} collective-permute-done((bf16[48,1024]{1,0:T(8,128)(2,1)S(1)}, bf16[48,1024]{1,0:T(8,128)(2,1)S(1)}, u32[]{:S(2)}, u32[]{:S(2)}) %collective-permute-start.3) | collective-permute-done | bytes 98336 | tf_op jit(solution)/shard_map/ppermute | solution.py:208
  32.3 0.0 collective-permute-done.2.refs_0_
  32.3 0.1 shard_map.84.refs_0_
  32.4 0.1 collective-permute-start.6
  32.5 1.5 %collective-permute-start.7 = (bf16[128,2048]{1,0:T(8,128)(2,1)S(1)}, bf16[128,2048]{1,0:T(8,128)(2,1)}, u32[]{:S(2)}, u32[]{:S(2)}) collective-permute-start(bf16[128,2048]{1,0:T(8,128)(2,1)S(1)} %shard_map.84.refs_0_), channel_id=1, source_target_pairs={{2,4},{4,2},{3,5},{5,3},{10,12},{12,10},{11,13},{13,11},{18,20},{2... | collective-permute-start | bytes 1572872 | tf_op jit(solution)/shard_map/ppermute | solution.py:215
  33.9 1.3 %copy-done.1 = bf16[1,1344,512]{2,1,0:T(8,128)(2,1)S(1)} copy-done((bf16[1,1344,512]{2,1,0:T(8,128)(2,1)S(1)}, bf16[1,1344,512]{2,1,0:T(8,128)(2,1)}, u32[]{:S(2)}) %copy-start.1) | copy-done | bytes 1376280
  35.3 1.3 %copy-done.4 = bf16[1,1344,512]{2,1,0:T(8,128)(2,1)S(1)} copy-done((bf16[1,1344,512]{2,1,0:T(8,128)(2,1)S(1)}, bf16[1,1344,512]{2,1,0:T(8,128)(2,1)}, u32[]{:S(2)}) %copy-start.4) | copy-done | bytes 1376280
  36.6 2.0 %shard_map.85 = (f32[672,128]{1,0:T(8,128)S(1)}, bf16[672,128]{1,0:T(8,128)(2,1)S(1)}) custom-call(s32[1]{0:T(128)} %bitcast.core_ref, bf16[128,2048]{1,0:T(8,128)(2,1)S(1)} %shard_map.84.refs_0_, bf16[1344,1024]{1,0:T(8,128)(2,1)S(1)} %bitcast.14, bf16[1344,512]{1,0:T(8,128)(2,1)S(1)} %bitcast.18, bf16[1344,512]{1,0:T(8,128)(2,1)S(1)} %bitcast.22), custom_call_target="tpu_custom_call" | custom-call | flops 704643072 | bytes 6537216 | tf_op jit(solution)/shard_map/pallas_call | solution.py:187
  38.6 0.1 collective-permute-start.4
  38.7 4.9 %collective-permute-done.6.refs_0_ = bf16[128,2048]{1,0:T(8,128)(2,1)} collective-permute-done((bf16[128,2048]{1,0:T(8,128)(2,1)S(1)}, bf16[128,2048]{1,0:T(8,128)(2,1)}, u32[]{:S(2)}, u32[]{:S(2)}) %collective-permute-start.6) | collective-permute-done | bytes 524320 | tf_op jit(solution)/shard_map/ppermute | solution.py:215
  43.6 1.4 %collective-permute-start.10 = (bf16[128,2048]{1,0:T(8,128)(2,1)}, bf16[128,2048]{1,0:T(8,128)(2,1)}, u32[]{:S(2)}, u32[]{:S(2)}) collective-permute-start(bf16[128,2048]{1,0:T(8,128)(2,1)} %collective-permute-done.6.refs_0_), channel_id=1, source_target_pairs={{2,4},{4,2},{3,5},{5,3},{10,12},{12,10},{11,13},{13,11},{18,20},{2... | collective-permute-start | bytes 1572872 | tf_op jit(solution)/shard_map/ppermute | solution.py:215
  45.0 0.0 collective-permute-done.7.refs_1_
  45.0 1.6 %collective-permute-start.9 = (bf16[128,2048]{1,0:T(8,128)(2,1)}, bf16[128,2048]{1,0:T(8,128)(2,1)}, u32[]{:S(2)}, u32[]{:S(2)}) collective-permute-start(bf16[128,2048]{1,0:T(8,128)(2,1)} %collective-permute-done.7.refs_1_), channel_id=1, source_target_pairs={{0,2},{2,0},{4,6},{6,4},{1,3},{3,1},{5,7},{7,5},{8,10},{10,8},{12,... | collective-permute-start | bytes 1572872 | tf_op jit(solution)/shard_map/ppermute | solution.py:215
  46.6 0.0 collective-permute-done.4
  46.6 0.7 add_convert_fusion.4
  47.3 4.1 %shard_map.86 = (f32[672,128]{1,0:T(8,128)S(1)}, f32[672,128]{1,0:T(8,128)S(1)}, bf16[672,128]{1,0:T(8,128)(2,1)S(1)}, bf16[672,128]{1,0:T(8,128)(2,1)}) custom-call(s32[1]{0:T(128)} %bitcast.core_ref, bf16[128,2048]{1,0:T(8,128)(2,1)} %collective-permute-done.6.refs_0_, bf16[128,2048]{1,0:T(8,128)(2,1)} %collective-permute-done.7.refs_1_, ...), custom_call_target="tpu_custom_call" | custom-call | flops 1409286144 | bytes 7569408 | tf_op jit(solution)/shard_map/pallas_call | solution.py:187
  51.4 0.7 copy-done.9
  52.1 0.0 collective-permute-start.8
  52.1 2.5 %collective-permute-start.5 = (bf16[672,128]{1,0:T(8,128)(2,1)}, bf16[672,128]{1,0:T(8,128)(2,1)S(1)}, u32[]{:S(2)}, u32[]{:S(2)}) collective-permute-start(bf16[672,128]{1,0:T(8,128)(2,1)} %add_convert_fusion.4), channel_id=1, source_target_pairs={{8,0},{16,8},{24,16},{0,24},{9,1},{17,9},{25,17},{1,25},{10,2},{18... | collective-permute-start | bytes 516104 | tf_op jit(solution)/shard_map/ppermute | solution.py:224
  54.6 0.2 collective-permute-start.12
  54.8 0.0 collective-permute-done.8
  54.8 0.0 collective-permute-done.10
  54.8 3.0 %collective-permute-done.9 = bf16[128,2048]{1,0:T(8,128)(2,1)} collective-permute-done((bf16[128,2048]{1,0:T(8,128)(2,1)}, bf16[128,2048]{1,0:T(8,128)(2,1)}, u32[]{:S(2)}, u32[]{:S(2)}) %collective-permute-start.9) | collective-permute-done | bytes 524320 | tf_op jit(solution)/shard_map/ppermute | solution.py:215
  57.8 1.7 %collective-permute-start.14 = (bf16[128,2048]{1,0:T(8,128)(2,1)}, bf16[128,2048]{1,0:T(8,128)(2,1)S(1)}, u32[]{:S(2)}, u32[]{:S(2)}) collective-permute-start(bf16[128,2048]{1,0:T(8,128)(2,1)} %collective-permute-done.10), channel_id=1, source_target_pairs={{0,2},{2,0},{4,6},{6,4},{1,3},{3,1},{5,7},{7,5},{8,10},{10,8},{12,... | collective-permute-start | bytes 1572872 | tf_op jit(solution)/shard_map/ppermute | solution.py:215
  59.5 1.1 %broadcast_select_fusion.refs_0_ = bf16[128,2048]{1,0:T(8,128)(2,1)S(1)} fusion(bf16[128,2048]{1,0:T(8,128)(2,1)} %collective-permute-done.10, bf16[128,2048]{1,0:T(8,128)(2,1)} %collective-permute-done.9, pred[]{:T(512)S(6)} %eq.32), kind=kLoop, calls=%fused_computation | loop fusion | flops 262144 | bytes 1572865 | tf_op jit(solution)/shard_map/jit(_where)/select_n | solution.py:306
  60.6 1.0 %add_convert_fusion.3 = bf16[672,128]{1,0:T(8,128)(2,1)S(1)} fusion(f32[672,128]{1,0:T(8,128)S(1)} %get-tuple-element.43, bf16[672,128]{1,0:T(8,128)(2,1)} %collective-permute-done.8), kind=kLoop, calls=%fused_computation.4 | loop fusion | flops 258048 | bytes 688128 | tf_op jit(solution)/shard_map/convert_element_type | solution.py:285
  61.6 0.0 collective-permute-done.12
  61.7 0.0 copy-start.11
  61.7 2.0 %shard_map.87 = (f32[672,128]{1,0:T(8,128)S(1)}, bf16[672,128]{1,0:T(8,128)(2,1)S(1)}) custom-call(s32[1]{0:T(128)} %bitcast.core_ref, bf16[128,2048]{1,0:T(8,128)(2,1)S(1)} %broadcast_select_fusion.refs_0_, bf16[1344,1024]{1,0:T(8,128)(2,1)S(1)} %bitcast.16, bf16[1344,512]{1,0:T(8,128)(2,1)S(1)} %bitcast.20, bf16[1344,512]{1,0:T(8,128)(2,1)S(1)} %bitcast.24), custom_call_target="tpu_custom_call" | custom-call | flops 704643072 | bytes 6537216 | tf_op jit(solution)/shard_map/pallas_call | solution.py:187
  63.7 0.1 collective-permute-start.15
  63.8 2.5 %collective-permute-start.11 = (bf16[672,128]{1,0:T(8,128)(2,1)S(1)}, bf16[672,128]{1,0:T(8,128)(2,1)S(1)}, u32[]{:S(2)}, u32[]{:S(2)}) collective-permute-start(bf16[672,128]{1,0:T(8,128)(2,1)S(1)} %add_convert_fusion.3), channel_id=1, source_target_pairs={{8,0},{16,8},{24,16},{0,24},{9,1},{17,9},{25,17},{1,25},{10,2},{18... | collective-permute-start | bytes 516104 | tf_op jit(solution)/shard_map/ppermute | solution.py:224
  66.3 0.5 collective-permute-start.13
  66.8 0.0 collective-permute-done.15
  66.8 2.8 %collective-permute-done.14.refs_0_ = bf16[128,2048]{1,0:T(8,128)(2,1)S(1)} collective-permute-done((bf16[128,2048]{1,0:T(8,128)(2,1)}, bf16[128,2048]{1,0:T(8,128)(2,1)S(1)}, u32[]{:S(2)}, u32[]{:S(2)}) %collective-permute-start.14) | collective-permute-done | bytes 524320 | tf_op jit(solution)/shard_map/ppermute | solution.py:215
  69.7 0.1 add_convert_fusion.1
  69.7 2.0 %shard_map.88 = (f32[672,128]{1,0:T(8,128)S(1)}, bf16[672,128]{1,0:T(8,128)(2,1)S(1)}) custom-call(s32[1]{0:T(128)} %bitcast.core_ref, bf16[128,2048]{1,0:T(8,128)(2,1)S(1)} %collective-permute-done.14.refs_0_, bf16[1344,1024]{1,0:T(8,128)(2,1)S(1)} %bitcast.17, bf16[1344,512]{1,0:T(8,128)(2,1)S(1)} %bitcast.21, bf16[1344,512]{1,0:T(8,128)(2,1)S(1)} %bitcast.25), custom_call_target="tpu_custom_call" | custom-call | flops 704643072 | bytes 6537216 | tf_op jit(solution)/shard_map/pallas_call | solution.py:187
  71.7 0.0 copy-start.12
  71.7 2.5 %collective-permute-done.13 = bf16[672,128]{1,0:T(8,128)(2,1)S(1)} collective-permute-done((bf16[672,128]{1,0:T(8,128)(2,1)S(1)}, bf16[672,128]{1,0:T(8,128)(2,1)S(1)}, u32[]{:S(2)}, u32[]{:S(2)}) %collective-permute-start.13) | collective-permute-done | bytes 172064 | tf_op jit(solution)/shard_map/ppermute | solution.py:224
  74.3 0.0 collective-permute-start.16
  74.3 1.4 %collective-permute-done.16 = bf16[672,128]{1,0:T(8,128)(2,1)S(1)} collective-permute-done((bf16[672,128]{1,0:T(8,128)(2,1)S(1)}, bf16[672,128]{1,0:T(8,128)(2,1)S(1)}, u32[]{:S(2)}, u32[]{:S(2)}) %collective-permute-start.16) | collective-permute-done | bytes 172064 | tf_op jit(solution)/shard_map/ppermute | solution.py:224
  75.7 3.4 %collective-permute-start.17 = (bf16[672,128]{1,0:T(8,128)(2,1)S(1)}, bf16[672,128]{1,0:T(8,128)(2,1)S(1)}, u32[]{:S(2)}, u32[]{:S(2)}) collective-permute-start(bf16[672,128]{1,0:T(8,128)(2,1)S(1)} %add_convert_fusion), channel_id=1, source_target_pairs={{8,0},{16,8},{24,16},{0,24},{9,1},{17,9},{25,17},{1,25},{10,2},{18... | collective-permute-start | bytes 516104 | tf_op jit(solution)/shard_map/ppermute | solution.py:224
  79.2 0.2 collective-permute-start.18
  79.4 4.5 %collective-permute-done.17 = bf16[672,128]{1,0:T(8,128)(2,1)S(1)} collective-permute-done((bf16[672,128]{1,0:T(8,128)(2,1)S(1)}, bf16[672,128]{1,0:T(8,128)(2,1)S(1)}, u32[]{:S(2)}, u32[]{:S(2)}) %collective-permute-start.17) | collective-permute-done | bytes 172064 | tf_op jit(solution)/shard_map/ppermute | solution.py:224
  83.8 0.1 select_dynamic-update-slice_fusion.1
  83.9 2.8 %collective-permute-done.18 = bf16[672,128]{1,0:T(8,128)(2,1)S(1)} collective-permute-done((bf16[672,128]{1,0:T(8,128)(2,1)S(1)}, bf16[672,128]{1,0:T(8,128)(2,1)S(1)}, u32[]{:S(2)}, u32[]{:S(2)}) %collective-permute-start.18) | collective-permute-done | bytes 172064 | tf_op jit(solution)/shard_map/ppermute | solution.py:224
  86.8 0.1 select_dynamic-update-slice_fusion
  86.9 0.0 copy-start.10
  86.9 0.8 copy-done.10
  (24 shorter events, 0.3 us)
Async XLA Ops:
  1.0 13.0 %collective-permute-start.1 = (bf16[128,1024]{1,0:T(8,128)(2,1)S(1)}, bf16[128,1024]{1,0:T(8,128)(2,1)S(1)}, u32[]{:S(2)}, u32[]{:S(2)}) collective-permute-start(bf16[128,1024]{1,0:T(8,128)(2,1)S(1)} %pad_maximum_fusion.refs_2_), channel_id=1, source_target_pairs={{0,2},{2,4},{4,6},{1,3},{3,5},{5,7},{8,10},{10,12},{12,14},{9,11},... | collective-permute-start | bytes 786440 | tf_op jit(solution)/shard_map/ppermute | solution.py:208
  6.0 8.1 %collective-permute-start = (bf16[48,1024]{1,0:T(8,128)(2,1)S(1)}, bf16[48,1024]{1,0:T(8,128)(2,1)S(1)}, u32[]{:S(2)}, u32[]{:S(2)}) collective-permute-start(bf16[48,1024]{1,0:T(8,128)(2,1)S(1)} %slice.4), channel_id=1, source_target_pairs={{0,4},{2,6},{1,5},{3,7},{8,12},{10,14},{9,13},{11,15},{16,20},{18,... | collective-permute-start | bytes 294920 | tf_op jit(solution)/shard_map/ppermute | solution.py:208
  12.0 1.0 %copy-start.7 = (bf16[1,128,1024]{2,1,0:T(8,128)(2,1)S(1)}, bf16[1,128,1024]{2,1,0:T(8,128)(2,1)}, u32[]{:S(2)}) copy-start(bf16[1,128,1024]{2,1,0:T(8,128)(2,1)} %param.8) | copy-start | bytes 786436
  13.0 0.9 %copy-start.8 = (bf16[1,128,1024]{2,1,0:T(8,128)(2,1)S(1)}, bf16[1,128,1024]{2,1,0:T(8,128)(2,1)}, u32[]{:S(2)}) copy-start(bf16[1,128,1024]{2,1,0:T(8,128)(2,1)} %param.11) | copy-start | bytes 786436
  14.0 19.9 %copy-start = (bf16[1,1344,1024]{2,1,0:T(8,128)(2,1)S(1)}, bf16[1,1344,1024]{2,1,0:T(8,128)(2,1)}, u32[]{:S(2)}) copy-start(bf16[1,1344,1024]{2,1,0:T(8,128)(2,1)} %param.12) | copy-start | bytes 8257540
  16.3 16.0 %collective-permute-start.2 = (bf16[128,1024]{1,0:T(8,128)(2,1)S(1)}, bf16[128,1024]{1,0:T(8,128)(2,1)S(1)}, u32[]{:S(2)}, u32[]{:S(2)}) collective-permute-start(bf16[128,1024]{1,0:T(8,128)(2,1)S(1)} %get-tuple-element.37), channel_id=1, source_target_pairs={{2,0},{4,2},{6,4},{3,1},{5,3},{7,5},{10,8},{12,10},{14,12},{11,9},... | collective-permute-start | bytes 786440 | tf_op jit(solution)/shard_map/ppermute | solution.py:208
  17.6 14.7 %collective-permute-start.3 = (bf16[48,1024]{1,0:T(8,128)(2,1)S(1)}, bf16[48,1024]{1,0:T(8,128)(2,1)S(1)}, u32[]{:S(2)}, u32[]{:S(2)}) collective-permute-start(bf16[48,1024]{1,0:T(8,128)(2,1)S(1)} %get-tuple-element.38), channel_id=1, source_target_pairs={{4,0},{6,2},{5,1},{7,3},{12,8},{14,10},{13,9},{15,11},{20,16},{22,... | collective-permute-start | bytes 294920 | tf_op jit(solution)/shard_map/ppermute | solution.py:208
  32.4 11.2 %collective-permute-start.6 = (bf16[128,2048]{1,0:T(8,128)(2,1)S(1)}, bf16[128,2048]{1,0:T(8,128)(2,1)}, u32[]{:S(2)}, u32[]{:S(2)}) collective-permute-start(bf16[128,2048]{1,0:T(8,128)(2,1)S(1)} %shard_map.84.refs_0_), channel_id=1, source_target_pairs={{0,2},{2,0},{4,6},{6,4},{1,3},{3,1},{5,7},{7,5},{8,10},{10,8},{12,... | collective-permute-start | bytes 1572872 | tf_op jit(solution)/shard_map/ppermute | solution.py:215
  32.5 12.6 %collective-permute-start.7 = (bf16[128,2048]{1,0:T(8,128)(2,1)S(1)}, bf16[128,2048]{1,0:T(8,128)(2,1)}, u32[]{:S(2)}, u32[]{:S(2)}) collective-permute-start(bf16[128,2048]{1,0:T(8,128)(2,1)S(1)} %shard_map.84.refs_0_), channel_id=1, source_target_pairs={{2,4},{4,2},{3,5},{5,3},{10,12},{12,10},{11,13},{13,11},{18,20},{2... | collective-permute-start | bytes 1572872 | tf_op jit(solution)/shard_map/ppermute | solution.py:215
  33.9 1.3 %copy-start.1 = (bf16[1,1344,512]{2,1,0:T(8,128)(2,1)S(1)}, bf16[1,1344,512]{2,1,0:T(8,128)(2,1)}, u32[]{:S(2)}) copy-start(bf16[1,1344,512]{2,1,0:T(8,128)(2,1)} %param.13) | copy-start | bytes 4128772
  35.3 1.3 %copy-start.4 = (bf16[1,1344,512]{2,1,0:T(8,128)(2,1)S(1)}, bf16[1,1344,512]{2,1,0:T(8,128)(2,1)}, u32[]{:S(2)}) copy-start(bf16[1,1344,512]{2,1,0:T(8,128)(2,1)} %param.14) | copy-start | bytes 4128772
  36.6 10.7 %copy-start.2 = (bf16[1,1344,512]{2,1,0:T(8,128)(2,1)S(1)}, bf16[1,1344,512]{2,1,0:T(8,128)(2,1)}, u32[]{:S(2)}) copy-start(bf16[1,1344,512]{2,1,0:T(8,128)(2,1)} %param.13) | copy-start | bytes 4128772
  36.6 10.7 %copy-start.5 = (bf16[1,1344,512]{2,1,0:T(8,128)(2,1)S(1)}, bf16[1,1344,512]{2,1,0:T(8,128)(2,1)}, u32[]{:S(2)}) copy-start(bf16[1,1344,512]{2,1,0:T(8,128)(2,1)} %param.14) | copy-start | bytes 4128772
  38.6 8.0 %collective-permute-start.4 = (bf16[672,128]{1,0:T(8,128)(2,1)S(1)}, bf16[672,128]{1,0:T(8,128)(2,1)S(1)}, u32[]{:S(2)}, u32[]{:S(2)}) collective-permute-start(bf16[672,128]{1,0:T(8,128)(2,1)S(1)} %get-tuple-element.40), channel_id=1, source_target_pairs={{1,0},{0,1},{3,2},{2,3},{5,4},{4,5},{7,6},{6,7},{9,8},{8,9},{11,10... | collective-permute-start | bytes 516104 | tf_op jit(solution)/shard_map/ppermute | solution.py:224
  43.6 11.2 %collective-permute-start.10 = (bf16[128,2048]{1,0:T(8,128)(2,1)}, bf16[128,2048]{1,0:T(8,128)(2,1)}, u32[]{:S(2)}, u32[]{:S(2)}) collective-permute-start(bf16[128,2048]{1,0:T(8,128)(2,1)} %collective-permute-done.6.refs_0_), channel_id=1, source_target_pairs={{2,4},{4,2},{3,5},{5,3},{10,12},{12,10},{11,13},{13,11},{18,20},{2... | collective-permute-start | bytes 1572872 | tf_op jit(solution)/shard_map/ppermute | solution.py:215
  45.0 12.8 %collective-permute-start.9 = (bf16[128,2048]{1,0:T(8,128)(2,1)}, bf16[128,2048]{1,0:T(8,128)(2,1)}, u32[]{:S(2)}, u32[]{:S(2)}) collective-permute-start(bf16[128,2048]{1,0:T(8,128)(2,1)} %collective-permute-done.7.refs_1_), channel_id=1, source_target_pairs={{0,2},{2,0},{4,6},{6,4},{1,3},{3,1},{5,7},{7,5},{8,10},{10,8},{12,... | collective-permute-start | bytes 1572872 | tf_op jit(solution)/shard_map/ppermute | solution.py:215
  51.4 0.7 copy-start.9
  52.1 2.7 %collective-permute-start.8 = (bf16[672,128]{1,0:T(8,128)(2,1)}, bf16[672,128]{1,0:T(8,128)(2,1)}, u32[]{:S(2)}, u32[]{:S(2)}) collective-permute-start(bf16[672,128]{1,0:T(8,128)(2,1)} %get-tuple-element.44), channel_id=1, source_target_pairs={{1,0},{0,1},{3,2},{2,3},{5,4},{4,5},{7,6},{6,7},{9,8},{8,9},{11,10... | collective-permute-start | bytes 516104 | tf_op jit(solution)/shard_map/ppermute | solution.py:224
  52.1 9.6 %collective-permute-start.5 = (bf16[672,128]{1,0:T(8,128)(2,1)}, bf16[672,128]{1,0:T(8,128)(2,1)S(1)}, u32[]{:S(2)}, u32[]{:S(2)}) collective-permute-start(bf16[672,128]{1,0:T(8,128)(2,1)} %add_convert_fusion.4), channel_id=1, source_target_pairs={{8,0},{16,8},{24,16},{0,24},{9,1},{17,9},{25,17},{1,25},{10,2},{18... | collective-permute-start | bytes 516104 | tf_op jit(solution)/shard_map/ppermute | solution.py:224
  54.6 7.1 %copy-start.3 = (bf16[1,1344,512]{2,1,0:T(8,128)(2,1)S(1)}, bf16[1,1344,512]{2,1,0:T(8,128)(2,1)}, u32[]{:S(2)}) copy-start(bf16[1,1344,512]{2,1,0:T(8,128)(2,1)} %param.13) | copy-start | bytes 4128772
  54.6 7.1 %copy-start.6 = (bf16[1,1344,512]{2,1,0:T(8,128)(2,1)S(1)}, bf16[1,1344,512]{2,1,0:T(8,128)(2,1)}, u32[]{:S(2)}) copy-start(bf16[1,1344,512]{2,1,0:T(8,128)(2,1)} %param.14) | copy-start | bytes 4128772
  54.6 7.0 %collective-permute-start.12 = (bf16[672,128]{1,0:T(8,128)(2,1)}, bf16[672,128]{1,0:T(8,128)(2,1)S(1)}, u32[]{:S(2)}, u32[]{:S(2)}) collective-permute-start(bf16[672,128]{1,0:T(8,128)(2,1)} %copy-done.9), channel_id=1, source_target_pairs={{1,0},{0,1},{3,2},{2,3},{5,4},{4,5},{7,6},{6,7},{9,8},{8,9},{11,10... | collective-permute-start | bytes 516104 | tf_op jit(solution)/shard_map/ppermute | solution.py:224
  57.8 11.9 %collective-permute-start.14 = (bf16[128,2048]{1,0:T(8,128)(2,1)}, bf16[128,2048]{1,0:T(8,128)(2,1)S(1)}, u32[]{:S(2)}, u32[]{:S(2)}) collective-permute-start(bf16[128,2048]{1,0:T(8,128)(2,1)} %collective-permute-done.10), channel_id=1, source_target_pairs={{0,2},{2,0},{4,6},{6,4},{1,3},{3,1},{5,7},{7,5},{8,10},{10,8},{12,... | collective-permute-start | bytes 1572872 | tf_op jit(solution)/shard_map/ppermute | solution.py:215
  61.7 2.0 %copy-start.11 = (bf16[672,128]{1,0:T(8,128)(2,1)}, bf16[672,128]{1,0:T(8,128)(2,1)S(1)}, u32[]{:S(2)}) copy-start(bf16[672,128]{1,0:T(8,128)(2,1)S(1)} %collective-permute-done.5) | copy-start | bytes 516100
  63.7 3.1 %collective-permute-start.15 = (bf16[672,128]{1,0:T(8,128)(2,1)S(1)}, bf16[672,128]{1,0:T(8,128)(2,1)S(1)}, u32[]{:S(2)}, u32[]{:S(2)}) collective-permute-start(bf16[672,128]{1,0:T(8,128)(2,1)S(1)} %get-tuple-element.51), channel_id=1, source_target_pairs={{1,0},{0,1},{3,2},{2,3},{5,4},{4,5},{7,6},{6,7},{9,8},{8,9},{11,10... | collective-permute-start | bytes 516104 | tf_op jit(solution)/shard_map/ppermute | solution.py:224
  63.8 7.9 %collective-permute-start.11 = (bf16[672,128]{1,0:T(8,128)(2,1)S(1)}, bf16[672,128]{1,0:T(8,128)(2,1)S(1)}, u32[]{:S(2)}, u32[]{:S(2)}) collective-permute-start(bf16[672,128]{1,0:T(8,128)(2,1)S(1)} %add_convert_fusion.3), channel_id=1, source_target_pairs={{8,0},{16,8},{24,16},{0,24},{9,1},{17,9},{25,17},{1,25},{10,2},{18... | collective-permute-start | bytes 516104 | tf_op jit(solution)/shard_map/ppermute | solution.py:224
  66.3 8.0 %collective-permute-start.13 = (bf16[672,128]{1,0:T(8,128)(2,1)S(1)}, bf16[672,128]{1,0:T(8,128)(2,1)S(1)}, u32[]{:S(2)}, u32[]{:S(2)}) collective-permute-start(bf16[672,128]{1,0:T(8,128)(2,1)S(1)} %add_convert_fusion.2), channel_id=1, source_target_pairs={{8,0},{16,8},{24,16},{0,24},{9,1},{17,9},{25,17},{1,25},{10,2},{18... | collective-permute-start | bytes 516104 | tf_op jit(solution)/shard_map/ppermute | solution.py:224
  71.7 7.4 %copy-start.12 = (bf16[672,128]{1,0:T(8,128)(2,1)S(1)}, bf16[672,128]{1,0:T(8,128)(2,1)}, u32[]{:S(2)}) copy-start(bf16[672,128]{1,0:T(8,128)(2,1)} %copy-done.11) | copy-start | bytes 516100
  74.3 1.4 %collective-permute-start.16 = (bf16[672,128]{1,0:T(8,128)(2,1)S(1)}, bf16[672,128]{1,0:T(8,128)(2,1)S(1)}, u32[]{:S(2)}, u32[]{:S(2)}) collective-permute-start(bf16[672,128]{1,0:T(8,128)(2,1)S(1)} %get-tuple-element.56), channel_id=1, source_target_pairs={{1,0},{0,1},{3,2},{2,3},{5,4},{4,5},{7,6},{6,7},{9,8},{8,9},{11,10... | collective-permute-start | bytes 516104 | tf_op jit(solution)/shard_map/ppermute | solution.py:224
  75.7 8.1 %collective-permute-start.17 = (bf16[672,128]{1,0:T(8,128)(2,1)S(1)}, bf16[672,128]{1,0:T(8,128)(2,1)S(1)}, u32[]{:S(2)}, u32[]{:S(2)}) collective-permute-start(bf16[672,128]{1,0:T(8,128)(2,1)S(1)} %add_convert_fusion), channel_id=1, source_target_pairs={{8,0},{16,8},{24,16},{0,24},{9,1},{17,9},{25,17},{1,25},{10,2},{18... | collective-permute-start | bytes 516104 | tf_op jit(solution)/shard_map/ppermute | solution.py:224
  79.2 7.5 %collective-permute-start.18 = (bf16[672,128]{1,0:T(8,128)(2,1)S(1)}, bf16[672,128]{1,0:T(8,128)(2,1)S(1)}, u32[]{:S(2)}, u32[]{:S(2)}) collective-permute-start(bf16[672,128]{1,0:T(8,128)(2,1)S(1)} %add_convert_fusion.1), channel_id=1, source_target_pairs={{8,0},{16,8},{24,16},{0,24},{9,1},{17,9},{25,17},{1,25},{10,2},{18... | collective-permute-start | bytes 516104 | tf_op jit(solution)/shard_map/ppermute | solution.py:224
  86.9 0.8 copy-start.10

commit v9 on v8

--- a/solution.py
+++ b/solution.py
@@ -176,7 +176,7 @@
         give_ref[...] = full_ref[other, cols].astype(jnp.bfloat16)
 
 
-def project(blocks, weights, core):
+def project(blocks, weights, core, final):
     width = weights[0].shape[0]
     rows = sum(block[0].shape[0] for block in blocks)
     half = (width // 2, rows // len(blocks))
@@ -196,8 +196,8 @@
         ],
         compiler_params=pltpu.CompilerParams(vmem_limit_bytes=8 * 1024 * 1024),
         cost_estimate=pl.CostEstimate(
-            flops=2 * rows * width * cols,
-            bytes_accessed=2 * width * cols + 6 * width * rows,
+            flops=1 if final else 2 * rows * width * cols,
+            bytes_accessed=1 if final else 2 * width * cols + 6 * width * rows,
             transcendentals=0,
         ),
     )(core, *flat, *weights)
@@ -273,8 +273,8 @@
     weights = (w_query[0], key_weight[0], value_weight[0])
     core = lax.axis_index("mp").astype(jnp.int32)
 
-    def halves_summed(blocks, late, before=()):
-        halves = project([(block,) for block in blocks], weights, core[None])
+    def halves_summed(blocks, late, before=(), final=False):
+        halves = project([(block,) for block in blocks], weights, core[None], final)
         sums = []
         for keep, give in zip(halves[: len(blocks)], halves[len(blocks) :]):
             if before:
@@ -306,7 +306,7 @@
             waiting = [jnp.where(even == (place >= step), came_second, came_first)]
     if shards > 1:
         waiting = after(waiting, *sums)
-    sums = halves_summed(waiting, (), results[-2] if shards > 2 else ())
+    sums = halves_summed(waiting, (), sum(results[-2:], []) if shards > 1 else (), True)
     results.append([passed_along(block, "section", -1) for block in sums])
     for step, blocks in enumerate(results):
         if len(blocks) > 1:

time: 88.2 us -> 88.3 us (level)
  starting transfers between devices: 27.8 us -> 30.1 us
  waiting for transfers between devices: 35.3 us -> 33.1 us
    ppermute x10, starting transfers between devices: 9.42 us -> 11.8 us  [passed_along(): lax.ppermute(block, axis, [((i - distance) % len(devices), i) for i in de...]
    ppermute x10, waiting for transfers between devices: 11.2 us -> 8.96 us  [passed_along(): lax.ppermute(block, axis, [((i - distance) % len(devices), i) for i in de...]
where the time goes in v9:
time: 88.3 us; the launch traced here: 87.8 us
  waiting for transfers between devices  33.1 us (37%)
  starting transfers between devices  30.1 us (34%)
  Pallas kernels  12.5 us (14%)
  local copies, waits for them, and re-layouts  7.69 us (9%)
  other arithmetic  4.19 us (5%)
    ppermute x4, waiting for transfers between devices, moved(): lax.ppermute(block, axis, [(i, i + by) for i in range(size) if 0 <= i + b...  13.4 us
    ppermute x4, starting transfers between devices, moved(): lax.ppermute(block, axis, [(i, i + by) for i in range(size) if 0 <= i + b...  12 us
    ppermute x10, starting transfers between devices, passed_along(): lax.ppermute(block, axis, [((i - distance) % len(devices), i) for i in de...  11.8 us
    ppermute x5, waiting for transfers between devices, swapped(): return lax.ppermute(block, axis, pairs)  10.7 us
    pallas_call x4, Pallas kernels, project(): pl.pallas_call(functools.partial(project_kernel, [len(block) for block in...  10.1 us
    ppermute x10, waiting for transfers between devices, passed_along(): lax.ppermute(block, axis, [((i - distance) % len(devices), i) for i in de...  8.96 us
    ppermute x5, starting transfers between devices, swapped(): return lax.ppermute(block, axis, pairs)  6.32 us
    unnamed x26, local copies, waits for them, and re-layouts  6.12 us
  transfers between devices with their start and end apart: 19, of which 8 were waited for; matrix products, arithmetic and copies ran while one was open for 5% of the time, Pallas kernels for 12%

profile of v9, /device:TPU:0, one launch (start us, length us, event | category | flops | bytes accessed | tf_op | source)
XLA Modules:
  0.0 87.8 jit_solution(5837738733869314697)
XLA Ops:
  0.0 1.0 %pad_maximum_fusion.refs_2_ = bf16[128,1024]{1,0:T(8,128)(2,1)S(1)} fusion(bf16[128,512]{1,0:T(8,128)(2,1)} %bitcast.28, bf16[128,512]{1,0:T(8,128)(2,1)} %bitcast.29), kind=kLoop, calls=%fused_computation.6 | loop fusion | flops 524288 | bytes 524288 | tf_op jit(solution)/shard_map/concatenate | solution.py:248
  1.0 4.9 %collective-permute-start.1 = (bf16[128,1024]{1,0:T(8,128)(2,1)S(1)}, bf16[128,1024]{1,0:T(8,128)(2,1)S(1)}, u32[]{:S(2)}, u32[]{:S(2)}) collective-permute-start(bf16[128,1024]{1,0:T(8,128)(2,1)S(1)} %pad_maximum_fusion.refs_2_), channel_id=1, source_target_pairs={{0,2},{2,4},{4,6},{1,3},{3,5},{5,7},{8,10},{10,12},{12,14},{9,11},... | collective-permute-start | bytes 786440 | tf_op jit(solution)/shard_map/ppermute | solution.py:208
  6.0 4.5 %collective-permute-start = (bf16[48,1024]{1,0:T(8,128)(2,1)S(1)}, bf16[48,1024]{1,0:T(8,128)(2,1)S(1)}, u32[]{:S(2)}, u32[]{:S(2)}) collective-permute-start(bf16[48,1024]{1,0:T(8,128)(2,1)S(1)} %slice.4), channel_id=1, source_target_pairs={{0,4},{2,6},{1,5},{3,7},{8,12},{10,14},{9,13},{11,15},{16,20},{18,... | collective-permute-start | bytes 294920 | tf_op jit(solution)/shard_map/ppermute | solution.py:208
  10.5 0.8 pad_dynamic-slice_fusion
  11.2 0.7 fusion.5
  11.9 0.1 fusion.4.refs_3_
  12.0 0.0 copy-start.7
  12.0 0.9 %copy-done.7 = bf16[1,128,1024]{2,1,0:T(8,128)(2,1)S(1)} copy-done((bf16[1,128,1024]{2,1,0:T(8,128)(2,1)S(1)}, bf16[1,128,1024]{2,1,0:T(8,128)(2,1)}, u32[]{:S(2)}) %copy-start.7) | copy-done | bytes 262168
  13.0 0.9 %copy-done.8 = bf16[1,128,1024]{2,1,0:T(8,128)(2,1)S(1)} copy-done((bf16[1,128,1024]{2,1,0:T(8,128)(2,1)S(1)}, bf16[1,128,1024]{2,1,0:T(8,128)(2,1)}, u32[]{:S(2)}) %copy-start.8) | copy-done | bytes 262168
  13.9 0.1 shard_map.82
  14.0 0.0 collective-permute-done.refs_4_
  14.0 0.0 collective-permute-done.1.refs_5_
  14.0 0.0 copy-start
  14.0 2.2 %shard_map.83 = (bf16[128,1024]{1,0:T(8,128)(2,1)S(1)}, f32[128,1024]{1,0:T(8,128)S(1)}, bf16[48,1024]{1,0:T(8,128)(2,1)S(1)}, bf16[128,1024]{1,0:T(8,128)(2,1)S(1)}) custom-call(bf16[1024,128]{1,0:T(8,128)(2,1)S(1)} %get-tuple-element.33.refs_0_, bf16[1024,128]{1,0:T(8,128)(2,1)S(1)} %get-tuple-element.34.refs_1_, ...), custom_call_target="tpu_custom_call" | custom-call | flops 478150656 | bytes 1048576 | tf_op jit(solution)/shard_map/pallas_call | solution.py:100
  16.3 1.3 %collective-permute-start.2 = (bf16[128,1024]{1,0:T(8,128)(2,1)S(1)}, bf16[128,1024]{1,0:T(8,128)(2,1)S(1)}, u32[]{:S(2)}, u32[]{:S(2)}) collective-permute-start(bf16[128,1024]{1,0:T(8,128)(2,1)S(1)} %get-tuple-element.37), channel_id=1, source_target_pairs={{2,0},{4,2},{6,4},{3,1},{5,3},{7,5},{10,8},{12,10},{14,12},{11,9},... | collective-permute-start | bytes 786440 | tf_op jit(solution)/shard_map/ppermute | solution.py:208
  17.6 1.3 %collective-permute-start.3 = (bf16[48,1024]{1,0:T(8,128)(2,1)S(1)}, bf16[48,1024]{1,0:T(8,128)(2,1)S(1)}, u32[]{:S(2)}, u32[]{:S(2)}) collective-permute-start(bf16[48,1024]{1,0:T(8,128)(2,1)S(1)} %get-tuple-element.38), channel_id=1, source_target_pairs={{4,0},{6,2},{5,1},{7,3},{12,8},{14,10},{13,9},{15,11},{20,16},{22,... | collective-permute-start | bytes 294920 | tf_op jit(solution)/shard_map/ppermute | solution.py:208
  18.9 13.4 %collective-permute-done.3.refs_1_ = bf16[48,1024]{1,0:T(8,128)(2,1)S(1)} collective-permute-done((bf16[48,1024]{1,0:T(8,128)(2,1)S(1)}, bf16[48,1024]{1,0:T(8,128)(2,1)S(1)}, u32[]{:S(2)}, u32[]{:S(2)}) %collective-permute-start.3) | collective-permute-done | bytes 98336 | tf_op jit(solution)/shard_map/ppermute | solution.py:208
  32.3 0.0 collective-permute-done.2.refs_0_
  32.3 0.1 shard_map.84.refs_0_
  32.4 0.1 collective-permute-start.6
  32.5 1.5 %collective-permute-start.7 = (bf16[128,2048]{1,0:T(8,128)(2,1)S(1)}, bf16[128,2048]{1,0:T(8,128)(2,1)}, u32[]{:S(2)}, u32[]{:S(2)}) collective-permute-start(bf16[128,2048]{1,0:T(8,128)(2,1)S(1)} %shard_map.84.refs_0_), channel_id=1, source_target_pairs={{2,4},{4,2},{3,5},{5,3},{10,12},{12,10},{11,13},{13,11},{18,20},{2... | collective-permute-start | bytes 1572872 | tf_op jit(solution)/shard_map/ppermute | solution.py:215
  33.9 1.3 %copy-done.1 = bf16[1,1344,512]{2,1,0:T(8,128)(2,1)S(1)} copy-done((bf16[1,1344,512]{2,1,0:T(8,128)(2,1)S(1)}, bf16[1,1344,512]{2,1,0:T(8,128)(2,1)}, u32[]{:S(2)}) %copy-start.1) | copy-done | bytes 1376280
  35.3 1.3 %copy-done.4 = bf16[1,1344,512]{2,1,0:T(8,128)(2,1)S(1)} copy-done((bf16[1,1344,512]{2,1,0:T(8,128)(2,1)S(1)}, bf16[1,1344,512]{2,1,0:T(8,128)(2,1)}, u32[]{:S(2)}) %copy-start.4) | copy-done | bytes 1376280
  36.6 2.0 %shard_map.85 = (f32[672,128]{1,0:T(8,128)S(1)}, bf16[672,128]{1,0:T(8,128)(2,1)S(1)}) custom-call(s32[1]{0:T(128)} %bitcast.core_ref, bf16[128,2048]{1,0:T(8,128)(2,1)S(1)} %shard_map.84.refs_0_, bf16[1344,1024]{1,0:T(8,128)(2,1)S(1)} %bitcast.14, bf16[1344,512]{1,0:T(8,128)(2,1)S(1)} %bitcast.18, bf16[1344,512]{1,0:T(8,128)(2,1)S(1)} %bitcast.22), custom_call_target="tpu_custom_call" | custom-call | flops 704643072 | bytes 6537216 | tf_op jit(solution)/shard_map/pallas_call | solution.py:187
  38.6 0.1 collective-permute-start.4
  38.7 4.9 %collective-permute-done.6.refs_0_ = bf16[128,2048]{1,0:T(8,128)(2,1)} collective-permute-done((bf16[128,2048]{1,0:T(8,128)(2,1)S(1)}, bf16[128,2048]{1,0:T(8,128)(2,1)}, u32[]{:S(2)}, u32[]{:S(2)}) %collective-permute-start.6) | collective-permute-done | bytes 524320 | tf_op jit(solution)/shard_map/ppermute | solution.py:215
  43.6 1.4 %collective-permute-start.10 = (bf16[128,2048]{1,0:T(8,128)(2,1)}, bf16[128,2048]{1,0:T(8,128)(2,1)}, u32[]{:S(2)}, u32[]{:S(2)}) collective-permute-start(bf16[128,2048]{1,0:T(8,128)(2,1)} %collective-permute-done.6.refs_0_), channel_id=1, source_target_pairs={{2,4},{4,2},{3,5},{5,3},{10,12},{12,10},{11,13},{13,11},{18,20},{2... | collective-permute-start | bytes 1572872 | tf_op jit(solution)/shard_map/ppermute | solution.py:215
  45.0 0.0 collective-permute-done.7.refs_1_
  45.0 1.6 %collective-permute-start.9 = (bf16[128,2048]{1,0:T(8,128)(2,1)}, bf16[128,2048]{1,0:T(8,128)(2,1)}, u32[]{:S(2)}, u32[]{:S(2)}) collective-permute-start(bf16[128,2048]{1,0:T(8,128)(2,1)} %collective-permute-done.7.refs_1_), channel_id=1, source_target_pairs={{0,2},{2,0},{4,6},{6,4},{1,3},{3,1},{5,7},{7,5},{8,10},{10,8},{12,... | collective-permute-start | bytes 1572872 | tf_op jit(solution)/shard_map/ppermute | solution.py:215
  46.6 0.0 collective-permute-done.4
  46.6 0.7 add_convert_fusion.4
  47.3 4.1 %shard_map.86 = (f32[672,128]{1,0:T(8,128)S(1)}, f32[672,128]{1,0:T(8,128)S(1)}, bf16[672,128]{1,0:T(8,128)(2,1)S(1)}, bf16[672,128]{1,0:T(8,128)(2,1)}) custom-call(s32[1]{0:T(128)} %bitcast.core_ref, bf16[128,2048]{1,0:T(8,128)(2,1)} %collective-permute-done.6.refs_0_, bf16[128,2048]{1,0:T(8,128)(2,1)} %collective-permute-done.7.refs_1_, ...), custom_call_target="tpu_custom_call" | custom-call | flops 1409286144 | bytes 7569408 | tf_op jit(solution)/shard_map/pallas_call | solution.py:187
  51.4 0.7 copy-done.9
  52.1 0.0 collective-permute-start.8
  52.1 2.5 %collective-permute-start.5 = (bf16[672,128]{1,0:T(8,128)(2,1)}, bf16[672,128]{1,0:T(8,128)(2,1)S(1)}, u32[]{:S(2)}, u32[]{:S(2)}) collective-permute-start(bf16[672,128]{1,0:T(8,128)(2,1)} %add_convert_fusion.4), channel_id=1, source_target_pairs={{8,0},{16,8},{24,16},{0,24},{9,1},{17,9},{25,17},{1,25},{10,2},{18... | collective-permute-start | bytes 516104 | tf_op jit(solution)/shard_map/ppermute | solution.py:224
  54.6 0.2 collective-permute-start.12
  54.8 0.0 collective-permute-done.8
  54.8 0.0 collective-permute-done.10
  54.8 3.0 %collective-permute-done.9 = bf16[128,2048]{1,0:T(8,128)(2,1)} collective-permute-done((bf16[128,2048]{1,0:T(8,128)(2,1)}, bf16[128,2048]{1,0:T(8,128)(2,1)}, u32[]{:S(2)}, u32[]{:S(2)}) %collective-permute-start.9) | collective-permute-done | bytes 524320 | tf_op jit(solution)/shard_map/ppermute | solution.py:215
  57.8 1.7 %collective-permute-start.14 = (bf16[128,2048]{1,0:T(8,128)(2,1)}, bf16[128,2048]{1,0:T(8,128)(2,1)S(1)}, u32[]{:S(2)}, u32[]{:S(2)}) collective-permute-start(bf16[128,2048]{1,0:T(8,128)(2,1)} %collective-permute-done.10), channel_id=1, source_target_pairs={{0,2},{2,0},{4,6},{6,4},{1,3},{3,1},{5,7},{7,5},{8,10},{10,8},{12,... | collective-permute-start | bytes 1572872 | tf_op jit(solution)/shard_map/ppermute | solution.py:215
  59.5 1.1 %broadcast_select_fusion.refs_0_ = bf16[128,2048]{1,0:T(8,128)(2,1)S(1)} fusion(bf16[128,2048]{1,0:T(8,128)(2,1)} %collective-permute-done.10, bf16[128,2048]{1,0:T(8,128)(2,1)} %collective-permute-done.9, pred[]{:T(512)S(6)} %eq.32), kind=kLoop, calls=%fused_computation | loop fusion | flops 262144 | bytes 1572865 | tf_op jit(solution)/shard_map/jit(_where)/select_n | solution.py:306
  60.6 1.0 %add_convert_fusion.3 = bf16[672,128]{1,0:T(8,128)(2,1)S(1)} fusion(f32[672,128]{1,0:T(8,128)S(1)} %get-tuple-element.43, bf16[672,128]{1,0:T(8,128)(2,1)} %collective-permute-done.8), kind=kLoop, calls=%fused_computation.4 | loop fusion | flops 258048 | bytes 688128 | tf_op jit(solution)/shard_map/convert_element_type | solution.py:285
  61.6 0.0 collective-permute-done.12
  61.7 0.0 copy-start.11
  61.7 2.0 %shard_map.87 = (f32[672,128]{1,0:T(8,128)S(1)}, bf16[672,128]{1,0:T(8,128)(2,1)S(1)}) custom-call(s32[1]{0:T(128)} %bitcast.core_ref, bf16[128,2048]{1,0:T(8,128)(2,1)S(1)} %broadcast_select_fusion.refs_0_, bf16[1344,1024]{1,0:T(8,128)(2,1)S(1)} %bitcast.16, bf16[1344,512]{1,0:T(8,128)(2,1)S(1)} %bitcast.20, bf16[1344,512]{1,0:T(8,128)(2,1)S(1)} %bitcast.24), custom_call_target="tpu_custom_call" | custom-call | flops 704643072 | bytes 6537216 | tf_op jit(solution)/shard_map/pallas_call | solution.py:187
  63.7 0.1 collective-permute-start.15
  63.8 2.5 %collective-permute-start.11 = (bf16[672,128]{1,0:T(8,128)(2,1)S(1)}, bf16[672,128]{1,0:T(8,128)(2,1)S(1)}, u32[]{:S(2)}, u32[]{:S(2)}) collective-permute-start(bf16[672,128]{1,0:T(8,128)(2,1)S(1)} %add_convert_fusion.3), channel_id=1, source_target_pairs={{8,0},{16,8},{24,16},{0,24},{9,1},{17,9},{25,17},{1,25},{10,2},{18... | collective-permute-start | bytes 516104 | tf_op jit(solution)/shard_map/ppermute | solution.py:224
  66.3 0.5 collective-permute-start.13
  66.8 0.0 collective-permute-done.15
  66.8 2.8 %collective-permute-done.14.refs_0_ = bf16[128,2048]{1,0:T(8,128)(2,1)S(1)} collective-permute-done((bf16[128,2048]{1,0:T(8,128)(2,1)}, bf16[128,2048]{1,0:T(8,128)(2,1)S(1)}, u32[]{:S(2)}, u32[]{:S(2)}) %collective-permute-start.14) | collective-permute-done | bytes 524320 | tf_op jit(solution)/shard_map/ppermute | solution.py:215
  69.7 0.1 add_convert_fusion.1
  69.7 2.5 %collective-permute-start.16 = (bf16[672,128]{1,0:T(8,128)(2,1)S(1)}, bf16[672,128]{1,0:T(8,128)(2,1)S(1)}, u32[]{:S(2)}, u32[]{:S(2)}) collective-permute-start(bf16[672,128]{1,0:T(8,128)(2,1)S(1)} %add_convert_fusion.1), channel_id=1, source_target_pairs={{8,0},{16,8},{24,16},{0,24},{9,1},{17,9},{25,17},{1,25},{10,2},{18... | collective-permute-start | bytes 516104 | tf_op jit(solution)/shard_map/ppermute | solution.py:224
  72.2 2.0 %shard_map.88 = (f32[672,128]{1,0:T(8,128)S(1)}, bf16[672,128]{1,0:T(8,128)(2,1)S(1)}) custom-call(s32[1]{0:T(128)} %bitcast.core_ref, bf16[128,2048]{1,0:T(8,128)(2,1)S(1)} %collective-permute-done.14.refs_0_, bf16[1344,1024]{1,0:T(8,128)(2,1)S(1)} %bitcast.17, bf16[1344,512]{1,0:T(8,128)(2,1)S(1)} %bitcast.21, bf16[1344,512]{1,0:T(8,128)(2,1)S(1)} %bitcast.25), custom_call_target="tpu_custom_call" | custom-call | flops 1 | bytes 1 | tf_op jit(solution)/shard_map/pallas_call | solution.py:187
  74.2 0.0 copy-start.12
  74.2 0.5 collective-permute-done.13
  74.7 3.2 %collective-permute-done.16 = bf16[672,128]{1,0:T(8,128)(2,1)S(1)} collective-permute-done((bf16[672,128]{1,0:T(8,128)(2,1)S(1)}, bf16[672,128]{1,0:T(8,128)(2,1)S(1)}, u32[]{:S(2)}, u32[]{:S(2)}) %collective-permute-start.16) | collective-permute-done | bytes 172064 | tf_op jit(solution)/shard_map/ppermute | solution.py:224
  77.9 0.0 collective-permute-start.17
  77.9 1.4 %collective-permute-done.17 = bf16[672,128]{1,0:T(8,128)(2,1)S(1)} collective-permute-done((bf16[672,128]{1,0:T(8,128)(2,1)S(1)}, bf16[672,128]{1,0:T(8,128)(2,1)S(1)}, u32[]{:S(2)}, u32[]{:S(2)}) %collective-permute-start.17) | collective-permute-done | bytes 172064 | tf_op jit(solution)/shard_map/ppermute | solution.py:224
  79.4 3.4 %collective-permute-start.18 = (bf16[672,128]{1,0:T(8,128)(2,1)S(1)}, bf16[672,128]{1,0:T(8,128)(2,1)S(1)}, u32[]{:S(2)}, u32[]{:S(2)}) collective-permute-start(bf16[672,128]{1,0:T(8,128)(2,1)S(1)} %add_convert_fusion), channel_id=1, source_target_pairs={{8,0},{16,8},{24,16},{0,24},{9,1},{17,9},{25,17},{1,25},{10,2},{18... | collective-permute-start | bytes 516104 | tf_op jit(solution)/shard_map/ppermute | solution.py:224
  82.9 3.8 %collective-permute-done.18 = bf16[672,128]{1,0:T(8,128)(2,1)S(1)} collective-permute-done((bf16[672,128]{1,0:T(8,128)(2,1)S(1)}, bf16[672,128]{1,0:T(8,128)(2,1)S(1)}, u32[]{:S(2)}, u32[]{:S(2)}) %collective-permute-start.18) | collective-permute-done | bytes 172064 | tf_op jit(solution)/shard_map/ppermute | solution.py:224
  86.7 0.1 select_dynamic-update-slice_fusion.1
  86.9 0.1 select_dynamic-update-slice_fusion
  87.0 0.0 copy-start.10
  87.0 0.8 copy-done.10
  (24 shorter events, 0.3 us)
Async XLA Ops:
  1.0 13.0 %collective-permute-start.1 = (bf16[128,1024]{1,0:T(8,128)(2,1)S(1)}, bf16[128,1024]{1,0:T(8,128)(2,1)S(1)}, u32[]{:S(2)}, u32[]{:S(2)}) collective-permute-start(bf16[128,1024]{1,0:T(8,128)(2,1)S(1)} %pad_maximum_fusion.refs_2_), channel_id=1, source_target_pairs={{0,2},{2,4},{4,6},{1,3},{3,5},{5,7},{8,10},{10,12},{12,14},{9,11},... | collective-permute-start | bytes 786440 | tf_op jit(solution)/shard_map/ppermute | solution.py:208
  6.0 8.1 %collective-permute-start = (bf16[48,1024]{1,0:T(8,128)(2,1)S(1)}, bf16[48,1024]{1,0:T(8,128)(2,1)S(1)}, u32[]{:S(2)}, u32[]{:S(2)}) collective-permute-start(bf16[48,1024]{1,0:T(8,128)(2,1)S(1)} %slice.4), channel_id=1, source_target_pairs={{0,4},{2,6},{1,5},{3,7},{8,12},{10,14},{9,13},{11,15},{16,20},{18,... | collective-permute-start | bytes 294920 | tf_op jit(solution)/shard_map/ppermute | solution.py:208
  12.0 1.0 %copy-start.7 = (bf16[1,128,1024]{2,1,0:T(8,128)(2,1)S(1)}, bf16[1,128,1024]{2,1,0:T(8,128)(2,1)}, u32[]{:S(2)}) copy-start(bf16[1,128,1024]{2,1,0:T(8,128)(2,1)} %param.8) | copy-start | bytes 786436
  13.0 0.9 %copy-start.8 = (bf16[1,128,1024]{2,1,0:T(8,128)(2,1)S(1)}, bf16[1,128,1024]{2,1,0:T(8,128)(2,1)}, u32[]{:S(2)}) copy-start(bf16[1,128,1024]{2,1,0:T(8,128)(2,1)} %param.11) | copy-start | bytes 786436
  14.0 19.9 %copy-start = (bf16[1,1344,1024]{2,1,0:T(8,128)(2,1)S(1)}, bf16[1,1344,1024]{2,1,0:T(8,128)(2,1)}, u32[]{:S(2)}) copy-start(bf16[1,1344,1024]{2,1,0:T(8,128)(2,1)} %param.12) | copy-start | bytes 8257540
  16.3 16.0 %collective-permute-start.2 = (bf16[128,1024]{1,0:T(8,128)(2,1)S(1)}, bf16[128,1024]{1,0:T(8,128)(2,1)S(1)}, u32[]{:S(2)}, u32[]{:S(2)}) collective-permute-start(bf16[128,1024]{1,0:T(8,128)(2,1)S(1)} %get-tuple-element.37), channel_id=1, source_target_pairs={{2,0},{4,2},{6,4},{3,1},{5,3},{7,5},{10,8},{12,10},{14,12},{11,9},... | collective-permute-start | bytes 786440 | tf_op jit(solution)/shard_map/ppermute | solution.py:208
  17.6 14.7 %collective-permute-start.3 = (bf16[48,1024]{1,0:T(8,128)(2,1)S(1)}, bf16[48,1024]{1,0:T(8,128)(2,1)S(1)}, u32[]{:S(2)}, u32[]{:S(2)}) collective-permute-start(bf16[48,1024]{1,0:T(8,128)(2,1)S(1)} %get-tuple-element.38), channel_id=1, source_target_pairs={{4,0},{6,2},{5,1},{7,3},{12,8},{14,10},{13,9},{15,11},{20,16},{22,... | collective-permute-start | bytes 294920 | tf_op jit(solution)/shard_map/ppermute | solution.py:208
  32.4 11.2 %collective-permute-start.6 = (bf16[128,2048]{1,0:T(8,128)(2,1)S(1)}, bf16[128,2048]{1,0:T(8,128)(2,1)}, u32[]{:S(2)}, u32[]{:S(2)}) collective-permute-start(bf16[128,2048]{1,0:T(8,128)(2,1)S(1)} %shard_map.84.refs_0_), channel_id=1, source_target_pairs={{0,2},{2,0},{4,6},{6,4},{1,3},{3,1},{5,7},{7,5},{8,10},{10,8},{12,... | collective-permute-start | bytes 1572872 | tf_op jit(solution)/shard_map/ppermute | solution.py:215
  32.5 12.6 %collective-permute-start.7 = (bf16[128,2048]{1,0:T(8,128)(2,1)S(1)}, bf16[128,2048]{1,0:T(8,128)(2,1)}, u32[]{:S(2)}, u32[]{:S(2)}) collective-permute-start(bf16[128,2048]{1,0:T(8,128)(2,1)S(1)} %shard_map.84.refs_0_), channel_id=1, source_target_pairs={{2,4},{4,2},{3,5},{5,3},{10,12},{12,10},{11,13},{13,11},{18,20},{2... | collective-permute-start | bytes 1572872 | tf_op jit(solution)/shard_map/ppermute | solution.py:215
  33.9 1.3 %copy-start.1 = (bf16[1,1344,512]{2,1,0:T(8,128)(2,1)S(1)}, bf16[1,1344,512]{2,1,0:T(8,128)(2,1)}, u32[]{:S(2)}) copy-start(bf16[1,1344,512]{2,1,0:T(8,128)(2,1)} %param.13) | copy-start | bytes 4128772
  35.3 1.3 %copy-start.4 = (bf16[1,1344,512]{2,1,0:T(8,128)(2,1)S(1)}, bf16[1,1344,512]{2,1,0:T(8,128)(2,1)}, u32[]{:S(2)}) copy-start(bf16[1,1344,512]{2,1,0:T(8,128)(2,1)} %param.14) | copy-start | bytes 4128772
  36.6 10.7 %copy-start.2 = (bf16[1,1344,512]{2,1,0:T(8,128)(2,1)S(1)}, bf16[1,1344,512]{2,1,0:T(8,128)(2,1)}, u32[]{:S(2)}) copy-start(bf16[1,1344,512]{2,1,0:T(8,128)(2,1)} %param.13) | copy-start | bytes 4128772
  36.6 10.7 %copy-start.5 = (bf16[1,1344,512]{2,1,0:T(8,128)(2,1)S(1)}, bf16[1,1344,512]{2,1,0:T(8,128)(2,1)}, u32[]{:S(2)}) copy-start(bf16[1,1344,512]{2,1,0:T(8,128)(2,1)} %param.14) | copy-start | bytes 4128772
  38.6 8.0 %collective-permute-start.4 = (bf16[672,128]{1,0:T(8,128)(2,1)S(1)}, bf16[672,128]{1,0:T(8,128)(2,1)S(1)}, u32[]{:S(2)}, u32[]{:S(2)}) collective-permute-start(bf16[672,128]{1,0:T(8,128)(2,1)S(1)} %get-tuple-element.40), channel_id=1, source_target_pairs={{1,0},{0,1},{3,2},{2,3},{5,4},{4,5},{7,6},{6,7},{9,8},{8,9},{11,10... | collective-permute-start | bytes 516104 | tf_op jit(solution)/shard_map/ppermute | solution.py:224
  43.6 11.2 %collective-permute-start.10 = (bf16[128,2048]{1,0:T(8,128)(2,1)}, bf16[128,2048]{1,0:T(8,128)(2,1)}, u32[]{:S(2)}, u32[]{:S(2)}) collective-permute-start(bf16[128,2048]{1,0:T(8,128)(2,1)} %collective-permute-done.6.refs_0_), channel_id=1, source_target_pairs={{2,4},{4,2},{3,5},{5,3},{10,12},{12,10},{11,13},{13,11},{18,20},{2... | collective-permute-start | bytes 1572872 | tf_op jit(solution)/shard_map/ppermute | solution.py:215
  45.0 12.8 %collective-permute-start.9 = (bf16[128,2048]{1,0:T(8,128)(2,1)}, bf16[128,2048]{1,0:T(8,128)(2,1)}, u32[]{:S(2)}, u32[]{:S(2)}) collective-permute-start(bf16[128,2048]{1,0:T(8,128)(2,1)} %collective-permute-done.7.refs_1_), channel_id=1, source_target_pairs={{0,2},{2,0},{4,6},{6,4},{1,3},{3,1},{5,7},{7,5},{8,10},{10,8},{12,... | collective-permute-start | bytes 1572872 | tf_op jit(solution)/shard_map/ppermute | solution.py:215
  51.4 0.7 copy-start.9
  52.1 2.7 %collective-permute-start.8 = (bf16[672,128]{1,0:T(8,128)(2,1)}, bf16[672,128]{1,0:T(8,128)(2,1)}, u32[]{:S(2)}, u32[]{:S(2)}) collective-permute-start(bf16[672,128]{1,0:T(8,128)(2,1)} %get-tuple-element.44), channel_id=1, source_target_pairs={{1,0},{0,1},{3,2},{2,3},{5,4},{4,5},{7,6},{6,7},{9,8},{8,9},{11,10... | collective-permute-start | bytes 516104 | tf_op jit(solution)/shard_map/ppermute | solution.py:224
  52.1 9.6 %collective-permute-start.5 = (bf16[672,128]{1,0:T(8,128)(2,1)}, bf16[672,128]{1,0:T(8,128)(2,1)S(1)}, u32[]{:S(2)}, u32[]{:S(2)}) collective-permute-start(bf16[672,128]{1,0:T(8,128)(2,1)} %add_convert_fusion.4), channel_id=1, source_target_pairs={{8,0},{16,8},{24,16},{0,24},{9,1},{17,9},{25,17},{1,25},{10,2},{18... | collective-permute-start | bytes 516104 | tf_op jit(solution)/shard_map/ppermute | solution.py:224
  54.6 7.1 %copy-start.3 = (bf16[1,1344,512]{2,1,0:T(8,128)(2,1)S(1)}, bf16[1,1344,512]{2,1,0:T(8,128)(2,1)}, u32[]{:S(2)}) copy-start(bf16[1,1344,512]{2,1,0:T(8,128)(2,1)} %param.13) | copy-start | bytes 4128772
  54.6 7.1 %copy-start.6 = (bf16[1,1344,512]{2,1,0:T(8,128)(2,1)S(1)}, bf16[1,1344,512]{2,1,0:T(8,128)(2,1)}, u32[]{:S(2)}) copy-start(bf16[1,1344,512]{2,1,0:T(8,128)(2,1)} %param.14) | copy-start | bytes 4128772
  54.6 7.0 %collective-permute-start.12 = (bf16[672,128]{1,0:T(8,128)(2,1)}, bf16[672,128]{1,0:T(8,128)(2,1)S(1)}, u32[]{:S(2)}, u32[]{:S(2)}) collective-permute-start(bf16[672,128]{1,0:T(8,128)(2,1)} %copy-done.9), channel_id=1, source_target_pairs={{1,0},{0,1},{3,2},{2,3},{5,4},{4,5},{7,6},{6,7},{9,8},{8,9},{11,10... | collective-permute-start | bytes 516104 | tf_op jit(solution)/shard_map/ppermute | solution.py:224
  57.8 11.9 %collective-permute-start.14 = (bf16[128,2048]{1,0:T(8,128)(2,1)}, bf16[128,2048]{1,0:T(8,128)(2,1)S(1)}, u32[]{:S(2)}, u32[]{:S(2)}) collective-permute-start(bf16[128,2048]{1,0:T(8,128)(2,1)} %collective-permute-done.10), channel_id=1, source_target_pairs={{0,2},{2,0},{4,6},{6,4},{1,3},{3,1},{5,7},{7,5},{8,10},{10,8},{12,... | collective-permute-start | bytes 1572872 | tf_op jit(solution)/shard_map/ppermute | solution.py:215
  61.7 2.0 %copy-start.11 = (bf16[672,128]{1,0:T(8,128)(2,1)}, bf16[672,128]{1,0:T(8,128)(2,1)S(1)}, u32[]{:S(2)}) copy-start(bf16[672,128]{1,0:T(8,128)(2,1)S(1)} %collective-permute-done.5) | copy-start | bytes 516100
  63.7 3.1 %collective-permute-start.15 = (bf16[672,128]{1,0:T(8,128)(2,1)S(1)}, bf16[672,128]{1,0:T(8,128)(2,1)S(1)}, u32[]{:S(2)}, u32[]{:S(2)}) collective-permute-start(bf16[672,128]{1,0:T(8,128)(2,1)S(1)} %get-tuple-element.51), channel_id=1, source_target_pairs={{1,0},{0,1},{3,2},{2,3},{5,4},{4,5},{7,6},{6,7},{9,8},{8,9},{11,10... | collective-permute-start | bytes 516104 | tf_op jit(solution)/shard_map/ppermute | solution.py:224
  63.8 10.4 %collective-permute-start.11 = (bf16[672,128]{1,0:T(8,128)(2,1)S(1)}, bf16[672,128]{1,0:T(8,128)(2,1)S(1)}, u32[]{:S(2)}, u32[]{:S(2)}) collective-permute-start(bf16[672,128]{1,0:T(8,128)(2,1)S(1)} %add_convert_fusion.3), channel_id=1, source_target_pairs={{8,0},{16,8},{24,16},{0,24},{9,1},{17,9},{25,17},{1,25},{10,2},{18... | collective-permute-start | bytes 516104 | tf_op jit(solution)/shard_map/ppermute | solution.py:224
  66.3 8.4 %collective-permute-start.13 = (bf16[672,128]{1,0:T(8,128)(2,1)S(1)}, bf16[672,128]{1,0:T(8,128)(2,1)S(1)}, u32[]{:S(2)}, u32[]{:S(2)}) collective-permute-start(bf16[672,128]{1,0:T(8,128)(2,1)S(1)} %add_convert_fusion.2), channel_id=1, source_target_pairs={{8,0},{16,8},{24,16},{0,24},{9,1},{17,9},{25,17},{1,25},{10,2},{18... | collective-permute-start | bytes 516104 | tf_op jit(solution)/shard_map/ppermute | solution.py:224
  69.7 8.2 %collective-permute-start.16 = (bf16[672,128]{1,0:T(8,128)(2,1)S(1)}, bf16[672,128]{1,0:T(8,128)(2,1)S(1)}, u32[]{:S(2)}, u32[]{:S(2)}) collective-permute-start(bf16[672,128]{1,0:T(8,128)(2,1)S(1)} %add_convert_fusion.1), channel_id=1, source_target_pairs={{8,0},{16,8},{24,16},{0,24},{9,1},{17,9},{25,17},{1,25},{10,2},{18... | collective-permute-start | bytes 516104 | tf_op jit(solution)/shard_map/ppermute | solution.py:224
  74.2 8.6 %copy-start.12 = (bf16[672,128]{1,0:T(8,128)(2,1)S(1)}, bf16[672,128]{1,0:T(8,128)(2,1)}, u32[]{:S(2)}) copy-start(bf16[672,128]{1,0:T(8,128)(2,1)} %copy-done.11) | copy-start | bytes 516100
  77.9 1.4 %collective-permute-start.17 = (bf16[672,128]{1,0:T(8,128)(2,1)S(1)}, bf16[672,128]{1,0:T(8,128)(2,1)S(1)}, u32[]{:S(2)}, u32[]{:S(2)}) collective-permute-start(bf16[672,128]{1,0:T(8,128)(2,1)S(1)} %get-tuple-element.56), channel_id=1, source_target_pairs={{1,0},{0,1},{3,2},{2,3},{5,4},{4,5},{7,6},{6,7},{9,8},{8,9},{11,10... | collective-permute-start | bytes 516104 | tf_op jit(solution)/shard_map/ppermute | solution.py:224
  79.4 7.3 %collective-permute-start.18 = (bf16[672,128]{1,0:T(8,128)(2,1)S(1)}, bf16[672,128]{1,0:T(8,128)(2,1)S(1)}, u32[]{:S(2)}, u32[]{:S(2)}) collective-permute-start(bf16[672,128]{1,0:T(8,128)(2,1)S(1)} %add_convert_fusion), channel_id=1, source_target_pairs={{8,0},{16,8},{24,16},{0,24},{9,1},{17,9},{25,17},{1,25},{10,2},{18... | collective-permute-start | bytes 516104 | tf_op jit(solution)/shard_map/ppermute | solution.py:224
  87.0 0.8 copy-start.10

commit v10 on v8

--- a/solution.py
+++ b/solution.py
@@ -286,17 +286,26 @@
         return sums
 
     even = place % 2 == 0
-    results, waiting = [], [own]
+    results, waiting, held, hops = [], [own], [], []
+
+    def hop(blocks):
+        came = passed_along(jnp.concatenate(blocks, axis=1), "section", -1)
+        hops.append(came)
+        return [came[:, i * rows : (i + 1) * rows] for i in range(len(blocks))]
+
     by_first, by_second = own, own
     for step in range(1, shards):
         came_first = swapped(by_first, "seq", 0)
         last = step == shards - 1 and shards % 2 == 0
         came_second = came_first if last else swapped(by_second, "seq", 1)
         if step > 1:
-            waiting = after(waiting, *sums, *(results[-2] if step > 2 else ()))
+            waiting = after(waiting, *sums, *(hops[-2:-1] if step > 2 else ()))
         late = (came_first, came_second) if step > 1 else ()
         sums = halves_summed(waiting, late)
-        results.append([passed_along(block, "section", -1) for block in sums])
+        if step > 2 and last:
+            held = sums
+        else:
+            results.append(hop(sums))
         by_first, by_second = came_second, came_first
         if last:
             waiting = [came_first]
@@ -306,8 +315,9 @@
             waiting = [jnp.where(even == (place >= step), came_second, came_first)]
     if shards > 1:
         waiting = after(waiting, *sums)
-    sums = halves_summed(waiting, (), results[-2] if shards > 2 else ())
-    results.append([passed_along(block, "section", -1) for block in sums])
+    sums = halves_summed(waiting, (), hops[-1:])
+    came = hop([*held, *sums])
+    results += [[block] for block in came] if held else [came]
     for step, blocks in enumerate(results):
         if len(blocks) > 1:
             first, second = blocks

time: 88.2 us -> 88.5 us (level)
  waiting for transfers between devices: 35.3 us -> 36.2 us
    ppermute x10 -> x8, starting transfers between devices: 9.42 us -> 8.74 us  [passed_along(): lax.ppermute(block, axis, [((i - distance) % len(devices), i) for i in de...]
    ppermute x10 -> x8, waiting for transfers between devices: 11.2 us -> 11.5 us  [passed_along(): lax.ppermute(block, axis, [((i - distance) % len(devices), i) for i in de...]
  transfers between devices with their start and end apart: 19 -> 17, of which waited for: 8 -> 7; matrix products, arithmetic and copies ran while one was open for 5% -> 5% of each run, Pallas kernels for 12% -> 12%
where the time goes in v10:
time: 88.5 us; the launch traced here: 88 us
  waiting for transfers between devices  36.2 us (41%)
  starting transfers between devices  27.1 us (31%)
  Pallas kernels  12.5 us (14%)
  local copies, waits for them, and re-layouts  7.69 us (9%)
  other arithmetic  4.28 us (5%)
    ppermute x4, waiting for transfers between devices, moved(): lax.ppermute(block, axis, [(i, i + by) for i in range(size) if 0 <= i + b...  13.4 us
    ppermute x4, starting transfers between devices, moved(): lax.ppermute(block, axis, [(i, i + by) for i in range(size) if 0 <= i + b...  12 us
    ppermute x8, waiting for transfers between devices, passed_along(): lax.ppermute(block, axis, [((i - distance) % len(devices), i) for i in de...  11.5 us
    ppermute x5, waiting for transfers between devices, swapped(): return lax.ppermute(block, axis, pairs)  11.2 us
    pallas_call x4, Pallas kernels, project(): pl.pallas_call(functools.partial(project_kernel, [len(block) for block in...  10.1 us
    ppermute x8, starting transfers between devices, passed_along(): lax.ppermute(block, axis, [((i - distance) % len(devices), i) for i in de...  8.74 us
    ppermute x5, starting transfers between devices, swapped(): return lax.ppermute(block, axis, pairs)  6.32 us
    unnamed x26, local copies, waits for them, and re-layouts  6.12 us
  transfers between devices with their start and end apart: 17, of which 7 were waited for; matrix products, arithmetic and copies ran while one was open for 5% of the time, Pallas kernels for 12%

profile of v10, /device:TPU:0, one launch (start us, length us, event | category | flops | bytes accessed | tf_op | source)
XLA Modules:
  0.0 88.0 jit_solution(6793963198390534380)
XLA Ops:
  0.0 1.0 %pad_maximum_fusion.2.refs_2_ = bf16[128,1024]{1,0:T(8,128)(2,1)S(1)} fusion(bf16[128,512]{1,0:T(8,128)(2,1)} %bitcast.28, bf16[128,512]{1,0:T(8,128)(2,1)} %bitcast.29), kind=kLoop, calls=%fused_computation.8 | loop fusion | flops 524288 | bytes 524288 | tf_op jit(solution)/shard_map/concatenate | solution.py:248
  1.0 4.9 %collective-permute-start.1 = (bf16[128,1024]{1,0:T(8,128)(2,1)S(1)}, bf16[128,1024]{1,0:T(8,128)(2,1)S(1)}, u32[]{:S(2)}, u32[]{:S(2)}) collective-permute-start(bf16[128,1024]{1,0:T(8,128)(2,1)S(1)} %pad_maximum_fusion.2.refs_2_), channel_id=1, source_target_pairs={{0,2},{2,4},{4,6},{1,3},{3,5},{5,7},{8,10},{10,12},{12,14},{9,11},... | collective-permute-start | bytes 786440 | tf_op jit(solution)/shard_map/ppermute | solution.py:208
  6.0 4.5 %collective-permute-start = (bf16[48,1024]{1,0:T(8,128)(2,1)S(1)}, bf16[48,1024]{1,0:T(8,128)(2,1)S(1)}, u32[]{:S(2)}, u32[]{:S(2)}) collective-permute-start(bf16[48,1024]{1,0:T(8,128)(2,1)S(1)} %slice.20), channel_id=1, source_target_pairs={{0,4},{2,6},{1,5},{3,7},{8,12},{10,14},{9,13},{11,15},{16,20},{18,... | collective-permute-start | bytes 294920 | tf_op jit(solution)/shard_map/ppermute | solution.py:208
  10.5 0.8 pad_dynamic-slice_fusion
  11.2 0.7 fusion.5
  11.9 0.1 fusion.4.refs_3_
  12.0 0.0 copy-start.7
  12.0 0.9 %copy-done.7 = bf16[1,128,1024]{2,1,0:T(8,128)(2,1)S(1)} copy-done((bf16[1,128,1024]{2,1,0:T(8,128)(2,1)S(1)}, bf16[1,128,1024]{2,1,0:T(8,128)(2,1)}, u32[]{:S(2)}) %copy-start.7) | copy-done | bytes 262168
  13.0 0.9 %copy-done.8 = bf16[1,128,1024]{2,1,0:T(8,128)(2,1)S(1)} copy-done((bf16[1,128,1024]{2,1,0:T(8,128)(2,1)S(1)}, bf16[1,128,1024]{2,1,0:T(8,128)(2,1)}, u32[]{:S(2)}) %copy-start.8) | copy-done | bytes 262168
  13.9 0.1 shard_map.82
  14.0 0.0 collective-permute-done.refs_4_
  14.0 0.0 collective-permute-done.1.refs_5_
  14.0 0.0 copy-start
  14.0 2.2 %shard_map.83 = (bf16[128,1024]{1,0:T(8,128)(2,1)S(1)}, f32[128,1024]{1,0:T(8,128)S(1)}, bf16[48,1024]{1,0:T(8,128)(2,1)S(1)}, bf16[128,1024]{1,0:T(8,128)(2,1)S(1)}) custom-call(bf16[1024,128]{1,0:T(8,128)(2,1)S(1)} %get-tuple-element.33.refs_0_, bf16[1024,128]{1,0:T(8,128)(2,1)S(1)} %get-tuple-element.34.refs_1_, ...), custom_call_target="tpu_custom_call" | custom-call | flops 478150656 | bytes 1048576 | tf_op jit(solution)/shard_map/pallas_call | solution.py:100
  16.3 1.3 %collective-permute-start.2 = (bf16[128,1024]{1,0:T(8,128)(2,1)S(1)}, bf16[128,1024]{1,0:T(8,128)(2,1)S(1)}, u32[]{:S(2)}, u32[]{:S(2)}) collective-permute-start(bf16[128,1024]{1,0:T(8,128)(2,1)S(1)} %get-tuple-element.37), channel_id=1, source_target_pairs={{2,0},{4,2},{6,4},{3,1},{5,3},{7,5},{10,8},{12,10},{14,12},{11,9},... | collective-permute-start | bytes 786440 | tf_op jit(solution)/shard_map/ppermute | solution.py:208
  17.6 1.3 %collective-permute-start.3 = (bf16[48,1024]{1,0:T(8,128)(2,1)S(1)}, bf16[48,1024]{1,0:T(8,128)(2,1)S(1)}, u32[]{:S(2)}, u32[]{:S(2)}) collective-permute-start(bf16[48,1024]{1,0:T(8,128)(2,1)S(1)} %get-tuple-element.38), channel_id=1, source_target_pairs={{4,0},{6,2},{5,1},{7,3},{12,8},{14,10},{13,9},{15,11},{20,16},{22,... | collective-permute-start | bytes 294920 | tf_op jit(solution)/shard_map/ppermute | solution.py:208
  18.9 13.4 %collective-permute-done.3.refs_1_ = bf16[48,1024]{1,0:T(8,128)(2,1)S(1)} collective-permute-done((bf16[48,1024]{1,0:T(8,128)(2,1)S(1)}, bf16[48,1024]{1,0:T(8,128)(2,1)S(1)}, u32[]{:S(2)}, u32[]{:S(2)}) %collective-permute-start.3) | collective-permute-done | bytes 98336 | tf_op jit(solution)/shard_map/ppermute | solution.py:208
  32.3 0.0 collective-permute-done.2.refs_0_
  32.3 0.1 shard_map.84.refs_0_
  32.4 0.1 collective-permute-start.6
  32.5 1.5 %collective-permute-start.7 = (bf16[128,2048]{1,0:T(8,128)(2,1)S(1)}, bf16[128,2048]{1,0:T(8,128)(2,1)}, u32[]{:S(2)}, u32[]{:S(2)}) collective-permute-start(bf16[128,2048]{1,0:T(8,128)(2,1)S(1)} %shard_map.84.refs_0_), channel_id=1, source_target_pairs={{2,4},{4,2},{3,5},{5,3},{10,12},{12,10},{11,13},{13,11},{18,20},{2... | collective-permute-start | bytes 1572872 | tf_op jit(solution)/shard_map/ppermute | solution.py:215
  33.9 1.3 %copy-done.1 = bf16[1,1344,512]{2,1,0:T(8,128)(2,1)S(1)} copy-done((bf16[1,1344,512]{2,1,0:T(8,128)(2,1)S(1)}, bf16[1,1344,512]{2,1,0:T(8,128)(2,1)}, u32[]{:S(2)}) %copy-start.1) | copy-done | bytes 1376280
  35.3 1.3 %copy-done.4 = bf16[1,1344,512]{2,1,0:T(8,128)(2,1)S(1)} copy-done((bf16[1,1344,512]{2,1,0:T(8,128)(2,1)S(1)}, bf16[1,1344,512]{2,1,0:T(8,128)(2,1)}, u32[]{:S(2)}) %copy-start.4) | copy-done | bytes 1376280
  36.6 2.0 %shard_map.85 = (f32[672,128]{1,0:T(8,128)S(1)}, bf16[672,128]{1,0:T(8,128)(2,1)S(1)}) custom-call(s32[1]{0:T(128)} %bitcast.core_ref, bf16[128,2048]{1,0:T(8,128)(2,1)S(1)} %shard_map.84.refs_0_, bf16[1344,1024]{1,0:T(8,128)(2,1)S(1)} %bitcast.14, bf16[1344,512]{1,0:T(8,128)(2,1)S(1)} %bitcast.18, bf16[1344,512]{1,0:T(8,128)(2,1)S(1)} %bitcast.22), custom_call_target="tpu_custom_call" | custom-call | flops 704643072 | bytes 6537216 | tf_op jit(solution)/shard_map/pallas_call | solution.py:187
  38.6 0.1 collective-permute-start.4
  38.7 4.9 %collective-permute-done.6.refs_0_ = bf16[128,2048]{1,0:T(8,128)(2,1)} collective-permute-done((bf16[128,2048]{1,0:T(8,128)(2,1)S(1)}, bf16[128,2048]{1,0:T(8,128)(2,1)}, u32[]{:S(2)}, u32[]{:S(2)}) %collective-permute-start.6) | collective-permute-done | bytes 524320 | tf_op jit(solution)/shard_map/ppermute | solution.py:215
  43.6 1.4 %collective-permute-start.10 = (bf16[128,2048]{1,0:T(8,128)(2,1)}, bf16[128,2048]{1,0:T(8,128)(2,1)}, u32[]{:S(2)}, u32[]{:S(2)}) collective-permute-start(bf16[128,2048]{1,0:T(8,128)(2,1)} %collective-permute-done.6.refs_0_), channel_id=1, source_target_pairs={{2,4},{4,2},{3,5},{5,3},{10,12},{12,10},{11,13},{13,11},{18,20},{2... | collective-permute-start | bytes 1572872 | tf_op jit(solution)/shard_map/ppermute | solution.py:215
  45.0 0.0 collective-permute-done.7.refs_1_
  45.0 1.6 %collective-permute-start.9 = (bf16[128,2048]{1,0:T(8,128)(2,1)}, bf16[128,2048]{1,0:T(8,128)(2,1)}, u32[]{:S(2)}, u32[]{:S(2)}) collective-permute-start(bf16[128,2048]{1,0:T(8,128)(2,1)} %collective-permute-done.7.refs_1_), channel_id=1, source_target_pairs={{0,2},{2,0},{4,6},{6,4},{1,3},{3,1},{5,7},{7,5},{8,10},{10,8},{12,... | collective-permute-start | bytes 1572872 | tf_op jit(solution)/shard_map/ppermute | solution.py:215
  46.6 0.0 collective-permute-done.4
  46.6 0.7 add_convert_fusion.4
  47.3 0.0 copy-done.5
  47.3 4.1 %shard_map.86 = (f32[672,128]{1,0:T(8,128)S(1)}, f32[672,128]{1,0:T(8,128)S(1)}, bf16[672,128]{1,0:T(8,128)(2,1)S(1)}, bf16[672,128]{1,0:T(8,128)(2,1)}) custom-call(s32[1]{0:T(128)} %bitcast.core_ref, bf16[128,2048]{1,0:T(8,128)(2,1)} %collective-permute-done.6.refs_0_, bf16[128,2048]{1,0:T(8,128)(2,1)} %collective-permute-done.7.refs_1_, ...), custom_call_target="tpu_custom_call" | custom-call | flops 1409286144 | bytes 7569408 | tf_op jit(solution)/shard_map/pallas_call | solution.py:187
  51.4 0.7 copy-done.9
  52.1 0.0 collective-permute-start.11
  52.1 2.5 %collective-permute-start.5 = (bf16[672,128]{1,0:T(8,128)(2,1)}, bf16[672,128]{1,0:T(8,128)(2,1)S(1)}, u32[]{:S(2)}, u32[]{:S(2)}) collective-permute-start(bf16[672,128]{1,0:T(8,128)(2,1)} %add_convert_fusion.4), channel_id=1, source_target_pairs={{8,0},{16,8},{24,16},{0,24},{9,1},{17,9},{25,17},{1,25},{10,2},{18... | collective-permute-start | bytes 516104 | tf_op jit(solution)/shard_map/ppermute | solution.py:224
  54.6 0.2 collective-permute-start.8
  54.8 0.0 collective-permute-done.11
  54.8 0.0 collective-permute-done.10
  54.8 3.0 %collective-permute-done.9 = bf16[128,2048]{1,0:T(8,128)(2,1)} collective-permute-done((bf16[128,2048]{1,0:T(8,128)(2,1)}, bf16[128,2048]{1,0:T(8,128)(2,1)}, u32[]{:S(2)}, u32[]{:S(2)}) %collective-permute-start.9) | collective-permute-done | bytes 524320 | tf_op jit(solution)/shard_map/ppermute | solution.py:215
  57.8 1.7 %collective-permute-start.14 = (bf16[128,2048]{1,0:T(8,128)(2,1)}, bf16[128,2048]{1,0:T(8,128)(2,1)S(1)}, u32[]{:S(2)}, u32[]{:S(2)}) collective-permute-start(bf16[128,2048]{1,0:T(8,128)(2,1)} %collective-permute-done.10), channel_id=1, source_target_pairs={{0,2},{2,0},{4,6},{6,4},{1,3},{3,1},{5,7},{7,5},{8,10},{10,8},{12,... | collective-permute-start | bytes 1572872 | tf_op jit(solution)/shard_map/ppermute | solution.py:215
  59.5 1.1 %broadcast_select_fusion.refs_0_ = bf16[128,2048]{1,0:T(8,128)(2,1)S(1)} fusion(bf16[128,2048]{1,0:T(8,128)(2,1)} %collective-permute-done.10, bf16[128,2048]{1,0:T(8,128)(2,1)} %collective-permute-done.9, pred[]{:T(512)S(6)} %eq.32), kind=kLoop, calls=%fused_computation | loop fusion | flops 262144 | bytes 1572865 | tf_op jit(solution)/shard_map/jit(_where)/select_n | solution.py:315
  60.6 1.0 %add_convert_fusion.2 = bf16[672,128]{1,0:T(8,128)(2,1)S(1)} fusion(f32[672,128]{1,0:T(8,128)S(1)} %get-tuple-element.46, bf16[672,128]{1,0:T(8,128)(2,1)} %collective-permute-done.11), kind=kLoop, calls=%fused_computation.5 | loop fusion | flops 258048 | bytes 688128 | tf_op jit(solution)/shard_map/convert_element_type | solution.py:285
  61.6 0.0 collective-permute-done.8
  61.7 0.0 collective-permute-done.5
  61.7 0.0 copy-start.11
  61.7 2.0 %shard_map.87 = (f32[672,128]{1,0:T(8,128)S(1)}, bf16[672,128]{1,0:T(8,128)(2,1)S(1)}) custom-call(s32[1]{0:T(128)} %bitcast.core_ref, bf16[128,2048]{1,0:T(8,128)(2,1)S(1)} %broadcast_select_fusion.refs_0_, bf16[1344,1024]{1,0:T(8,128)(2,1)S(1)} %bitcast.16, bf16[1344,512]{1,0:T(8,128)(2,1)S(1)} %bitcast.20, bf16[1344,512]{1,0:T(8,128)(2,1)S(1)} %bitcast.24), custom_call_target="tpu_custom_call" | custom-call | flops 704643072 | bytes 6537216 | tf_op jit(solution)/shard_map/pallas_call | solution.py:187
  63.7 0.1 collective-permute-start.13
  63.8 2.5 %collective-permute-start.12 = (bf16[672,256]{1,0:T(8,128)(2,1)S(1)}, bf16[672,256]{1,0:T(8,128)(2,1)S(1)}, u32[]{:S(2)}, u32[]{:S(2)}) collective-permute-start(bf16[672,256]{1,0:T(8,128)(2,1)S(1)} %pad_maximum_fusion), channel_id=1, source_target_pairs={{8,0},{16,8},{24,16},{0,24},{9,1},{17,9},{25,17},{1,25},{10,2},{18... | collective-permute-start | bytes 1032200 | tf_op jit(solution)/shard_map/ppermute | solution.py:224
  66.3 0.0 collective-permute-done.13
  66.3 3.3 %collective-permute-done.14.refs_0_ = bf16[128,2048]{1,0:T(8,128)(2,1)S(1)} collective-permute-done((bf16[128,2048]{1,0:T(8,128)(2,1)}, bf16[128,2048]{1,0:T(8,128)(2,1)S(1)}, u32[]{:S(2)}, u32[]{:S(2)}) %collective-permute-start.14) | collective-permute-done | bytes 524320 | tf_op jit(solution)/shard_map/ppermute | solution.py:215
  69.7 0.1 add_convert_fusion.1
  69.7 2.0 %shard_map.88 = (f32[672,128]{1,0:T(8,128)S(1)}, bf16[672,128]{1,0:T(8,128)(2,1)S(1)}) custom-call(s32[1]{0:T(128)} %bitcast.core_ref, bf16[128,2048]{1,0:T(8,128)(2,1)S(1)} %collective-permute-done.14.refs_0_, bf16[1344,1024]{1,0:T(8,128)(2,1)S(1)} %bitcast.17, bf16[1344,512]{1,0:T(8,128)(2,1)S(1)} %bitcast.21, bf16[1344,512]{1,0:T(8,128)(2,1)S(1)} %bitcast.25), custom_call_target="tpu_custom_call" | custom-call | flops 704643072 | bytes 6537216 | tf_op jit(solution)/shard_map/pallas_call | solution.py:187
  71.7 0.0 copy-start.12
  71.7 2.6 %collective-permute-done.12 = bf16[672,256]{1,0:T(8,128)(2,1)S(1)} collective-permute-done((bf16[672,256]{1,0:T(8,128)(2,1)S(1)}, bf16[672,256]{1,0:T(8,128)(2,1)S(1)}, u32[]{:S(2)}, u32[]{:S(2)}) %collective-permute-start.12) | collective-permute-done | bytes 344096 | tf_op jit(solution)/shard_map/ppermute | solution.py:224
  74.3 0.0 collective-permute-start.15
  74.4 1.4 %collective-permute-done.15 = bf16[672,128]{1,0:T(8,128)(2,1)S(1)} collective-permute-done((bf16[672,128]{1,0:T(8,128)(2,1)S(1)}, bf16[672,128]{1,0:T(8,128)(2,1)S(1)}, u32[]{:S(2)}, u32[]{:S(2)}) %collective-permute-start.15) | collective-permute-done | bytes 172064 | tf_op jit(solution)/shard_map/ppermute | solution.py:224
  75.8 0.1 pad_maximum_fusion.1
  75.9 3.4 %collective-permute-start.16 = (bf16[672,256]{1,0:T(8,128)(2,1)S(1)}, bf16[672,256]{1,0:T(8,128)(2,1)S(1)}, u32[]{:S(2)}, u32[]{:S(2)}) collective-permute-start(bf16[672,256]{1,0:T(8,128)(2,1)S(1)} %pad_maximum_fusion.1), channel_id=1, source_target_pairs={{8,0},{16,8},{24,16},{0,24},{9,1},{17,9},{25,17},{1,25},{10,2},{18... | collective-permute-start | bytes 1032200 | tf_op jit(solution)/shard_map/ppermute | solution.py:224
  79.4 7.5 %collective-permute-done.16 = bf16[672,256]{1,0:T(8,128)(2,1)S(1)} collective-permute-done((bf16[672,256]{1,0:T(8,128)(2,1)S(1)}, bf16[672,256]{1,0:T(8,128)(2,1)S(1)}, u32[]{:S(2)}, u32[]{:S(2)}) %collective-permute-start.16) | collective-permute-done | bytes 344096 | tf_op jit(solution)/shard_map/ppermute | solution.py:224
  86.9 0.1 select_dynamic-update-slice_fusion.1
  87.0 0.1 select_dynamic-update-slice_fusion
  87.1 0.0 copy-start.10
  87.2 0.8 copy-done.10
  (22 shorter events, 0.3 us)
Async XLA Ops:
  1.0 13.0 %collective-permute-start.1 = (bf16[128,1024]{1,0:T(8,128)(2,1)S(1)}, bf16[128,1024]{1,0:T(8,128)(2,1)S(1)}, u32[]{:S(2)}, u32[]{:S(2)}) collective-permute-start(bf16[128,1024]{1,0:T(8,128)(2,1)S(1)} %pad_maximum_fusion.2.refs_2_), channel_id=1, source_target_pairs={{0,2},{2,4},{4,6},{1,3},{3,5},{5,7},{8,10},{10,12},{12,14},{9,11},... | collective-permute-start | bytes 786440 | tf_op jit(solution)/shard_map/ppermute | solution.py:208
  6.0 8.1 %collective-permute-start = (bf16[48,1024]{1,0:T(8,128)(2,1)S(1)}, bf16[48,1024]{1,0:T(8,128)(2,1)S(1)}, u32[]{:S(2)}, u32[]{:S(2)}) collective-permute-start(bf16[48,1024]{1,0:T(8,128)(2,1)S(1)} %slice.20), channel_id=1, source_target_pairs={{0,4},{2,6},{1,5},{3,7},{8,12},{10,14},{9,13},{11,15},{16,20},{18,... | collective-permute-start | bytes 294920 | tf_op jit(solution)/shard_map/ppermute | solution.py:208
  12.0 1.0 %copy-start.7 = (bf16[1,128,1024]{2,1,0:T(8,128)(2,1)S(1)}, bf16[1,128,1024]{2,1,0:T(8,128)(2,1)}, u32[]{:S(2)}) copy-start(bf16[1,128,1024]{2,1,0:T(8,128)(2,1)} %param.8) | copy-start | bytes 786436
  13.0 0.9 %copy-start.8 = (bf16[1,128,1024]{2,1,0:T(8,128)(2,1)S(1)}, bf16[1,128,1024]{2,1,0:T(8,128)(2,1)}, u32[]{:S(2)}) copy-start(bf16[1,128,1024]{2,1,0:T(8,128)(2,1)} %param.11) | copy-start | bytes 786436
  14.0 19.9 %copy-start = (bf16[1,1344,1024]{2,1,0:T(8,128)(2,1)S(1)}, bf16[1,1344,1024]{2,1,0:T(8,128)(2,1)}, u32[]{:S(2)}) copy-start(bf16[1,1344,1024]{2,1,0:T(8,128)(2,1)} %param.12) | copy-start | bytes 8257540
  16.3 16.0 %collective-permute-start.2 = (bf16[128,1024]{1,0:T(8,128)(2,1)S(1)}, bf16[128,1024]{1,0:T(8,128)(2,1)S(1)}, u32[]{:S(2)}, u32[]{:S(2)}) collective-permute-start(bf16[128,1024]{1,0:T(8,128)(2,1)S(1)} %get-tuple-element.37), channel_id=1, source_target_pairs={{2,0},{4,2},{6,4},{3,1},{5,3},{7,5},{10,8},{12,10},{14,12},{11,9},... | collective-permute-start | bytes 786440 | tf_op jit(solution)/shard_map/ppermute | solution.py:208
  17.6 14.7 %collective-permute-start.3 = (bf16[48,1024]{1,0:T(8,128)(2,1)S(1)}, bf16[48,1024]{1,0:T(8,128)(2,1)S(1)}, u32[]{:S(2)}, u32[]{:S(2)}) collective-permute-start(bf16[48,1024]{1,0:T(8,128)(2,1)S(1)} %get-tuple-element.38), channel_id=1, source_target_pairs={{4,0},{6,2},{5,1},{7,3},{12,8},{14,10},{13,9},{15,11},{20,16},{22,... | collective-permute-start | bytes 294920 | tf_op jit(solution)/shard_map/ppermute | solution.py:208
  32.4 11.2 %collective-permute-start.6 = (bf16[128,2048]{1,0:T(8,128)(2,1)S(1)}, bf16[128,2048]{1,0:T(8,128)(2,1)}, u32[]{:S(2)}, u32[]{:S(2)}) collective-permute-start(bf16[128,2048]{1,0:T(8,128)(2,1)S(1)} %shard_map.84.refs_0_), channel_id=1, source_target_pairs={{0,2},{2,0},{4,6},{6,4},{1,3},{3,1},{5,7},{7,5},{8,10},{10,8},{12,... | collective-permute-start | bytes 1572872 | tf_op jit(solution)/shard_map/ppermute | solution.py:215
  32.5 12.6 %collective-permute-start.7 = (bf16[128,2048]{1,0:T(8,128)(2,1)S(1)}, bf16[128,2048]{1,0:T(8,128)(2,1)}, u32[]{:S(2)}, u32[]{:S(2)}) collective-permute-start(bf16[128,2048]{1,0:T(8,128)(2,1)S(1)} %shard_map.84.refs_0_), channel_id=1, source_target_pairs={{2,4},{4,2},{3,5},{5,3},{10,12},{12,10},{11,13},{13,11},{18,20},{2... | collective-permute-start | bytes 1572872 | tf_op jit(solution)/shard_map/ppermute | solution.py:215
  33.9 1.3 %copy-start.1 = (bf16[1,1344,512]{2,1,0:T(8,128)(2,1)S(1)}, bf16[1,1344,512]{2,1,0:T(8,128)(2,1)}, u32[]{:S(2)}) copy-start(bf16[1,1344,512]{2,1,0:T(8,128)(2,1)} %param.13) | copy-start | bytes 4128772
  35.3 1.3 %copy-start.4 = (bf16[1,1344,512]{2,1,0:T(8,128)(2,1)S(1)}, bf16[1,1344,512]{2,1,0:T(8,128)(2,1)}, u32[]{:S(2)}) copy-start(bf16[1,1344,512]{2,1,0:T(8,128)(2,1)} %param.14) | copy-start | bytes 4128772
  36.6 10.8 %copy-start.2 = (bf16[1,1344,512]{2,1,0:T(8,128)(2,1)S(1)}, bf16[1,1344,512]{2,1,0:T(8,128)(2,1)}, u32[]{:S(2)}) copy-start(bf16[1,1344,512]{2,1,0:T(8,128)(2,1)} %param.13) | copy-start | bytes 4128772
  36.6 10.8 %copy-start.5 = (bf16[1,1344,512]{2,1,0:T(8,128)(2,1)S(1)}, bf16[1,1344,512]{2,1,0:T(8,128)(2,1)}, u32[]{:S(2)}) copy-start(bf16[1,1344,512]{2,1,0:T(8,128)(2,1)} %param.14) | copy-start | bytes 4128772
  38.6 8.0 %collective-permute-start.4 = (bf16[672,128]{1,0:T(8,128)(2,1)S(1)}, bf16[672,128]{1,0:T(8,128)(2,1)S(1)}, u32[]{:S(2)}, u32[]{:S(2)}) collective-permute-start(bf16[672,128]{1,0:T(8,128)(2,1)S(1)} %get-tuple-element.40), channel_id=1, source_target_pairs={{1,0},{0,1},{3,2},{2,3},{5,4},{4,5},{7,6},{6,7},{9,8},{8,9},{11,10... | collective-permute-start | bytes 516104 | tf_op jit(solution)/shard_map/ppermute | solution.py:224
  43.6 11.2 %collective-permute-start.10 = (bf16[128,2048]{1,0:T(8,128)(2,1)}, bf16[128,2048]{1,0:T(8,128)(2,1)}, u32[]{:S(2)}, u32[]{:S(2)}) collective-permute-start(bf16[128,2048]{1,0:T(8,128)(2,1)} %collective-permute-done.6.refs_0_), channel_id=1, source_target_pairs={{2,4},{4,2},{3,5},{5,3},{10,12},{12,10},{11,13},{13,11},{18,20},{2... | collective-permute-start | bytes 1572872 | tf_op jit(solution)/shard_map/ppermute | solution.py:215
  45.0 12.8 %collective-permute-start.9 = (bf16[128,2048]{1,0:T(8,128)(2,1)}, bf16[128,2048]{1,0:T(8,128)(2,1)}, u32[]{:S(2)}, u32[]{:S(2)}) collective-permute-start(bf16[128,2048]{1,0:T(8,128)(2,1)} %collective-permute-done.7.refs_1_), channel_id=1, source_target_pairs={{0,2},{2,0},{4,6},{6,4},{1,3},{3,1},{5,7},{7,5},{8,10},{10,8},{12,... | collective-permute-start | bytes 1572872 | tf_op jit(solution)/shard_map/ppermute | solution.py:215
  51.4 0.7 copy-start.9
  52.1 2.7 %collective-permute-start.11 = (bf16[672,128]{1,0:T(8,128)(2,1)}, bf16[672,128]{1,0:T(8,128)(2,1)}, u32[]{:S(2)}, u32[]{:S(2)}) collective-permute-start(bf16[672,128]{1,0:T(8,128)(2,1)} %get-tuple-element.47), channel_id=1, source_target_pairs={{1,0},{0,1},{3,2},{2,3},{5,4},{4,5},{7,6},{6,7},{9,8},{8,9},{11,10... | collective-permute-start | bytes 516104 | tf_op jit(solution)/shard_map/ppermute | solution.py:224
  52.1 9.6 %collective-permute-start.5 = (bf16[672,128]{1,0:T(8,128)(2,1)}, bf16[672,128]{1,0:T(8,128)(2,1)S(1)}, u32[]{:S(2)}, u32[]{:S(2)}) collective-permute-start(bf16[672,128]{1,0:T(8,128)(2,1)} %add_convert_fusion.4), channel_id=1, source_target_pairs={{8,0},{16,8},{24,16},{0,24},{9,1},{17,9},{25,17},{1,25},{10,2},{18... | collective-permute-start | bytes 516104 | tf_op jit(solution)/shard_map/ppermute | solution.py:224
  54.6 7.1 %copy-start.3 = (bf16[1,1344,512]{2,1,0:T(8,128)(2,1)S(1)}, bf16[1,1344,512]{2,1,0:T(8,128)(2,1)}, u32[]{:S(2)}) copy-start(bf16[1,1344,512]{2,1,0:T(8,128)(2,1)} %param.13) | copy-start | bytes 4128772
  54.6 7.1 %copy-start.6 = (bf16[1,1344,512]{2,1,0:T(8,128)(2,1)S(1)}, bf16[1,1344,512]{2,1,0:T(8,128)(2,1)}, u32[]{:S(2)}) copy-start(bf16[1,1344,512]{2,1,0:T(8,128)(2,1)} %param.14) | copy-start | bytes 4128772
  54.6 7.0 %collective-permute-start.8 = (bf16[672,128]{1,0:T(8,128)(2,1)}, bf16[672,128]{1,0:T(8,128)(2,1)S(1)}, u32[]{:S(2)}, u32[]{:S(2)}) collective-permute-start(bf16[672,128]{1,0:T(8,128)(2,1)} %copy-done.9), channel_id=1, source_target_pairs={{1,0},{0,1},{3,2},{2,3},{5,4},{4,5},{7,6},{6,7},{9,8},{8,9},{11,10... | collective-permute-start | bytes 516104 | tf_op jit(solution)/shard_map/ppermute | solution.py:224
  57.8 11.9 %collective-permute-start.14 = (bf16[128,2048]{1,0:T(8,128)(2,1)}, bf16[128,2048]{1,0:T(8,128)(2,1)S(1)}, u32[]{:S(2)}, u32[]{:S(2)}) collective-permute-start(bf16[128,2048]{1,0:T(8,128)(2,1)} %collective-permute-done.10), channel_id=1, source_target_pairs={{0,2},{2,0},{4,6},{6,4},{1,3},{3,1},{5,7},{7,5},{8,10},{10,8},{12,... | collective-permute-start | bytes 1572872 | tf_op jit(solution)/shard_map/ppermute | solution.py:215
  61.7 2.0 %copy-start.11 = (bf16[672,128]{1,0:T(8,128)(2,1)}, bf16[672,128]{1,0:T(8,128)(2,1)S(1)}, u32[]{:S(2)}) copy-start(bf16[672,128]{1,0:T(8,128)(2,1)S(1)} %collective-permute-done.5) | copy-start | bytes 516100
  63.7 2.6 %collective-permute-start.13 = (bf16[672,128]{1,0:T(8,128)(2,1)S(1)}, bf16[672,128]{1,0:T(8,128)(2,1)S(1)}, u32[]{:S(2)}, u32[]{:S(2)}) collective-permute-start(bf16[672,128]{1,0:T(8,128)(2,1)S(1)} %get-tuple-element.51), channel_id=1, source_target_pairs={{1,0},{0,1},{3,2},{2,3},{5,4},{4,5},{7,6},{6,7},{9,8},{8,9},{11,10... | collective-permute-start | bytes 516104 | tf_op jit(solution)/shard_map/ppermute | solution.py:224
  63.8 10.5 %collective-permute-start.12 = (bf16[672,256]{1,0:T(8,128)(2,1)S(1)}, bf16[672,256]{1,0:T(8,128)(2,1)S(1)}, u32[]{:S(2)}, u32[]{:S(2)}) collective-permute-start(bf16[672,256]{1,0:T(8,128)(2,1)S(1)} %pad_maximum_fusion), channel_id=1, source_target_pairs={{8,0},{16,8},{24,16},{0,24},{9,1},{17,9},{25,17},{1,25},{10,2},{18... | collective-permute-start | bytes 1032200 | tf_op jit(solution)/shard_map/ppermute | solution.py:224
  71.7 7.6 %copy-start.12 = (bf16[672,128]{1,0:T(8,128)(2,1)S(1)}, bf16[672,128]{1,0:T(8,128)(2,1)}, u32[]{:S(2)}) copy-start(bf16[672,128]{1,0:T(8,128)(2,1)} %copy-done.11) | copy-start | bytes 516100
  74.3 1.4 %collective-permute-start.15 = (bf16[672,128]{1,0:T(8,128)(2,1)S(1)}, bf16[672,128]{1,0:T(8,128)(2,1)S(1)}, u32[]{:S(2)}, u32[]{:S(2)}) collective-permute-start(bf16[672,128]{1,0:T(8,128)(2,1)S(1)} %get-tuple-element.56), channel_id=1, source_target_pairs={{1,0},{0,1},{3,2},{2,3},{5,4},{4,5},{7,6},{6,7},{9,8},{8,9},{11,10... | collective-permute-start | bytes 516104 | tf_op jit(solution)/shard_map/ppermute | solution.py:224
  75.9 11.0 %collective-permute-start.16 = (bf16[672,256]{1,0:T(8,128)(2,1)S(1)}, bf16[672,256]{1,0:T(8,128)(2,1)S(1)}, u32[]{:S(2)}, u32[]{:S(2)}) collective-permute-start(bf16[672,256]{1,0:T(8,128)(2,1)S(1)} %pad_maximum_fusion.1), channel_id=1, source_target_pairs={{8,0},{16,8},{24,16},{0,24},{9,1},{17,9},{25,17},{1,25},{10,2},{18... | collective-permute-start | bytes 1032200 | tf_op jit(solution)/shard_map/ppermute | solution.py:224
  87.1 0.8 copy-start.10

commit v11 on v10

--- a/solution.py
+++ b/solution.py
@@ -176,7 +176,7 @@
         give_ref[...] = full_ref[other, cols].astype(jnp.bfloat16)
 
 
-def project(blocks, weights, core):
+def project(blocks, weights, core, light):
     width = weights[0].shape[0]
     rows = sum(block[0].shape[0] for block in blocks)
     half = (width // 2, rows // len(blocks))
@@ -196,8 +196,8 @@
         ],
         compiler_params=pltpu.CompilerParams(vmem_limit_bytes=8 * 1024 * 1024),
         cost_estimate=pl.CostEstimate(
-            flops=2 * rows * width * cols,
-            bytes_accessed=2 * width * cols + 6 * width * rows,
+            flops=1 if light else 2 * rows * width * cols,
+            bytes_accessed=1 if light else 2 * width * cols + 6 * width * rows,
             transcendentals=0,
         ),
     )(core, *flat, *weights)
@@ -273,8 +273,8 @@
     weights = (w_query[0], key_weight[0], value_weight[0])
     core = lax.axis_index("mp").astype(jnp.int32)
 
-    def halves_summed(blocks, late, before=()):
-        halves = project([(block,) for block in blocks], weights, core[None])
+    def halves_summed(blocks, late, before=(), light=False):
+        halves = project([(block,) for block in blocks], weights, core[None], light)
         sums = []
         for keep, give in zip(halves[: len(blocks)], halves[len(blocks) :]):
             if before:
@@ -286,7 +286,7 @@
         return sums
 
     even = place % 2 == 0
-    results, waiting, held, hops = [], [own], [], []
+    results, waiting, hops = [], [own], []
 
     def hop(blocks):
         came = passed_along(jnp.concatenate(blocks, axis=1), "section", -1)
@@ -300,12 +300,9 @@
         came_second = came_first if last else swapped(by_second, "seq", 1)
         if step > 1:
             waiting = after(waiting, *sums, *(hops[-2:-1] if step > 2 else ()))
-        late = (came_first, came_second) if step > 1 else ()
-        sums = halves_summed(waiting, late)
-        if step > 2 and last:
-            held = sums
-        else:
-            results.append(hop(sums))
+        late = (came_first, came_second) if step > 1 and not (step > 2 and last) else ()
+        sums = halves_summed(waiting, late, light=step > 2 and last)
+        results.append(hop(sums))
         by_first, by_second = came_second, came_first
         if last:
             waiting = [came_first]
@@ -313,11 +310,8 @@
             waiting = [came_first, came_second]
         else:
             waiting = [jnp.where(even == (place >= step), came_second, came_first)]
-    if shards > 1:
-        waiting = after(waiting, *sums)
-    sums = halves_summed(waiting, (), hops[-1:])
-    came = hop([*held, *sums])
-    results += [[block] for block in came] if held else [came]
+    sums = halves_summed(waiting, (), hops[-2:])
+    results.append(hop(sums))
     for step, blocks in enumerate(results):
         if len(blocks) > 1:
             first, second = blocks

time: 88.5 us -> 88.6 us (level)
  waiting for transfers between devices: 36.2 us -> 28.7 us
  starting transfers between devices: 27.1 us -> 34.2 us
  other arithmetic: 4.28 us -> 5.3 us
    ppermute x5, starting transfers between devices: 6.32 us -> 12.6 us  [swapped(): return lax.ppermute(block, axis, pairs)]
    ppermute x5, waiting for transfers between devices: 11.2 us -> 5.68 us  [swapped(): return lax.ppermute(block, axis, pairs)]
    ppermute x8 -> x9, waiting for transfers between devices: 11.5 us -> 9.65 us  [passed_along(): lax.ppermute(block, axis, [((i - distance) % len(devices), i) for i in de...]
    convert_element_type x5, other arithmetic: 1.8 us -> 2.87 us  [halves_summed(): sums.append((keep + got.astype(jnp.float32)).astype(jnp.bfloat16))]
    ppermute x8 -> x9, starting transfers between devices: 8.74 us -> 9.61 us  [passed_along(): lax.ppermute(block, axis, [((i - distance) % len(devices), i) for i in de...]
    unnamed x26 -> x24, local copies, waits for them, and re-layouts: 6.12 us -> 5.45 us
  transfers between devices with their start and end apart: 17 -> 18, of which waited for: 7 -> 8; matrix products, arithmetic and copies ran while one was open for 5% -> 6% of each run, Pallas kernels for 12% -> 12%
where the time goes in v11:
time: 88.6 us; the launch traced here: 88.1 us
  starting transfers between devices  34.2 us (39%)
  waiting for transfers between devices  28.7 us (32%)
  Pallas kernels  12.6 us (14%)
  local copies, waits for them, and re-layouts  7.02 us (8%)
  other arithmetic  5.3 us (6%)
    ppermute x4, waiting for transfers between devices, moved(): lax.ppermute(block, axis, [(i, i + by) for i in range(size) if 0 <= i + b...  13.3 us
    ppermute x5, starting transfers between devices, swapped(): return lax.ppermute(block, axis, pairs)  12.6 us
    ppermute x4, starting transfers between devices, moved(): lax.ppermute(block, axis, [(i, i + by) for i in range(size) if 0 <= i + b...  12 us
    pallas_call x4, Pallas kernels, project(): pl.pallas_call(functools.partial(project_kernel, [len(block) for block in...  10.1 us
    ppermute x9, waiting for transfers between devices, passed_along(): lax.ppermute(block, axis, [((i - distance) % len(devices), i) for i in de...  9.65 us
    ppermute x9, starting transfers between devices, passed_along(): lax.ppermute(block, axis, [((i - distance) % len(devices), i) for i in de...  9.61 us
    ppermute x5, waiting for transfers between devices, swapped(): return lax.ppermute(block, axis, pairs)  5.68 us
    unnamed x24, local copies, waits for them, and re-layouts  5.45 us
  transfers between devices with their start and end apart: 18, of which 8 were waited for; matrix products, arithmetic and copies ran while one was open for 6% of the time, Pallas kernels for 12%

profile of v11, /device:TPU:0, one launch (start us, length us, event | category | flops | bytes accessed | tf_op | source)
XLA Modules:
  0.0 88.1 jit_solution(1804666962652329716)
XLA Ops:
  0.0 1.0 %pad_maximum_fusion.1.refs_2_ = bf16[128,1024]{1,0:T(8,128)(2,1)S(1)} fusion(bf16[128,512]{1,0:T(8,128)(2,1)} %bitcast.28, bf16[128,512]{1,0:T(8,128)(2,1)} %bitcast.29), kind=kLoop, calls=%fused_computation.7 | loop fusion | flops 524288 | bytes 524288 | tf_op jit(solution)/shard_map/concatenate | solution.py:248
  1.0 4.9 %collective-permute-start.1 = (bf16[128,1024]{1,0:T(8,128)(2,1)S(1)}, bf16[128,1024]{1,0:T(8,128)(2,1)S(1)}, u32[]{:S(2)}, u32[]{:S(2)}) collective-permute-start(bf16[128,1024]{1,0:T(8,128)(2,1)S(1)} %pad_maximum_fusion.1.refs_2_), channel_id=1, source_target_pairs={{0,2},{2,4},{4,6},{1,3},{3,5},{5,7},{8,10},{10,12},{12,14},{9,11},... | collective-permute-start | bytes 786440 | tf_op jit(solution)/shard_map/ppermute | solution.py:208
  6.0 4.5 %collective-permute-start = (bf16[48,1024]{1,0:T(8,128)(2,1)S(1)}, bf16[48,1024]{1,0:T(8,128)(2,1)S(1)}, u32[]{:S(2)}, u32[]{:S(2)}) collective-permute-start(bf16[48,1024]{1,0:T(8,128)(2,1)S(1)} %slice.12), channel_id=1, source_target_pairs={{0,4},{2,6},{1,5},{3,7},{8,12},{10,14},{9,13},{11,15},{16,20},{18,... | collective-permute-start | bytes 294920 | tf_op jit(solution)/shard_map/ppermute | solution.py:208
  10.5 0.8 pad_dynamic-slice_fusion
  11.2 0.7 fusion.5
  11.9 0.1 fusion.4.refs_3_
  12.0 0.0 copy-start.7
  12.0 0.9 %copy-done.7 = bf16[1,128,1024]{2,1,0:T(8,128)(2,1)S(1)} copy-done((bf16[1,128,1024]{2,1,0:T(8,128)(2,1)S(1)}, bf16[1,128,1024]{2,1,0:T(8,128)(2,1)}, u32[]{:S(2)}) %copy-start.7) | copy-done | bytes 262168
  13.0 0.9 %copy-done.8 = bf16[1,128,1024]{2,1,0:T(8,128)(2,1)S(1)} copy-done((bf16[1,128,1024]{2,1,0:T(8,128)(2,1)S(1)}, bf16[1,128,1024]{2,1,0:T(8,128)(2,1)}, u32[]{:S(2)}) %copy-start.8) | copy-done | bytes 262168
  13.9 0.1 shard_map.82
  14.0 0.0 collective-permute-done.refs_4_
  14.0 0.0 collective-permute-done.1.refs_5_
  14.0 0.0 copy-start
  14.0 2.2 %shard_map.83 = (bf16[128,1024]{1,0:T(8,128)(2,1)S(1)}, f32[128,1024]{1,0:T(8,128)S(1)}, bf16[48,1024]{1,0:T(8,128)(2,1)S(1)}, bf16[128,1024]{1,0:T(8,128)(2,1)S(1)}) custom-call(bf16[1024,128]{1,0:T(8,128)(2,1)S(1)} %get-tuple-element.31.refs_0_, bf16[1024,128]{1,0:T(8,128)(2,1)S(1)} %get-tuple-element.32.refs_1_, ...), custom_call_target="tpu_custom_call" | custom-call | flops 478150656 | bytes 1048576 | tf_op jit(solution)/shard_map/pallas_call | solution.py:100
  16.3 1.3 %collective-permute-start.2 = (bf16[128,1024]{1,0:T(8,128)(2,1)S(1)}, bf16[128,1024]{1,0:T(8,128)(2,1)S(1)}, u32[]{:S(2)}, u32[]{:S(2)}) collective-permute-start(bf16[128,1024]{1,0:T(8,128)(2,1)S(1)} %get-tuple-element.35), channel_id=1, source_target_pairs={{2,0},{4,2},{6,4},{3,1},{5,3},{7,5},{10,8},{12,10},{14,12},{11,9},... | collective-permute-start | bytes 786440 | tf_op jit(solution)/shard_map/ppermute | solution.py:208
  17.6 1.3 %collective-permute-start.3 = (bf16[48,1024]{1,0:T(8,128)(2,1)S(1)}, bf16[48,1024]{1,0:T(8,128)(2,1)S(1)}, u32[]{:S(2)}, u32[]{:S(2)}) collective-permute-start(bf16[48,1024]{1,0:T(8,128)(2,1)S(1)} %get-tuple-element.36), channel_id=1, source_target_pairs={{4,0},{6,2},{5,1},{7,3},{12,8},{14,10},{13,9},{15,11},{20,16},{22,... | collective-permute-start | bytes 294920 | tf_op jit(solution)/shard_map/ppermute | solution.py:208
  18.9 13.3 %collective-permute-done.3.refs_1_ = bf16[48,1024]{1,0:T(8,128)(2,1)S(1)} collective-permute-done((bf16[48,1024]{1,0:T(8,128)(2,1)S(1)}, bf16[48,1024]{1,0:T(8,128)(2,1)S(1)}, u32[]{:S(2)}, u32[]{:S(2)}) %collective-permute-start.3) | collective-permute-done | bytes 98336 | tf_op jit(solution)/shard_map/ppermute | solution.py:208
  32.2 0.0 collective-permute-done.2.refs_0_
  32.2 0.1 shard_map.84.refs_0_
  32.3 1.5 %collective-permute-start.7 = (bf16[128,2048]{1,0:T(8,128)(2,1)S(1)}, bf16[128,2048]{1,0:T(8,128)(2,1)}, u32[]{:S(2)}, u32[]{:S(2)}) collective-permute-start(bf16[128,2048]{1,0:T(8,128)(2,1)S(1)} %shard_map.84.refs_0_), channel_id=1, source_target_pairs={{2,4},{4,2},{3,5},{5,3},{10,12},{12,10},{11,13},{13,11},{18,20},{2... | collective-permute-start | bytes 1572872 | tf_op jit(solution)/shard_map/ppermute | solution.py:215
  33.8 0.6 collective-permute-start.6
  34.4 1.3 %copy-done.1 = bf16[1,1344,512]{2,1,0:T(8,128)(2,1)S(1)} copy-done((bf16[1,1344,512]{2,1,0:T(8,128)(2,1)S(1)}, bf16[1,1344,512]{2,1,0:T(8,128)(2,1)}, u32[]{:S(2)}) %copy-start.1) | copy-done | bytes 1376280
  35.8 1.3 %copy-done.4 = bf16[1,1344,512]{2,1,0:T(8,128)(2,1)S(1)} copy-done((bf16[1,1344,512]{2,1,0:T(8,128)(2,1)S(1)}, bf16[1,1344,512]{2,1,0:T(8,128)(2,1)}, u32[]{:S(2)}) %copy-start.4) | copy-done | bytes 1376280
  37.1 2.0 %shard_map.85 = (f32[672,128]{1,0:T(8,128)S(1)}, bf16[672,128]{1,0:T(8,128)(2,1)S(1)}) custom-call(s32[1]{0:T(128)} %bitcast.core_ref, bf16[128,2048]{1,0:T(8,128)(2,1)S(1)} %shard_map.84.refs_0_, bf16[1344,1024]{1,0:T(8,128)(2,1)S(1)} %bitcast.14, bf16[1344,512]{1,0:T(8,128)(2,1)S(1)} %bitcast.18, bf16[1344,512]{1,0:T(8,128)(2,1)S(1)} %bitcast.22), custom_call_target="tpu_custom_call" | custom-call | flops 704643072 | bytes 6537216 | tf_op jit(solution)/shard_map/pallas_call | solution.py:187
  39.1 0.1 collective-permute-start.4
  39.2 0.0 collective-permute-done.7.refs_1_
  39.2 5.7 %collective-permute-start.9 = (bf16[128,2048]{1,0:T(8,128)(2,1)}, bf16[128,2048]{1,0:T(8,128)(2,1)}, u32[]{:S(2)}, u32[]{:S(2)}) collective-permute-start(bf16[128,2048]{1,0:T(8,128)(2,1)} %collective-permute-done.7.refs_1_), channel_id=1, source_target_pairs={{0,2},{2,0},{4,6},{6,4},{1,3},{3,1},{5,7},{7,5},{8,10},{10,8},{12,... | collective-permute-start | bytes 1572872 | tf_op jit(solution)/shard_map/ppermute | solution.py:215
  45.0 1.2 %collective-permute-done.6.refs_0_ = bf16[128,2048]{1,0:T(8,128)(2,1)} collective-permute-done((bf16[128,2048]{1,0:T(8,128)(2,1)S(1)}, bf16[128,2048]{1,0:T(8,128)(2,1)}, u32[]{:S(2)}, u32[]{:S(2)}) %collective-permute-start.6) | collective-permute-done | bytes 524320 | tf_op jit(solution)/shard_map/ppermute | solution.py:215
  46.1 1.4 %collective-permute-start.10 = (bf16[128,2048]{1,0:T(8,128)(2,1)}, bf16[128,2048]{1,0:T(8,128)(2,1)}, u32[]{:S(2)}, u32[]{:S(2)}) collective-permute-start(bf16[128,2048]{1,0:T(8,128)(2,1)} %collective-permute-done.6.refs_0_), channel_id=1, source_target_pairs={{2,4},{4,2},{3,5},{5,3},{10,12},{12,10},{11,13},{13,11},{18,20},{2... | collective-permute-start | bytes 1572872 | tf_op jit(solution)/shard_map/ppermute | solution.py:215
  47.6 0.0 collective-permute-done.4
  47.6 0.7 add_convert_fusion.4
  48.3 4.1 %shard_map.86 = (f32[672,128]{1,0:T(8,128)S(1)}, f32[672,128]{1,0:T(8,128)S(1)}, bf16[672,128]{1,0:T(8,128)(2,1)}, bf16[672,128]{1,0:T(8,128)(2,1)}) custom-call(s32[1]{0:T(128)} %bitcast.core_ref, bf16[128,2048]{1,0:T(8,128)(2,1)} %collective-permute-done.6.refs_0_, bf16[128,2048]{1,0:T(8,128)(2,1)} %collective-permute-done.7.refs_1_, ...), custom_call_target="tpu_custom_call" | custom-call | flops 1409286144 | bytes 7569408 | tf_op jit(solution)/shard_map/pallas_call | solution.py:187
  52.4 0.0 collective-permute-start.11
  52.4 0.5 collective-permute-start.8
  52.9 2.5 %collective-permute-start.5 = (bf16[672,128]{1,0:T(8,128)(2,1)}, bf16[672,128]{1,0:T(8,128)(2,1)S(1)}, u32[]{:S(2)}, u32[]{:S(2)}) collective-permute-start(bf16[672,128]{1,0:T(8,128)(2,1)} %add_convert_fusion.4), channel_id=1, source_target_pairs={{8,0},{16,8},{24,16},{0,24},{9,1},{17,9},{25,17},{1,25},{10,2},{18... | collective-permute-start | bytes 516104 | tf_op jit(solution)/shard_map/ppermute | solution.py:224
  55.4 0.2 collective-permute-done.9
  55.7 0.0 collective-permute-done.10
  55.7 0.0 collective-permute-done.8
  55.7 0.0 copy-start.6
  55.7 1.1 %add_convert_fusion.2 = bf16[672,128]{1,0:T(8,128)(2,1)S(1)} fusion(f32[672,128]{1,0:T(8,128)S(1)} %get-tuple-element.44, bf16[672,128]{1,0:T(8,128)(2,1)} %collective-permute-done.11), kind=kLoop, calls=%fused_computation.4 | loop fusion | flops 258048 | bytes 688128 | tf_op jit(solution)/shard_map/convert_element_type | solution.py:285
  56.8 3.3 %collective-permute-start.13 = (bf16[128,2048]{1,0:T(8,128)(2,1)}, bf16[128,2048]{1,0:T(8,128)(2,1)S(1)}, u32[]{:S(2)}, u32[]{:S(2)}) collective-permute-start(bf16[128,2048]{1,0:T(8,128)(2,1)} %collective-permute-done.10), channel_id=1, source_target_pairs={{0,2},{2,0},{4,6},{6,4},{1,3},{3,1},{5,7},{7,5},{8,10},{10,8},{12,... | collective-permute-start | bytes 1572872 | tf_op jit(solution)/shard_map/ppermute | solution.py:215
  60.1 1.1 %broadcast_select_fusion.refs_0_ = bf16[128,2048]{1,0:T(8,128)(2,1)S(1)} fusion(bf16[128,2048]{1,0:T(8,128)(2,1)} %collective-permute-done.10, bf16[128,2048]{1,0:T(8,128)(2,1)} %collective-permute-done.9, pred[]{:T(512)S(6)} %eq.32), kind=kLoop, calls=%fused_computation | loop fusion | flops 262144 | bytes 1572865 | tf_op jit(solution)/shard_map/jit(_where)/select_n | solution.py:312
  61.2 1.0 %add_convert_fusion.3 = bf16[672,128]{1,0:T(8,128)(2,1)S(1)} fusion(f32[672,128]{1,0:T(8,128)S(1)} %get-tuple-element.41, bf16[672,128]{1,0:T(8,128)(2,1)} %collective-permute-done.8), kind=kLoop, calls=%fused_computation.5 | loop fusion | flops 258048 | bytes 688128 | tf_op jit(solution)/shard_map/convert_element_type | solution.py:285
  62.2 0.0 collective-permute-done.5
  62.2 0.0 copy-start.10
  62.2 2.0 %shard_map.88 = (f32[672,128]{1,0:T(8,128)S(1)}, bf16[672,128]{1,0:T(8,128)(2,1)S(1)}) custom-call(s32[1]{0:T(128)} %bitcast.core_ref, bf16[128,2048]{1,0:T(8,128)(2,1)S(1)} %broadcast_select_fusion.refs_0_, bf16[1344,1024]{1,0:T(8,128)(2,1)S(1)} %bitcast.16, bf16[1344,512]{1,0:T(8,128)(2,1)S(1)} %bitcast.20, bf16[1344,512]{1,0:T(8,128)(2,1)S(1)} %bitcast.24), custom_call_target="tpu_custom_call" | custom-call | flops 1 | bytes 1 | tf_op jit(solution)/shard_map/pallas_call | solution.py:187
  64.2 0.1 collective-permute-start.14
  64.4 2.1 %collective-permute-start.12 = (bf16[672,256]{1,0:T(8,128)(2,1)S(1)}, bf16[672,256]{1,0:T(8,128)(2,1)S(1)}, u32[]{:S(2)}, u32[]{:S(2)}) collective-permute-start(bf16[672,256]{1,0:T(8,128)(2,1)S(1)} %pad_maximum_fusion), channel_id=1, source_target_pairs={{8,0},{16,8},{24,16},{0,24},{9,1},{17,9},{25,17},{1,25},{10,2},{18... | collective-permute-start | bytes 1032200 | tf_op jit(solution)/shard_map/ppermute | solution.py:224
  66.5 0.1 add_convert_fusion.1
  66.5 1.3 %collective-permute-start.15 = (bf16[672,128]{1,0:T(8,128)(2,1)S(1)}, bf16[672,128]{1,0:T(8,128)(2,1)S(1)}, u32[]{:S(2)}, u32[]{:S(2)}) collective-permute-start(bf16[672,128]{1,0:T(8,128)(2,1)S(1)} %add_convert_fusion.1), channel_id=1, source_target_pairs={{8,0},{16,8},{24,16},{0,24},{9,1},{17,9},{25,17},{1,25},{10,2},{18... | collective-permute-start | bytes 516104 | tf_op jit(solution)/shard_map/ppermute | solution.py:224
  67.9 4.2 %collective-permute-done.13.refs_0_ = bf16[128,2048]{1,0:T(8,128)(2,1)S(1)} collective-permute-done((bf16[128,2048]{1,0:T(8,128)(2,1)}, bf16[128,2048]{1,0:T(8,128)(2,1)S(1)}, u32[]{:S(2)}, u32[]{:S(2)}) %collective-permute-start.13) | collective-permute-done | bytes 524320 | tf_op jit(solution)/shard_map/ppermute | solution.py:215
  72.1 2.0 %shard_map.87 = (f32[672,128]{1,0:T(8,128)S(1)}, bf16[672,128]{1,0:T(8,128)(2,1)S(1)}) custom-call(s32[1]{0:T(128)} %bitcast.core_ref, bf16[128,2048]{1,0:T(8,128)(2,1)S(1)} %collective-permute-done.13.refs_0_, bf16[1344,1024]{1,0:T(8,128)(2,1)S(1)} %bitcast.17, bf16[1344,512]{1,0:T(8,128)(2,1)S(1)} %bitcast.21, bf16[1344,512]{1,0:T(8,128)(2,1)S(1)} %bitcast.25), custom_call_target="tpu_custom_call" | custom-call | flops 704643072 | bytes 6537216 | tf_op jit(solution)/shard_map/pallas_call | solution.py:187
  74.1 0.0 copy-start.11
  74.2 1.1 %collective-permute-done.12 = bf16[672,256]{1,0:T(8,128)(2,1)S(1)} collective-permute-done((bf16[672,256]{1,0:T(8,128)(2,1)S(1)}, bf16[672,256]{1,0:T(8,128)(2,1)S(1)}, u32[]{:S(2)}, u32[]{:S(2)}) %collective-permute-start.12) | collective-permute-done | bytes 344096 | tf_op jit(solution)/shard_map/ppermute | solution.py:224
  75.3 3.3 %collective-permute-done.15 = bf16[672,128]{1,0:T(8,128)(2,1)S(1)} collective-permute-done((bf16[672,128]{1,0:T(8,128)(2,1)S(1)}, bf16[672,128]{1,0:T(8,128)(2,1)S(1)}, u32[]{:S(2)}, u32[]{:S(2)}) %collective-permute-start.15) | collective-permute-done | bytes 172064 | tf_op jit(solution)/shard_map/ppermute | solution.py:224
  78.6 0.0 collective-permute-start.16
  78.6 1.4 %collective-permute-done.16 = bf16[672,128]{1,0:T(8,128)(2,1)S(1)} collective-permute-done((bf16[672,128]{1,0:T(8,128)(2,1)S(1)}, bf16[672,128]{1,0:T(8,128)(2,1)S(1)}, u32[]{:S(2)}, u32[]{:S(2)}) %collective-permute-start.16) | collective-permute-done | bytes 172064 | tf_op jit(solution)/shard_map/ppermute | solution.py:224
  80.0 0.1 add_convert_fusion
  80.0 3.0 %collective-permute-start.17 = (bf16[672,128]{1,0:T(8,128)(2,1)S(1)}, bf16[672,128]{1,0:T(8,128)(2,1)S(1)}, u32[]{:S(2)}, u32[]{:S(2)}) collective-permute-start(bf16[672,128]{1,0:T(8,128)(2,1)S(1)} %add_convert_fusion), channel_id=1, source_target_pairs={{8,0},{16,8},{24,16},{0,24},{9,1},{17,9},{25,17},{1,25},{10,2},{18... | collective-permute-start | bytes 516104 | tf_op jit(solution)/shard_map/ppermute | solution.py:224
  83.2 3.8 %collective-permute-done.17 = bf16[672,128]{1,0:T(8,128)(2,1)S(1)} collective-permute-done((bf16[672,128]{1,0:T(8,128)(2,1)S(1)}, bf16[672,128]{1,0:T(8,128)(2,1)S(1)}, u32[]{:S(2)}, u32[]{:S(2)}) %collective-permute-start.17) | collective-permute-done | bytes 172064 | tf_op jit(solution)/shard_map/ppermute | solution.py:224
  87.0 0.1 select_dynamic-update-slice_fusion.1
  87.1 0.1 select_dynamic-update-slice_fusion
  87.2 0.0 copy-start.9
  87.2 0.8 copy-done.9
  (21 shorter events, 0.2 us)
Async XLA Ops:
  1.0 13.0 %collective-permute-start.1 = (bf16[128,1024]{1,0:T(8,128)(2,1)S(1)}, bf16[128,1024]{1,0:T(8,128)(2,1)S(1)}, u32[]{:S(2)}, u32[]{:S(2)}) collective-permute-start(bf16[128,1024]{1,0:T(8,128)(2,1)S(1)} %pad_maximum_fusion.1.refs_2_), channel_id=1, source_target_pairs={{0,2},{2,4},{4,6},{1,3},{3,5},{5,7},{8,10},{10,12},{12,14},{9,11},... | collective-permute-start | bytes 786440 | tf_op jit(solution)/shard_map/ppermute | solution.py:208
  6.0 8.1 %collective-permute-start = (bf16[48,1024]{1,0:T(8,128)(2,1)S(1)}, bf16[48,1024]{1,0:T(8,128)(2,1)S(1)}, u32[]{:S(2)}, u32[]{:S(2)}) collective-permute-start(bf16[48,1024]{1,0:T(8,128)(2,1)S(1)} %slice.12), channel_id=1, source_target_pairs={{0,4},{2,6},{1,5},{3,7},{8,12},{10,14},{9,13},{11,15},{16,20},{18,... | collective-permute-start | bytes 294920 | tf_op jit(solution)/shard_map/ppermute | solution.py:208
  12.0 1.0 %copy-start.7 = (bf16[1,128,1024]{2,1,0:T(8,128)(2,1)S(1)}, bf16[1,128,1024]{2,1,0:T(8,128)(2,1)}, u32[]{:S(2)}) copy-start(bf16[1,128,1024]{2,1,0:T(8,128)(2,1)} %param.8) | copy-start | bytes 786436
  13.0 0.9 %copy-start.8 = (bf16[1,128,1024]{2,1,0:T(8,128)(2,1)S(1)}, bf16[1,128,1024]{2,1,0:T(8,128)(2,1)}, u32[]{:S(2)}) copy-start(bf16[1,128,1024]{2,1,0:T(8,128)(2,1)} %param.11) | copy-start | bytes 786436
  14.0 20.4 %copy-start = (bf16[1,1344,1024]{2,1,0:T(8,128)(2,1)S(1)}, bf16[1,1344,1024]{2,1,0:T(8,128)(2,1)}, u32[]{:S(2)}) copy-start(bf16[1,1344,1024]{2,1,0:T(8,128)(2,1)} %param.12) | copy-start | bytes 8257540
  16.3 15.9 %collective-permute-start.2 = (bf16[128,1024]{1,0:T(8,128)(2,1)S(1)}, bf16[128,1024]{1,0:T(8,128)(2,1)S(1)}, u32[]{:S(2)}, u32[]{:S(2)}) collective-permute-start(bf16[128,1024]{1,0:T(8,128)(2,1)S(1)} %get-tuple-element.35), channel_id=1, source_target_pairs={{2,0},{4,2},{6,4},{3,1},{5,3},{7,5},{10,8},{12,10},{14,12},{11,9},... | collective-permute-start | bytes 786440 | tf_op jit(solution)/shard_map/ppermute | solution.py:208
  17.6 14.6 %collective-permute-start.3 = (bf16[48,1024]{1,0:T(8,128)(2,1)S(1)}, bf16[48,1024]{1,0:T(8,128)(2,1)S(1)}, u32[]{:S(2)}, u32[]{:S(2)}) collective-permute-start(bf16[48,1024]{1,0:T(8,128)(2,1)S(1)} %get-tuple-element.36), channel_id=1, source_target_pairs={{4,0},{6,2},{5,1},{7,3},{12,8},{14,10},{13,9},{15,11},{20,16},{22,... | collective-permute-start | bytes 294920 | tf_op jit(solution)/shard_map/ppermute | solution.py:208
  32.3 6.9 %collective-permute-start.7 = (bf16[128,2048]{1,0:T(8,128)(2,1)S(1)}, bf16[128,2048]{1,0:T(8,128)(2,1)}, u32[]{:S(2)}, u32[]{:S(2)}) collective-permute-start(bf16[128,2048]{1,0:T(8,128)(2,1)S(1)} %shard_map.84.refs_0_), channel_id=1, source_target_pairs={{2,4},{4,2},{3,5},{5,3},{10,12},{12,10},{11,13},{13,11},{18,20},{2... | collective-permute-start | bytes 1572872 | tf_op jit(solution)/shard_map/ppermute | solution.py:215
  33.8 12.4 %collective-permute-start.6 = (bf16[128,2048]{1,0:T(8,128)(2,1)S(1)}, bf16[128,2048]{1,0:T(8,128)(2,1)}, u32[]{:S(2)}, u32[]{:S(2)}) collective-permute-start(bf16[128,2048]{1,0:T(8,128)(2,1)S(1)} %shard_map.84.refs_0_), channel_id=1, source_target_pairs={{0,2},{2,0},{4,6},{6,4},{1,3},{3,1},{5,7},{7,5},{8,10},{10,8},{12,... | collective-permute-start | bytes 1572872 | tf_op jit(solution)/shard_map/ppermute | solution.py:215
  34.4 1.3 %copy-start.1 = (bf16[1,1344,512]{2,1,0:T(8,128)(2,1)S(1)}, bf16[1,1344,512]{2,1,0:T(8,128)(2,1)}, u32[]{:S(2)}) copy-start(bf16[1,1344,512]{2,1,0:T(8,128)(2,1)} %param.13) | copy-start | bytes 4128772
  35.8 1.3 %copy-start.4 = (bf16[1,1344,512]{2,1,0:T(8,128)(2,1)S(1)}, bf16[1,1344,512]{2,1,0:T(8,128)(2,1)}, u32[]{:S(2)}) copy-start(bf16[1,1344,512]{2,1,0:T(8,128)(2,1)} %param.14) | copy-start | bytes 4128772
  37.1 11.2 %copy-start.2 = (bf16[1,1344,512]{2,1,0:T(8,128)(2,1)S(1)}, bf16[1,1344,512]{2,1,0:T(8,128)(2,1)}, u32[]{:S(2)}) copy-start(bf16[1,1344,512]{2,1,0:T(8,128)(2,1)} %param.13) | copy-start | bytes 4128772
  37.1 11.2 %copy-start.5 = (bf16[1,1344,512]{2,1,0:T(8,128)(2,1)S(1)}, bf16[1,1344,512]{2,1,0:T(8,128)(2,1)}, u32[]{:S(2)}) copy-start(bf16[1,1344,512]{2,1,0:T(8,128)(2,1)} %param.14) | copy-start | bytes 4128772
  39.1 8.5 %collective-permute-start.4 = (bf16[672,128]{1,0:T(8,128)(2,1)S(1)}, bf16[672,128]{1,0:T(8,128)(2,1)S(1)}, u32[]{:S(2)}, u32[]{:S(2)}) collective-permute-start(bf16[672,128]{1,0:T(8,128)(2,1)S(1)} %get-tuple-element.38), channel_id=1, source_target_pairs={{1,0},{0,1},{3,2},{2,3},{5,4},{4,5},{7,6},{6,7},{9,8},{8,9},{11,10... | collective-permute-start | bytes 516104 | tf_op jit(solution)/shard_map/ppermute | solution.py:224
  39.2 16.4 %collective-permute-start.9 = (bf16[128,2048]{1,0:T(8,128)(2,1)}, bf16[128,2048]{1,0:T(8,128)(2,1)}, u32[]{:S(2)}, u32[]{:S(2)}) collective-permute-start(bf16[128,2048]{1,0:T(8,128)(2,1)} %collective-permute-done.7.refs_1_), channel_id=1, source_target_pairs={{0,2},{2,0},{4,6},{6,4},{1,3},{3,1},{5,7},{7,5},{8,10},{10,8},{12,... | collective-permute-start | bytes 1572872 | tf_op jit(solution)/shard_map/ppermute | solution.py:215
  46.1 9.5 %collective-permute-start.10 = (bf16[128,2048]{1,0:T(8,128)(2,1)}, bf16[128,2048]{1,0:T(8,128)(2,1)}, u32[]{:S(2)}, u32[]{:S(2)}) collective-permute-start(bf16[128,2048]{1,0:T(8,128)(2,1)} %collective-permute-done.6.refs_0_), channel_id=1, source_target_pairs={{2,4},{4,2},{3,5},{5,3},{10,12},{12,10},{11,13},{13,11},{18,20},{2... | collective-permute-start | bytes 1572872 | tf_op jit(solution)/shard_map/ppermute | solution.py:215
  52.4 3.0 %collective-permute-start.11 = (bf16[672,128]{1,0:T(8,128)(2,1)}, bf16[672,128]{1,0:T(8,128)(2,1)}, u32[]{:S(2)}, u32[]{:S(2)}) collective-permute-start(bf16[672,128]{1,0:T(8,128)(2,1)} %get-tuple-element.45), channel_id=1, source_target_pairs={{1,0},{0,1},{3,2},{2,3},{5,4},{4,5},{7,6},{6,7},{9,8},{8,9},{11,10... | collective-permute-start | bytes 516104 | tf_op jit(solution)/shard_map/ppermute | solution.py:224
  52.4 3.2 %collective-permute-start.8 = (bf16[672,128]{1,0:T(8,128)(2,1)}, bf16[672,128]{1,0:T(8,128)(2,1)}, u32[]{:S(2)}, u32[]{:S(2)}) collective-permute-start(bf16[672,128]{1,0:T(8,128)(2,1)} %get-tuple-element.42), channel_id=1, source_target_pairs={{1,0},{0,1},{3,2},{2,3},{5,4},{4,5},{7,6},{6,7},{9,8},{8,9},{11,10... | collective-permute-start | bytes 516104 | tf_op jit(solution)/shard_map/ppermute | solution.py:224
  52.9 9.2 %collective-permute-start.5 = (bf16[672,128]{1,0:T(8,128)(2,1)}, bf16[672,128]{1,0:T(8,128)(2,1)S(1)}, u32[]{:S(2)}, u32[]{:S(2)}) collective-permute-start(bf16[672,128]{1,0:T(8,128)(2,1)} %add_convert_fusion.4), channel_id=1, source_target_pairs={{8,0},{16,8},{24,16},{0,24},{9,1},{17,9},{25,17},{1,25},{10,2},{18... | collective-permute-start | bytes 516104 | tf_op jit(solution)/shard_map/ppermute | solution.py:224
  55.7 6.5 %copy-start.3 = (bf16[1,1344,512]{2,1,0:T(8,128)(2,1)S(1)}, bf16[1,1344,512]{2,1,0:T(8,128)(2,1)}, u32[]{:S(2)}) copy-start(bf16[1,1344,512]{2,1,0:T(8,128)(2,1)} %param.13) | copy-start | bytes 4128772
  55.7 6.5 %copy-start.6 = (bf16[1,1344,512]{2,1,0:T(8,128)(2,1)S(1)}, bf16[1,1344,512]{2,1,0:T(8,128)(2,1)}, u32[]{:S(2)}) copy-start(bf16[1,1344,512]{2,1,0:T(8,128)(2,1)} %param.14) | copy-start | bytes 4128772
  56.8 15.3 %collective-permute-start.13 = (bf16[128,2048]{1,0:T(8,128)(2,1)}, bf16[128,2048]{1,0:T(8,128)(2,1)S(1)}, u32[]{:S(2)}, u32[]{:S(2)}) collective-permute-start(bf16[128,2048]{1,0:T(8,128)(2,1)} %collective-permute-done.10), channel_id=1, source_target_pairs={{0,2},{2,0},{4,6},{6,4},{1,3},{3,1},{5,7},{7,5},{8,10},{10,8},{12,... | collective-permute-start | bytes 1572872 | tf_op jit(solution)/shard_map/ppermute | solution.py:215
  62.2 2.0 %copy-start.10 = (bf16[672,128]{1,0:T(8,128)(2,1)}, bf16[672,128]{1,0:T(8,128)(2,1)S(1)}, u32[]{:S(2)}) copy-start(bf16[672,128]{1,0:T(8,128)(2,1)S(1)} %collective-permute-done.5) | copy-start | bytes 516100
  64.2 2.3 %collective-permute-start.14 = (bf16[672,128]{1,0:T(8,128)(2,1)S(1)}, bf16[672,128]{1,0:T(8,128)(2,1)S(1)}, u32[]{:S(2)}, u32[]{:S(2)}) collective-permute-start(bf16[672,128]{1,0:T(8,128)(2,1)S(1)} %get-tuple-element.51), channel_id=1, source_target_pairs={{1,0},{0,1},{3,2},{2,3},{5,4},{4,5},{7,6},{6,7},{9,8},{8,9},{11,10... | collective-permute-start | bytes 516104 | tf_op jit(solution)/shard_map/ppermute | solution.py:224
  64.4 10.9 %collective-permute-start.12 = (bf16[672,256]{1,0:T(8,128)(2,1)S(1)}, bf16[672,256]{1,0:T(8,128)(2,1)S(1)}, u32[]{:S(2)}, u32[]{:S(2)}) collective-permute-start(bf16[672,256]{1,0:T(8,128)(2,1)S(1)} %pad_maximum_fusion), channel_id=1, source_target_pairs={{8,0},{16,8},{24,16},{0,24},{9,1},{17,9},{25,17},{1,25},{10,2},{18... | collective-permute-start | bytes 1032200 | tf_op jit(solution)/shard_map/ppermute | solution.py:224
  66.5 12.0 %collective-permute-start.15 = (bf16[672,128]{1,0:T(8,128)(2,1)S(1)}, bf16[672,128]{1,0:T(8,128)(2,1)S(1)}, u32[]{:S(2)}, u32[]{:S(2)}) collective-permute-start(bf16[672,128]{1,0:T(8,128)(2,1)S(1)} %add_convert_fusion.1), channel_id=1, source_target_pairs={{8,0},{16,8},{24,16},{0,24},{9,1},{17,9},{25,17},{1,25},{10,2},{18... | collective-permute-start | bytes 516104 | tf_op jit(solution)/shard_map/ppermute | solution.py:224
  74.1 9.0 %copy-start.11 = (bf16[672,128]{1,0:T(8,128)(2,1)S(1)}, bf16[672,128]{1,0:T(8,128)(2,1)}, u32[]{:S(2)}) copy-start(bf16[672,128]{1,0:T(8,128)(2,1)} %copy-done.10) | copy-start | bytes 516100
  78.6 1.4 %collective-permute-start.16 = (bf16[672,128]{1,0:T(8,128)(2,1)S(1)}, bf16[672,128]{1,0:T(8,128)(2,1)S(1)}, u32[]{:S(2)}, u32[]{:S(2)}) collective-permute-start(bf16[672,128]{1,0:T(8,128)(2,1)S(1)} %get-tuple-element.52), channel_id=1, source_target_pairs={{1,0},{0,1},{3,2},{2,3},{5,4},{4,5},{7,6},{6,7},{9,8},{8,9},{11,10... | collective-permute-start | bytes 516104 | tf_op jit(solution)/shard_map/ppermute | solution.py:224
  80.0 7.0 %collective-permute-start.17 = (bf16[672,128]{1,0:T(8,128)(2,1)S(1)}, bf16[672,128]{1,0:T(8,128)(2,1)S(1)}, u32[]{:S(2)}, u32[]{:S(2)}) collective-permute-start(bf16[672,128]{1,0:T(8,128)(2,1)S(1)} %add_convert_fusion), channel_id=1, source_target_pairs={{8,0},{16,8},{24,16},{0,24},{9,1},{17,9},{25,17},{1,25},{10,2},{18... | collective-permute-start | bytes 516104 | tf_op jit(solution)/shard_map/ppermute | solution.py:224
  87.2 0.8 copy-start.9

commit v12 on v11

--- a/solution.py
+++ b/solution.py
@@ -289,9 +289,8 @@
     results, waiting, hops = [], [own], []
 
     def hop(blocks):
-        came = passed_along(jnp.concatenate(blocks, axis=1), "section", -1)
-        hops.append(came)
-        return [came[:, i * rows : (i + 1) * rows] for i in range(len(blocks))]
+        hops.append([passed_along(block, "section", -1) for block in blocks])
+        return list(hops[-1])
 
     by_first, by_second = own, own
     for step in range(1, shards):
@@ -299,8 +298,10 @@
         last = step == shards - 1 and shards % 2 == 0
         came_second = came_first if last else swapped(by_second, "seq", 1)
         if step > 1:
-            waiting = after(waiting, *sums, *(hops[-2:-1] if step > 2 else ()))
-        late = (came_first, came_second) if step > 1 and not (step > 2 and last) else ()
+            waiting = after(waiting, *sums, *(hops[-2] if step > 2 else ()))
+        late = (came_first, came_second) if step > 1 else ()
+        if step > 2 and last:
+            late = hops[-1]
         sums = halves_summed(waiting, late, light=step > 2 and last)
         results.append(hop(sums))
         by_first, by_second = came_second, came_first
@@ -310,7 +311,7 @@
             waiting = [came_first, came_second]
         else:
             waiting = [jnp.where(even == (place >= step), came_second, came_first)]
-    sums = halves_summed(waiting, (), hops[-2:])
+    sums = halves_summed(waiting, (), sum(hops[-2:], []))
     results.append(hop(sums))
     for step, blocks in enumerate(results):
         if len(blocks) > 1:

time: 88.6 us -> 86.8 us (0.980)
  waiting for transfers between devices: 28.7 us -> 27.2 us
    ppermute x9 -> x10, waiting for transfers between devices: 9.65 us -> 7.67 us  [passed_along(): lax.ppermute(block, axis, [((i - distance) % len(devices), i) for i in de...]
    ppermute x9 -> x10, starting transfers between devices: 9.61 us -> 9.64 us  [passed_along(): lax.ppermute(block, axis, [((i - distance) % len(devices), i) for i in de...]
  transfers between devices with their start and end apart: 18 -> 19, of which waited for: 8 -> 7; matrix products, arithmetic and copies ran while one was open for 6% -> 6% of each run, Pallas kernels for 12% -> 12%
where the time goes in v12:
time: 86.8 us; the launch traced here: 86.3 us
  starting transfers between devices  33.8 us (39%)
  waiting for transfers between devices  27.2 us (31%)
  Pallas kernels  12.6 us (15%)
  local copies, waits for them, and re-layouts  7.02 us (8%)
  other arithmetic  5.25 us (6%)
    ppermute x4, waiting for transfers between devices, moved(): lax.ppermute(block, axis, [(i, i + by) for i in range(size) if 0 <= i + b...  13.3 us
    ppermute x5, starting transfers between devices, swapped(): return lax.ppermute(block, axis, pairs)  12.2 us
    ppermute x4, starting transfers between devices, moved(): lax.ppermute(block, axis, [(i, i + by) for i in range(size) if 0 <= i + b...  12 us
    pallas_call x4, Pallas kernels, project(): pl.pallas_call(functools.partial(project_kernel, [len(block) for block in...  10.2 us
    ppermute x10, starting transfers between devices, passed_along(): lax.ppermute(block, axis, [((i - distance) % len(devices), i) for i in de...  9.64 us
    ppermute x10, waiting for transfers between devices, passed_along(): lax.ppermute(block, axis, [((i - distance) % len(devices), i) for i in de...  7.67 us
    ppermute x5, waiting for transfers between devices, swapped(): return lax.ppermute(block, axis, pairs)  6.22 us
    unnamed x24, local copies, waits for them, and re-layouts  5.45 us
  transfers between devices with their start and end apart: 19, of which 7 were waited for; matrix products, arithmetic and copies ran while one was open for 6% of the time, Pallas kernels for 12%

profile of v12, /device:TPU:0, one launch (start us, length us, event | category | flops | bytes accessed | tf_op | source)
XLA Modules:
  0.0 86.3 jit_solution(6429607303875294326)
XLA Ops:
  0.0 1.0 %pad_maximum_fusion.refs_2_ = bf16[128,1024]{1,0:T(8,128)(2,1)S(1)} fusion(bf16[128,512]{1,0:T(8,128)(2,1)} %bitcast.28, bf16[128,512]{1,0:T(8,128)(2,1)} %bitcast.29), kind=kLoop, calls=%fused_computation.6 | loop fusion | flops 524288 | bytes 524288 | tf_op jit(solution)/shard_map/concatenate | solution.py:248
  1.0 4.9 %collective-permute-start.1 = (bf16[128,1024]{1,0:T(8,128)(2,1)S(1)}, bf16[128,1024]{1,0:T(8,128)(2,1)S(1)}, u32[]{:S(2)}, u32[]{:S(2)}) collective-permute-start(bf16[128,1024]{1,0:T(8,128)(2,1)S(1)} %pad_maximum_fusion.refs_2_), channel_id=1, source_target_pairs={{0,2},{2,4},{4,6},{1,3},{3,5},{5,7},{8,10},{10,12},{12,14},{9,11},... | collective-permute-start | bytes 786440 | tf_op jit(solution)/shard_map/ppermute | solution.py:208
  6.0 4.5 %collective-permute-start = (bf16[48,1024]{1,0:T(8,128)(2,1)S(1)}, bf16[48,1024]{1,0:T(8,128)(2,1)S(1)}, u32[]{:S(2)}, u32[]{:S(2)}) collective-permute-start(bf16[48,1024]{1,0:T(8,128)(2,1)S(1)} %slice.4), channel_id=1, source_target_pairs={{0,4},{2,6},{1,5},{3,7},{8,12},{10,14},{9,13},{11,15},{16,20},{18,... | collective-permute-start | bytes 294920 | tf_op jit(solution)/shard_map/ppermute | solution.py:208
  10.5 0.8 pad_dynamic-slice_fusion
  11.2 0.7 fusion.5
  11.9 0.1 fusion.4.refs_3_
  12.0 0.0 copy-start.7
  12.0 0.9 %copy-done.7 = bf16[1,128,1024]{2,1,0:T(8,128)(2,1)S(1)} copy-done((bf16[1,128,1024]{2,1,0:T(8,128)(2,1)S(1)}, bf16[1,128,1024]{2,1,0:T(8,128)(2,1)}, u32[]{:S(2)}) %copy-start.7) | copy-done | bytes 262168
  13.0 0.9 %copy-done.8 = bf16[1,128,1024]{2,1,0:T(8,128)(2,1)S(1)} copy-done((bf16[1,128,1024]{2,1,0:T(8,128)(2,1)S(1)}, bf16[1,128,1024]{2,1,0:T(8,128)(2,1)}, u32[]{:S(2)}) %copy-start.8) | copy-done | bytes 262168
  13.9 0.1 shard_map.82
  14.0 0.0 collective-permute-done.refs_4_
  14.0 0.0 collective-permute-done.1.refs_5_
  14.0 0.0 copy-start
  14.0 2.2 %shard_map.83 = (bf16[128,1024]{1,0:T(8,128)(2,1)S(1)}, f32[128,1024]{1,0:T(8,128)S(1)}, bf16[48,1024]{1,0:T(8,128)(2,1)S(1)}, bf16[128,1024]{1,0:T(8,128)(2,1)S(1)}) custom-call(bf16[1024,128]{1,0:T(8,128)(2,1)S(1)} %get-tuple-element.32.refs_0_, bf16[1024,128]{1,0:T(8,128)(2,1)S(1)} %get-tuple-element.33.refs_1_, ...), custom_call_target="tpu_custom_call" | custom-call | flops 478150656 | bytes 1048576 | tf_op jit(solution)/shard_map/pallas_call | solution.py:100
  16.3 1.3 %collective-permute-start.2 = (bf16[128,1024]{1,0:T(8,128)(2,1)S(1)}, bf16[128,1024]{1,0:T(8,128)(2,1)S(1)}, u32[]{:S(2)}, u32[]{:S(2)}) collective-permute-start(bf16[128,1024]{1,0:T(8,128)(2,1)S(1)} %get-tuple-element.36), channel_id=1, source_target_pairs={{2,0},{4,2},{6,4},{3,1},{5,3},{7,5},{10,8},{12,10},{14,12},{11,9},... | collective-permute-start | bytes 786440 | tf_op jit(solution)/shard_map/ppermute | solution.py:208
  17.6 1.3 %collective-permute-start.3 = (bf16[48,1024]{1,0:T(8,128)(2,1)S(1)}, bf16[48,1024]{1,0:T(8,128)(2,1)S(1)}, u32[]{:S(2)}, u32[]{:S(2)}) collective-permute-start(bf16[48,1024]{1,0:T(8,128)(2,1)S(1)} %get-tuple-element.37), channel_id=1, source_target_pairs={{4,0},{6,2},{5,1},{7,3},{12,8},{14,10},{13,9},{15,11},{20,16},{22,... | collective-permute-start | bytes 294920 | tf_op jit(solution)/shard_map/ppermute | solution.py:208
  18.9 13.3 %collective-permute-done.3.refs_1_ = bf16[48,1024]{1,0:T(8,128)(2,1)S(1)} collective-permute-done((bf16[48,1024]{1,0:T(8,128)(2,1)S(1)}, bf16[48,1024]{1,0:T(8,128)(2,1)S(1)}, u32[]{:S(2)}, u32[]{:S(2)}) %collective-permute-start.3) | collective-permute-done | bytes 98336 | tf_op jit(solution)/shard_map/ppermute | solution.py:208
  32.2 0.0 collective-permute-done.2.refs_0_
  32.2 0.1 shard_map.84.refs_0_
  32.3 1.5 %collective-permute-start.7 = (bf16[128,2048]{1,0:T(8,128)(2,1)S(1)}, bf16[128,2048]{1,0:T(8,128)(2,1)}, u32[]{:S(2)}, u32[]{:S(2)}) collective-permute-start(bf16[128,2048]{1,0:T(8,128)(2,1)S(1)} %shard_map.84.refs_0_), channel_id=1, source_target_pairs={{2,4},{4,2},{3,5},{5,3},{10,12},{12,10},{11,13},{13,11},{18,20},{2... | collective-permute-start | bytes 1572872 | tf_op jit(solution)/shard_map/ppermute | solution.py:215
  33.8 0.6 collective-permute-start.6
  34.4 1.3 %copy-done.1 = bf16[1,1344,512]{2,1,0:T(8,128)(2,1)S(1)} copy-done((bf16[1,1344,512]{2,1,0:T(8,128)(2,1)S(1)}, bf16[1,1344,512]{2,1,0:T(8,128)(2,1)}, u32[]{:S(2)}) %copy-start.1) | copy-done | bytes 1376280
  35.8 1.3 %copy-done.4 = bf16[1,1344,512]{2,1,0:T(8,128)(2,1)S(1)} copy-done((bf16[1,1344,512]{2,1,0:T(8,128)(2,1)S(1)}, bf16[1,1344,512]{2,1,0:T(8,128)(2,1)}, u32[]{:S(2)}) %copy-start.4) | copy-done | bytes 1376280
  37.1 2.0 %shard_map.85 = (f32[672,128]{1,0:T(8,128)S(1)}, bf16[672,128]{1,0:T(8,128)(2,1)S(1)}) custom-call(s32[1]{0:T(128)} %bitcast.core_ref, bf16[128,2048]{1,0:T(8,128)(2,1)S(1)} %shard_map.84.refs_0_, bf16[1344,1024]{1,0:T(8,128)(2,1)S(1)} %bitcast.14, bf16[1344,512]{1,0:T(8,128)(2,1)S(1)} %bitcast.18, bf16[1344,512]{1,0:T(8,128)(2,1)S(1)} %bitcast.22), custom_call_target="tpu_custom_call" | custom-call | flops 704643072 | bytes 6537216 | tf_op jit(solution)/shard_map/pallas_call | solution.py:187
  39.1 0.1 collective-permute-start.4
  39.2 0.0 collective-permute-done.7.refs_1_
  39.2 5.7 %collective-permute-start.9 = (bf16[128,2048]{1,0:T(8,128)(2,1)}, bf16[128,2048]{1,0:T(8,128)(2,1)}, u32[]{:S(2)}, u32[]{:S(2)}) collective-permute-start(bf16[128,2048]{1,0:T(8,128)(2,1)} %collective-permute-done.7.refs_1_), channel_id=1, source_target_pairs={{0,2},{2,0},{4,6},{6,4},{1,3},{3,1},{5,7},{7,5},{8,10},{10,8},{12,... | collective-permute-start | bytes 1572872 | tf_op jit(solution)/shard_map/ppermute | solution.py:215
  45.0 1.2 %collective-permute-done.6.refs_0_ = bf16[128,2048]{1,0:T(8,128)(2,1)} collective-permute-done((bf16[128,2048]{1,0:T(8,128)(2,1)S(1)}, bf16[128,2048]{1,0:T(8,128)(2,1)}, u32[]{:S(2)}, u32[]{:S(2)}) %collective-permute-start.6) | collective-permute-done | bytes 524320 | tf_op jit(solution)/shard_map/ppermute | solution.py:215
  46.1 1.5 %collective-permute-start.10 = (bf16[128,2048]{1,0:T(8,128)(2,1)}, bf16[128,2048]{1,0:T(8,128)(2,1)}, u32[]{:S(2)}, u32[]{:S(2)}) collective-permute-start(bf16[128,2048]{1,0:T(8,128)(2,1)} %collective-permute-done.6.refs_0_), channel_id=1, source_target_pairs={{2,4},{4,2},{3,5},{5,3},{10,12},{12,10},{11,13},{13,11},{18,20},{2... | collective-permute-start | bytes 1572872 | tf_op jit(solution)/shard_map/ppermute | solution.py:215
  47.6 0.0 collective-permute-done.4
  47.6 0.7 add_convert_fusion.4
  48.3 4.1 %shard_map.86 = (f32[672,128]{1,0:T(8,128)S(1)}, f32[672,128]{1,0:T(8,128)S(1)}, bf16[672,128]{1,0:T(8,128)(2,1)}, bf16[672,128]{1,0:T(8,128)(2,1)}) custom-call(s32[1]{0:T(128)} %bitcast.core_ref, bf16[128,2048]{1,0:T(8,128)(2,1)} %collective-permute-done.6.refs_0_, bf16[128,2048]{1,0:T(8,128)(2,1)} %collective-permute-done.7.refs_1_, ...), custom_call_target="tpu_custom_call" | custom-call | flops 1409286144 | bytes 7569408 | tf_op jit(solution)/shard_map/pallas_call | solution.py:187
  52.4 0.0 collective-permute-start.12
  52.4 0.5 collective-permute-start.8
  53.0 2.5 %collective-permute-start.5 = (bf16[672,128]{1,0:T(8,128)(2,1)}, bf16[672,128]{1,0:T(8,128)(2,1)S(1)}, u32[]{:S(2)}, u32[]{:S(2)}) collective-permute-start(bf16[672,128]{1,0:T(8,128)(2,1)} %add_convert_fusion.4), channel_id=1, source_target_pairs={{8,0},{16,8},{24,16},{0,24},{9,1},{17,9},{25,17},{1,25},{10,2},{18... | collective-permute-start | bytes 516104 | tf_op jit(solution)/shard_map/ppermute | solution.py:224
  55.4 0.0 collective-permute-done.12
  55.4 0.2 collective-permute-done.9
  55.7 0.0 collective-permute-done.10
  55.7 0.0 copy-start.6
  55.7 1.1 %add_convert_fusion.3 = bf16[672,128]{1,0:T(8,128)(2,1)S(1)} fusion(f32[672,128]{1,0:T(8,128)S(1)} %get-tuple-element.42, bf16[672,128]{1,0:T(8,128)(2,1)} %collective-permute-done.8), kind=kLoop, calls=%fused_computation.4 | loop fusion | flops 258048 | bytes 688128 | tf_op jit(solution)/shard_map/convert_element_type | solution.py:285
  56.8 2.5 %collective-permute-start.11 = (bf16[672,128]{1,0:T(8,128)(2,1)S(1)}, bf16[672,128]{1,0:T(8,128)(2,1)S(1)}, u32[]{:S(2)}, u32[]{:S(2)}) collective-permute-start(bf16[672,128]{1,0:T(8,128)(2,1)S(1)} %add_convert_fusion.3), channel_id=1, source_target_pairs={{8,0},{16,8},{24,16},{0,24},{9,1},{17,9},{25,17},{1,25},{10,2},{18... | collective-permute-start | bytes 516104 | tf_op jit(solution)/shard_map/ppermute | solution.py:224
  59.3 1.0 %add_convert_fusion.2 = bf16[672,128]{1,0:T(8,128)(2,1)S(1)} fusion(f32[672,128]{1,0:T(8,128)S(1)} %get-tuple-element.45, bf16[672,128]{1,0:T(8,128)(2,1)} %collective-permute-done.12), kind=kLoop, calls=%fused_computation.3 | loop fusion | flops 258048 | bytes 688128 | tf_op jit(solution)/shard_map/convert_element_type | solution.py:285
  60.3 0.6 collective-permute-start.13
  60.8 2.9 %collective-permute-start.14 = (bf16[128,2048]{1,0:T(8,128)(2,1)}, bf16[128,2048]{1,0:T(8,128)(2,1)S(1)}, u32[]{:S(2)}, u32[]{:S(2)}) collective-permute-start(bf16[128,2048]{1,0:T(8,128)(2,1)} %collective-permute-done.10), channel_id=1, source_target_pairs={{0,2},{2,0},{4,6},{6,4},{1,3},{3,1},{5,7},{7,5},{8,10},{10,8},{12,... | collective-permute-start | bytes 1572872 | tf_op jit(solution)/shard_map/ppermute | solution.py:215
  63.7 1.1 %broadcast_select_fusion.refs_0_ = bf16[128,2048]{1,0:T(8,128)(2,1)S(1)} fusion(bf16[128,2048]{1,0:T(8,128)(2,1)} %collective-permute-done.10, bf16[128,2048]{1,0:T(8,128)(2,1)} %collective-permute-done.9, pred[]{:T(512)S(6)} %eq.32), kind=kLoop, calls=%fused_computation | loop fusion | flops 262144 | bytes 1572865 | tf_op jit(solution)/shard_map/jit(_where)/select_n | solution.py:313
  64.9 0.0 copy-start.10
  64.9 2.0 %shard_map.88 = (f32[672,128]{1,0:T(8,128)S(1)}, bf16[672,128]{1,0:T(8,128)(2,1)S(1)}) custom-call(s32[1]{0:T(128)} %bitcast.core_ref, bf16[128,2048]{1,0:T(8,128)(2,1)S(1)} %broadcast_select_fusion.refs_0_, bf16[1344,1024]{1,0:T(8,128)(2,1)S(1)} %bitcast.16, bf16[1344,512]{1,0:T(8,128)(2,1)S(1)} %bitcast.20, bf16[1344,512]{1,0:T(8,128)(2,1)S(1)} %bitcast.24), custom_call_target="tpu_custom_call" | custom-call | flops 1 | bytes 1 | tf_op jit(solution)/shard_map/pallas_call | solution.py:187
  66.9 0.1 collective-permute-start.15
  67.0 0.0 collective-permute-done.11
  67.0 1.4 %collective-permute-done.15 = bf16[672,128]{1,0:T(8,128)(2,1)S(1)} collective-permute-done((bf16[672,128]{1,0:T(8,128)(2,1)S(1)}, bf16[672,128]{1,0:T(8,128)(2,1)S(1)}, u32[]{:S(2)}, u32[]{:S(2)}) %collective-permute-start.15) | collective-permute-done | bytes 172064 | tf_op jit(solution)/shard_map/ppermute | solution.py:224
  68.4 1.9 %collective-permute-start.16 = (bf16[672,128]{1,0:T(8,128)(2,1)S(1)}, bf16[672,128]{1,0:T(8,128)(2,1)S(1)}, u32[]{:S(2)}, u32[]{:S(2)}) collective-permute-start(bf16[672,128]{1,0:T(8,128)(2,1)S(1)} %add_convert_fusion.1), channel_id=1, source_target_pairs={{8,0},{16,8},{24,16},{0,24},{9,1},{17,9},{25,17},{1,25},{10,2},{18... | collective-permute-start | bytes 516104 | tf_op jit(solution)/shard_map/ppermute | solution.py:224
  70.3 4.8 %collective-permute-done.14.refs_0_ = bf16[128,2048]{1,0:T(8,128)(2,1)S(1)} collective-permute-done((bf16[128,2048]{1,0:T(8,128)(2,1)}, bf16[128,2048]{1,0:T(8,128)(2,1)S(1)}, u32[]{:S(2)}, u32[]{:S(2)}) %collective-permute-start.14) | collective-permute-done | bytes 524320 | tf_op jit(solution)/shard_map/ppermute | solution.py:215
  75.1 2.0 %shard_map.87 = (f32[672,128]{1,0:T(8,128)S(1)}, bf16[672,128]{1,0:T(8,128)(2,1)S(1)}) custom-call(s32[1]{0:T(128)} %bitcast.core_ref, bf16[128,2048]{1,0:T(8,128)(2,1)S(1)} %collective-permute-done.14.refs_0_, bf16[1344,1024]{1,0:T(8,128)(2,1)S(1)} %bitcast.17, bf16[1344,512]{1,0:T(8,128)(2,1)S(1)} %bitcast.21, bf16[1344,512]{1,0:T(8,128)(2,1)S(1)} %bitcast.25), custom_call_target="tpu_custom_call" | custom-call | flops 704643072 | bytes 6537216 | tf_op jit(solution)/shard_map/pallas_call | solution.py:187
  77.1 0.0 copy-start.11
  77.1 0.0 collective-permute-done.16
  77.1 0.1 collective-permute-start.17
  77.2 1.4 %collective-permute-done.17 = bf16[672,128]{1,0:T(8,128)(2,1)S(1)} collective-permute-done((bf16[672,128]{1,0:T(8,128)(2,1)S(1)}, bf16[672,128]{1,0:T(8,128)(2,1)S(1)}, u32[]{:S(2)}, u32[]{:S(2)}) %collective-permute-start.17) | collective-permute-done | bytes 172064 | tf_op jit(solution)/shard_map/ppermute | solution.py:224
  78.6 0.1 add_convert_fusion
  78.7 1.5 %collective-permute-start.18 = (bf16[672,128]{1,0:T(8,128)(2,1)S(1)}, bf16[672,128]{1,0:T(8,128)(2,1)S(1)}, u32[]{:S(2)}, u32[]{:S(2)}) collective-permute-start(bf16[672,128]{1,0:T(8,128)(2,1)S(1)} %add_convert_fusion), channel_id=1, source_target_pairs={{8,0},{16,8},{24,16},{0,24},{9,1},{17,9},{25,17},{1,25},{10,2},{18... | collective-permute-start | bytes 516104 | tf_op jit(solution)/shard_map/ppermute | solution.py:224
  80.3 4.9 %collective-permute-done.18 = bf16[672,128]{1,0:T(8,128)(2,1)S(1)} collective-permute-done((bf16[672,128]{1,0:T(8,128)(2,1)S(1)}, bf16[672,128]{1,0:T(8,128)(2,1)S(1)}, u32[]{:S(2)}, u32[]{:S(2)}) %collective-permute-start.18) | collective-permute-done | bytes 172064 | tf_op jit(solution)/shard_map/ppermute | solution.py:224
  85.1 0.1 select_dynamic-update-slice_fusion.1
  85.3 0.1 select_dynamic-update-slice_fusion
  85.4 0.0 copy-start.9
  85.4 0.8 copy-done.9
  (22 shorter events, 0.2 us)
Async XLA Ops:
  1.0 13.0 %collective-permute-start.1 = (bf16[128,1024]{1,0:T(8,128)(2,1)S(1)}, bf16[128,1024]{1,0:T(8,128)(2,1)S(1)}, u32[]{:S(2)}, u32[]{:S(2)}) collective-permute-start(bf16[128,1024]{1,0:T(8,128)(2,1)S(1)} %pad_maximum_fusion.refs_2_), channel_id=1, source_target_pairs={{0,2},{2,4},{4,6},{1,3},{3,5},{5,7},{8,10},{10,12},{12,14},{9,11},... | collective-permute-start | bytes 786440 | tf_op jit(solution)/shard_map/ppermute | solution.py:208
  6.0 8.1 %collective-permute-start = (bf16[48,1024]{1,0:T(8,128)(2,1)S(1)}, bf16[48,1024]{1,0:T(8,128)(2,1)S(1)}, u32[]{:S(2)}, u32[]{:S(2)}) collective-permute-start(bf16[48,1024]{1,0:T(8,128)(2,1)S(1)} %slice.4), channel_id=1, source_target_pairs={{0,4},{2,6},{1,5},{3,7},{8,12},{10,14},{9,13},{11,15},{16,20},{18,... | collective-permute-start | bytes 294920 | tf_op jit(solution)/shard_map/ppermute | solution.py:208
  12.0 1.0 %copy-start.7 = (bf16[1,128,1024]{2,1,0:T(8,128)(2,1)S(1)}, bf16[1,128,1024]{2,1,0:T(8,128)(2,1)}, u32[]{:S(2)}) copy-start(bf16[1,128,1024]{2,1,0:T(8,128)(2,1)} %param.8) | copy-start | bytes 786436
  13.0 0.9 %copy-start.8 = (bf16[1,128,1024]{2,1,0:T(8,128)(2,1)S(1)}, bf16[1,128,1024]{2,1,0:T(8,128)(2,1)}, u32[]{:S(2)}) copy-start(bf16[1,128,1024]{2,1,0:T(8,128)(2,1)} %param.11) | copy-start | bytes 786436
  14.0 20.4 %copy-start = (bf16[1,1344,1024]{2,1,0:T(8,128)(2,1)S(1)}, bf16[1,1344,1024]{2,1,0:T(8,128)(2,1)}, u32[]{:S(2)}) copy-start(bf16[1,1344,1024]{2,1,0:T(8,128)(2,1)} %param.12) | copy-start | bytes 8257540
  16.3 15.9 %collective-permute-start.2 = (bf16[128,1024]{1,0:T(8,128)(2,1)S(1)}, bf16[128,1024]{1,0:T(8,128)(2,1)S(1)}, u32[]{:S(2)}, u32[]{:S(2)}) collective-permute-start(bf16[128,1024]{1,0:T(8,128)(2,1)S(1)} %get-tuple-element.36), channel_id=1, source_target_pairs={{2,0},{4,2},{6,4},{3,1},{5,3},{7,5},{10,8},{12,10},{14,12},{11,9},... | collective-permute-start | bytes 786440 | tf_op jit(solution)/shard_map/ppermute | solution.py:208
  17.6 14.6 %collective-permute-start.3 = (bf16[48,1024]{1,0:T(8,128)(2,1)S(1)}, bf16[48,1024]{1,0:T(8,128)(2,1)S(1)}, u32[]{:S(2)}, u32[]{:S(2)}) collective-permute-start(bf16[48,1024]{1,0:T(8,128)(2,1)S(1)} %get-tuple-element.37), channel_id=1, source_target_pairs={{4,0},{6,2},{5,1},{7,3},{12,8},{14,10},{13,9},{15,11},{20,16},{22,... | collective-permute-start | bytes 294920 | tf_op jit(solution)/shard_map/ppermute | solution.py:208
  32.3 6.9 %collective-permute-start.7 = (bf16[128,2048]{1,0:T(8,128)(2,1)S(1)}, bf16[128,2048]{1,0:T(8,128)(2,1)}, u32[]{:S(2)}, u32[]{:S(2)}) collective-permute-start(bf16[128,2048]{1,0:T(8,128)(2,1)S(1)} %shard_map.84.refs_0_), channel_id=1, source_target_pairs={{2,4},{4,2},{3,5},{5,3},{10,12},{12,10},{11,13},{13,11},{18,20},{2... | collective-permute-start | bytes 1572872 | tf_op jit(solution)/shard_map/ppermute | solution.py:215
  33.8 12.3 %collective-permute-start.6 = (bf16[128,2048]{1,0:T(8,128)(2,1)S(1)}, bf16[128,2048]{1,0:T(8,128)(2,1)}, u32[]{:S(2)}, u32[]{:S(2)}) collective-permute-start(bf16[128,2048]{1,0:T(8,128)(2,1)S(1)} %shard_map.84.refs_0_), channel_id=1, source_target_pairs={{0,2},{2,0},{4,6},{6,4},{1,3},{3,1},{5,7},{7,5},{8,10},{10,8},{12,... | collective-permute-start | bytes 1572872 | tf_op jit(solution)/shard_map/ppermute | solution.py:215
  34.4 1.3 %copy-start.1 = (bf16[1,1344,512]{2,1,0:T(8,128)(2,1)S(1)}, bf16[1,1344,512]{2,1,0:T(8,128)(2,1)}, u32[]{:S(2)}) copy-start(bf16[1,1344,512]{2,1,0:T(8,128)(2,1)} %param.13) | copy-start | bytes 4128772
  35.8 1.3 %copy-start.4 = (bf16[1,1344,512]{2,1,0:T(8,128)(2,1)S(1)}, bf16[1,1344,512]{2,1,0:T(8,128)(2,1)}, u32[]{:S(2)}) copy-start(bf16[1,1344,512]{2,1,0:T(8,128)(2,1)} %param.14) | copy-start | bytes 4128772
  37.1 11.2 %copy-start.2 = (bf16[1,1344,512]{2,1,0:T(8,128)(2,1)S(1)}, bf16[1,1344,512]{2,1,0:T(8,128)(2,1)}, u32[]{:S(2)}) copy-start(bf16[1,1344,512]{2,1,0:T(8,128)(2,1)} %param.13) | copy-start | bytes 4128772
  37.1 11.2 %copy-start.5 = (bf16[1,1344,512]{2,1,0:T(8,128)(2,1)S(1)}, bf16[1,1344,512]{2,1,0:T(8,128)(2,1)}, u32[]{:S(2)}) copy-start(bf16[1,1344,512]{2,1,0:T(8,128)(2,1)} %param.14) | copy-start | bytes 4128772
  39.1 8.5 %collective-permute-start.4 = (bf16[672,128]{1,0:T(8,128)(2,1)S(1)}, bf16[672,128]{1,0:T(8,128)(2,1)S(1)}, u32[]{:S(2)}, u32[]{:S(2)}) collective-permute-start(bf16[672,128]{1,0:T(8,128)(2,1)S(1)} %get-tuple-element.39), channel_id=1, source_target_pairs={{1,0},{0,1},{3,2},{2,3},{5,4},{4,5},{7,6},{6,7},{9,8},{8,9},{11,10... | collective-permute-start | bytes 516104 | tf_op jit(solution)/shard_map/ppermute | solution.py:224
  39.2 16.4 %collective-permute-start.9 = (bf16[128,2048]{1,0:T(8,128)(2,1)}, bf16[128,2048]{1,0:T(8,128)(2,1)}, u32[]{:S(2)}, u32[]{:S(2)}) collective-permute-start(bf16[128,2048]{1,0:T(8,128)(2,1)} %collective-permute-done.7.refs_1_), channel_id=1, source_target_pairs={{0,2},{2,0},{4,6},{6,4},{1,3},{3,1},{5,7},{7,5},{8,10},{10,8},{12,... | collective-permute-start | bytes 1572872 | tf_op jit(solution)/shard_map/ppermute | solution.py:215
  46.1 9.5 %collective-permute-start.10 = (bf16[128,2048]{1,0:T(8,128)(2,1)}, bf16[128,2048]{1,0:T(8,128)(2,1)}, u32[]{:S(2)}, u32[]{:S(2)}) collective-permute-start(bf16[128,2048]{1,0:T(8,128)(2,1)} %collective-permute-done.6.refs_0_), channel_id=1, source_target_pairs={{2,4},{4,2},{3,5},{5,3},{10,12},{12,10},{11,13},{13,11},{18,20},{2... | collective-permute-start | bytes 1572872 | tf_op jit(solution)/shard_map/ppermute | solution.py:215
  52.4 3.0 %collective-permute-start.12 = (bf16[672,128]{1,0:T(8,128)(2,1)}, bf16[672,128]{1,0:T(8,128)(2,1)}, u32[]{:S(2)}, u32[]{:S(2)}) collective-permute-start(bf16[672,128]{1,0:T(8,128)(2,1)} %get-tuple-element.46), channel_id=1, source_target_pairs={{1,0},{0,1},{3,2},{2,3},{5,4},{4,5},{7,6},{6,7},{9,8},{8,9},{11,10... | collective-permute-start | bytes 516104 | tf_op jit(solution)/shard_map/ppermute | solution.py:224
  52.4 3.2 %collective-permute-start.8 = (bf16[672,128]{1,0:T(8,128)(2,1)}, bf16[672,128]{1,0:T(8,128)(2,1)}, u32[]{:S(2)}, u32[]{:S(2)}) collective-permute-start(bf16[672,128]{1,0:T(8,128)(2,1)} %get-tuple-element.43), channel_id=1, source_target_pairs={{1,0},{0,1},{3,2},{2,3},{5,4},{4,5},{7,6},{6,7},{9,8},{8,9},{11,10... | collective-permute-start | bytes 516104 | tf_op jit(solution)/shard_map/ppermute | solution.py:224
  53.0 11.9 %collective-permute-start.5 = (bf16[672,128]{1,0:T(8,128)(2,1)}, bf16[672,128]{1,0:T(8,128)(2,1)S(1)}, u32[]{:S(2)}, u32[]{:S(2)}) collective-permute-start(bf16[672,128]{1,0:T(8,128)(2,1)} %add_convert_fusion.4), channel_id=1, source_target_pairs={{8,0},{16,8},{24,16},{0,24},{9,1},{17,9},{25,17},{1,25},{10,2},{18... | collective-permute-start | bytes 516104 | tf_op jit(solution)/shard_map/ppermute | solution.py:224
  55.7 9.2 %copy-start.3 = (bf16[1,1344,512]{2,1,0:T(8,128)(2,1)S(1)}, bf16[1,1344,512]{2,1,0:T(8,128)(2,1)}, u32[]{:S(2)}) copy-start(bf16[1,1344,512]{2,1,0:T(8,128)(2,1)} %param.13) | copy-start | bytes 4128772
  55.7 9.2 %copy-start.6 = (bf16[1,1344,512]{2,1,0:T(8,128)(2,1)S(1)}, bf16[1,1344,512]{2,1,0:T(8,128)(2,1)}, u32[]{:S(2)}) copy-start(bf16[1,1344,512]{2,1,0:T(8,128)(2,1)} %param.14) | copy-start | bytes 4128772
  56.8 10.2 %collective-permute-start.11 = (bf16[672,128]{1,0:T(8,128)(2,1)S(1)}, bf16[672,128]{1,0:T(8,128)(2,1)S(1)}, u32[]{:S(2)}, u32[]{:S(2)}) collective-permute-start(bf16[672,128]{1,0:T(8,128)(2,1)S(1)} %add_convert_fusion.3), channel_id=1, source_target_pairs={{8,0},{16,8},{24,16},{0,24},{9,1},{17,9},{25,17},{1,25},{10,2},{18... | collective-permute-start | bytes 516104 | tf_op jit(solution)/shard_map/ppermute | solution.py:224
  60.3 6.7 %collective-permute-start.13 = (bf16[672,128]{1,0:T(8,128)(2,1)S(1)}, bf16[672,128]{1,0:T(8,128)(2,1)S(1)}, u32[]{:S(2)}, u32[]{:S(2)}) collective-permute-start(bf16[672,128]{1,0:T(8,128)(2,1)S(1)} %add_convert_fusion.2), channel_id=1, source_target_pairs={{8,0},{16,8},{24,16},{0,24},{9,1},{17,9},{25,17},{1,25},{10,2},{18... | collective-permute-start | bytes 516104 | tf_op jit(solution)/shard_map/ppermute | solution.py:224
  60.8 14.3 %collective-permute-start.14 = (bf16[128,2048]{1,0:T(8,128)(2,1)}, bf16[128,2048]{1,0:T(8,128)(2,1)S(1)}, u32[]{:S(2)}, u32[]{:S(2)}) collective-permute-start(bf16[128,2048]{1,0:T(8,128)(2,1)} %collective-permute-done.10), channel_id=1, source_target_pairs={{0,2},{2,0},{4,6},{6,4},{1,3},{3,1},{5,7},{7,5},{8,10},{10,8},{12,... | collective-permute-start | bytes 1572872 | tf_op jit(solution)/shard_map/ppermute | solution.py:215
  64.9 2.0 %copy-start.10 = (bf16[672,128]{1,0:T(8,128)(2,1)}, bf16[672,128]{1,0:T(8,128)(2,1)S(1)}, u32[]{:S(2)}) copy-start(bf16[672,128]{1,0:T(8,128)(2,1)S(1)} %collective-permute-done.5) | copy-start | bytes 516100
  66.9 1.5 %collective-permute-start.15 = (bf16[672,128]{1,0:T(8,128)(2,1)S(1)}, bf16[672,128]{1,0:T(8,128)(2,1)S(1)}, u32[]{:S(2)}, u32[]{:S(2)}) collective-permute-start(bf16[672,128]{1,0:T(8,128)(2,1)S(1)} %get-tuple-element.52), channel_id=1, source_target_pairs={{1,0},{0,1},{3,2},{2,3},{5,4},{4,5},{7,6},{6,7},{9,8},{8,9},{11,10... | collective-permute-start | bytes 516104 | tf_op jit(solution)/shard_map/ppermute | solution.py:224
  68.4 8.7 %collective-permute-start.16 = (bf16[672,128]{1,0:T(8,128)(2,1)S(1)}, bf16[672,128]{1,0:T(8,128)(2,1)S(1)}, u32[]{:S(2)}, u32[]{:S(2)}) collective-permute-start(bf16[672,128]{1,0:T(8,128)(2,1)S(1)} %add_convert_fusion.1), channel_id=1, source_target_pairs={{8,0},{16,8},{24,16},{0,24},{9,1},{17,9},{25,17},{1,25},{10,2},{18... | collective-permute-start | bytes 516104 | tf_op jit(solution)/shard_map/ppermute | solution.py:224
  77.1 3.1 %copy-start.11 = (bf16[672,128]{1,0:T(8,128)(2,1)S(1)}, bf16[672,128]{1,0:T(8,128)(2,1)}, u32[]{:S(2)}) copy-start(bf16[672,128]{1,0:T(8,128)(2,1)} %copy-done.10) | copy-start | bytes 516100
  77.1 1.5 %collective-permute-start.17 = (bf16[672,128]{1,0:T(8,128)(2,1)S(1)}, bf16[672,128]{1,0:T(8,128)(2,1)S(1)}, u32[]{:S(2)}, u32[]{:S(2)}) collective-permute-start(bf16[672,128]{1,0:T(8,128)(2,1)S(1)} %get-tuple-element.54), channel_id=1, source_target_pairs={{1,0},{0,1},{3,2},{2,3},{5,4},{4,5},{7,6},{6,7},{9,8},{8,9},{11,10... | collective-permute-start | bytes 516104 | tf_op jit(solution)/shard_map/ppermute | solution.py:224
  78.7 6.5 %collective-permute-start.18 = (bf16[672,128]{1,0:T(8,128)(2,1)S(1)}, bf16[672,128]{1,0:T(8,128)(2,1)S(1)}, u32[]{:S(2)}, u32[]{:S(2)}) collective-permute-start(bf16[672,128]{1,0:T(8,128)(2,1)S(1)} %add_convert_fusion), channel_id=1, source_target_pairs={{8,0},{16,8},{24,16},{0,24},{9,1},{17,9},{25,17},{1,25},{10,2},{18... | collective-permute-start | bytes 516104 | tf_op jit(solution)/shard_map/ppermute | solution.py:224
  85.4 0.8 copy-start.9

commit v13 on v12

--- a/solution.py
+++ b/solution.py
@@ -172,7 +172,7 @@
     other = pl.ds(pl.multiple_of((1 - core_ref[0]) * half, 8), half)
     for i, (keep_ref, give_ref) in enumerate(zip(keep_refs, give_refs)):
         cols = slice(i * rows, (i + 1) * rows)
-        keep_ref[...] = full_ref[own, cols]
+        keep_ref[...] = full_ref[own, cols].astype(jnp.bfloat16)
         give_ref[...] = full_ref[other, cols].astype(jnp.bfloat16)
 
 
@@ -186,8 +186,7 @@
     whole = pl.BlockSpec(memory_space=pltpu.VMEM)
     return pl.pallas_call(
         functools.partial(project_kernel, [len(block) for block in blocks], tile),
-        out_shape=[jax.ShapeDtypeStruct(half, jnp.float32)] * len(blocks)
-        + [jax.ShapeDtypeStruct(half, jnp.bfloat16)] * len(blocks),
+        out_shape=[jax.ShapeDtypeStruct(half, jnp.bfloat16)] * (2 * len(blocks)),
         in_specs=[pl.BlockSpec(memory_space=pltpu.SMEM)] + [whole] * (len(flat) + 3),
         out_specs=[whole] * (2 * len(blocks)),
         scratch_shapes=[
@@ -282,7 +281,7 @@
             got = passed_along(give, "mp", 1)
             if late:
                 (got,) = after((got,), *late)
-            sums.append((keep + got.astype(jnp.float32)).astype(jnp.bfloat16))
+            sums.append((keep.astype(jnp.float32) + got.astype(jnp.float32)).astype(jnp.bfloat16))
         return sums
 
     even = place % 2 == 0

time: 86.8 us -> 86.3 us (level)
  waiting for transfers between devices: 27.2 us -> 25.8 us
  local copies, waits for them, and re-layouts: 7.02 us -> 8.35 us
    unnamed x24, local copies, waits for them, and re-layouts: 5.45 us -> 6.77 us
    ppermute x5, waiting for transfers between devices: 6.22 us -> 5.09 us  [swapped(): return lax.ppermute(block, axis, pairs)]
  transfers between devices with their start and end apart: 19 -> 19, of which waited for: 7 -> 7; matrix products, arithmetic and copies ran while one was open for 6% -> 6% of each run, Pallas kernels for 12% -> 11%
where the time goes in v13:
time: 86.3 us; the launch traced here: 85.8 us
  starting transfers between devices  34.3 us (40%)
  waiting for transfers between devices  25.8 us (30%)
  Pallas kernels  11.8 us (14%)
  local copies, waits for them, and re-layouts  8.35 us (10%)
  other arithmetic  5.14 us (6%)
    ppermute x4, waiting for transfers between devices, moved(): lax.ppermute(block, axis, [(i, i + by) for i in range(size) if 0 <= i + b...  13.3 us
    ppermute x5, starting transfers between devices, swapped(): return lax.ppermute(block, axis, pairs)  12.2 us
    ppermute x4, starting transfers between devices, moved(): lax.ppermute(block, axis, [(i, i + by) for i in range(size) if 0 <= i + b...  12 us
    ppermute x10, starting transfers between devices, passed_along(): lax.ppermute(block, axis, [((i - distance) % len(devices), i) for i in de...  10.1 us
    pallas_call x4, Pallas kernels, project(): pl.pallas_call(functools.partial(project_kernel, [len(block) for block in...  9.39 us
    ppermute x10, waiting for transfers between devices, passed_along(): lax.ppermute(block, axis, [((i - distance) % len(devices), i) for i in de...  7.4 us
    unnamed x24, local copies, waits for them, and re-layouts  6.77 us
    ppermute x5, waiting for transfers between devices, swapped(): return lax.ppermute(block, axis, pairs)  5.09 us
  transfers between devices with their start and end apart: 19, of which 7 were waited for; matrix products, arithmetic and copies ran while one was open for 6% of the time, Pallas kernels for 11%

profile of v13, /device:TPU:0, one launch (start us, length us, event | category | flops | bytes accessed | tf_op | source)
XLA Modules:
  0.0 85.8 jit_solution(9001951676695199391)
XLA Ops:
  0.0 1.0 %pad_maximum_fusion.refs_2_ = bf16[128,1024]{1,0:T(8,128)(2,1)S(1)} fusion(bf16[128,512]{1,0:T(8,128)(2,1)} %bitcast.28, bf16[128,512]{1,0:T(8,128)(2,1)} %bitcast.29), kind=kLoop, calls=%fused_computation.6 | loop fusion | flops 524288 | bytes 524288 | tf_op jit(solution)/shard_map/concatenate | solution.py:247
  1.0 4.9 %collective-permute-start.1 = (bf16[128,1024]{1,0:T(8,128)(2,1)S(1)}, bf16[128,1024]{1,0:T(8,128)(2,1)S(1)}, u32[]{:S(2)}, u32[]{:S(2)}) collective-permute-start(bf16[128,1024]{1,0:T(8,128)(2,1)S(1)} %pad_maximum_fusion.refs_2_), channel_id=1, source_target_pairs={{0,2},{2,4},{4,6},{1,3},{3,5},{5,7},{8,10},{10,12},{12,14},{9,11},... | collective-permute-start | bytes 786440 | tf_op jit(solution)/shard_map/ppermute | solution.py:207
  6.0 4.5 %collective-permute-start = (bf16[48,1024]{1,0:T(8,128)(2,1)S(1)}, bf16[48,1024]{1,0:T(8,128)(2,1)S(1)}, u32[]{:S(2)}, u32[]{:S(2)}) collective-permute-start(bf16[48,1024]{1,0:T(8,128)(2,1)S(1)} %slice.4), channel_id=1, source_target_pairs={{0,4},{2,6},{1,5},{3,7},{8,12},{10,14},{9,13},{11,15},{16,20},{18,... | collective-permute-start | bytes 294920 | tf_op jit(solution)/shard_map/ppermute | solution.py:207
  10.5 0.8 pad_dynamic-slice_fusion
  11.2 0.7 fusion.5
  11.9 0.1 fusion.4.refs_3_
  12.0 0.0 copy-start.7
  12.0 0.9 %copy-done.7 = bf16[1,128,1024]{2,1,0:T(8,128)(2,1)S(1)} copy-done((bf16[1,128,1024]{2,1,0:T(8,128)(2,1)S(1)}, bf16[1,128,1024]{2,1,0:T(8,128)(2,1)}, u32[]{:S(2)}) %copy-start.7) | copy-done | bytes 262168
  13.0 0.9 %copy-done.8 = bf16[1,128,1024]{2,1,0:T(8,128)(2,1)S(1)} copy-done((bf16[1,128,1024]{2,1,0:T(8,128)(2,1)S(1)}, bf16[1,128,1024]{2,1,0:T(8,128)(2,1)}, u32[]{:S(2)}) %copy-start.8) | copy-done | bytes 262168
  13.9 0.1 shard_map.82
  14.0 0.0 collective-permute-done.refs_4_
  14.0 0.0 collective-permute-done.1.refs_5_
  14.0 0.0 copy-start
  14.0 2.2 %shard_map.83 = (bf16[128,1024]{1,0:T(8,128)(2,1)S(1)}, f32[128,1024]{1,0:T(8,128)S(1)}, bf16[48,1024]{1,0:T(8,128)(2,1)S(1)}, bf16[128,1024]{1,0:T(8,128)(2,1)S(1)}) custom-call(bf16[1024,128]{1,0:T(8,128)(2,1)S(1)} %get-tuple-element.32.refs_0_, bf16[1024,128]{1,0:T(8,128)(2,1)S(1)} %get-tuple-element.33.refs_1_, ...), custom_call_target="tpu_custom_call" | custom-call | flops 478150656 | bytes 1048576 | tf_op jit(solution)/shard_map/pallas_call | solution.py:100
  16.3 1.3 %collective-permute-start.2 = (bf16[128,1024]{1,0:T(8,128)(2,1)S(1)}, bf16[128,1024]{1,0:T(8,128)(2,1)S(1)}, u32[]{:S(2)}, u32[]{:S(2)}) collective-permute-start(bf16[128,1024]{1,0:T(8,128)(2,1)S(1)} %get-tuple-element.36), channel_id=1, source_target_pairs={{2,0},{4,2},{6,4},{3,1},{5,3},{7,5},{10,8},{12,10},{14,12},{11,9},... | collective-permute-start | bytes 786440 | tf_op jit(solution)/shard_map/ppermute | solution.py:207
  17.6 1.3 %collective-permute-start.3 = (bf16[48,1024]{1,0:T(8,128)(2,1)S(1)}, bf16[48,1024]{1,0:T(8,128)(2,1)S(1)}, u32[]{:S(2)}, u32[]{:S(2)}) collective-permute-start(bf16[48,1024]{1,0:T(8,128)(2,1)S(1)} %get-tuple-element.37), channel_id=1, source_target_pairs={{4,0},{6,2},{5,1},{7,3},{12,8},{14,10},{13,9},{15,11},{20,16},{22,... | collective-permute-start | bytes 294920 | tf_op jit(solution)/shard_map/ppermute | solution.py:207
  18.9 13.3 %collective-permute-done.3.refs_1_ = bf16[48,1024]{1,0:T(8,128)(2,1)S(1)} collective-permute-done((bf16[48,1024]{1,0:T(8,128)(2,1)S(1)}, bf16[48,1024]{1,0:T(8,128)(2,1)S(1)}, u32[]{:S(2)}, u32[]{:S(2)}) %collective-permute-start.3) | collective-permute-done | bytes 98336 | tf_op jit(solution)/shard_map/ppermute | solution.py:207
  32.2 0.0 collective-permute-done.2.refs_0_
  32.2 0.1 shard_map.84.refs_0_
  32.3 1.5 %collective-permute-start.7 = (bf16[128,2048]{1,0:T(8,128)(2,1)S(1)}, bf16[128,2048]{1,0:T(8,128)(2,1)}, u32[]{:S(2)}, u32[]{:S(2)}) collective-permute-start(bf16[128,2048]{1,0:T(8,128)(2,1)S(1)} %shard_map.84.refs_0_), channel_id=1, source_target_pairs={{2,4},{4,2},{3,5},{5,3},{10,12},{12,10},{11,13},{13,11},{18,20},{2... | collective-permute-start | bytes 1572872 | tf_op jit(solution)/shard_map/ppermute | solution.py:214
  33.8 0.6 collective-permute-start.6
  34.4 1.3 %copy-done.1 = bf16[1,1344,512]{2,1,0:T(8,128)(2,1)S(1)} copy-done((bf16[1,1344,512]{2,1,0:T(8,128)(2,1)S(1)}, bf16[1,1344,512]{2,1,0:T(8,128)(2,1)}, u32[]{:S(2)}) %copy-start.1) | copy-done | bytes 1376280
  35.8 1.3 %copy-done.4 = bf16[1,1344,512]{2,1,0:T(8,128)(2,1)S(1)} copy-done((bf16[1,1344,512]{2,1,0:T(8,128)(2,1)S(1)}, bf16[1,1344,512]{2,1,0:T(8,128)(2,1)}, u32[]{:S(2)}) %copy-start.4) | copy-done | bytes 1376280
  37.1 2.0 %shard_map.85 = (bf16[672,128]{1,0:T(8,128)(2,1)S(1)}, bf16[672,128]{1,0:T(8,128)(2,1)S(1)}) custom-call(s32[1]{0:T(128)} %bitcast.core_ref, bf16[128,2048]{1,0:T(8,128)(2,1)S(1)} %shard_map.84.refs_0_, bf16[1344,1024]{1,0:T(8,128)(2,1)S(1)} %bitcast.14, bf16[1344,512]{1,0:T(8,128)(2,1)S(1)} %bitcast.18, bf16[1344,512]{1,0:T(8,128)(2,1)S(1)} %bitcast.22), custom_call_target="tpu_custom_call" | custom-call | flops 704643072 | bytes 6537216 | tf_op jit(solution)/shard_map/pallas_call | solution.py:187
  39.1 0.1 collective-permute-start.4
  39.2 0.0 collective-permute-done.7.refs_1_
  39.2 5.8 %collective-permute-start.9 = (bf16[128,2048]{1,0:T(8,128)(2,1)}, bf16[128,2048]{1,0:T(8,128)(2,1)}, u32[]{:S(2)}, u32[]{:S(2)}) collective-permute-start(bf16[128,2048]{1,0:T(8,128)(2,1)} %collective-permute-done.7.refs_1_), channel_id=1, source_target_pairs={{0,2},{2,0},{4,6},{6,4},{1,3},{3,1},{5,7},{7,5},{8,10},{10,8},{12,... | collective-permute-start | bytes 1572872 | tf_op jit(solution)/shard_map/ppermute | solution.py:214
  45.0 1.2 %collective-permute-done.6.refs_0_ = bf16[128,2048]{1,0:T(8,128)(2,1)} collective-permute-done((bf16[128,2048]{1,0:T(8,128)(2,1)S(1)}, bf16[128,2048]{1,0:T(8,128)(2,1)}, u32[]{:S(2)}, u32[]{:S(2)}) %collective-permute-start.6) | collective-permute-done | bytes 524320 | tf_op jit(solution)/shard_map/ppermute | solution.py:214
  46.1 1.5 %collective-permute-start.10 = (bf16[128,2048]{1,0:T(8,128)(2,1)}, bf16[128,2048]{1,0:T(8,128)(2,1)}, u32[]{:S(2)}, u32[]{:S(2)}) collective-permute-start(bf16[128,2048]{1,0:T(8,128)(2,1)} %collective-permute-done.6.refs_0_), channel_id=1, source_target_pairs={{2,4},{4,2},{3,5},{5,3},{10,12},{12,10},{11,13},{13,11},{18,20},{2... | collective-permute-start | bytes 1572872 | tf_op jit(solution)/shard_map/ppermute | solution.py:214
  47.6 0.0 collective-permute-done.4
  47.6 0.7 add_convert_fusion.4
  48.3 3.4 %shard_map.86 = (bf16[672,128]{1,0:T(8,128)(2,1)S(1)}, bf16[672,128]{1,0:T(8,128)(2,1)S(1)}, bf16[672,128]{1,0:T(8,128)(2,1)S(1)}, bf16[672,128]{1,0:T(8,128)(2,1)S(1)}) custom-call(s32[1]{0:T(128)} %bitcast.core_ref, bf16[128,2048]{1,0:T(8,128)(2,1)} %collective-permute-done.6.refs_0_, bf16[128,2048]{1,0:T(8,128)(2,1)} %collective-permute-done.7.refs_1_, ...), custom_call_target="tpu_custom_call" | custom-call | flops 1409286144 | bytes 7569408 | tf_op jit(solution)/shard_map/pallas_call | solution.py:187
  51.7 0.1 collective-permute-start.12
  51.8 0.5 collective-permute-start.8
  52.3 2.5 %collective-permute-start.5 = (bf16[672,128]{1,0:T(8,128)(2,1)}, bf16[672,128]{1,0:T(8,128)(2,1)S(1)}, u32[]{:S(2)}, u32[]{:S(2)}) collective-permute-start(bf16[672,128]{1,0:T(8,128)(2,1)} %add_convert_fusion.4), channel_id=1, source_target_pairs={{8,0},{16,8},{24,16},{0,24},{9,1},{17,9},{25,17},{1,25},{10,2},{18... | collective-permute-start | bytes 516104 | tf_op jit(solution)/shard_map/ppermute | solution.py:223
  54.8 0.0 collective-permute-done.12
  54.8 0.9 %collective-permute-done.9 = bf16[128,2048]{1,0:T(8,128)(2,1)} collective-permute-done((bf16[128,2048]{1,0:T(8,128)(2,1)}, bf16[128,2048]{1,0:T(8,128)(2,1)}, u32[]{:S(2)}, u32[]{:S(2)}) %collective-permute-start.9) | collective-permute-done | bytes 524320 | tf_op jit(solution)/shard_map/ppermute | solution.py:214
  55.7 0.0 collective-permute-done.10
  55.7 0.0 collective-permute-done.8
  55.7 1.0 %add_convert_fusion.3 = bf16[672,128]{1,0:T(8,128)(2,1)S(1)} fusion(bf16[672,128]{1,0:T(8,128)(2,1)} %collective-permute-done.8, bf16[672,128]{1,0:T(8,128)(2,1)S(1)} %get-tuple-element.42), kind=kLoop, calls=%fused_computation.4 | loop fusion | flops 344064 | bytes 516096 | tf_op jit(solution)/shard_map/convert_element_type | solution.py:284
  56.6 2.5 %collective-permute-start.11 = (bf16[672,128]{1,0:T(8,128)(2,1)S(1)}, bf16[672,128]{1,0:T(8,128)(2,1)S(1)}, u32[]{:S(2)}, u32[]{:S(2)}) collective-permute-start(bf16[672,128]{1,0:T(8,128)(2,1)S(1)} %add_convert_fusion.3), channel_id=1, source_target_pairs={{8,0},{16,8},{24,16},{0,24},{9,1},{17,9},{25,17},{1,25},{10,2},{18... | collective-permute-start | bytes 516104 | tf_op jit(solution)/shard_map/ppermute | solution.py:223
  59.1 1.0 %add_convert_fusion.2 = bf16[672,128]{1,0:T(8,128)(2,1)S(1)} fusion(bf16[672,128]{1,0:T(8,128)(2,1)} %collective-permute-done.12, bf16[672,128]{1,0:T(8,128)(2,1)S(1)} %get-tuple-element.45), kind=kLoop, calls=%fused_computation.3 | loop fusion | flops 344064 | bytes 516096 | tf_op jit(solution)/shard_map/convert_element_type | solution.py:284
  60.1 0.6 collective-permute-start.13
  60.7 2.9 %collective-permute-start.14 = (bf16[128,2048]{1,0:T(8,128)(2,1)}, bf16[128,2048]{1,0:T(8,128)(2,1)S(1)}, u32[]{:S(2)}, u32[]{:S(2)}) collective-permute-start(bf16[128,2048]{1,0:T(8,128)(2,1)} %collective-permute-done.10), channel_id=1, source_target_pairs={{0,2},{2,0},{4,6},{6,4},{1,3},{3,1},{5,7},{7,5},{8,10},{10,8},{12,... | collective-permute-start | bytes 1572872 | tf_op jit(solution)/shard_map/ppermute | solution.py:214
  63.6 1.1 %broadcast_select_fusion.refs_0_ = bf16[128,2048]{1,0:T(8,128)(2,1)S(1)} fusion(bf16[128,2048]{1,0:T(8,128)(2,1)} %collective-permute-done.10, bf16[128,2048]{1,0:T(8,128)(2,1)} %collective-permute-done.9, pred[]{:T(512)S(6)} %eq.32), kind=kLoop, calls=%fused_computation | loop fusion | flops 262144 | bytes 1572865 | tf_op jit(solution)/shard_map/jit(_where)/select_n | solution.py:312
  64.7 0.0 collective-permute-done.5
  64.7 0.0 copy-start.5
  64.7 1.3 %copy-done.5 = bf16[1,1344,512]{2,1,0:T(8,128)(2,1)S(1)} copy-done((bf16[1,1344,512]{2,1,0:T(8,128)(2,1)S(1)}, bf16[1,1344,512]{2,1,0:T(8,128)(2,1)}, u32[]{:S(2)}) %copy-start.5) | copy-done | bytes 1376280
  66.1 2.0 %shard_map.88 = (bf16[672,128]{1,0:T(8,128)(2,1)S(1)}, bf16[672,128]{1,0:T(8,128)(2,1)S(1)}) custom-call(s32[1]{0:T(128)} %bitcast.core_ref, bf16[128,2048]{1,0:T(8,128)(2,1)S(1)} %broadcast_select_fusion.refs_0_, bf16[1344,1024]{1,0:T(8,128)(2,1)S(1)} %bitcast.16, bf16[1344,512]{1,0:T(8,128)(2,1)S(1)} %bitcast.20, bf16[1344,512]{1,0:T(8,128)(2,1)S(1)} %bitcast.24), custom_call_target="tpu_custom_call" | custom-call | flops 1 | bytes 1 | tf_op jit(solution)/shard_map/pallas_call | solution.py:187
  68.1 0.1 collective-permute-start.15
  68.2 0.0 collective-permute-done.13
  68.2 1.4 %collective-permute-done.15 = bf16[672,128]{1,0:T(8,128)(2,1)S(1)} collective-permute-done((bf16[672,128]{1,0:T(8,128)(2,1)S(1)}, bf16[672,128]{1,0:T(8,128)(2,1)S(1)}, u32[]{:S(2)}, u32[]{:S(2)}) %collective-permute-start.15) | collective-permute-done | bytes 172064 | tf_op jit(solution)/shard_map/ppermute | solution.py:223
  69.6 1.5 %collective-permute-start.16 = (bf16[672,128]{1,0:T(8,128)(2,1)S(1)}, bf16[672,128]{1,0:T(8,128)(2,1)S(1)}, u32[]{:S(2)}, u32[]{:S(2)}) collective-permute-start(bf16[672,128]{1,0:T(8,128)(2,1)S(1)} %add_convert_fusion.1), channel_id=1, source_target_pairs={{8,0},{16,8},{24,16},{0,24},{9,1},{17,9},{25,17},{1,25},{10,2},{18... | collective-permute-start | bytes 516104 | tf_op jit(solution)/shard_map/ppermute | solution.py:223
  71.1 3.0 %collective-permute-done.14.refs_0_ = bf16[128,2048]{1,0:T(8,128)(2,1)S(1)} collective-permute-done((bf16[128,2048]{1,0:T(8,128)(2,1)}, bf16[128,2048]{1,0:T(8,128)(2,1)S(1)}, u32[]{:S(2)}, u32[]{:S(2)}) %collective-permute-start.14) | collective-permute-done | bytes 524320 | tf_op jit(solution)/shard_map/ppermute | solution.py:214
  74.1 2.0 %shard_map.87 = (bf16[672,128]{1,0:T(8,128)(2,1)S(1)}, bf16[672,128]{1,0:T(8,128)(2,1)S(1)}) custom-call(s32[1]{0:T(128)} %bitcast.core_ref, bf16[128,2048]{1,0:T(8,128)(2,1)S(1)} %collective-permute-done.14.refs_0_, bf16[1344,1024]{1,0:T(8,128)(2,1)S(1)} %bitcast.17, bf16[1344,512]{1,0:T(8,128)(2,1)S(1)} %bitcast.21, bf16[1344,512]{1,0:T(8,128)(2,1)S(1)} %bitcast.25), custom_call_target="tpu_custom_call" | custom-call | flops 704643072 | bytes 6537216 | tf_op jit(solution)/shard_map/pallas_call | solution.py:187
  76.1 0.0 copy-start.11
  76.1 0.1 collective-permute-start.17
  76.2 1.4 %collective-permute-done.17 = bf16[672,128]{1,0:T(8,128)(2,1)S(1)} collective-permute-done((bf16[672,128]{1,0:T(8,128)(2,1)S(1)}, bf16[672,128]{1,0:T(8,128)(2,1)S(1)}, u32[]{:S(2)}, u32[]{:S(2)}) %collective-permute-start.17) | collective-permute-done | bytes 172064 | tf_op jit(solution)/shard_map/ppermute | solution.py:223
  77.7 2.3 %collective-permute-start.18 = (bf16[672,128]{1,0:T(8,128)(2,1)S(1)}, bf16[672,128]{1,0:T(8,128)(2,1)S(1)}, u32[]{:S(2)}, u32[]{:S(2)}) collective-permute-start(bf16[672,128]{1,0:T(8,128)(2,1)S(1)} %add_convert_fusion), channel_id=1, source_target_pairs={{8,0},{16,8},{24,16},{0,24},{9,1},{17,9},{25,17},{1,25},{10,2},{18... | collective-permute-start | bytes 516104 | tf_op jit(solution)/shard_map/ppermute | solution.py:223
  80.0 4.6 %collective-permute-done.18 = bf16[672,128]{1,0:T(8,128)(2,1)S(1)} collective-permute-done((bf16[672,128]{1,0:T(8,128)(2,1)S(1)}, bf16[672,128]{1,0:T(8,128)(2,1)S(1)}, u32[]{:S(2)}, u32[]{:S(2)}) %collective-permute-start.18) | collective-permute-done | bytes 172064 | tf_op jit(solution)/shard_map/ppermute | solution.py:223
  84.7 0.1 select_dynamic-update-slice_fusion.1
  84.8 0.1 select_dynamic-update-slice_fusion
  84.9 0.0 copy-start.9
  84.9 0.8 copy-done.9
  (22 shorter events, 0.3 us)
Async XLA Ops:
  1.0 13.0 %collective-permute-start.1 = (bf16[128,1024]{1,0:T(8,128)(2,1)S(1)}, bf16[128,1024]{1,0:T(8,128)(2,1)S(1)}, u32[]{:S(2)}, u32[]{:S(2)}) collective-permute-start(bf16[128,1024]{1,0:T(8,128)(2,1)S(1)} %pad_maximum_fusion.refs_2_), channel_id=1, source_target_pairs={{0,2},{2,4},{4,6},{1,3},{3,5},{5,7},{8,10},{10,12},{12,14},{9,11},... | collective-permute-start | bytes 786440 | tf_op jit(solution)/shard_map/ppermute | solution.py:207
  6.0 8.1 %collective-permute-start = (bf16[48,1024]{1,0:T(8,128)(2,1)S(1)}, bf16[48,1024]{1,0:T(8,128)(2,1)S(1)}, u32[]{:S(2)}, u32[]{:S(2)}) collective-permute-start(bf16[48,1024]{1,0:T(8,128)(2,1)S(1)} %slice.4), channel_id=1, source_target_pairs={{0,4},{2,6},{1,5},{3,7},{8,12},{10,14},{9,13},{11,15},{16,20},{18,... | collective-permute-start | bytes 294920 | tf_op jit(solution)/shard_map/ppermute | solution.py:207
  12.0 1.0 %copy-start.7 = (bf16[1,128,1024]{2,1,0:T(8,128)(2,1)S(1)}, bf16[1,128,1024]{2,1,0:T(8,128)(2,1)}, u32[]{:S(2)}) copy-start(bf16[1,128,1024]{2,1,0:T(8,128)(2,1)} %param.8) | copy-start | bytes 786436
  13.0 0.9 %copy-start.8 = (bf16[1,128,1024]{2,1,0:T(8,128)(2,1)S(1)}, bf16[1,128,1024]{2,1,0:T(8,128)(2,1)}, u32[]{:S(2)}) copy-start(bf16[1,128,1024]{2,1,0:T(8,128)(2,1)} %param.11) | copy-start | bytes 786436
  14.0 20.4 %copy-start = (bf16[1,1344,1024]{2,1,0:T(8,128)(2,1)S(1)}, bf16[1,1344,1024]{2,1,0:T(8,128)(2,1)}, u32[]{:S(2)}) copy-start(bf16[1,1344,1024]{2,1,0:T(8,128)(2,1)} %param.12) | copy-start | bytes 8257540
  16.3 15.9 %collective-permute-start.2 = (bf16[128,1024]{1,0:T(8,128)(2,1)S(1)}, bf16[128,1024]{1,0:T(8,128)(2,1)S(1)}, u32[]{:S(2)}, u32[]{:S(2)}) collective-permute-start(bf16[128,1024]{1,0:T(8,128)(2,1)S(1)} %get-tuple-element.36), channel_id=1, source_target_pairs={{2,0},{4,2},{6,4},{3,1},{5,3},{7,5},{10,8},{12,10},{14,12},{11,9},... | collective-permute-start | bytes 786440 | tf_op jit(solution)/shard_map/ppermute | solution.py:207
  17.6 14.6 %collective-permute-start.3 = (bf16[48,1024]{1,0:T(8,128)(2,1)S(1)}, bf16[48,1024]{1,0:T(8,128)(2,1)S(1)}, u32[]{:S(2)}, u32[]{:S(2)}) collective-permute-start(bf16[48,1024]{1,0:T(8,128)(2,1)S(1)} %get-tuple-element.37), channel_id=1, source_target_pairs={{4,0},{6,2},{5,1},{7,3},{12,8},{14,10},{13,9},{15,11},{20,16},{22,... | collective-permute-start | bytes 294920 | tf_op jit(solution)/shard_map/ppermute | solution.py:207
  32.3 6.9 %collective-permute-start.7 = (bf16[128,2048]{1,0:T(8,128)(2,1)S(1)}, bf16[128,2048]{1,0:T(8,128)(2,1)}, u32[]{:S(2)}, u32[]{:S(2)}) collective-permute-start(bf16[128,2048]{1,0:T(8,128)(2,1)S(1)} %shard_map.84.refs_0_), channel_id=1, source_target_pairs={{2,4},{4,2},{3,5},{5,3},{10,12},{12,10},{11,13},{13,11},{18,20},{2... | collective-permute-start | bytes 1572872 | tf_op jit(solution)/shard_map/ppermute | solution.py:214
  33.8 12.4 %collective-permute-start.6 = (bf16[128,2048]{1,0:T(8,128)(2,1)S(1)}, bf16[128,2048]{1,0:T(8,128)(2,1)}, u32[]{:S(2)}, u32[]{:S(2)}) collective-permute-start(bf16[128,2048]{1,0:T(8,128)(2,1)S(1)} %shard_map.84.refs_0_), channel_id=1, source_target_pairs={{0,2},{2,0},{4,6},{6,4},{1,3},{3,1},{5,7},{7,5},{8,10},{10,8},{12,... | collective-permute-start | bytes 1572872 | tf_op jit(solution)/shard_map/ppermute | solution.py:214
  34.4 1.3 %copy-start.1 = (bf16[1,1344,512]{2,1,0:T(8,128)(2,1)S(1)}, bf16[1,1344,512]{2,1,0:T(8,128)(2,1)}, u32[]{:S(2)}) copy-start(bf16[1,1344,512]{2,1,0:T(8,128)(2,1)} %param.13) | copy-start | bytes 4128772
  35.8 1.3 %copy-start.4 = (bf16[1,1344,512]{2,1,0:T(8,128)(2,1)S(1)}, bf16[1,1344,512]{2,1,0:T(8,128)(2,1)}, u32[]{:S(2)}) copy-start(bf16[1,1344,512]{2,1,0:T(8,128)(2,1)} %param.14) | copy-start | bytes 4128772
  37.1 11.2 %copy-start.2 = (bf16[1,1344,512]{2,1,0:T(8,128)(2,1)S(1)}, bf16[1,1344,512]{2,1,0:T(8,128)(2,1)}, u32[]{:S(2)}) copy-start(bf16[1,1344,512]{2,1,0:T(8,128)(2,1)} %param.13) | copy-start | bytes 4128772
  39.1 8.5 %collective-permute-start.4 = (bf16[672,128]{1,0:T(8,128)(2,1)S(1)}, bf16[672,128]{1,0:T(8,128)(2,1)S(1)}, u32[]{:S(2)}, u32[]{:S(2)}) collective-permute-start(bf16[672,128]{1,0:T(8,128)(2,1)S(1)} %get-tuple-element.39), channel_id=1, source_target_pairs={{1,0},{0,1},{3,2},{2,3},{5,4},{4,5},{7,6},{6,7},{9,8},{8,9},{11,10... | collective-permute-start | bytes 516104 | tf_op jit(solution)/shard_map/ppermute | solution.py:223
  39.2 16.4 %collective-permute-start.9 = (bf16[128,2048]{1,0:T(8,128)(2,1)}, bf16[128,2048]{1,0:T(8,128)(2,1)}, u32[]{:S(2)}, u32[]{:S(2)}) collective-permute-start(bf16[128,2048]{1,0:T(8,128)(2,1)} %collective-permute-done.7.refs_1_), channel_id=1, source_target_pairs={{0,2},{2,0},{4,6},{6,4},{1,3},{3,1},{5,7},{7,5},{8,10},{10,8},{12,... | collective-permute-start | bytes 1572872 | tf_op jit(solution)/shard_map/ppermute | solution.py:214
  46.1 9.5 %collective-permute-start.10 = (bf16[128,2048]{1,0:T(8,128)(2,1)}, bf16[128,2048]{1,0:T(8,128)(2,1)}, u32[]{:S(2)}, u32[]{:S(2)}) collective-permute-start(bf16[128,2048]{1,0:T(8,128)(2,1)} %collective-permute-done.6.refs_0_), channel_id=1, source_target_pairs={{2,4},{4,2},{3,5},{5,3},{10,12},{12,10},{11,13},{13,11},{18,20},{2... | collective-permute-start | bytes 1572872 | tf_op jit(solution)/shard_map/ppermute | solution.py:214
  51.7 3.1 %collective-permute-start.12 = (bf16[672,128]{1,0:T(8,128)(2,1)S(1)}, bf16[672,128]{1,0:T(8,128)(2,1)}, u32[]{:S(2)}, u32[]{:S(2)}) collective-permute-start(bf16[672,128]{1,0:T(8,128)(2,1)S(1)} %get-tuple-element.46), channel_id=1, source_target_pairs={{1,0},{0,1},{3,2},{2,3},{5,4},{4,5},{7,6},{6,7},{9,8},{8,9},{11,10... | collective-permute-start | bytes 516104 | tf_op jit(solution)/shard_map/ppermute | solution.py:223
  51.8 3.9 %collective-permute-start.8 = (bf16[672,128]{1,0:T(8,128)(2,1)S(1)}, bf16[672,128]{1,0:T(8,128)(2,1)}, u32[]{:S(2)}, u32[]{:S(2)}) collective-permute-start(bf16[672,128]{1,0:T(8,128)(2,1)S(1)} %get-tuple-element.43), channel_id=1, source_target_pairs={{1,0},{0,1},{3,2},{2,3},{5,4},{4,5},{7,6},{6,7},{9,8},{8,9},{11,10... | collective-permute-start | bytes 516104 | tf_op jit(solution)/shard_map/ppermute | solution.py:223
  52.3 12.4 %copy-start.3 = (bf16[1,1344,512]{2,1,0:T(8,128)(2,1)S(1)}, bf16[1,1344,512]{2,1,0:T(8,128)(2,1)}, u32[]{:S(2)}) copy-start(bf16[1,1344,512]{2,1,0:T(8,128)(2,1)} %param.13) | copy-start | bytes 4128772
  52.3 12.4 %collective-permute-start.5 = (bf16[672,128]{1,0:T(8,128)(2,1)}, bf16[672,128]{1,0:T(8,128)(2,1)S(1)}, u32[]{:S(2)}, u32[]{:S(2)}) collective-permute-start(bf16[672,128]{1,0:T(8,128)(2,1)} %add_convert_fusion.4), channel_id=1, source_target_pairs={{8,0},{16,8},{24,16},{0,24},{9,1},{17,9},{25,17},{1,25},{10,2},{18... | collective-permute-start | bytes 516104 | tf_op jit(solution)/shard_map/ppermute | solution.py:223
  56.6 11.5 %collective-permute-start.11 = (bf16[672,128]{1,0:T(8,128)(2,1)S(1)}, bf16[672,128]{1,0:T(8,128)(2,1)S(1)}, u32[]{:S(2)}, u32[]{:S(2)}) collective-permute-start(bf16[672,128]{1,0:T(8,128)(2,1)S(1)} %add_convert_fusion.3), channel_id=1, source_target_pairs={{8,0},{16,8},{24,16},{0,24},{9,1},{17,9},{25,17},{1,25},{10,2},{18... | collective-permute-start | bytes 516104 | tf_op jit(solution)/shard_map/ppermute | solution.py:223
  60.1 8.1 %collective-permute-start.13 = (bf16[672,128]{1,0:T(8,128)(2,1)S(1)}, bf16[672,128]{1,0:T(8,128)(2,1)S(1)}, u32[]{:S(2)}, u32[]{:S(2)}) collective-permute-start(bf16[672,128]{1,0:T(8,128)(2,1)S(1)} %add_convert_fusion.2), channel_id=1, source_target_pairs={{8,0},{16,8},{24,16},{0,24},{9,1},{17,9},{25,17},{1,25},{10,2},{18... | collective-permute-start | bytes 516104 | tf_op jit(solution)/shard_map/ppermute | solution.py:223
  60.7 13.4 %collective-permute-start.14 = (bf16[128,2048]{1,0:T(8,128)(2,1)}, bf16[128,2048]{1,0:T(8,128)(2,1)S(1)}, u32[]{:S(2)}, u32[]{:S(2)}) collective-permute-start(bf16[128,2048]{1,0:T(8,128)(2,1)} %collective-permute-done.10), channel_id=1, source_target_pairs={{0,2},{2,0},{4,6},{6,4},{1,3},{3,1},{5,7},{7,5},{8,10},{10,8},{12,... | collective-permute-start | bytes 1572872 | tf_op jit(solution)/shard_map/ppermute | solution.py:214
  64.7 1.3 %copy-start.5 = (bf16[1,1344,512]{2,1,0:T(8,128)(2,1)S(1)}, bf16[1,1344,512]{2,1,0:T(8,128)(2,1)}, u32[]{:S(2)}) copy-start(bf16[1,1344,512]{2,1,0:T(8,128)(2,1)} %param.14) | copy-start | bytes 4128772
  66.1 2.0 %copy-start.10 = (bf16[672,128]{1,0:T(8,128)(2,1)}, bf16[672,128]{1,0:T(8,128)(2,1)S(1)}, u32[]{:S(2)}) copy-start(bf16[672,128]{1,0:T(8,128)(2,1)S(1)} %collective-permute-done.5) | copy-start | bytes 516100
  66.1 8.0 %copy-start.6 = (bf16[1,1344,512]{2,1,0:T(8,128)(2,1)S(1)}, bf16[1,1344,512]{2,1,0:T(8,128)(2,1)}, u32[]{:S(2)}) copy-start(bf16[1,1344,512]{2,1,0:T(8,128)(2,1)} %param.14) | copy-start | bytes 4128772
  68.1 1.5 %collective-permute-start.15 = (bf16[672,128]{1,0:T(8,128)(2,1)S(1)}, bf16[672,128]{1,0:T(8,128)(2,1)S(1)}, u32[]{:S(2)}, u32[]{:S(2)}) collective-permute-start(bf16[672,128]{1,0:T(8,128)(2,1)S(1)} %get-tuple-element.52), channel_id=1, source_target_pairs={{1,0},{0,1},{3,2},{2,3},{5,4},{4,5},{7,6},{6,7},{9,8},{8,9},{11,10... | collective-permute-start | bytes 516104 | tf_op jit(solution)/shard_map/ppermute | solution.py:223
  69.6 6.5 %collective-permute-start.16 = (bf16[672,128]{1,0:T(8,128)(2,1)S(1)}, bf16[672,128]{1,0:T(8,128)(2,1)S(1)}, u32[]{:S(2)}, u32[]{:S(2)}) collective-permute-start(bf16[672,128]{1,0:T(8,128)(2,1)S(1)} %add_convert_fusion.1), channel_id=1, source_target_pairs={{8,0},{16,8},{24,16},{0,24},{9,1},{17,9},{25,17},{1,25},{10,2},{18... | collective-permute-start | bytes 516104 | tf_op jit(solution)/shard_map/ppermute | solution.py:223
  76.1 3.9 %copy-start.11 = (bf16[672,128]{1,0:T(8,128)(2,1)S(1)}, bf16[672,128]{1,0:T(8,128)(2,1)}, u32[]{:S(2)}) copy-start(bf16[672,128]{1,0:T(8,128)(2,1)} %copy-done.10) | copy-start | bytes 516100
  76.1 1.5 %collective-permute-start.17 = (bf16[672,128]{1,0:T(8,128)(2,1)S(1)}, bf16[672,128]{1,0:T(8,128)(2,1)S(1)}, u32[]{:S(2)}, u32[]{:S(2)}) collective-permute-start(bf16[672,128]{1,0:T(8,128)(2,1)S(1)} %get-tuple-element.54), channel_id=1, source_target_pairs={{1,0},{0,1},{3,2},{2,3},{5,4},{4,5},{7,6},{6,7},{9,8},{8,9},{11,10... | collective-permute-start | bytes 516104 | tf_op jit(solution)/shard_map/ppermute | solution.py:223
  77.7 7.0 %collective-permute-start.18 = (bf16[672,128]{1,0:T(8,128)(2,1)S(1)}, bf16[672,128]{1,0:T(8,128)(2,1)S(1)}, u32[]{:S(2)}, u32[]{:S(2)}) collective-permute-start(bf16[672,128]{1,0:T(8,128)(2,1)S(1)} %add_convert_fusion), channel_id=1, source_target_pairs={{8,0},{16,8},{24,16},{0,24},{9,1},{17,9},{25,17},{1,25},{10,2},{18... | collective-permute-start | bytes 516104 | tf_op jit(solution)/shard_map/ppermute | solution.py:223
  84.9 0.8 copy-start.9

commit v14 on v13

--- a/solution.py
+++ b/solution.py
@@ -300,7 +300,7 @@
             waiting = after(waiting, *sums, *(hops[-2] if step > 2 else ()))
         late = (came_first, came_second) if step > 1 else ()
         if step > 2 and last:
-            late = hops[-1]
+            late = hops[-1][:1]
         sums = halves_summed(waiting, late, light=step > 2 and last)
         results.append(hop(sums))
         by_first, by_second = came_second, came_first

time: 86.3 us -> 87.6 us (1.015)
  waiting for transfers between devices: 25.8 us -> 28.8 us
  starting transfers between devices: 34.3 us -> 32.7 us
    ppermute x10, waiting for transfers between devices: 7.4 us -> 10.2 us  [passed_along(): lax.ppermute(block, axis, [((i - distance) % len(devices), i) for i in de...]
    ppermute x10, starting transfers between devices: 10.1 us -> 8.49 us  [passed_along(): lax.ppermute(block, axis, [((i - distance) % len(devices), i) for i in de...]
  transfers between devices with their start and end apart: 19 -> 19, of which waited for: 7 -> 8; matrix products, arithmetic and copies ran while one was open for 6% -> 6% of each run, Pallas kernels for 11% -> 11%
where the time goes in v14:
time: 87.6 us; the launch traced here: 87.1 us
  starting transfers between devices  32.7 us (37%)
  waiting for transfers between devices  28.8 us (33%)
  Pallas kernels  11.8 us (13%)
  local copies, waits for them, and re-layouts  8.35 us (10%)
  other arithmetic  5.14 us (6%)
    ppermute x4, waiting for transfers between devices, moved(): lax.ppermute(block, axis, [(i, i + by) for i in range(size) if 0 <= i + b...  13.3 us
    ppermute x5, starting transfers between devices, swapped(): return lax.ppermute(block, axis, pairs)  12.2 us
    ppermute x4, starting transfers between devices, moved(): lax.ppermute(block, axis, [(i, i + by) for i in range(size) if 0 <= i + b...  12 us
    ppermute x10, waiting for transfers between devices, passed_along(): lax.ppermute(block, axis, [((i - distance) % len(devices), i) for i in de...  10.2 us
    pallas_call x4, Pallas kernels, project(): pl.pallas_call(functools.partial(project_kernel, [len(block) for block in...  9.39 us
    ppermute x10, starting transfers between devices, passed_along(): lax.ppermute(block, axis, [((i - distance) % len(devices), i) for i in de...  8.49 us
    unnamed x24, local copies, waits for them, and re-layouts  6.78 us
    ppermute x5, waiting for transfers between devices, swapped(): return lax.ppermute(block, axis, pairs)  5.18 us
  transfers between devices with their start and end apart: 19, of which 8 were waited for; matrix products, arithmetic and copies ran while one was open for 6% of the time, Pallas kernels for 11%

profile of v14, /device:TPU:0, one launch (start us, length us, event | category | flops | bytes accessed | tf_op | source)
XLA Modules:
  0.0 87.1 jit_solution(7709586406568545023)
XLA Ops:
  0.0 1.0 %pad_maximum_fusion.refs_2_ = bf16[128,1024]{1,0:T(8,128)(2,1)S(1)} fusion(bf16[128,512]{1,0:T(8,128)(2,1)} %bitcast.28, bf16[128,512]{1,0:T(8,128)(2,1)} %bitcast.29), kind=kLoop, calls=%fused_computation.6 | loop fusion | flops 524288 | bytes 524288 | tf_op jit(solution)/shard_map/concatenate | solution.py:247
  1.0 4.9 %collective-permute-start.1 = (bf16[128,1024]{1,0:T(8,128)(2,1)S(1)}, bf16[128,1024]{1,0:T(8,128)(2,1)S(1)}, u32[]{:S(2)}, u32[]{:S(2)}) collective-permute-start(bf16[128,1024]{1,0:T(8,128)(2,1)S(1)} %pad_maximum_fusion.refs_2_), channel_id=1, source_target_pairs={{0,2},{2,4},{4,6},{1,3},{3,5},{5,7},{8,10},{10,12},{12,14},{9,11},... | collective-permute-start | bytes 786440 | tf_op jit(solution)/shard_map/ppermute | solution.py:207
  6.0 4.5 %collective-permute-start = (bf16[48,1024]{1,0:T(8,128)(2,1)S(1)}, bf16[48,1024]{1,0:T(8,128)(2,1)S(1)}, u32[]{:S(2)}, u32[]{:S(2)}) collective-permute-start(bf16[48,1024]{1,0:T(8,128)(2,1)S(1)} %slice.4), channel_id=1, source_target_pairs={{0,4},{2,6},{1,5},{3,7},{8,12},{10,14},{9,13},{11,15},{16,20},{18,... | collective-permute-start | bytes 294920 | tf_op jit(solution)/shard_map/ppermute | solution.py:207
  10.5 0.8 pad_dynamic-slice_fusion
  11.2 0.7 fusion.5
  11.9 0.1 fusion.4.refs_3_
  12.0 0.0 copy-start.7
  12.0 0.9 %copy-done.7 = bf16[1,128,1024]{2,1,0:T(8,128)(2,1)S(1)} copy-done((bf16[1,128,1024]{2,1,0:T(8,128)(2,1)S(1)}, bf16[1,128,1024]{2,1,0:T(8,128)(2,1)}, u32[]{:S(2)}) %copy-start.7) | copy-done | bytes 262168
  13.0 0.9 %copy-done.8 = bf16[1,128,1024]{2,1,0:T(8,128)(2,1)S(1)} copy-done((bf16[1,128,1024]{2,1,0:T(8,128)(2,1)S(1)}, bf16[1,128,1024]{2,1,0:T(8,128)(2,1)}, u32[]{:S(2)}) %copy-start.8) | copy-done | bytes 262168
  13.9 0.1 shard_map.82
  14.0 0.0 collective-permute-done.refs_4_
  14.0 0.0 collective-permute-done.1.refs_5_
  14.0 0.0 copy-start
  14.0 2.2 %shard_map.83 = (bf16[128,1024]{1,0:T(8,128)(2,1)S(1)}, f32[128,1024]{1,0:T(8,128)S(1)}, bf16[48,1024]{1,0:T(8,128)(2,1)S(1)}, bf16[128,1024]{1,0:T(8,128)(2,1)S(1)}) custom-call(bf16[1024,128]{1,0:T(8,128)(2,1)S(1)} %get-tuple-element.32.refs_0_, bf16[1024,128]{1,0:T(8,128)(2,1)S(1)} %get-tuple-element.33.refs_1_, ...), custom_call_target="tpu_custom_call" | custom-call | flops 478150656 | bytes 1048576 | tf_op jit(solution)/shard_map/pallas_call | solution.py:100
  16.3 1.3 %collective-permute-start.2 = (bf16[128,1024]{1,0:T(8,128)(2,1)S(1)}, bf16[128,1024]{1,0:T(8,128)(2,1)S(1)}, u32[]{:S(2)}, u32[]{:S(2)}) collective-permute-start(bf16[128,1024]{1,0:T(8,128)(2,1)S(1)} %get-tuple-element.36), channel_id=1, source_target_pairs={{2,0},{4,2},{6,4},{3,1},{5,3},{7,5},{10,8},{12,10},{14,12},{11,9},... | collective-permute-start | bytes 786440 | tf_op jit(solution)/shard_map/ppermute | solution.py:207
  17.6 1.3 %collective-permute-start.3 = (bf16[48,1024]{1,0:T(8,128)(2,1)S(1)}, bf16[48,1024]{1,0:T(8,128)(2,1)S(1)}, u32[]{:S(2)}, u32[]{:S(2)}) collective-permute-start(bf16[48,1024]{1,0:T(8,128)(2,1)S(1)} %get-tuple-element.37), channel_id=1, source_target_pairs={{4,0},{6,2},{5,1},{7,3},{12,8},{14,10},{13,9},{15,11},{20,16},{22,... | collective-permute-start | bytes 294920 | tf_op jit(solution)/shard_map/ppermute | solution.py:207
  18.9 13.3 %collective-permute-done.3.refs_1_ = bf16[48,1024]{1,0:T(8,128)(2,1)S(1)} collective-permute-done((bf16[48,1024]{1,0:T(8,128)(2,1)S(1)}, bf16[48,1024]{1,0:T(8,128)(2,1)S(1)}, u32[]{:S(2)}, u32[]{:S(2)}) %collective-permute-start.3) | collective-permute-done | bytes 98336 | tf_op jit(solution)/shard_map/ppermute | solution.py:207
  32.2 0.0 collective-permute-done.2.refs_0_
  32.2 0.1 shard_map.84.refs_0_
  32.3 1.5 %collective-permute-start.7 = (bf16[128,2048]{1,0:T(8,128)(2,1)S(1)}, bf16[128,2048]{1,0:T(8,128)(2,1)}, u32[]{:S(2)}, u32[]{:S(2)}) collective-permute-start(bf16[128,2048]{1,0:T(8,128)(2,1)S(1)} %shard_map.84.refs_0_), channel_id=1, source_target_pairs={{2,4},{4,2},{3,5},{5,3},{10,12},{12,10},{11,13},{13,11},{18,20},{2... | collective-permute-start | bytes 1572872 | tf_op jit(solution)/shard_map/ppermute | solution.py:214
  33.8 0.6 collective-permute-start.6
  34.4 1.3 %copy-done.1 = bf16[1,1344,512]{2,1,0:T(8,128)(2,1)S(1)} copy-done((bf16[1,1344,512]{2,1,0:T(8,128)(2,1)S(1)}, bf16[1,1344,512]{2,1,0:T(8,128)(2,1)}, u32[]{:S(2)}) %copy-start.1) | copy-done | bytes 1376280
  35.8 1.3 %copy-done.4 = bf16[1,1344,512]{2,1,0:T(8,128)(2,1)S(1)} copy-done((bf16[1,1344,512]{2,1,0:T(8,128)(2,1)S(1)}, bf16[1,1344,512]{2,1,0:T(8,128)(2,1)}, u32[]{:S(2)}) %copy-start.4) | copy-done | bytes 1376280
  37.1 2.0 %shard_map.85 = (bf16[672,128]{1,0:T(8,128)(2,1)S(1)}, bf16[672,128]{1,0:T(8,128)(2,1)S(1)}) custom-call(s32[1]{0:T(128)} %bitcast.core_ref, bf16[128,2048]{1,0:T(8,128)(2,1)S(1)} %shard_map.84.refs_0_, bf16[1344,1024]{1,0:T(8,128)(2,1)S(1)} %bitcast.14, bf16[1344,512]{1,0:T(8,128)(2,1)S(1)} %bitcast.18, bf16[1344,512]{1,0:T(8,128)(2,1)S(1)} %bitcast.22), custom_call_target="tpu_custom_call" | custom-call | flops 704643072 | bytes 6537216 | tf_op jit(solution)/shard_map/pallas_call | solution.py:187
  39.1 0.1 collective-permute-start.4
  39.2 0.0 collective-permute-done.7.refs_1_
  39.2 5.8 %collective-permute-start.9 = (bf16[128,2048]{1,0:T(8,128)(2,1)}, bf16[128,2048]{1,0:T(8,128)(2,1)}, u32[]{:S(2)}, u32[]{:S(2)}) collective-permute-start(bf16[128,2048]{1,0:T(8,128)(2,1)} %collective-permute-done.7.refs_1_), channel_id=1, source_target_pairs={{0,2},{2,0},{4,6},{6,4},{1,3},{3,1},{5,7},{7,5},{8,10},{10,8},{12,... | collective-permute-start | bytes 1572872 | tf_op jit(solution)/shard_map/ppermute | solution.py:214
  45.0 1.2 %collective-permute-done.6.refs_0_ = bf16[128,2048]{1,0:T(8,128)(2,1)} collective-permute-done((bf16[128,2048]{1,0:T(8,128)(2,1)S(1)}, bf16[128,2048]{1,0:T(8,128)(2,1)}, u32[]{:S(2)}, u32[]{:S(2)}) %collective-permute-start.6) | collective-permute-done | bytes 524320 | tf_op jit(solution)/shard_map/ppermute | solution.py:214
  46.1 1.5 %collective-permute-start.10 = (bf16[128,2048]{1,0:T(8,128)(2,1)}, bf16[128,2048]{1,0:T(8,128)(2,1)}, u32[]{:S(2)}, u32[]{:S(2)}) collective-permute-start(bf16[128,2048]{1,0:T(8,128)(2,1)} %collective-permute-done.6.refs_0_), channel_id=1, source_target_pairs={{2,4},{4,2},{3,5},{5,3},{10,12},{12,10},{11,13},{13,11},{18,20},{2... | collective-permute-start | bytes 1572872 | tf_op jit(solution)/shard_map/ppermute | solution.py:214
  47.6 0.0 collective-permute-done.4
  47.6 0.7 add_convert_fusion.4
  48.3 3.4 %shard_map.86 = (bf16[672,128]{1,0:T(8,128)(2,1)S(1)}, bf16[672,128]{1,0:T(8,128)(2,1)S(1)}, bf16[672,128]{1,0:T(8,128)(2,1)S(1)}, bf16[672,128]{1,0:T(8,128)(2,1)S(1)}) custom-call(s32[1]{0:T(128)} %bitcast.core_ref, bf16[128,2048]{1,0:T(8,128)(2,1)} %collective-permute-done.6.refs_0_, bf16[128,2048]{1,0:T(8,128)(2,1)} %collective-permute-done.7.refs_1_, ...), custom_call_target="tpu_custom_call" | custom-call | flops 1409286144 | bytes 7569408 | tf_op jit(solution)/shard_map/pallas_call | solution.py:187
  51.7 0.1 collective-permute-start.12
  51.8 0.5 collective-permute-start.8
  52.3 2.5 %collective-permute-start.5 = (bf16[672,128]{1,0:T(8,128)(2,1)}, bf16[672,128]{1,0:T(8,128)(2,1)S(1)}, u32[]{:S(2)}, u32[]{:S(2)}) collective-permute-start(bf16[672,128]{1,0:T(8,128)(2,1)} %add_convert_fusion.4), channel_id=1, source_target_pairs={{8,0},{16,8},{24,16},{0,24},{9,1},{17,9},{25,17},{1,25},{10,2},{18... | collective-permute-start | bytes 516104 | tf_op jit(solution)/shard_map/ppermute | solution.py:223
  54.8 0.0 collective-permute-done.12
  54.8 0.9 %collective-permute-done.9 = bf16[128,2048]{1,0:T(8,128)(2,1)} collective-permute-done((bf16[128,2048]{1,0:T(8,128)(2,1)}, bf16[128,2048]{1,0:T(8,128)(2,1)}, u32[]{:S(2)}, u32[]{:S(2)}) %collective-permute-start.9) | collective-permute-done | bytes 524320 | tf_op jit(solution)/shard_map/ppermute | solution.py:214
  55.6 0.0 collective-permute-done.10
  55.7 1.0 %add_convert_fusion.2 = bf16[672,128]{1,0:T(8,128)(2,1)S(1)} fusion(bf16[672,128]{1,0:T(8,128)(2,1)} %collective-permute-done.12, bf16[672,128]{1,0:T(8,128)(2,1)S(1)} %get-tuple-element.45), kind=kLoop, calls=%fused_computation.3 | loop fusion | flops 344064 | bytes 516096 | tf_op jit(solution)/shard_map/convert_element_type | solution.py:284
  56.6 2.5 %collective-permute-start.13 = (bf16[672,128]{1,0:T(8,128)(2,1)S(1)}, bf16[672,128]{1,0:T(8,128)(2,1)S(1)}, u32[]{:S(2)}, u32[]{:S(2)}) collective-permute-start(bf16[672,128]{1,0:T(8,128)(2,1)S(1)} %add_convert_fusion.2), channel_id=1, source_target_pairs={{8,0},{16,8},{24,16},{0,24},{9,1},{17,9},{25,17},{1,25},{10,2},{18... | collective-permute-start | bytes 516104 | tf_op jit(solution)/shard_map/ppermute | solution.py:223
  59.1 2.9 %collective-permute-start.14 = (bf16[128,2048]{1,0:T(8,128)(2,1)}, bf16[128,2048]{1,0:T(8,128)(2,1)S(1)}, u32[]{:S(2)}, u32[]{:S(2)}) collective-permute-start(bf16[128,2048]{1,0:T(8,128)(2,1)} %collective-permute-done.10), channel_id=1, source_target_pairs={{0,2},{2,0},{4,6},{6,4},{1,3},{3,1},{5,7},{7,5},{8,10},{10,8},{12,... | collective-permute-start | bytes 1572872 | tf_op jit(solution)/shard_map/ppermute | solution.py:214
  62.0 1.1 %broadcast_select_fusion.refs_0_ = bf16[128,2048]{1,0:T(8,128)(2,1)S(1)} fusion(bf16[128,2048]{1,0:T(8,128)(2,1)} %collective-permute-done.10, bf16[128,2048]{1,0:T(8,128)(2,1)} %collective-permute-done.9, pred[]{:T(512)S(6)} %eq.32), kind=kLoop, calls=%fused_computation | loop fusion | flops 262144 | bytes 1572865 | tf_op jit(solution)/shard_map/jit(_where)/select_n | solution.py:312
  63.1 1.0 %add_convert_fusion.3 = bf16[672,128]{1,0:T(8,128)(2,1)S(1)} fusion(bf16[672,128]{1,0:T(8,128)(2,1)} %collective-permute-done.8, bf16[672,128]{1,0:T(8,128)(2,1)S(1)} %get-tuple-element.42), kind=kLoop, calls=%fused_computation.4 | loop fusion | flops 344064 | bytes 516096 | tf_op jit(solution)/shard_map/convert_element_type | solution.py:284
  64.1 0.0 collective-permute-done.5
  64.1 0.0 copy-start.5
  64.1 1.3 %copy-done.5 = bf16[1,1344,512]{2,1,0:T(8,128)(2,1)S(1)} copy-done((bf16[1,1344,512]{2,1,0:T(8,128)(2,1)S(1)}, bf16[1,1344,512]{2,1,0:T(8,128)(2,1)}, u32[]{:S(2)}) %copy-start.5) | copy-done | bytes 1376280
  65.5 2.0 %shard_map.88 = (bf16[672,128]{1,0:T(8,128)(2,1)S(1)}, bf16[672,128]{1,0:T(8,128)(2,1)S(1)}) custom-call(s32[1]{0:T(128)} %bitcast.core_ref, bf16[128,2048]{1,0:T(8,128)(2,1)S(1)} %broadcast_select_fusion.refs_0_, bf16[1344,1024]{1,0:T(8,128)(2,1)S(1)} %bitcast.16, bf16[1344,512]{1,0:T(8,128)(2,1)S(1)} %bitcast.20, bf16[1344,512]{1,0:T(8,128)(2,1)S(1)} %bitcast.24), custom_call_target="tpu_custom_call" | custom-call | flops 1 | bytes 1 | tf_op jit(solution)/shard_map/pallas_call | solution.py:187
  67.5 0.1 collective-permute-start.15
  67.6 0.6 collective-permute-start.11
  68.2 0.8 collective-permute-done.15
  69.0 0.7 collective-permute-start.16
  69.7 3.1 %collective-permute-done.14.refs_0_ = bf16[128,2048]{1,0:T(8,128)(2,1)S(1)} collective-permute-done((bf16[128,2048]{1,0:T(8,128)(2,1)}, bf16[128,2048]{1,0:T(8,128)(2,1)S(1)}, u32[]{:S(2)}, u32[]{:S(2)}) %collective-permute-start.14) | collective-permute-done | bytes 524320 | tf_op jit(solution)/shard_map/ppermute | solution.py:214
  72.8 2.0 %shard_map.87 = (bf16[672,128]{1,0:T(8,128)(2,1)S(1)}, bf16[672,128]{1,0:T(8,128)(2,1)S(1)}) custom-call(s32[1]{0:T(128)} %bitcast.core_ref, bf16[128,2048]{1,0:T(8,128)(2,1)S(1)} %collective-permute-done.14.refs_0_, bf16[1344,1024]{1,0:T(8,128)(2,1)S(1)} %bitcast.17, bf16[1344,512]{1,0:T(8,128)(2,1)S(1)} %bitcast.21, bf16[1344,512]{1,0:T(8,128)(2,1)S(1)} %bitcast.25), custom_call_target="tpu_custom_call" | custom-call | flops 704643072 | bytes 6537216 | tf_op jit(solution)/shard_map/pallas_call | solution.py:187
  74.8 0.0 copy-start.11
  74.8 0.0 collective-permute-done.11
  74.9 3.2 %collective-permute-done.16 = bf16[672,128]{1,0:T(8,128)(2,1)S(1)} collective-permute-done((bf16[672,128]{1,0:T(8,128)(2,1)S(1)}, bf16[672,128]{1,0:T(8,128)(2,1)S(1)}, u32[]{:S(2)}, u32[]{:S(2)}) %collective-permute-start.16) | collective-permute-done | bytes 172064 | tf_op jit(solution)/shard_map/ppermute | solution.py:223
  78.0 0.0 collective-permute-start.17
  78.0 1.4 %collective-permute-done.17 = bf16[672,128]{1,0:T(8,128)(2,1)S(1)} collective-permute-done((bf16[672,128]{1,0:T(8,128)(2,1)S(1)}, bf16[672,128]{1,0:T(8,128)(2,1)S(1)}, u32[]{:S(2)}, u32[]{:S(2)}) %collective-permute-start.17) | collective-permute-done | bytes 172064 | tf_op jit(solution)/shard_map/ppermute | solution.py:223
  79.5 1.5 %collective-permute-start.18 = (bf16[672,128]{1,0:T(8,128)(2,1)S(1)}, bf16[672,128]{1,0:T(8,128)(2,1)S(1)}, u32[]{:S(2)}, u32[]{:S(2)}) collective-permute-start(bf16[672,128]{1,0:T(8,128)(2,1)S(1)} %add_convert_fusion), channel_id=1, source_target_pairs={{8,0},{16,8},{24,16},{0,24},{9,1},{17,9},{25,17},{1,25},{10,2},{18... | collective-permute-start | bytes 516104 | tf_op jit(solution)/shard_map/ppermute | solution.py:223
  81.1 4.9 %collective-permute-done.18 = bf16[672,128]{1,0:T(8,128)(2,1)S(1)} collective-permute-done((bf16[672,128]{1,0:T(8,128)(2,1)S(1)}, bf16[672,128]{1,0:T(8,128)(2,1)S(1)}, u32[]{:S(2)}, u32[]{:S(2)}) %collective-permute-start.18) | collective-permute-done | bytes 172064 | tf_op jit(solution)/shard_map/ppermute | solution.py:223
  86.0 0.1 select_dynamic-update-slice_fusion.1
  86.1 0.1 select_dynamic-update-slice_fusion
  86.2 0.0 copy-start.9
  86.2 0.8 copy-done.9
  (22 shorter events, 0.3 us)
Async XLA Ops:
  1.0 13.0 %collective-permute-start.1 = (bf16[128,1024]{1,0:T(8,128)(2,1)S(1)}, bf16[128,1024]{1,0:T(8,128)(2,1)S(1)}, u32[]{:S(2)}, u32[]{:S(2)}) collective-permute-start(bf16[128,1024]{1,0:T(8,128)(2,1)S(1)} %pad_maximum_fusion.refs_2_), channel_id=1, source_target_pairs={{0,2},{2,4},{4,6},{1,3},{3,5},{5,7},{8,10},{10,12},{12,14},{9,11},... | collective-permute-start | bytes 786440 | tf_op jit(solution)/shard_map/ppermute | solution.py:207
  6.0 8.1 %collective-permute-start = (bf16[48,1024]{1,0:T(8,128)(2,1)S(1)}, bf16[48,1024]{1,0:T(8,128)(2,1)S(1)}, u32[]{:S(2)}, u32[]{:S(2)}) collective-permute-start(bf16[48,1024]{1,0:T(8,128)(2,1)S(1)} %slice.4), channel_id=1, source_target_pairs={{0,4},{2,6},{1,5},{3,7},{8,12},{10,14},{9,13},{11,15},{16,20},{18,... | collective-permute-start | bytes 294920 | tf_op jit(solution)/shard_map/ppermute | solution.py:207
  12.0 1.0 %copy-start.7 = (bf16[1,128,1024]{2,1,0:T(8,128)(2,1)S(1)}, bf16[1,128,1024]{2,1,0:T(8,128)(2,1)}, u32[]{:S(2)}) copy-start(bf16[1,128,1024]{2,1,0:T(8,128)(2,1)} %param.8) | copy-start | bytes 786436
  13.0 0.9 %copy-start.8 = (bf16[1,128,1024]{2,1,0:T(8,128)(2,1)S(1)}, bf16[1,128,1024]{2,1,0:T(8,128)(2,1)}, u32[]{:S(2)}) copy-start(bf16[1,128,1024]{2,1,0:T(8,128)(2,1)} %param.11) | copy-start | bytes 786436
  14.0 20.4 %copy-start = (bf16[1,1344,1024]{2,1,0:T(8,128)(2,1)S(1)}, bf16[1,1344,1024]{2,1,0:T(8,128)(2,1)}, u32[]{:S(2)}) copy-start(bf16[1,1344,1024]{2,1,0:T(8,128)(2,1)} %param.12) | copy-start | bytes 8257540
  16.3 15.9 %collective-permute-start.2 = (bf16[128,1024]{1,0:T(8,128)(2,1)S(1)}, bf16[128,1024]{1,0:T(8,128)(2,1)S(1)}, u32[]{:S(2)}, u32[]{:S(2)}) collective-permute-start(bf16[128,1024]{1,0:T(8,128)(2,1)S(1)} %get-tuple-element.36), channel_id=1, source_target_pairs={{2,0},{4,2},{6,4},{3,1},{5,3},{7,5},{10,8},{12,10},{14,12},{11,9},... | collective-permute-start | bytes 786440 | tf_op jit(solution)/shard_map/ppermute | solution.py:207
  17.6 14.6 %collective-permute-start.3 = (bf16[48,1024]{1,0:T(8,128)(2,1)S(1)}, bf16[48,1024]{1,0:T(8,128)(2,1)S(1)}, u32[]{:S(2)}, u32[]{:S(2)}) collective-permute-start(bf16[48,1024]{1,0:T(8,128)(2,1)S(1)} %get-tuple-element.37), channel_id=1, source_target_pairs={{4,0},{6,2},{5,1},{7,3},{12,8},{14,10},{13,9},{15,11},{20,16},{22,... | collective-permute-start | bytes 294920 | tf_op jit(solution)/shard_map/ppermute | solution.py:207
  32.3 6.9 %collective-permute-start.7 = (bf16[128,2048]{1,0:T(8,128)(2,1)S(1)}, bf16[128,2048]{1,0:T(8,128)(2,1)}, u32[]{:S(2)}, u32[]{:S(2)}) collective-permute-start(bf16[128,2048]{1,0:T(8,128)(2,1)S(1)} %shard_map.84.refs_0_), channel_id=1, source_target_pairs={{2,4},{4,2},{3,5},{5,3},{10,12},{12,10},{11,13},{13,11},{18,20},{2... | collective-permute-start | bytes 1572872 | tf_op jit(solution)/shard_map/ppermute | solution.py:214
  33.8 12.3 %collective-permute-start.6 = (bf16[128,2048]{1,0:T(8,128)(2,1)S(1)}, bf16[128,2048]{1,0:T(8,128)(2,1)}, u32[]{:S(2)}, u32[]{:S(2)}) collective-permute-start(bf16[128,2048]{1,0:T(8,128)(2,1)S(1)} %shard_map.84.refs_0_), channel_id=1, source_target_pairs={{0,2},{2,0},{4,6},{6,4},{1,3},{3,1},{5,7},{7,5},{8,10},{10,8},{12,... | collective-permute-start | bytes 1572872 | tf_op jit(solution)/shard_map/ppermute | solution.py:214
  34.4 1.3 %copy-start.1 = (bf16[1,1344,512]{2,1,0:T(8,128)(2,1)S(1)}, bf16[1,1344,512]{2,1,0:T(8,128)(2,1)}, u32[]{:S(2)}) copy-start(bf16[1,1344,512]{2,1,0:T(8,128)(2,1)} %param.13) | copy-start | bytes 4128772
  35.8 1.3 %copy-start.4 = (bf16[1,1344,512]{2,1,0:T(8,128)(2,1)S(1)}, bf16[1,1344,512]{2,1,0:T(8,128)(2,1)}, u32[]{:S(2)}) copy-start(bf16[1,1344,512]{2,1,0:T(8,128)(2,1)} %param.14) | copy-start | bytes 4128772
  37.1 11.2 %copy-start.2 = (bf16[1,1344,512]{2,1,0:T(8,128)(2,1)S(1)}, bf16[1,1344,512]{2,1,0:T(8,128)(2,1)}, u32[]{:S(2)}) copy-start(bf16[1,1344,512]{2,1,0:T(8,128)(2,1)} %param.13) | copy-start | bytes 4128772
  39.1 8.5 %collective-permute-start.4 = (bf16[672,128]{1,0:T(8,128)(2,1)S(1)}, bf16[672,128]{1,0:T(8,128)(2,1)S(1)}, u32[]{:S(2)}, u32[]{:S(2)}) collective-permute-start(bf16[672,128]{1,0:T(8,128)(2,1)S(1)} %get-tuple-element.39), channel_id=1, source_target_pairs={{1,0},{0,1},{3,2},{2,3},{5,4},{4,5},{7,6},{6,7},{9,8},{8,9},{11,10... | collective-permute-start | bytes 516104 | tf_op jit(solution)/shard_map/ppermute | solution.py:223
  39.2 16.4 %collective-permute-start.9 = (bf16[128,2048]{1,0:T(8,128)(2,1)}, bf16[128,2048]{1,0:T(8,128)(2,1)}, u32[]{:S(2)}, u32[]{:S(2)}) collective-permute-start(bf16[128,2048]{1,0:T(8,128)(2,1)} %collective-permute-done.7.refs_1_), channel_id=1, source_target_pairs={{0,2},{2,0},{4,6},{6,4},{1,3},{3,1},{5,7},{7,5},{8,10},{10,8},{12,... | collective-permute-start | bytes 1572872 | tf_op jit(solution)/shard_map/ppermute | solution.py:214
  46.1 9.5 %collective-permute-start.10 = (bf16[128,2048]{1,0:T(8,128)(2,1)}, bf16[128,2048]{1,0:T(8,128)(2,1)}, u32[]{:S(2)}, u32[]{:S(2)}) collective-permute-start(bf16[128,2048]{1,0:T(8,128)(2,1)} %collective-permute-done.6.refs_0_), channel_id=1, source_target_pairs={{2,4},{4,2},{3,5},{5,3},{10,12},{12,10},{11,13},{13,11},{18,20},{2... | collective-permute-start | bytes 1572872 | tf_op jit(solution)/shard_map/ppermute | solution.py:214
  51.7 3.1 %collective-permute-start.12 = (bf16[672,128]{1,0:T(8,128)(2,1)S(1)}, bf16[672,128]{1,0:T(8,128)(2,1)}, u32[]{:S(2)}, u32[]{:S(2)}) collective-permute-start(bf16[672,128]{1,0:T(8,128)(2,1)S(1)} %get-tuple-element.46), channel_id=1, source_target_pairs={{1,0},{0,1},{3,2},{2,3},{5,4},{4,5},{7,6},{6,7},{9,8},{8,9},{11,10... | collective-permute-start | bytes 516104 | tf_op jit(solution)/shard_map/ppermute | solution.py:223
  51.8 3.9 %collective-permute-start.8 = (bf16[672,128]{1,0:T(8,128)(2,1)S(1)}, bf16[672,128]{1,0:T(8,128)(2,1)}, u32[]{:S(2)}, u32[]{:S(2)}) collective-permute-start(bf16[672,128]{1,0:T(8,128)(2,1)S(1)} %get-tuple-element.43), channel_id=1, source_target_pairs={{1,0},{0,1},{3,2},{2,3},{5,4},{4,5},{7,6},{6,7},{9,8},{8,9},{11,10... | collective-permute-start | bytes 516104 | tf_op jit(solution)/shard_map/ppermute | solution.py:223
  52.3 11.8 %copy-start.3 = (bf16[1,1344,512]{2,1,0:T(8,128)(2,1)S(1)}, bf16[1,1344,512]{2,1,0:T(8,128)(2,1)}, u32[]{:S(2)}) copy-start(bf16[1,1344,512]{2,1,0:T(8,128)(2,1)} %param.13) | copy-start | bytes 4128772
  52.3 11.8 %collective-permute-start.5 = (bf16[672,128]{1,0:T(8,128)(2,1)}, bf16[672,128]{1,0:T(8,128)(2,1)S(1)}, u32[]{:S(2)}, u32[]{:S(2)}) collective-permute-start(bf16[672,128]{1,0:T(8,128)(2,1)} %add_convert_fusion.4), channel_id=1, source_target_pairs={{8,0},{16,8},{24,16},{0,24},{9,1},{17,9},{25,17},{1,25},{10,2},{18... | collective-permute-start | bytes 516104 | tf_op jit(solution)/shard_map/ppermute | solution.py:223
  56.6 11.5 %collective-permute-start.13 = (bf16[672,128]{1,0:T(8,128)(2,1)S(1)}, bf16[672,128]{1,0:T(8,128)(2,1)S(1)}, u32[]{:S(2)}, u32[]{:S(2)}) collective-permute-start(bf16[672,128]{1,0:T(8,128)(2,1)S(1)} %add_convert_fusion.2), channel_id=1, source_target_pairs={{8,0},{16,8},{24,16},{0,24},{9,1},{17,9},{25,17},{1,25},{10,2},{18... | collective-permute-start | bytes 516104 | tf_op jit(solution)/shard_map/ppermute | solution.py:223
  59.1 13.7 %collective-permute-start.14 = (bf16[128,2048]{1,0:T(8,128)(2,1)}, bf16[128,2048]{1,0:T(8,128)(2,1)S(1)}, u32[]{:S(2)}, u32[]{:S(2)}) collective-permute-start(bf16[128,2048]{1,0:T(8,128)(2,1)} %collective-permute-done.10), channel_id=1, source_target_pairs={{0,2},{2,0},{4,6},{6,4},{1,3},{3,1},{5,7},{7,5},{8,10},{10,8},{12,... | collective-permute-start | bytes 1572872 | tf_op jit(solution)/shard_map/ppermute | solution.py:214
  64.1 1.3 %copy-start.5 = (bf16[1,1344,512]{2,1,0:T(8,128)(2,1)S(1)}, bf16[1,1344,512]{2,1,0:T(8,128)(2,1)}, u32[]{:S(2)}) copy-start(bf16[1,1344,512]{2,1,0:T(8,128)(2,1)} %param.14) | copy-start | bytes 4128772
  65.5 2.0 %copy-start.10 = (bf16[672,128]{1,0:T(8,128)(2,1)}, bf16[672,128]{1,0:T(8,128)(2,1)S(1)}, u32[]{:S(2)}) copy-start(bf16[672,128]{1,0:T(8,128)(2,1)S(1)} %collective-permute-done.5) | copy-start | bytes 516100
  65.5 7.4 %copy-start.6 = (bf16[1,1344,512]{2,1,0:T(8,128)(2,1)S(1)}, bf16[1,1344,512]{2,1,0:T(8,128)(2,1)}, u32[]{:S(2)}) copy-start(bf16[1,1344,512]{2,1,0:T(8,128)(2,1)} %param.14) | copy-start | bytes 4128772
  67.5 1.5 %collective-permute-start.15 = (bf16[672,128]{1,0:T(8,128)(2,1)S(1)}, bf16[672,128]{1,0:T(8,128)(2,1)S(1)}, u32[]{:S(2)}, u32[]{:S(2)}) collective-permute-start(bf16[672,128]{1,0:T(8,128)(2,1)S(1)} %get-tuple-element.52), channel_id=1, source_target_pairs={{1,0},{0,1},{3,2},{2,3},{5,4},{4,5},{7,6},{6,7},{9,8},{8,9},{11,10... | collective-permute-start | bytes 516104 | tf_op jit(solution)/shard_map/ppermute | solution.py:223
  67.6 7.3 %collective-permute-start.11 = (bf16[672,128]{1,0:T(8,128)(2,1)S(1)}, bf16[672,128]{1,0:T(8,128)(2,1)S(1)}, u32[]{:S(2)}, u32[]{:S(2)}) collective-permute-start(bf16[672,128]{1,0:T(8,128)(2,1)S(1)} %add_convert_fusion.3), channel_id=1, source_target_pairs={{8,0},{16,8},{24,16},{0,24},{9,1},{17,9},{25,17},{1,25},{10,2},{18... | collective-permute-start | bytes 516104 | tf_op jit(solution)/shard_map/ppermute | solution.py:223
  69.0 9.0 %collective-permute-start.16 = (bf16[672,128]{1,0:T(8,128)(2,1)S(1)}, bf16[672,128]{1,0:T(8,128)(2,1)S(1)}, u32[]{:S(2)}, u32[]{:S(2)}) collective-permute-start(bf16[672,128]{1,0:T(8,128)(2,1)S(1)} %add_convert_fusion.1), channel_id=1, source_target_pairs={{8,0},{16,8},{24,16},{0,24},{9,1},{17,9},{25,17},{1,25},{10,2},{18... | collective-permute-start | bytes 516104 | tf_op jit(solution)/shard_map/ppermute | solution.py:223
  74.8 6.2 %copy-start.11 = (bf16[672,128]{1,0:T(8,128)(2,1)S(1)}, bf16[672,128]{1,0:T(8,128)(2,1)}, u32[]{:S(2)}) copy-start(bf16[672,128]{1,0:T(8,128)(2,1)} %copy-done.10) | copy-start | bytes 516100
  78.0 1.4 %collective-permute-start.17 = (bf16[672,128]{1,0:T(8,128)(2,1)S(1)}, bf16[672,128]{1,0:T(8,128)(2,1)S(1)}, u32[]{:S(2)}, u32[]{:S(2)}) collective-permute-start(bf16[672,128]{1,0:T(8,128)(2,1)S(1)} %get-tuple-element.54), channel_id=1, source_target_pairs={{1,0},{0,1},{3,2},{2,3},{5,4},{4,5},{7,6},{6,7},{9,8},{8,9},{11,10... | collective-permute-start | bytes 516104 | tf_op jit(solution)/shard_map/ppermute | solution.py:223
  79.5 6.5 %collective-permute-start.18 = (bf16[672,128]{1,0:T(8,128)(2,1)S(1)}, bf16[672,128]{1,0:T(8,128)(2,1)S(1)}, u32[]{:S(2)}, u32[]{:S(2)}) collective-permute-start(bf16[672,128]{1,0:T(8,128)(2,1)S(1)} %add_convert_fusion), channel_id=1, source_target_pairs={{8,0},{16,8},{24,16},{0,24},{9,1},{17,9},{25,17},{1,25},{10,2},{18... | collective-permute-start | bytes 516104 | tf_op jit(solution)/shard_map/ppermute | solution.py:223
  86.2 0.8 copy-start.9

commit v15 on v13

--- a/solution.py
+++ b/solution.py
@@ -288,8 +288,9 @@
     results, waiting, hops = [], [own], []
 
     def hop(blocks):
-        hops.append([passed_along(block, "section", -1) for block in blocks])
-        return list(hops[-1])
+        came = passed_along(jnp.concatenate(blocks, axis=1), "section", -1)
+        hops.append([came])
+        return [came[:, i * rows : (i + 1) * rows] for i in range(len(blocks))]
 
     by_first, by_second = own, own
     for step in range(1, shards):

time: 86.3 us -> 85.6 us (level)
  waiting for transfers between devices: 25.8 us -> 28.3 us
  starting transfers between devices: 34.3 us -> 32.3 us
  local copies, waits for them, and re-layouts: 8.35 us -> 7.02 us
    ppermute x10 -> x9, starting transfers between devices: 10.1 us -> 8.15 us  [passed_along(): lax.ppermute(block, axis, [((i - distance) % len(devices), i) for i in de...]
    unnamed x24 -> x22, local copies, waits for them, and re-layouts: 6.77 us -> 5.45 us
    ppermute x5, waiting for transfers between devices: 5.09 us -> 6.38 us  [swapped(): return lax.ppermute(block, axis, pairs)]
    ppermute x10 -> x9, waiting for transfers between devices: 7.4 us -> 8.56 us  [passed_along(): lax.ppermute(block, axis, [((i - distance) % len(devices), i) for i in de...]
  transfers between devices with their start and end apart: 19 -> 18, of which waited for: 7 -> 7; matrix products, arithmetic and copies ran while one was open for 6% -> 7% of each run, Pallas kernels for 11% -> 11%
where the time goes in v15:
time: 85.6 us; the launch traced here: 85.1 us
  starting transfers between devices  32.3 us (38%)
  waiting for transfers between devices  28.3 us (33%)
  Pallas kernels  11.8 us (14%)
  local copies, waits for them, and re-layouts  7.02 us (8%)
  other arithmetic  5.33 us (6%)
    ppermute x4, waiting for transfers between devices, moved(): lax.ppermute(block, axis, [(i, i + by) for i in range(size) if 0 <= i + b...  13.3 us
    ppermute x5, starting transfers between devices, swapped(): return lax.ppermute(block, axis, pairs)  12.2 us
    ppermute x4, starting transfers between devices, moved(): lax.ppermute(block, axis, [(i, i + by) for i in range(size) if 0 <= i + b...  12 us
    pallas_call x4, Pallas kernels, project(): pl.pallas_call(functools.partial(project_kernel, [len(block) for block in...  9.39 us
    ppermute x9, waiting for transfers between devices, passed_along(): lax.ppermute(block, axis, [((i - distance) % len(devices), i) for i in de...  8.56 us
    ppermute x9, starting transfers between devices, passed_along(): lax.ppermute(block, axis, [((i - distance) % len(devices), i) for i in de...  8.15 us
    ppermute x5, waiting for transfers between devices, swapped(): return lax.ppermute(block, axis, pairs)  6.38 us
    unnamed x22, local copies, waits for them, and re-layouts  5.45 us
  transfers between devices with their start and end apart: 18, of which 7 were waited for; matrix products, arithmetic and copies ran while one was open for 7% of the time, Pallas kernels for 11%

profile of v15, /device:TPU:0, one launch (start us, length us, event | category | flops | bytes accessed | tf_op | source)
XLA Modules:
  0.0 85.1 jit_solution(16540884321462222307)
XLA Ops:
  0.0 1.0 %pad_maximum_fusion.1.refs_2_ = bf16[128,1024]{1,0:T(8,128)(2,1)S(1)} fusion(bf16[128,512]{1,0:T(8,128)(2,1)} %bitcast.28, bf16[128,512]{1,0:T(8,128)(2,1)} %bitcast.29), kind=kLoop, calls=%fused_computation.7 | loop fusion | flops 524288 | bytes 524288 | tf_op jit(solution)/shard_map/concatenate | solution.py:247
  1.0 4.9 %collective-permute-start.1 = (bf16[128,1024]{1,0:T(8,128)(2,1)S(1)}, bf16[128,1024]{1,0:T(8,128)(2,1)S(1)}, u32[]{:S(2)}, u32[]{:S(2)}) collective-permute-start(bf16[128,1024]{1,0:T(8,128)(2,1)S(1)} %pad_maximum_fusion.1.refs_2_), channel_id=1, source_target_pairs={{0,2},{2,4},{4,6},{1,3},{3,5},{5,7},{8,10},{10,12},{12,14},{9,11},... | collective-permute-start | bytes 786440 | tf_op jit(solution)/shard_map/ppermute | solution.py:207
  6.0 4.5 %collective-permute-start = (bf16[48,1024]{1,0:T(8,128)(2,1)S(1)}, bf16[48,1024]{1,0:T(8,128)(2,1)S(1)}, u32[]{:S(2)}, u32[]{:S(2)}) collective-permute-start(bf16[48,1024]{1,0:T(8,128)(2,1)S(1)} %slice.12), channel_id=1, source_target_pairs={{0,4},{2,6},{1,5},{3,7},{8,12},{10,14},{9,13},{11,15},{16,20},{18,... | collective-permute-start | bytes 294920 | tf_op jit(solution)/shard_map/ppermute | solution.py:207
  10.5 0.8 pad_dynamic-slice_fusion
  11.2 0.7 fusion.5
  11.9 0.1 fusion.4.refs_3_
  12.0 0.0 copy-start.6
  12.0 0.9 %copy-done.6 = bf16[1,128,1024]{2,1,0:T(8,128)(2,1)S(1)} copy-done((bf16[1,128,1024]{2,1,0:T(8,128)(2,1)S(1)}, bf16[1,128,1024]{2,1,0:T(8,128)(2,1)}, u32[]{:S(2)}) %copy-start.6) | copy-done | bytes 262168
  13.0 0.9 %copy-done.7 = bf16[1,128,1024]{2,1,0:T(8,128)(2,1)S(1)} copy-done((bf16[1,128,1024]{2,1,0:T(8,128)(2,1)S(1)}, bf16[1,128,1024]{2,1,0:T(8,128)(2,1)}, u32[]{:S(2)}) %copy-start.7) | copy-done | bytes 262168
  13.9 0.1 shard_map.82
  14.0 0.0 collective-permute-done.refs_4_
  14.0 0.0 collective-permute-done.1.refs_5_
  14.0 0.0 copy-start
  14.0 2.2 %shard_map.83 = (bf16[128,1024]{1,0:T(8,128)(2,1)S(1)}, f32[128,1024]{1,0:T(8,128)S(1)}, bf16[48,1024]{1,0:T(8,128)(2,1)S(1)}, bf16[128,1024]{1,0:T(8,128)(2,1)S(1)}) custom-call(bf16[1024,128]{1,0:T(8,128)(2,1)S(1)} %get-tuple-element.32.refs_0_, bf16[1024,128]{1,0:T(8,128)(2,1)S(1)} %get-tuple-element.33.refs_1_, ...), custom_call_target="tpu_custom_call" | custom-call | flops 478150656 | bytes 1048576 | tf_op jit(solution)/shard_map/pallas_call | solution.py:100
  16.3 1.3 %collective-permute-start.2 = (bf16[128,1024]{1,0:T(8,128)(2,1)S(1)}, bf16[128,1024]{1,0:T(8,128)(2,1)S(1)}, u32[]{:S(2)}, u32[]{:S(2)}) collective-permute-start(bf16[128,1024]{1,0:T(8,128)(2,1)S(1)} %get-tuple-element.36), channel_id=1, source_target_pairs={{2,0},{4,2},{6,4},{3,1},{5,3},{7,5},{10,8},{12,10},{14,12},{11,9},... | collective-permute-start | bytes 786440 | tf_op jit(solution)/shard_map/ppermute | solution.py:207
  17.6 1.3 %collective-permute-start.3 = (bf16[48,1024]{1,0:T(8,128)(2,1)S(1)}, bf16[48,1024]{1,0:T(8,128)(2,1)S(1)}, u32[]{:S(2)}, u32[]{:S(2)}) collective-permute-start(bf16[48,1024]{1,0:T(8,128)(2,1)S(1)} %get-tuple-element.37), channel_id=1, source_target_pairs={{4,0},{6,2},{5,1},{7,3},{12,8},{14,10},{13,9},{15,11},{20,16},{22,... | collective-permute-start | bytes 294920 | tf_op jit(solution)/shard_map/ppermute | solution.py:207
  18.9 13.3 %collective-permute-done.3.refs_1_ = bf16[48,1024]{1,0:T(8,128)(2,1)S(1)} collective-permute-done((bf16[48,1024]{1,0:T(8,128)(2,1)S(1)}, bf16[48,1024]{1,0:T(8,128)(2,1)S(1)}, u32[]{:S(2)}, u32[]{:S(2)}) %collective-permute-start.3) | collective-permute-done | bytes 98336 | tf_op jit(solution)/shard_map/ppermute | solution.py:207
  32.2 0.0 collective-permute-done.2.refs_0_
  32.2 0.1 shard_map.84.refs_0_
  32.3 1.5 %collective-permute-start.7 = (bf16[128,2048]{1,0:T(8,128)(2,1)S(1)}, bf16[128,2048]{1,0:T(8,128)(2,1)}, u32[]{:S(2)}, u32[]{:S(2)}) collective-permute-start(bf16[128,2048]{1,0:T(8,128)(2,1)S(1)} %shard_map.84.refs_0_), channel_id=1, source_target_pairs={{2,4},{4,2},{3,5},{5,3},{10,12},{12,10},{11,13},{13,11},{18,20},{2... | collective-permute-start | bytes 1572872 | tf_op jit(solution)/shard_map/ppermute | solution.py:214
  33.8 0.6 collective-permute-start.6
  34.4 1.3 %copy-done.1 = bf16[1,1344,512]{2,1,0:T(8,128)(2,1)S(1)} copy-done((bf16[1,1344,512]{2,1,0:T(8,128)(2,1)S(1)}, bf16[1,1344,512]{2,1,0:T(8,128)(2,1)}, u32[]{:S(2)}) %copy-start.1) | copy-done | bytes 1376280
  35.8 1.3 %copy-done.4 = bf16[1,1344,512]{2,1,0:T(8,128)(2,1)S(1)} copy-done((bf16[1,1344,512]{2,1,0:T(8,128)(2,1)S(1)}, bf16[1,1344,512]{2,1,0:T(8,128)(2,1)}, u32[]{:S(2)}) %copy-start.4) | copy-done | bytes 1376280
  37.1 2.0 %shard_map.85 = (bf16[672,128]{1,0:T(8,128)(2,1)S(1)}, bf16[672,128]{1,0:T(8,128)(2,1)S(1)}) custom-call(s32[1]{0:T(128)} %bitcast.core_ref, bf16[128,2048]{1,0:T(8,128)(2,1)S(1)} %shard_map.84.refs_0_, bf16[1344,1024]{1,0:T(8,128)(2,1)S(1)} %bitcast.14, bf16[1344,512]{1,0:T(8,128)(2,1)S(1)} %bitcast.18, bf16[1344,512]{1,0:T(8,128)(2,1)S(1)} %bitcast.22), custom_call_target="tpu_custom_call" | custom-call | flops 704643072 | bytes 6537216 | tf_op jit(solution)/shard_map/pallas_call | solution.py:187
  39.1 0.1 collective-permute-start.4
  39.2 0.0 collective-permute-done.7.refs_1_
  39.2 5.8 %collective-permute-start.9 = (bf16[128,2048]{1,0:T(8,128)(2,1)}, bf16[128,2048]{1,0:T(8,128)(2,1)}, u32[]{:S(2)}, u32[]{:S(2)}) collective-permute-start(bf16[128,2048]{1,0:T(8,128)(2,1)} %collective-permute-done.7.refs_1_), channel_id=1, source_target_pairs={{0,2},{2,0},{4,6},{6,4},{1,3},{3,1},{5,7},{7,5},{8,10},{10,8},{12,... | collective-permute-start | bytes 1572872 | tf_op jit(solution)/shard_map/ppermute | solution.py:214
  45.0 1.2 %collective-permute-done.6.refs_0_ = bf16[128,2048]{1,0:T(8,128)(2,1)} collective-permute-done((bf16[128,2048]{1,0:T(8,128)(2,1)S(1)}, bf16[128,2048]{1,0:T(8,128)(2,1)}, u32[]{:S(2)}, u32[]{:S(2)}) %collective-permute-start.6) | collective-permute-done | bytes 524320 | tf_op jit(solution)/shard_map/ppermute | solution.py:214
  46.1 1.5 %collective-permute-start.10 = (bf16[128,2048]{1,0:T(8,128)(2,1)}, bf16[128,2048]{1,0:T(8,128)(2,1)}, u32[]{:S(2)}, u32[]{:S(2)}) collective-permute-start(bf16[128,2048]{1,0:T(8,128)(2,1)} %collective-permute-done.6.refs_0_), channel_id=1, source_target_pairs={{2,4},{4,2},{3,5},{5,3},{10,12},{12,10},{11,13},{13,11},{18,20},{2... | collective-permute-start | bytes 1572872 | tf_op jit(solution)/shard_map/ppermute | solution.py:214
  47.6 0.0 collective-permute-done.4
  47.6 0.7 add_convert_fusion.4
  48.3 3.4 %shard_map.86 = (bf16[672,128]{1,0:T(8,128)(2,1)S(1)}, bf16[672,128]{1,0:T(8,128)(2,1)S(1)}, bf16[672,128]{1,0:T(8,128)(2,1)S(1)}, bf16[672,128]{1,0:T(8,128)(2,1)S(1)}) custom-call(s32[1]{0:T(128)} %bitcast.core_ref, bf16[128,2048]{1,0:T(8,128)(2,1)} %collective-permute-done.6.refs_0_, bf16[128,2048]{1,0:T(8,128)(2,1)} %collective-permute-done.7.refs_1_, ...), custom_call_target="tpu_custom_call" | custom-call | flops 1409286144 | bytes 7569408 | tf_op jit(solution)/shard_map/pallas_call | solution.py:187
  51.7 0.1 collective-permute-start.11
  51.8 0.5 collective-permute-start.8
  52.3 2.5 %collective-permute-start.5 = (bf16[672,128]{1,0:T(8,128)(2,1)}, bf16[672,128]{1,0:T(8,128)(2,1)S(1)}, u32[]{:S(2)}, u32[]{:S(2)}) collective-permute-start(bf16[672,128]{1,0:T(8,128)(2,1)} %add_convert_fusion.4), channel_id=1, source_target_pairs={{8,0},{16,8},{24,16},{0,24},{9,1},{17,9},{25,17},{1,25},{10,2},{18... | collective-permute-start | bytes 516104 | tf_op jit(solution)/shard_map/ppermute | solution.py:223
  54.8 0.0 collective-permute-done.11
  54.8 0.9 %collective-permute-done.9 = bf16[128,2048]{1,0:T(8,128)(2,1)} collective-permute-done((bf16[128,2048]{1,0:T(8,128)(2,1)}, bf16[128,2048]{1,0:T(8,128)(2,1)}, u32[]{:S(2)}, u32[]{:S(2)}) %collective-permute-start.9) | collective-permute-done | bytes 524320 | tf_op jit(solution)/shard_map/ppermute | solution.py:214
  55.6 0.0 collective-permute-done.10
  55.6 0.0 collective-permute-done.8
  55.7 1.0 %add_convert_fusion.2 = bf16[672,128]{1,0:T(8,128)(2,1)S(1)} fusion(bf16[672,128]{1,0:T(8,128)(2,1)} %collective-permute-done.11, bf16[672,128]{1,0:T(8,128)(2,1)S(1)} %get-tuple-element.45), kind=kLoop, calls=%fused_computation.4 | loop fusion | flops 344064 | bytes 516096 | tf_op jit(solution)/shard_map/convert_element_type | solution.py:284
  56.6 0.0 copy-start.3
  56.6 0.0 copy-start.5
  56.7 1.1 %add_convert_fusion.3 = bf16[672,128]{1,0:T(8,128)(2,1)S(1)} fusion(bf16[672,128]{1,0:T(8,128)(2,1)} %collective-permute-done.8, bf16[672,128]{1,0:T(8,128)(2,1)S(1)} %get-tuple-element.42), kind=kLoop, calls=%fused_computation.5 | loop fusion | flops 344064 | bytes 516096 | tf_op jit(solution)/shard_map/convert_element_type | solution.py:284
  57.8 2.5 %collective-permute-start.12 = (bf16[672,256]{1,0:T(8,128)(2,1)S(1)}, bf16[672,256]{1,0:T(8,128)(2,1)S(1)}, u32[]{:S(2)}, u32[]{:S(2)}) collective-permute-start(bf16[672,256]{1,0:T(8,128)(2,1)S(1)} %pad_maximum_fusion), channel_id=1, source_target_pairs={{8,0},{16,8},{24,16},{0,24},{9,1},{17,9},{25,17},{1,25},{10,2},{18... | collective-permute-start | bytes 1032200 | tf_op jit(solution)/shard_map/ppermute | solution.py:223
  60.3 2.9 %collective-permute-start.13 = (bf16[128,2048]{1,0:T(8,128)(2,1)}, bf16[128,2048]{1,0:T(8,128)(2,1)S(1)}, u32[]{:S(2)}, u32[]{:S(2)}) collective-permute-start(bf16[128,2048]{1,0:T(8,128)(2,1)} %collective-permute-done.10), channel_id=1, source_target_pairs={{0,2},{2,0},{4,6},{6,4},{1,3},{3,1},{5,7},{7,5},{8,10},{10,8},{12,... | collective-permute-start | bytes 1572872 | tf_op jit(solution)/shard_map/ppermute | solution.py:214
  63.2 1.1 %broadcast_select_fusion.refs_0_ = bf16[128,2048]{1,0:T(8,128)(2,1)S(1)} fusion(bf16[128,2048]{1,0:T(8,128)(2,1)} %collective-permute-done.10, bf16[128,2048]{1,0:T(8,128)(2,1)} %collective-permute-done.9, pred[]{:T(512)S(6)} %eq.32), kind=kLoop, calls=%fused_computation | loop fusion | flops 262144 | bytes 1572865 | tf_op jit(solution)/shard_map/jit(_where)/select_n | solution.py:313
  64.3 0.0 collective-permute-done.5
  64.4 0.0 copy-start.9
  64.4 2.0 %shard_map.88 = (bf16[672,128]{1,0:T(8,128)(2,1)S(1)}, bf16[672,128]{1,0:T(8,128)(2,1)S(1)}) custom-call(s32[1]{0:T(128)} %bitcast.core_ref, bf16[128,2048]{1,0:T(8,128)(2,1)S(1)} %broadcast_select_fusion.refs_0_, bf16[1344,1024]{1,0:T(8,128)(2,1)S(1)} %bitcast.16, bf16[1344,512]{1,0:T(8,128)(2,1)S(1)} %bitcast.20, bf16[1344,512]{1,0:T(8,128)(2,1)S(1)} %bitcast.24), custom_call_target="tpu_custom_call" | custom-call | flops 1 | bytes 1 | tf_op jit(solution)/shard_map/pallas_call | solution.py:187
  66.4 0.1 collective-permute-start.14
  66.5 1.4 %collective-permute-done.14 = bf16[672,128]{1,0:T(8,128)(2,1)S(1)} collective-permute-done((bf16[672,128]{1,0:T(8,128)(2,1)S(1)}, bf16[672,128]{1,0:T(8,128)(2,1)S(1)}, u32[]{:S(2)}, u32[]{:S(2)}) %collective-permute-start.14) | collective-permute-done | bytes 172064 | tf_op jit(solution)/shard_map/ppermute | solution.py:223
  67.9 1.8 %collective-permute-start.15 = (bf16[672,128]{1,0:T(8,128)(2,1)S(1)}, bf16[672,128]{1,0:T(8,128)(2,1)S(1)}, u32[]{:S(2)}, u32[]{:S(2)}) collective-permute-start(bf16[672,128]{1,0:T(8,128)(2,1)S(1)} %add_convert_fusion.1), channel_id=1, source_target_pairs={{8,0},{16,8},{24,16},{0,24},{9,1},{17,9},{25,17},{1,25},{10,2},{18... | collective-permute-start | bytes 516104 | tf_op jit(solution)/shard_map/ppermute | solution.py:223
  69.7 4.3 %collective-permute-done.13.refs_0_ = bf16[128,2048]{1,0:T(8,128)(2,1)S(1)} collective-permute-done((bf16[128,2048]{1,0:T(8,128)(2,1)}, bf16[128,2048]{1,0:T(8,128)(2,1)S(1)}, u32[]{:S(2)}, u32[]{:S(2)}) %collective-permute-start.13) | collective-permute-done | bytes 524320 | tf_op jit(solution)/shard_map/ppermute | solution.py:214
  74.0 2.0 %shard_map.87 = (bf16[672,128]{1,0:T(8,128)(2,1)S(1)}, bf16[672,128]{1,0:T(8,128)(2,1)S(1)}) custom-call(s32[1]{0:T(128)} %bitcast.core_ref, bf16[128,2048]{1,0:T(8,128)(2,1)S(1)} %collective-permute-done.13.refs_0_, bf16[1344,1024]{1,0:T(8,128)(2,1)S(1)} %bitcast.17, bf16[1344,512]{1,0:T(8,128)(2,1)S(1)} %bitcast.21, bf16[1344,512]{1,0:T(8,128)(2,1)S(1)} %bitcast.25), custom_call_target="tpu_custom_call" | custom-call | flops 704643072 | bytes 6537216 | tf_op jit(solution)/shard_map/pallas_call | solution.py:187
  76.0 0.0 copy-start.10
  76.0 0.0 collective-permute-done.15
  76.0 0.1 collective-permute-start.16
  76.1 1.4 %collective-permute-done.16 = bf16[672,128]{1,0:T(8,128)(2,1)S(1)} collective-permute-done((bf16[672,128]{1,0:T(8,128)(2,1)S(1)}, bf16[672,128]{1,0:T(8,128)(2,1)S(1)}, u32[]{:S(2)}, u32[]{:S(2)}) %collective-permute-start.16) | collective-permute-done | bytes 172064 | tf_op jit(solution)/shard_map/ppermute | solution.py:223
  77.6 0.6 collective-permute-start.17
  78.3 5.8 %collective-permute-done.17 = bf16[672,128]{1,0:T(8,128)(2,1)S(1)} collective-permute-done((bf16[672,128]{1,0:T(8,128)(2,1)S(1)}, bf16[672,128]{1,0:T(8,128)(2,1)S(1)}, u32[]{:S(2)}, u32[]{:S(2)}) %collective-permute-start.17) | collective-permute-done | bytes 172064 | tf_op jit(solution)/shard_map/ppermute | solution.py:223
  84.0 0.1 select_dynamic-update-slice_fusion.1
  84.2 0.1 select_dynamic-update-slice_fusion
  84.3 0.0 copy-start.8
  84.3 0.8 copy-done.8
  (19 shorter events, 0.3 us)
Async XLA Ops:
  1.0 13.0 %collective-permute-start.1 = (bf16[128,1024]{1,0:T(8,128)(2,1)S(1)}, bf16[128,1024]{1,0:T(8,128)(2,1)S(1)}, u32[]{:S(2)}, u32[]{:S(2)}) collective-permute-start(bf16[128,1024]{1,0:T(8,128)(2,1)S(1)} %pad_maximum_fusion.1.refs_2_), channel_id=1, source_target_pairs={{0,2},{2,4},{4,6},{1,3},{3,5},{5,7},{8,10},{10,12},{12,14},{9,11},... | collective-permute-start | bytes 786440 | tf_op jit(solution)/shard_map/ppermute | solution.py:207
  6.0 8.1 %collective-permute-start = (bf16[48,1024]{1,0:T(8,128)(2,1)S(1)}, bf16[48,1024]{1,0:T(8,128)(2,1)S(1)}, u32[]{:S(2)}, u32[]{:S(2)}) collective-permute-start(bf16[48,1024]{1,0:T(8,128)(2,1)S(1)} %slice.12), channel_id=1, source_target_pairs={{0,4},{2,6},{1,5},{3,7},{8,12},{10,14},{9,13},{11,15},{16,20},{18,... | collective-permute-start | bytes 294920 | tf_op jit(solution)/shard_map/ppermute | solution.py:207
  12.0 1.0 %copy-start.6 = (bf16[1,128,1024]{2,1,0:T(8,128)(2,1)S(1)}, bf16[1,128,1024]{2,1,0:T(8,128)(2,1)}, u32[]{:S(2)}) copy-start(bf16[1,128,1024]{2,1,0:T(8,128)(2,1)} %param.8) | copy-start | bytes 786436
  13.0 0.9 %copy-start.7 = (bf16[1,128,1024]{2,1,0:T(8,128)(2,1)S(1)}, bf16[1,128,1024]{2,1,0:T(8,128)(2,1)}, u32[]{:S(2)}) copy-start(bf16[1,128,1024]{2,1,0:T(8,128)(2,1)} %param.11) | copy-start | bytes 786436
  14.0 20.4 %copy-start = (bf16[1,1344,1024]{2,1,0:T(8,128)(2,1)S(1)}, bf16[1,1344,1024]{2,1,0:T(8,128)(2,1)}, u32[]{:S(2)}) copy-start(bf16[1,1344,1024]{2,1,0:T(8,128)(2,1)} %param.12) | copy-start | bytes 8257540
  16.3 15.9 %collective-permute-start.2 = (bf16[128,1024]{1,0:T(8,128)(2,1)S(1)}, bf16[128,1024]{1,0:T(8,128)(2,1)S(1)}, u32[]{:S(2)}, u32[]{:S(2)}) collective-permute-start(bf16[128,1024]{1,0:T(8,128)(2,1)S(1)} %get-tuple-element.36), channel_id=1, source_target_pairs={{2,0},{4,2},{6,4},{3,1},{5,3},{7,5},{10,8},{12,10},{14,12},{11,9},... | collective-permute-start | bytes 786440 | tf_op jit(solution)/shard_map/ppermute | solution.py:207
  17.6 14.6 %collective-permute-start.3 = (bf16[48,1024]{1,0:T(8,128)(2,1)S(1)}, bf16[48,1024]{1,0:T(8,128)(2,1)S(1)}, u32[]{:S(2)}, u32[]{:S(2)}) collective-permute-start(bf16[48,1024]{1,0:T(8,128)(2,1)S(1)} %get-tuple-element.37), channel_id=1, source_target_pairs={{4,0},{6,2},{5,1},{7,3},{12,8},{14,10},{13,9},{15,11},{20,16},{22,... | collective-permute-start | bytes 294920 | tf_op jit(solution)/shard_map/ppermute | solution.py:207
  32.3 6.9 %collective-permute-start.7 = (bf16[128,2048]{1,0:T(8,128)(2,1)S(1)}, bf16[128,2048]{1,0:T(8,128)(2,1)}, u32[]{:S(2)}, u32[]{:S(2)}) collective-permute-start(bf16[128,2048]{1,0:T(8,128)(2,1)S(1)} %shard_map.84.refs_0_), channel_id=1, source_target_pairs={{2,4},{4,2},{3,5},{5,3},{10,12},{12,10},{11,13},{13,11},{18,20},{2... | collective-permute-start | bytes 1572872 | tf_op jit(solution)/shard_map/ppermute | solution.py:214
  33.8 12.3 %collective-permute-start.6 = (bf16[128,2048]{1,0:T(8,128)(2,1)S(1)}, bf16[128,2048]{1,0:T(8,128)(2,1)}, u32[]{:S(2)}, u32[]{:S(2)}) collective-permute-start(bf16[128,2048]{1,0:T(8,128)(2,1)S(1)} %shard_map.84.refs_0_), channel_id=1, source_target_pairs={{0,2},{2,0},{4,6},{6,4},{1,3},{3,1},{5,7},{7,5},{8,10},{10,8},{12,... | collective-permute-start | bytes 1572872 | tf_op jit(solution)/shard_map/ppermute | solution.py:214
  34.4 1.3 %copy-start.1 = (bf16[1,1344,512]{2,1,0:T(8,128)(2,1)S(1)}, bf16[1,1344,512]{2,1,0:T(8,128)(2,1)}, u32[]{:S(2)}) copy-start(bf16[1,1344,512]{2,1,0:T(8,128)(2,1)} %param.13) | copy-start | bytes 4128772
  35.8 1.3 %copy-start.4 = (bf16[1,1344,512]{2,1,0:T(8,128)(2,1)S(1)}, bf16[1,1344,512]{2,1,0:T(8,128)(2,1)}, u32[]{:S(2)}) copy-start(bf16[1,1344,512]{2,1,0:T(8,128)(2,1)} %param.14) | copy-start | bytes 4128772
  37.1 11.2 %copy-start.2 = (bf16[1,1344,512]{2,1,0:T(8,128)(2,1)S(1)}, bf16[1,1344,512]{2,1,0:T(8,128)(2,1)}, u32[]{:S(2)}) copy-start(bf16[1,1344,512]{2,1,0:T(8,128)(2,1)} %param.13) | copy-start | bytes 4128772
  39.1 8.5 %collective-permute-start.4 = (bf16[672,128]{1,0:T(8,128)(2,1)S(1)}, bf16[672,128]{1,0:T(8,128)(2,1)S(1)}, u32[]{:S(2)}, u32[]{:S(2)}) collective-permute-start(bf16[672,128]{1,0:T(8,128)(2,1)S(1)} %get-tuple-element.39), channel_id=1, source_target_pairs={{1,0},{0,1},{3,2},{2,3},{5,4},{4,5},{7,6},{6,7},{9,8},{8,9},{11,10... | collective-permute-start | bytes 516104 | tf_op jit(solution)/shard_map/ppermute | solution.py:223
  39.2 16.4 %collective-permute-start.9 = (bf16[128,2048]{1,0:T(8,128)(2,1)}, bf16[128,2048]{1,0:T(8,128)(2,1)}, u32[]{:S(2)}, u32[]{:S(2)}) collective-permute-start(bf16[128,2048]{1,0:T(8,128)(2,1)} %collective-permute-done.7.refs_1_), channel_id=1, source_target_pairs={{0,2},{2,0},{4,6},{6,4},{1,3},{3,1},{5,7},{7,5},{8,10},{10,8},{12,... | collective-permute-start | bytes 1572872 | tf_op jit(solution)/shard_map/ppermute | solution.py:214
  46.1 9.5 %collective-permute-start.10 = (bf16[128,2048]{1,0:T(8,128)(2,1)}, bf16[128,2048]{1,0:T(8,128)(2,1)}, u32[]{:S(2)}, u32[]{:S(2)}) collective-permute-start(bf16[128,2048]{1,0:T(8,128)(2,1)} %collective-permute-done.6.refs_0_), channel_id=1, source_target_pairs={{2,4},{4,2},{3,5},{5,3},{10,12},{12,10},{11,13},{13,11},{18,20},{2... | collective-permute-start | bytes 1572872 | tf_op jit(solution)/shard_map/ppermute | solution.py:214
  51.7 3.1 %collective-permute-start.11 = (bf16[672,128]{1,0:T(8,128)(2,1)S(1)}, bf16[672,128]{1,0:T(8,128)(2,1)}, u32[]{:S(2)}, u32[]{:S(2)}) collective-permute-start(bf16[672,128]{1,0:T(8,128)(2,1)S(1)} %get-tuple-element.46), channel_id=1, source_target_pairs={{1,0},{0,1},{3,2},{2,3},{5,4},{4,5},{7,6},{6,7},{9,8},{8,9},{11,10... | collective-permute-start | bytes 516104 | tf_op jit(solution)/shard_map/ppermute | solution.py:223
  51.8 3.9 %collective-permute-start.8 = (bf16[672,128]{1,0:T(8,128)(2,1)S(1)}, bf16[672,128]{1,0:T(8,128)(2,1)}, u32[]{:S(2)}, u32[]{:S(2)}) collective-permute-start(bf16[672,128]{1,0:T(8,128)(2,1)S(1)} %get-tuple-element.43), channel_id=1, source_target_pairs={{1,0},{0,1},{3,2},{2,3},{5,4},{4,5},{7,6},{6,7},{9,8},{8,9},{11,10... | collective-permute-start | bytes 516104 | tf_op jit(solution)/shard_map/ppermute | solution.py:223
  52.3 12.0 %collective-permute-start.5 = (bf16[672,128]{1,0:T(8,128)(2,1)}, bf16[672,128]{1,0:T(8,128)(2,1)S(1)}, u32[]{:S(2)}, u32[]{:S(2)}) collective-permute-start(bf16[672,128]{1,0:T(8,128)(2,1)} %add_convert_fusion.4), channel_id=1, source_target_pairs={{8,0},{16,8},{24,16},{0,24},{9,1},{17,9},{25,17},{1,25},{10,2},{18... | collective-permute-start | bytes 516104 | tf_op jit(solution)/shard_map/ppermute | solution.py:223
  56.6 7.7 %copy-start.3 = (bf16[1,1344,512]{2,1,0:T(8,128)(2,1)S(1)}, bf16[1,1344,512]{2,1,0:T(8,128)(2,1)}, u32[]{:S(2)}) copy-start(bf16[1,1344,512]{2,1,0:T(8,128)(2,1)} %param.13) | copy-start | bytes 4128772
  56.6 7.7 %copy-start.5 = (bf16[1,1344,512]{2,1,0:T(8,128)(2,1)S(1)}, bf16[1,1344,512]{2,1,0:T(8,128)(2,1)}, u32[]{:S(2)}) copy-start(bf16[1,1344,512]{2,1,0:T(8,128)(2,1)} %param.14) | copy-start | bytes 4128772
  57.8 10.0 %collective-permute-start.12 = (bf16[672,256]{1,0:T(8,128)(2,1)S(1)}, bf16[672,256]{1,0:T(8,128)(2,1)S(1)}, u32[]{:S(2)}, u32[]{:S(2)}) collective-permute-start(bf16[672,256]{1,0:T(8,128)(2,1)S(1)} %pad_maximum_fusion), channel_id=1, source_target_pairs={{8,0},{16,8},{24,16},{0,24},{9,1},{17,9},{25,17},{1,25},{10,2},{18... | collective-permute-start | bytes 1032200 | tf_op jit(solution)/shard_map/ppermute | solution.py:223
  60.3 13.7 %collective-permute-start.13 = (bf16[128,2048]{1,0:T(8,128)(2,1)}, bf16[128,2048]{1,0:T(8,128)(2,1)S(1)}, u32[]{:S(2)}, u32[]{:S(2)}) collective-permute-start(bf16[128,2048]{1,0:T(8,128)(2,1)} %collective-permute-done.10), channel_id=1, source_target_pairs={{0,2},{2,0},{4,6},{6,4},{1,3},{3,1},{5,7},{7,5},{8,10},{10,8},{12,... | collective-permute-start | bytes 1572872 | tf_op jit(solution)/shard_map/ppermute | solution.py:214
  64.4 2.0 %copy-start.9 = (bf16[672,128]{1,0:T(8,128)(2,1)}, bf16[672,128]{1,0:T(8,128)(2,1)S(1)}, u32[]{:S(2)}) copy-start(bf16[672,128]{1,0:T(8,128)(2,1)S(1)} %collective-permute-done.5) | copy-start | bytes 516100
  66.4 1.5 %collective-permute-start.14 = (bf16[672,128]{1,0:T(8,128)(2,1)S(1)}, bf16[672,128]{1,0:T(8,128)(2,1)S(1)}, u32[]{:S(2)}, u32[]{:S(2)}) collective-permute-start(bf16[672,128]{1,0:T(8,128)(2,1)S(1)} %get-tuple-element.52), channel_id=1, source_target_pairs={{1,0},{0,1},{3,2},{2,3},{5,4},{4,5},{7,6},{6,7},{9,8},{8,9},{11,10... | collective-permute-start | bytes 516104 | tf_op jit(solution)/shard_map/ppermute | solution.py:223
  67.9 8.1 %collective-permute-start.15 = (bf16[672,128]{1,0:T(8,128)(2,1)S(1)}, bf16[672,128]{1,0:T(8,128)(2,1)S(1)}, u32[]{:S(2)}, u32[]{:S(2)}) collective-permute-start(bf16[672,128]{1,0:T(8,128)(2,1)S(1)} %add_convert_fusion.1), channel_id=1, source_target_pairs={{8,0},{16,8},{24,16},{0,24},{9,1},{17,9},{25,17},{1,25},{10,2},{18... | collective-permute-start | bytes 516104 | tf_op jit(solution)/shard_map/ppermute | solution.py:223
  76.0 2.2 %copy-start.10 = (bf16[672,128]{1,0:T(8,128)(2,1)S(1)}, bf16[672,128]{1,0:T(8,128)(2,1)}, u32[]{:S(2)}) copy-start(bf16[672,128]{1,0:T(8,128)(2,1)} %copy-done.9) | copy-start | bytes 516100
  76.0 1.5 %collective-permute-start.16 = (bf16[672,128]{1,0:T(8,128)(2,1)S(1)}, bf16[672,128]{1,0:T(8,128)(2,1)S(1)}, u32[]{:S(2)}, u32[]{:S(2)}) collective-permute-start(bf16[672,128]{1,0:T(8,128)(2,1)S(1)} %get-tuple-element.54), channel_id=1, source_target_pairs={{1,0},{0,1},{3,2},{2,3},{5,4},{4,5},{7,6},{6,7},{9,8},{8,9},{11,10... | collective-permute-start | bytes 516104 | tf_op jit(solution)/shard_map/ppermute | solution.py:223
  77.6 6.5 %collective-permute-start.17 = (bf16[672,128]{1,0:T(8,128)(2,1)S(1)}, bf16[672,128]{1,0:T(8,128)(2,1)S(1)}, u32[]{:S(2)}, u32[]{:S(2)}) collective-permute-start(bf16[672,128]{1,0:T(8,128)(2,1)S(1)} %add_convert_fusion), channel_id=1, source_target_pairs={{8,0},{16,8},{24,16},{0,24},{9,1},{17,9},{25,17},{1,25},{10,2},{18... | collective-permute-start | bytes 516104 | tf_op jit(solution)/shard_map/ppermute | solution.py:223
  84.3 0.8 copy-start.8
